TPU v7x, 256 devices: a whole 4x4x8 slice. The times are simulated.
256 devices in a mesh: depth: 8 (over z), height: 32 (over y, x, core).
Axes of the slice: x: 4, y: 4, z: 8, core: 2. Of those that a mesh axis runs over, the one named last changes fastest.
Arguments:
- volume: float32 [256, 256, 2048], P('depth', 'height'), may hold values from -6 to 6
- colour_coef: float32 [3, 4], replicated, may hold values from -4 to 4
- opacity_coef: float32 [4], replicated, may hold values from -4 to 4
- light_dir: float32 [4, 3], replicated, may hold values from -4 to 4
- light_colour: float32 [4, 3], replicated, may hold values from 0.2 to 1.5
Outputs:
- composite_image: float32 [13, 256, 2048], P(None, 'height')
All inputs are finite; a program needn't handle non-finite values.
Results may differ from a plain program's by a relative error of at most 0.00002.
Values sent between devices are 32-bit elements; how exact they have to be, the bound alone decides.
No kernel may reach another device: no remote copies, remote signals or barrier semaphores. Data moves between devices by JAX's collectives and lax.ppermute only.
A program may use at most 128 MiB of HBM per device.

v0:
```python
import jax
import jax.numpy as jnp
from jax import lax
from jax.sharding import PartitionSpec as P


def with_halo(cells, sides, width):
    for axis, dim in sides:
        count = lax.axis_size(axis)
        ends = count - 1
        head = lax.slice_in_dim(cells, 0, width, axis=dim)
        tail = lax.slice_in_dim(cells, cells.shape[dim] - width, cells.shape[dim], axis=dim)
        cells = jnp.concatenate(
            [
                lax.ppermute(tail, axis, [(i, (i + 1) % count) for i in range(ends)]),
                cells,
                lax.ppermute(head, axis, [((i + 1) % count, i) for i in range(ends)]),
            ],
            axis=dim,
        )
    return cells


def diffuse(padded):
    centre = padded[1:-1, 1:-1]
    widened = jnp.pad(centre, ((0, 0), (0, 0), (1, 1)))
    neighbours = (
        padded[2:, 1:-1],
        padded[:-2, 1:-1],
        padded[1:-1, 2:],
        padded[1:-1, :-2],
        widened[:, :, 2:],
        widened[:, :, :-2],
    )
    flux_sum = jnp.zeros_like(centre)
    for neighbour in neighbours:
        differ = neighbour - centre
        flux_sum = flux_sum + differ / (1.0 + differ * differ)
    return centre + 0.12 * flux_sum


def slopes(padded):
    centre = padded[1:-1, 1:-1]
    widened = jnp.pad(centre, ((0, 0), (0, 0), (1, 1)))
    return (
        0.5 * (padded[2:, 1:-1] - padded[:-2, 1:-1]),
        0.5 * (padded[1:-1, 2:] - padded[1:-1, :-2]),
        0.5 * (widened[:, :, 2:] - widened[:, :, :-2]),
    )


def shade(
    values,
    grad_depth,
    grad_height,
    grad_width,
    colour_coef,
    opacity_coef,
    light_dir,
    light_colour,
    alpha_top,
):
    squared = values * values
    cubed = squared * values
    base_colour = [
        0.5
        + 0.5
        * jnp.tanh(
            colour_coef[channel, 0]
            + colour_coef[channel, 1] * values
            + colour_coef[channel, 2] * squared
            + colour_coef[channel, 3] * cubed
        )
        for channel in range(3)
    ]
    polynomial = (
        opacity_coef[0]
        + opacity_coef[1] * values
        + opacity_coef[2] * squared
        + opacity_coef[3] * cubed
    )
    strength = polynomial * polynomial
    opacity = alpha_top * strength / (1.0 + strength)
    inverse = lax.rsqrt(
        grad_depth * grad_depth + grad_height * grad_height + grad_width * grad_width + 1.0
    )
    colours = []
    for light_index in range(4):
        facing = jnp.abs(
            inverse
            * (
                grad_depth * light_dir[light_index, 0]
                + grad_height * light_dir[light_index, 1]
                + grad_width * light_dir[light_index, 2]
            )
        )
        for channel in range(3):
            colours.append(
                base_colour[channel] * light_colour[light_index, channel] * (0.2 + facing)
            )
    return (jnp.stack(colours), opacity)


def render_slab(
    smooth,
    grad_depth,
    grad_height,
    grad_width,
    colour_coef,
    opacity_coef,
    light_dir,
    light_colour,
    alpha_top,
):
    colours, opacity = shade(
        smooth,
        grad_depth,
        grad_height,
        grad_width,
        colour_coef,
        opacity_coef,
        light_dir,
        light_colour,
        alpha_top,
    )
    remaining = jnp.cumprod(1.0 - opacity, axis=0)
    before = jnp.concatenate([jnp.ones_like(remaining[:1]), remaining[:-1]], 0)
    weights = before * opacity
    colour_sum = jnp.sum(weights[None] * colours, axis=1)
    return jnp.concatenate([colour_sum, (1.0 - remaining[-1])[None]], 0)


def over(front, back):
    return front + (1.0 - front[12:13]) * back


def per_device(volume, colour_coef, opacity_coef, light_dir, light_colour):
    depth_count = lax.axis_size("depth")
    slab_cells, band_rows, width_cells = volume.shape
    alpha_top = 2.0 / (slab_cells * depth_count)

    def with_rim(cells):
        return with_halo(cells, (("depth", 0), ("height", 1)), 1)

    smooth_one = diffuse(with_rim(volume))
    smooth_two = diffuse(with_rim(smooth_one))
    padded_two = with_rim(smooth_two)
    grad_depth, grad_height, grad_width = slopes(padded_two)
    partial_value = render_slab(
        smooth_two,
        grad_depth,
        grad_height,
        grad_width,
        colour_coef,
        opacity_coef,
        light_dir,
        light_colour,
        alpha_top,
    )
    gathered = lax.all_gather(partial_value, "depth", axis=0, tiled=True).reshape(
        depth_count, 13, band_rows, width_cells
    )
    forward = gathered[0]
    for slab_index in range(1, depth_count):
        forward = over(forward, gathered[slab_index])
    return forward


def solution(mesh):
    placed = (P("depth", "height", None), P(), P(), P(), P())
    return jax.shard_map(
        per_device, mesh=mesh, in_specs=placed, out_specs=P(None, "height", None), check_vma=False
    )
```

profile of v0, /device:TPU:0, one launch (start us, length us, event | category | flops | bytes accessed | tf_op | source)
XLA Modules:
  0.0 273.8 jit_solution(13851763492206103754)
XLA Ops:
  6.5 0.9 fusion.55
  7.4 2.1 collective-permute-start.1
  9.5 1.3 collective-permute-start
  10.8 0.6 collective-permute-done.1
  11.4 1.9 constant_dynamic-update-slice_fusion.1
  13.3 2.4 collective-permute-done
  16.1 1.3 collective-permute-start.2
  17.4 3.0 %collective-permute-start.3 = (f32[34,1,2048]{2,1,0:T(1,128)S(1)}, f32[34,1,2048]{2,1,0:T(1,128)S(1)}, u32[]{:S(2)}, u32[]{:S(2)}) collective-permute-start(f32[34,1,2048]{2,1,0:T(1,128)S(1)} %get-tuple-element.12), channel_id=1, source_target_pairs={{0,1},{1,2},{2,3},{3,4},{4,5},{5,6},{6,7},{7,8},{8,9},{9,10},{10,1... | collective-permute-start | bytes 835592 | tf_op jit(solution)/shard_map/ppermute | solution.py:15
  20.4 1.1 collective-permute-done.3
  21.6 4.4 %multiply_add_fusion.1 = f32[32,8,2048]{2,1,0:T(8,128)S(1)} fusion(f32[32,8,2048]{2,1,0:T(8,128)S(1)} %copy-done.1, f32[34,8,2048]{2,1,0:T(8,128)S(1)} %constant_dynamic-update-slice_fusion, f32[34,1,2048]{2,1,0:T(1,128)S(1)} %collective-permute-done.3, f32[34,1,2048]{2,1,0:T(1,128)S(1)} %collective-permute-done.2, ...), kind=kLoop, calls=%fused_computation.87 | loop fusion | flops 18350080 | bytes 7110656 | tf_op jit(solution)/shard_map/add | solution.py:39
  26.0 3.8 %collective-permute-start.5 = (f32[1,8,2048]{2,1,0:T(8,128)S(1)}, f32[1,8,2048]{2,1,0:T(8,128)S(1)}, u32[]{:S(2)}, u32[]{:S(2)}) collective-permute-start(f32[1,8,2048]{2,1,0:T(8,128)S(1)} %get-tuple-element.15), channel_id=1, source_target_pairs={{0,32},{32,64},{64,96},{96,128},{128,160},{160,192},{192,224},{1,3... | collective-permute-start | bytes 196616 | tf_op jit(solution)/shard_map/ppermute | solution.py:15
  29.9 1.3 collective-permute-start.4
  31.2 0.7 fusion.57
  31.9 5.2 %collective-permute-done.4 = f32[1,8,2048]{2,1,0:T(8,128)S(1)} collective-permute-done((f32[1,8,2048]{2,1,0:T(8,128)S(1)}, f32[1,8,2048]{2,1,0:T(8,128)S(1)}, u32[]{:S(2)}, u32[]{:S(2)}) %collective-permute-start.4) | collective-permute-done | bytes 65568 | tf_op jit(solution)/shard_map/ppermute | solution.py:17
  37.4 1.3 collective-permute-start.6
  38.7 4.8 %collective-permute-start.7 = (f32[34,1,2048]{2,1,0:T(1,128)S(1)}, f32[34,1,2048]{2,1,0:T(1,128)S(1)}, u32[]{:S(2)}, u32[]{:S(2)}) collective-permute-start(f32[34,1,2048]{2,1,0:T(1,128)S(1)} %get-tuple-element.10), channel_id=1, source_target_pairs={{0,1},{1,2},{2,3},{3,4},{4,5},{5,6},{6,7},{7,8},{8,9},{9,10},{10,1... | collective-permute-start | bytes 835592 | tf_op jit(solution)/shard_map/ppermute | solution.py:15
  43.6 0.7 fusion.59
  51.8 0.7 fusion.58
  52.5 0.7 fusion.56
  53.2 5.4 %multiply_add_fusion = f32[32,8,2048]{2,1,0:T(8,128)S(1)} fusion(f32[32,8,2048]{2,1,0:T(8,128)S(1)} %multiply_add_fusion.1, f32[1,8,2048]{2,1,0:T(8,128)S(1)} %collective-permute-done.4, f32[1,8,2048]{2,1,0:T(8,128)S(1)} %collective-permute-done.5, f32[34,1,2048]{2,1,0:T(1,128)S(1)} %collective-permute-done.7, f32[34,1,2048]{2,1,0:T(1,128)S(1)} %collective-permute-done.6), kind=kLoop, calls=%fused_computation.86 | loop fusion | flops 20447232 | bytes 4882432 | tf_op jit(solution)/shard_map/add | solution.py:39
  58.6 5.1 %collective-permute-start.9 = (f32[1,8,2048]{2,1,0:T(8,128)S(1)}, f32[1,8,2048]{2,1,0:T(8,128)S(1)}, u32[]{:S(2)}, u32[]{:S(2)}) collective-permute-start(f32[1,8,2048]{2,1,0:T(8,128)S(1)} %get-tuple-element.13), channel_id=1, source_target_pairs={{0,32},{32,64},{64,96},{96,128},{128,160},{160,192},{192,224},{1,3... | collective-permute-start | bytes 196616 | tf_op jit(solution)/shard_map/ppermute | solution.py:15
  63.7 1.3 collective-permute-start.8
  65.0 4.1 %fusion.33 = f32[32,8,2048]{2,1,0:T(8,128)S(1)} fusion(f32[32,8,2048]{2,1,0:T(8,128)S(1)} %multiply_add_fusion, f32[]{:T(128)} %bitcast.3, f32[]{:T(128)} %bitcast.2, f32[]{:T(128)} %bitcast.1, f32[]{:T(128)} %bitcast), kind=kOutput, calls=%fused_computation.83 | output fusion | flops 23068672 | bytes 4194320 | tf_op jit(solution)/shard_map/jit(cumprod)/reduce_window | solution.py:126
  69.3 8.9 %pad_multiply_fusion = f32[32,8,2048]{2,1,0:T(8,128)S(1)} fusion(f32[31,8,2048]{2,1,0:T(8,128)S(1)} %slice.373, f32[]{:T(128)} %bitcast.3, f32[]{:T(128)} %bitcast.2, f32[]{:T(128)} %bitcast.1, f32[]{:T(128)} %bitcast, f32[32,8,2048]{2,1,0:T(8,128)S(1)} %multiply_add_fusion.1, f32[1,8,2048]{2,1,0:T(8,128)S(1)} %collective-permute-done.4, ...), kind=kLoop, calls=%fused_computation.82 | loop fusion | flops 27262976 | bytes 6914064 | tf_op jit(solution)/shard_map/mul | solution.py:128
  78.2 0.4 pad_maximum_fusion.23
  78.5 1.3 collective-permute-start.10
  79.8 6.1 %collective-permute-start.11 = (f32[34,1,2048]{2,1,0:T(1,128)S(1)}, f32[34,1,2048]{2,1,0:T(1,128)S(1)}, u32[]{:S(2)}, u32[]{:S(2)}) collective-permute-start(f32[34,1,2048]{2,1,0:T(1,128)S(1)} %get-tuple-element.8), channel_id=1, source_target_pairs={{0,1},{1,2},{2,3},{3,4},{4,5},{5,6},{6,7},{7,8},{8,9},{9,10},{10,1... | collective-permute-start | bytes 835592 | tf_op jit(solution)/shard_map/ppermute | solution.py:15
  85.9 0.9 collective-permute-done.11
  86.9 8.1 %bitcast_dynamic-update-slice_fusion.11 = (f32[12,32,8,2048]{3,2,1,0:T(8,128)S(1)}, f32[32,8,2048]{2,1,0:T(8,128)S(1)}) fusion(f32[]{:T(128)} %bitcast.8, f32[32,8,2048]{2,1,0:T(8,128)S(1)} %multiply_add_fusion, f32[]{:T(128)} %bitcast.7, f32[]{:T(128)} %bitcast.6, f32[]{:T(128)} %bitcast.5, f32[]{:T(128)} %bitcast.4, f32[]{:T(128)} %bitcast.11, ...), kind=kLoop, calls=%fused_computation.76 | loop fusion | flops 20971520 | bytes 6979616
  95.0 6.3 %bitcast_dynamic-update-slice_fusion.10 = f32[12,32,8,2048]{3,2,1,0:T(8,128)S(1)} fusion(f32[12,32,8,2048]{3,2,1,0:T(8,128)S(1)} %get-tuple-element.5, f32[]{:T(128)} %bitcast.17, f32[32,8,2048]{2,1,0:T(8,128)S(1)} %multiply_add_fusion, f32[]{:T(128)} %bitcast.16, f32[]{:T(128)} %bitcast.15, f32[]{:T(128)} %bitcast.14, f32[]{:T(128)} %bitcast.13, ...), kind=kLoop, calls=%fused_computation.75 | loop fusion | flops 20447232 | bytes 6979616
  101.3 6.3 %bitcast_dynamic-update-slice_fusion.9 = f32[12,32,8,2048]{3,2,1,0:T(8,128)S(1)} fusion(f32[12,32,8,2048]{3,2,1,0:T(8,128)S(1)} %bitcast_dynamic-update-slice_fusion.10, f32[]{:T(128)} %bitcast.23, f32[32,8,2048]{2,1,0:T(8,128)S(1)} %multiply_add_fusion, f32[]{:T(128)} %bitcast.22, f32[]{:T(128)} %bitcast.21, f32[]{:T(128)} %bitcast.20, f32[]{:T(128)} %bitcast.19, ...), kind=kLoop, calls=%fused_computation.74 | loop fusion | flops 20447232 | bytes 6979616
  107.5 6.3 %bitcast_dynamic-update-slice_fusion.8 = f32[12,32,8,2048]{3,2,1,0:T(8,128)S(1)} fusion(f32[12,32,8,2048]{3,2,1,0:T(8,128)S(1)} %bitcast_dynamic-update-slice_fusion.9, f32[]{:T(128)} %bitcast.25, f32[32,8,2048]{2,1,0:T(8,128)S(1)} %multiply_add_fusion, f32[]{:T(128)} %bitcast.7, f32[]{:T(128)} %bitcast.6, f32[]{:T(128)} %bitcast.5, f32[]{:T(128)} %bitcast.4, ...), kind=kLoop, calls=%fused_computation.73 | loop fusion | flops 20447232 | bytes 6979616
  113.8 6.1 %bitcast_dynamic-update-slice_fusion.7 = f32[12,32,8,2048]{3,2,1,0:T(8,128)S(1)} fusion(f32[12,32,8,2048]{3,2,1,0:T(8,128)S(1)} %bitcast_dynamic-update-slice_fusion.8, f32[]{:T(128)} %bitcast.30, f32[32,8,2048]{2,1,0:T(8,128)S(1)} %multiply_add_fusion, f32[]{:T(128)} %bitcast.16, f32[]{:T(128)} %bitcast.15, f32[]{:T(128)} %bitcast.14, f32[]{:T(128)} %bitcast.13, ...), kind=kLoop, calls=%fused_computation.72 | loop fusion | flops 20447232 | bytes 6979616
  120.0 6.2 %bitcast_dynamic-update-slice_fusion.6 = f32[12,32,8,2048]{3,2,1,0:T(8,128)S(1)} fusion(f32[12,32,8,2048]{3,2,1,0:T(8,128)S(1)} %bitcast_dynamic-update-slice_fusion.7, f32[]{:T(128)} %bitcast.32, f32[32,8,2048]{2,1,0:T(8,128)S(1)} %multiply_add_fusion, f32[]{:T(128)} %bitcast.22, f32[]{:T(128)} %bitcast.21, f32[]{:T(128)} %bitcast.20, f32[]{:T(128)} %bitcast.19, ...), kind=kLoop, calls=%fused_computation.71 | loop fusion | flops 20447232 | bytes 6979616
  126.2 6.4 %bitcast_dynamic-update-slice_fusion.5 = f32[12,32,8,2048]{3,2,1,0:T(8,128)S(1)} fusion(f32[12,32,8,2048]{3,2,1,0:T(8,128)S(1)} %bitcast_dynamic-update-slice_fusion.6, f32[]{:T(128)} %bitcast.34, f32[32,8,2048]{2,1,0:T(8,128)S(1)} %multiply_add_fusion, f32[]{:T(128)} %bitcast.7, f32[]{:T(128)} %bitcast.6, f32[]{:T(128)} %bitcast.5, f32[]{:T(128)} %bitcast.4, ...), kind=kLoop, calls=%fused_computation.70 | loop fusion | flops 20447232 | bytes 6979616
  132.6 6.4 %bitcast_dynamic-update-slice_fusion.4 = f32[12,32,8,2048]{3,2,1,0:T(8,128)S(1)} fusion(f32[12,32,8,2048]{3,2,1,0:T(8,128)S(1)} %bitcast_dynamic-update-slice_fusion.5, f32[]{:T(128)} %bitcast.39, f32[32,8,2048]{2,1,0:T(8,128)S(1)} %multiply_add_fusion, f32[]{:T(128)} %bitcast.16, f32[]{:T(128)} %bitcast.15, f32[]{:T(128)} %bitcast.14, f32[]{:T(128)} %bitcast.13, ...), kind=kLoop, calls=%fused_computation.69 | loop fusion | flops 20447232 | bytes 6979616
  139.0 6.2 %bitcast_dynamic-update-slice_fusion.3 = f32[12,32,8,2048]{3,2,1,0:T(8,128)S(1)} fusion(f32[12,32,8,2048]{3,2,1,0:T(8,128)S(1)} %bitcast_dynamic-update-slice_fusion.4, f32[]{:T(128)} %bitcast.41, f32[32,8,2048]{2,1,0:T(8,128)S(1)} %multiply_add_fusion, f32[]{:T(128)} %bitcast.22, f32[]{:T(128)} %bitcast.21, f32[]{:T(128)} %bitcast.20, f32[]{:T(128)} %bitcast.19, ...), kind=kLoop, calls=%fused_computation.68 | loop fusion | flops 20447232 | bytes 6979616
  145.3 6.3 %bitcast_dynamic-update-slice_fusion.2 = f32[12,32,8,2048]{3,2,1,0:T(8,128)S(1)} fusion(f32[12,32,8,2048]{3,2,1,0:T(8,128)S(1)} %bitcast_dynamic-update-slice_fusion.3, f32[]{:T(128)} %bitcast.43, f32[32,8,2048]{2,1,0:T(8,128)S(1)} %multiply_add_fusion, f32[]{:T(128)} %bitcast.7, f32[]{:T(128)} %bitcast.6, f32[]{:T(128)} %bitcast.5, f32[]{:T(128)} %bitcast.4, ...), kind=kLoop, calls=%fused_computation.67 | loop fusion | flops 20447232 | bytes 6979616
  151.6 6.3 %bitcast_dynamic-update-slice_fusion.1 = f32[12,32,8,2048]{3,2,1,0:T(8,128)S(1)} fusion(f32[12,32,8,2048]{3,2,1,0:T(8,128)S(1)} %bitcast_dynamic-update-slice_fusion.2, f32[]{:T(128)} %bitcast.48, f32[32,8,2048]{2,1,0:T(8,128)S(1)} %multiply_add_fusion, f32[]{:T(128)} %bitcast.16, f32[]{:T(128)} %bitcast.15, f32[]{:T(128)} %bitcast.14, f32[]{:T(128)} %bitcast.13, ...), kind=kLoop, calls=%fused_computation.66 | loop fusion | flops 20447232 | bytes 6979616
  157.9 6.1 %bitcast_dynamic-update-slice_fusion = f32[12,32,8,2048]{3,2,1,0:T(8,128)S(1)} fusion(f32[12,32,8,2048]{3,2,1,0:T(8,128)S(1)} %bitcast_dynamic-update-slice_fusion.1, f32[]{:T(128)} %bitcast.50, f32[32,8,2048]{2,1,0:T(8,128)S(1)} %multiply_add_fusion, f32[]{:T(128)} %bitcast.22, f32[]{:T(128)} %bitcast.21, f32[]{:T(128)} %bitcast.20, f32[]{:T(128)} %bitcast.19, ...), kind=kLoop, calls=%fused_computation.65 | loop fusion | flops 20447232 | bytes 6979616 | tf_op jit(solution)/shard_map/stack | solution.py:101
  164.0 3.7 %multiply_reduce_fusion = f32[12,8,2048]{2,1,0:T(8,128)S(1)} fusion(f32[12,32,8,2048]{3,2,1,0:T(8,128)S(1)} %bitcast_dynamic-update-slice_fusion, f32[32,8,2048]{2,1,0:T(8,128)S(1)} %pad_multiply_fusion), kind=kLoop, calls=%fused_computation | loop fusion | flops 12386304 | bytes 28049408 | tf_op jit(solution)/shard_map/reduce_sum | solution.py:129
  167.7 1.0 pad_maximum_fusion.20
  168.7 90.9 %all-gather.2.cloned.1.call-done = f32[104,8,2048]{2,1,0:T(8,128)} async-done(((f32[13,8,2048]{2,1,0:T(8,128)}), f32[104,8,2048]{2,1,0:T(8,128)}) %all-gather.2.cloned.1.call-update) | async-done | bytes 6815760 | tf_op jit(solution)/shard_map/all_gather | solution.py:160
  259.6 0.8 fusion.49
  260.4 1.7 fusion.42
  262.1 2.1 fusion.41
  264.3 1.3 fusion.40
  266.0 1.0 fusion.36
  (38 shorter events, 1.4 us)
Async XLA Ops:
  6.5 253.1 %all-gather.2.cloned.1.call-start = ((), (), s32[]{:S(2)}) async-start(), calls=%async_computation | async-start | bytes 7667712 | tf_op jit(solution)/shard_map/all_gather | solution.py:160
  7.4 4.0 %collective-permute-start.1 = (f32[1,8,2048]{2,1,0:T(8,128)S(1)}, f32[1,8,2048]{2,1,0:T(8,128)S(1)}, u32[]{:S(2)}, u32[]{:S(2)}) collective-permute-start(f32[1,8,2048]{2,1,0:T(8,128)S(1)} %get-tuple-element.18), channel_id=1, source_target_pairs={{0,32},{32,64},{64,96},{96,128},{128,160},{160,192},{192,224},{1,3... | collective-permute-start | bytes 196616 | tf_op jit(solution)/shard_map/ppermute | solution.py:15
  9.5 6.2 %collective-permute-start = (f32[1,8,2048]{2,1,0:T(8,128)S(1)}, f32[1,8,2048]{2,1,0:T(8,128)S(1)}, u32[]{:S(2)}, u32[]{:S(2)}) collective-permute-start(f32[1,8,2048]{2,1,0:T(8,128)S(1)} %get-tuple-element.17), channel_id=1, source_target_pairs={{32,0},{64,32},{96,64},{128,96},{160,128},{192,160},{224,192},{33,... | collective-permute-start | bytes 196616 | tf_op jit(solution)/shard_map/ppermute | solution.py:17
  11.4 10.2 %copy-start.1 = (f32[32,8,2048]{2,1,0:T(8,128)S(1)}, f32[32,8,2048]{2,1,0:T(8,128)}, u32[]{:S(2)}) copy-start(f32[32,8,2048]{2,1,0:T(8,128)} %param.5) | copy-start | bytes 6291460
  16.1 4.4 %collective-permute-start.2 = (f32[34,1,2048]{2,1,0:T(1,128)S(1)}, f32[34,1,2048]{2,1,0:T(1,128)S(1)}, u32[]{:S(2)}, u32[]{:S(2)}) collective-permute-start(f32[34,1,2048]{2,1,0:T(1,128)S(1)} %get-tuple-element.11), channel_id=1, source_target_pairs={{1,0},{2,1},{3,2},{4,3},{5,4},{6,5},{7,6},{8,7},{9,8},{10,9},{11,1... | collective-permute-start | bytes 835592 | tf_op jit(solution)/shard_map/ppermute | solution.py:17
  17.4 13.8 %copy-start.2 = (f32[4,3]{1,0:T(4,128)S(1)}, f32[4,3]{1,0:T(4,128)}, u32[]{:S(2)}) copy-start(f32[4,3]{1,0:T(4,128)} %param.8) | copy-start | bytes 148
  17.4 4.2 %collective-permute-start.3 = (f32[34,1,2048]{2,1,0:T(1,128)S(1)}, f32[34,1,2048]{2,1,0:T(1,128)S(1)}, u32[]{:S(2)}, u32[]{:S(2)}) collective-permute-start(f32[34,1,2048]{2,1,0:T(1,128)S(1)} %get-tuple-element.12), channel_id=1, source_target_pairs={{0,1},{1,2},{2,3},{3,4},{4,5},{5,6},{6,7},{7,8},{8,9},{9,10},{10,1... | collective-permute-start | bytes 835592 | tf_op jit(solution)/shard_map/ppermute | solution.py:15
  26.0 17.6 %copy-start.5 = (f32[4]{0:T(128)S(1)}, f32[4]{0:T(128)}, u32[]{:S(2)}) copy-start(f32[4]{0:T(128)} %param.7) | copy-start | bytes 52
  26.0 25.8 %copy-start.3 = (f32[3,4]{1,0:T(4,128)S(1)}, f32[3,4]{1,0:T(4,128)}, u32[]{:S(2)}) copy-start(f32[3,4]{1,0:T(4,128)} %param.6) | copy-start | bytes 148
  26.0 26.4 %copy-start.4 = (f32[4,3]{1,0:T(4,128)S(1)}, f32[4,3]{1,0:T(4,128)}, u32[]{:S(2)}) copy-start(f32[4,3]{1,0:T(4,128)} %param.9) | copy-start | bytes 148
  26.0 5.8 %collective-permute-start.5 = (f32[1,8,2048]{2,1,0:T(8,128)S(1)}, f32[1,8,2048]{2,1,0:T(8,128)S(1)}, u32[]{:S(2)}, u32[]{:S(2)}) collective-permute-start(f32[1,8,2048]{2,1,0:T(8,128)S(1)} %get-tuple-element.15), channel_id=1, source_target_pairs={{0,32},{32,64},{64,96},{96,128},{128,160},{160,192},{192,224},{1,3... | collective-permute-start | bytes 196616 | tf_op jit(solution)/shard_map/ppermute | solution.py:15
  29.9 7.2 %collective-permute-start.4 = (f32[1,8,2048]{2,1,0:T(8,128)S(1)}, f32[1,8,2048]{2,1,0:T(8,128)S(1)}, u32[]{:S(2)}, u32[]{:S(2)}) collective-permute-start(f32[1,8,2048]{2,1,0:T(8,128)S(1)} %get-tuple-element.16), channel_id=1, source_target_pairs={{32,0},{64,32},{96,64},{128,96},{160,128},{192,160},{224,192},{33,... | collective-permute-start | bytes 196616 | tf_op jit(solution)/shard_map/ppermute | solution.py:17
  37.4 15.7 %collective-permute-start.6 = (f32[34,1,2048]{2,1,0:T(1,128)S(1)}, f32[34,1,2048]{2,1,0:T(1,128)S(1)}, u32[]{:S(2)}, u32[]{:S(2)}) collective-permute-start(f32[34,1,2048]{2,1,0:T(1,128)S(1)} %get-tuple-element.9), channel_id=1, source_target_pairs={{1,0},{2,1},{3,2},{4,3},{5,4},{6,5},{7,6},{8,7},{9,8},{10,9},{11,1... | collective-permute-start | bytes 835592 | tf_op jit(solution)/shard_map/ppermute | solution.py:17
  38.7 14.4 %collective-permute-start.7 = (f32[34,1,2048]{2,1,0:T(1,128)S(1)}, f32[34,1,2048]{2,1,0:T(1,128)S(1)}, u32[]{:S(2)}, u32[]{:S(2)}) collective-permute-start(f32[34,1,2048]{2,1,0:T(1,128)S(1)} %get-tuple-element.10), channel_id=1, source_target_pairs={{0,1},{1,2},{2,3},{3,4},{4,5},{5,6},{6,7},{7,8},{8,9},{9,10},{10,1... | collective-permute-start | bytes 835592 | tf_op jit(solution)/shard_map/ppermute | solution.py:15
  58.6 19.6 %collective-permute-start.9 = (f32[1,8,2048]{2,1,0:T(8,128)S(1)}, f32[1,8,2048]{2,1,0:T(8,128)S(1)}, u32[]{:S(2)}, u32[]{:S(2)}) collective-permute-start(f32[1,8,2048]{2,1,0:T(8,128)S(1)} %get-tuple-element.13), channel_id=1, source_target_pairs={{0,32},{32,64},{64,96},{96,128},{128,160},{160,192},{192,224},{1,3... | collective-permute-start | bytes 196616 | tf_op jit(solution)/shard_map/ppermute | solution.py:15
  63.7 14.4 %collective-permute-start.8 = (f32[1,8,2048]{2,1,0:T(8,128)S(1)}, f32[1,8,2048]{2,1,0:T(8,128)S(1)}, u32[]{:S(2)}, u32[]{:S(2)}) collective-permute-start(f32[1,8,2048]{2,1,0:T(8,128)S(1)} %get-tuple-element.14), channel_id=1, source_target_pairs={{32,0},{64,32},{96,64},{128,96},{160,128},{192,160},{224,192},{33,... | collective-permute-start | bytes 196616 | tf_op jit(solution)/shard_map/ppermute | solution.py:17
  78.5 7.4 %collective-permute-start.10 = (f32[34,1,2048]{2,1,0:T(1,128)S(1)}, f32[34,1,2048]{2,1,0:T(1,128)S(1)}, u32[]{:S(2)}, u32[]{:S(2)}) collective-permute-start(f32[34,1,2048]{2,1,0:T(1,128)S(1)} %get-tuple-element.7), channel_id=1, source_target_pairs={{1,0},{2,1},{3,2},{4,3},{5,4},{6,5},{7,6},{8,7},{9,8},{10,9},{11,1... | collective-permute-start | bytes 835592 | tf_op jit(solution)/shard_map/ppermute | solution.py:17
  79.8 7.0 %collective-permute-start.11 = (f32[34,1,2048]{2,1,0:T(1,128)S(1)}, f32[34,1,2048]{2,1,0:T(1,128)S(1)}, u32[]{:S(2)}, u32[]{:S(2)}) collective-permute-start(f32[34,1,2048]{2,1,0:T(1,128)S(1)} %get-tuple-element.8), channel_id=1, source_target_pairs={{0,1},{1,2},{2,3},{3,4},{4,5},{5,6},{6,7},{7,8},{8,9},{9,10},{10,1... | collective-permute-start | bytes 835592 | tf_op jit(solution)/shard_map/ppermute | solution.py:15
  260.4 5.1 %copy-start = (f32[104,8,2048]{2,1,0:T(8,128)S(1)}, f32[104,8,2048]{2,1,0:T(8,128)}, u32[]{:S(2)}) copy-start(f32[104,8,2048]{2,1,0:T(8,128)} %all-gather.2.cloned.1.call-done) | copy-start | bytes 20447236
Sparse Core Ops, SparseCore 0:
  168.8 90.7 all-gather.1
where the time goes:
time: 278 us; the launch traced here: 274 us
  other arithmetic  112 us (40%)
  waiting for transfers between devices  101 us (36%)
  starting transfers between devices  32.7 us (12%)
  between operations  21.4 us (8%)
  local copies, waits for them, and re-layouts  6.11 us (2%)
    all_gather x1, waiting for transfers between devices, per_device(): lax.all_gather(partial_value, 'depth', axis=0, tiled=True)  90.9 us
    unnamed x11, other arithmetic  70.9 us
    ppermute x6, starting transfers between devices, with_halo(): lax.ppermute(tail, axis, [(i, (i + 1) % count) for i in range(ends)])  25 us
    add x2, other arithmetic, diffuse(): return centre + 0.12 * flux_sum  9.78 us
    mul x1, other arithmetic, render_slab(): weights = before * opacity  8.85 us
    ppermute x6, starting transfers between devices, with_halo(): lax.ppermute(head, axis, [((i + 1) % count, i) for i in range(ends)])  7.75 us
    ppermute x6, waiting for transfers between devices, with_halo(): lax.ppermute(head, axis, [((i + 1) % count, i) for i in range(ends)])  7.57 us
    add x7, other arithmetic, over(): return front + (1.0 - front[12:13]) * back  6.42 us
  transfers between devices with their start and end apart: 13, of which 6 were waited for; matrix products, arithmetic and copies ran while one was open for 6% of the time, Pallas kernels for 0%

commit v1 on v0

v1 whole, which is shorter than its diff:
```python
import functools

import jax
import jax.numpy as jnp
from jax import lax
from jax.experimental import pallas as pl
from jax.experimental.pallas import tpu as pltpu
from jax.sharding import PartitionSpec as P

VMEM = pltpu.VMEM
F32 = jnp.float32
LANES = 128
ROWS = 8


def flux(d):
    q = d * d + 1.0
    r = pl.reciprocal(q, approx=True)
    return d * (r * (2.0 - q * r))


def inverse_of(q):
    r = pl.reciprocal(q, approx=True)
    return r * (2.0 - q * r)


def pack_rows(vol_ref, down_ref, up_ref):
    cells, tiles = vol_ref.shape[0], vol_ref.shape[1]
    flat = vol_ref.reshape(cells * tiles * ROWS, LANES)
    stride = tiles * ROWS
    for row in range(3):
        for tile in range(tiles):
            for z in range(0, cells, 8):
                base = z * stride + tile * ROWS
                up_ref[row, tile, z : z + 8, :] = flat[pl.ds(base + row, 8, stride=stride), :]
                down_ref[row, tile, z : z + 8, :] = flat[
                    pl.ds(base + 5 + row, 8, stride=stride), :
                ]


def pack_corners(low_ref, high_ref, down_ref, up_ref):
    tiles = low_ref.shape[1]
    for tile in range(tiles):
        for slot, (ref, plane, depth) in enumerate(
            (
                (low_ref, 2, 0),
                (low_ref, 1, 0),
                (low_ref, 2, 1),
                (high_ref, 0, 0),
                (high_ref, 1, 0),
                (high_ref, 0, 1),
            )
        ):
            up_ref[tile, slot : slot + 1, :] = ref[plane, tile, depth : depth + 1, :]
            down_ref[tile, slot : slot + 1, :] = ref[plane, tile, 7 - depth : 8 - depth, :]
        for slot in (6, 7):
            up_ref[tile, slot : slot + 1, :] = jnp.zeros((1, LANES), F32)
            down_ref[tile, slot : slot + 1, :] = jnp.zeros((1, LANES), F32)


def diffuse_planes(src, dst, held, planes, rim):
    tiles = src.shape[1]
    lane = lax.broadcasted_iota(jnp.int32, (ROWS, LANES), 1)
    sub = lax.broadcasted_iota(jnp.int32, (ROWS, LANES), 0)
    last_lane, first_lane = lane == LANES - 1, lane == 0
    last_sub, first_sub = sub == ROWS - 1, sub == 0

    for tile in range(tiles):
        for part in range(2):
            held[tile, part] = flux(src[1, tile, part] - src[0, tile, part])

    def step(z, carry):
        here = z + 1
        previous = [None, None]
        now = [src[here, 0, part] for part in range(2)]
        turned = [pltpu.roll(now[part], LANES - 1, 1) for part in range(2)]
        for tile in range(tiles):
            if tile + 1 < tiles:
                later = [src[here, tile + 1, part] for part in range(2)]
                later_turned = [pltpu.roll(later[part], LANES - 1, 1) for part in range(2)]
            else:
                later = later_turned = [None, None]
            raised = [pltpu.roll(now[part], ROWS - 1, 0) for part in range(2)]
            across = []
            up = []
            for part in range(2):
                beside = jnp.where(
                    last_lane, 0.0 if later[part] is None else later_turned[part], turned[part]
                )
                across.append(flux(beside - now[part]))
                up.append(flux(jnp.where(last_sub, raised[1 - part], raised[part]) - now[part]))
            across_turned = [pltpu.roll(a, 1, 1) for a in across]
            up_turned = [pltpu.roll(a, 1, 0) for a in up]
            for part in range(2):
                left = jnp.where(
                    first_lane,
                    flux(now[part]) if previous[part] is None else previous[part],
                    across_turned[part],
                )
                below = jnp.where(first_sub, up_turned[1 - part], up_turned[part])
                ahead = flux(src[here + 1, tile, part] - now[part])
                total = ((across[part] - left) + (up[part] - below)) + (ahead - held[tile, part])
                held[tile, part] = ahead
                value = now[part] + 0.12 * total
                dst[z, tile, part] = value if part == 0 else value * rim
            previous, now, turned = across_turned, later, later_turned
        return carry

    lax.fori_loop(0, planes, step, 0)


def render(
    edge_ref,
    colour_ref,
    opacity_ref,
    dir_ref,
    light_ref,
    vol_ref,
    low_ref,
    high_ref,
    top_ref,
    bottom_ref,
    top_corner_ref,
    bottom_corner_ref,
    out_ref,
    field,
    once,
    twice,
    held,
    alpha_top,
):
    cells, tiles = vol_ref.shape[0], vol_ref.shape[1]
    sub = lax.broadcasted_iota(jnp.int32, (ROWS, LANES), 0)
    lane = lax.broadcasted_iota(jnp.int32, (ROWS, LANES), 1)
    keep_low, keep_high = edge_ref[0], edge_ref[1]
    keep_top, keep_bottom = edge_ref[2], edge_ref[3]
    rim = jnp.where(sub >= 4, jnp.full((ROWS, LANES), keep_top), jnp.full((ROWS, LANES), keep_bottom))

    for k in range(3):
        for tile in range(tiles):
            field[k, tile, 0] = low_ref[k, tile] * keep_low
            field[cells + 3 + k, tile, 0] = high_ref[k, tile] * keep_high
            field[k, tile, 1] = jnp.zeros((ROWS, LANES), F32)
            field[cells + 3 + k, tile, 1] = jnp.zeros((ROWS, LANES), F32)

    def fill(z, carry):
        for tile in range(tiles):
            field[z + 3, tile, 0] = vol_ref[z, tile]
            field[z + 3, tile, 1] = jnp.zeros((ROWS, LANES), F32)
        return carry

    lax.fori_loop(0, cells, fill, 0)
    flat = field.reshape((cells + 6) * tiles * 2 * ROWS, LANES)
    stride = tiles * 2 * ROWS
    for tile in range(tiles):
        offset = (tile * 2 + 1) * ROWS
        for row in range(3):
            for z in range(0, cells, 8):
                base = (z + 3) * stride + offset
                flat[pl.ds(base + 5 + row, 8, stride=stride), :] = (
                    top_ref[row, tile, z : z + 8, :] * keep_top
                )
                flat[pl.ds(base + row, 8, stride=stride), :] = (
                    bottom_ref[row, tile, z : z + 8, :] * keep_bottom
                )
        for slot, (plane, away) in enumerate(
            ((2, 0), (1, 0), (2, 1), (cells + 3, 0), (cells + 4, 0), (cells + 3, 1))
        ):
            keep_z = keep_low if slot < 3 else keep_high
            field[plane, tile, 1, 7 - away : 8 - away, :] = (
                top_corner_ref[tile, slot : slot + 1, :] * (keep_z * keep_top)
            )
            field[plane, tile, 1, away : away + 1, :] = (
                bottom_corner_ref[tile, slot : slot + 1, :] * (keep_z * keep_bottom)
            )

    diffuse_planes(field, once, held, cells + 4, rim)
    for k in range(2):
        for tile in range(tiles):
            for part in range(2):
                once[k, tile, part] = once[k, tile, part] * keep_low
                once[cells + 2 + k, tile, part] = once[cells + 2 + k, tile, part] * keep_high
    diffuse_planes(once, twice, held, cells + 2, rim)
    for tile in range(tiles):
        twice[0, tile, 0] = twice[0, tile, 0] * keep_low
        twice[cells + 1, tile, 0] = twice[cells + 1, tile, 0] * keep_high

    colour = [[colour_ref[c, j] for j in range(4)] for c in range(3)]
    opac = [opacity_ref[j] for j in range(4)]
    light = [[0.5 * dir_ref[l, d] for d in range(3)] for l in range(4)]

    def poly(c, v):
        return ((c[3] * v + c[2]) * v + c[1]) * v + c[0]

    def column(tile, carry):
        left_tile = jnp.maximum(tile - 1, 0)
        right_tile = jnp.minimum(tile + 1, tiles - 1)
        keep_left = jnp.where(tile > 0, 1.0, 0.0)
        keep_right = jnp.where(tile < tiles - 1, 1.0, 0.0)

        def cell(z, state):
            through, sums, base_sums = state
            v = twice[z + 1, tile, 0]
            beyond = twice[z + 1, tile, 1]
            g_z = twice[z + 2, tile, 0] - twice[z, tile, 0]
            g_h = jnp.where(
                sub == 7, pltpu.roll(beyond, 7, 0), pltpu.roll(v, 7, 0)
            ) - jnp.where(sub == 0, pltpu.roll(beyond, 1, 0), pltpu.roll(v, 1, 0))
            right = twice[z + 1, right_tile, 0] * keep_right
            left = twice[z + 1, left_tile, 0] * keep_left
            g_w = jnp.where(
                lane == LANES - 1, pltpu.roll(right, LANES - 1, 1), pltpu.roll(v, LANES - 1, 1)
            ) - jnp.where(lane == 0, pltpu.roll(left, 1, 1), pltpu.roll(v, 1, 1))
            inverse = lax.rsqrt(0.25 * (g_z * g_z + g_h * g_h + g_w * g_w) + 1.0)
            p = poly(opac, v)
            s = p * p
            opacity = (alpha_top * s) * inverse_of(1.0 + s)
            weight = through * opacity
            through = through - weight
            half = 0.5 * weight
            shaded = [half + half * jnp.tanh(poly(colour[c], v)) for c in range(3)]
            base_sums = [base_sums[c] + shaded[c] for c in range(3)]
            tilted = [inverse * shaded[c] for c in range(3)]
            new = []
            for l in range(4):
                facing = jnp.abs(g_z * light[l][0] + g_h * light[l][1] + g_w * light[l][2])
                for c in range(3):
                    new.append(sums[3 * l + c] + facing * tilted[c])
            return through, new, base_sums

        zero = jnp.zeros((ROWS, LANES), F32)
        state = (jnp.ones((ROWS, LANES), F32), [zero] * 12, [zero] * 3)

        def group(g, state):
            for k in range(4):
                state = cell(g * 4 + k, state)
            return state

        through, sums, base_sums = lax.fori_loop(0, cells // 4, group, state)
        for l in range(4):
            for c in range(3):
                out_ref[tile // 2, 3 * l + c, tile % 2] = light_ref[l, c] * (
                    0.2 * base_sums[c] + sums[3 * l + c]
                )
        out_ref[tile // 2, 12, tile % 2] = 1.0 - through
        return carry

    lax.fori_loop(0, tiles, column, 0)


def fold(parts_ref, out_ref):
    slabs, channels = parts_ref.shape[0], parts_ref.shape[1]
    for tile in range(2):
        through = 1.0 - parts_ref[0, 12, tile]
        total = [parts_ref[0, ch, tile] for ch in range(channels)]
        for slab in range(1, slabs):
            total = [total[ch] + through * parts_ref[slab, ch, tile] for ch in range(channels)]
            through = through * (1.0 - parts_ref[slab, 12, tile])
        for ch in range(channels):
            out_ref[ch, tile] = total[ch]


def spread(place_ref, *refs):
    pieces, out_ref = refs[:-1], refs[-1]
    count = len(pieces)
    channels = out_ref.shape[0]
    for step, ref in enumerate(pieces):
        offset = step if step <= count // 2 else count // 2 - step
        owner = lax.rem(place_ref[0] - offset + count, count)
        for tile in range(2):
            at = pl.multiple_of((owner * 2 + tile) * LANES, LANES)
            for ch in range(channels):
                out_ref[ch, :, pl.ds(at, LANES)] = ref[ch, tile]


def in_vmem(count):
    return [pl.BlockSpec(memory_space=VMEM)] * count


def in_smem(count):
    return [pl.BlockSpec(memory_space=pltpu.SMEM)] * count


def shape(*dims):
    return jax.ShapeDtypeStruct(dims, F32)


def ring(axis, by):
    count = lax.axis_size(axis)
    return [(i, (i + by) % count) for i in range(count)]


def per_device(volume, colour_coef, opacity_coef, light_dir, light_colour):
    slabs, bands = lax.axis_size("depth"), lax.axis_size("height")
    cells, rows, width = volume.shape
    tiles = width // LANES
    slab, band = lax.axis_index("depth"), lax.axis_index("height")
    limit = pltpu.CompilerParams(vmem_limit_bytes=56 << 20)
    field = volume.reshape(cells, rows, tiles, LANES).transpose(0, 2, 1, 3)

    low = lax.ppermute(field[cells - 3 :], "depth", ring("depth", 1))
    high = lax.ppermute(field[:3], "depth", ring("depth", -1))
    down, up = pl.pallas_call(
        pack_rows,
        out_shape=[shape(3, tiles, cells, LANES)] * 2,
        in_specs=in_vmem(1),
        out_specs=in_vmem(2),
        compiler_params=limit,
        name="pack_rows",
    )(field)
    top = lax.ppermute(down, "height", ring("height", 1))
    bottom = lax.ppermute(up, "height", ring("height", -1))
    corner_down, corner_up = pl.pallas_call(
        pack_corners,
        out_shape=[shape(tiles, rows, LANES)] * 2,
        in_specs=in_vmem(2),
        out_specs=in_vmem(2),
        compiler_params=limit,
        name="pack_corners",
    )(low, high)
    top_corner = lax.ppermute(corner_down, "height", ring("height", 1))
    bottom_corner = lax.ppermute(corner_up, "height", ring("height", -1))

    edges = jnp.stack([slab > 0, slab < slabs - 1, band > 0, band < bands - 1]).astype(F32)
    partial = pl.pallas_call(
        functools.partial(render, alpha_top=2.0 / (cells * slabs)),
        out_shape=shape(slabs, 13, tiles // slabs, rows, LANES),
        in_specs=in_smem(5) + in_vmem(7),
        out_specs=pl.BlockSpec(memory_space=VMEM),
        scratch_shapes=[
            VMEM((cells + 6, tiles, 2, rows, LANES), F32),
            VMEM((cells + 4, tiles, 2, rows, LANES), F32),
            VMEM((cells + 2, tiles, 2, rows, LANES), F32),
            VMEM((tiles, 2, rows, LANES), F32),
        ],
        compiler_params=limit,
        name="render",
    )(
        edges,
        colour_coef,
        opacity_coef,
        light_dir,
        light_colour,
        field,
        low,
        high,
        top,
        bottom,
        top_corner,
        bottom_corner,
    )
    exchanged = lax.all_to_all(partial, "depth", 0, 0, tiled=True)
    own = pl.pallas_call(
        fold,
        out_shape=shape(13, tiles // slabs, rows, LANES),
        in_specs=in_vmem(1),
        out_specs=pl.BlockSpec(memory_space=VMEM),
        compiler_params=limit,
        name="fold",
    )(exchanged)
    from_below, from_above = [own], [own]
    for _ in range(slabs // 2):
        from_below.append(lax.ppermute(from_below[-1], "depth", ring("depth", 1)))
        from_above.append(lax.ppermute(from_above[-1], "depth", ring("depth", -1)))
    pieces = from_below + from_above[1 : slabs // 2]
    return pl.pallas_call(
        spread,
        out_shape=shape(13, rows, width),
        in_specs=in_smem(1) + in_vmem(slabs),
        out_specs=pl.BlockSpec(memory_space=VMEM),
        compiler_params=limit,
        name="spread",
    )(slab[None], *pieces)


def solution(mesh):
    placed = (P("depth", "height", None), P(), P(), P(), P())
    return jax.shard_map(
        per_device, mesh=mesh, in_specs=placed, out_specs=P(None, "height", None), check_vma=False
    )
```

time: 278 us -> 126 us (0.45)
  the two profiles are of different devices: /device:TPU:0 before, /device:TPU:8 now
where the time goes in v1:
time: 126 us
  Pallas kernels  46.3 us (37%)
  blocking collectives  27.2 us (22%)
  starting transfers between devices  23.7 us (19%)
  waiting for transfers between devices  23.4 us (19%)
  local copies, waits for them, and re-layouts  4.2 us (3%)
    pallas_call x1, Pallas kernels, per_device(): pl.pallas_call(functools.partial(render, alpha_top=2.0 / (cells * slabs))...  36.8 us
    all_to_all x1, blocking collectives, per_device(): exchanged = lax.all_to_all(partial, 'depth', 0, 0, tiled=True)  27.2 us
    ppermute x4, waiting for transfers between devices, per_device(): from_below.append(lax.ppermute(from_below[-1], 'depth', ring('depth', 1)))  14.9 us
    ppermute x3, starting transfers between devices, per_device(): from_above.append(lax.ppermute(from_above[-1], 'depth', ring('depth', -1)))  9.5 us
    ppermute x1, starting transfers between devices, per_device(): high = lax.ppermute(field[:3], 'depth', ring('depth', -1))  5.93 us
    ppermute x1, starting transfers between devices, per_device(): bottom = lax.ppermute(up, 'height', ring('height', -1))  3.85 us
    ppermute x1, starting transfers between devices, per_device(): bottom_corner = lax.ppermute(corner_up, 'height', ring('height', -1))  3.85 us
    ppermute x1, waiting for transfers between devices, per_device(): low = lax.ppermute(field[cells - 3:], 'depth', ring('depth', 1))  3.69 us
  transfers between devices with their start and end apart: 13, of which 8 were waited for; matrix products, arithmetic and copies ran while one was open for 1% of the time, Pallas kernels for 1%

profile of v1, /device:TPU:8, one launch (start us, length us, event | category | flops | bytes accessed | tf_op | source)
XLA Modules:
  0.0 125.5 jit_solution(1147476716968239262)
XLA Ops:
  0.0 3.6 %pack_rows.1 = (f32[3,16,32,128]{3,2,1,0:T(8,128)}, f32[3,16,32,128]{3,2,1,0:T(8,128)}) custom-call(f32[32,16,8,128]{3,2,1,0:T(8,128)} %bitcast.8), custom_call_target="tpu_custom_call" | custom-call | tf_op jit(solution)/shard_map/pack_rows/pallas_call | solution.py:303
  3.6 0.0 collective-permute-start.2
  3.6 3.9 %collective-permute-start.3 = (f32[3,16,32,128]{3,2,1,0:T(8,128)}, f32[3,16,32,128]{3,2,1,0:T(8,128)S(1)}, u32[]{:S(2)}, u32[]{:S(2)}) collective-permute-start(f32[3,16,32,128]{3,2,1,0:T(8,128)} %get-tuple-element.10), channel_id=1, source_target_pairs={{0,31},{1,0},{2,1},{3,2},{4,3},{5,4},{6,5},{7,6},{8,7},{9,8},{10,9... | collective-permute-start | bytes 2359304 | tf_op jit(solution)/shard_map/ppermute | solution.py:312
  7.5 1.0 fusion
  8.5 5.9 %collective-permute-start.1 = (f32[3,16,8,128]{3,2,1,0:T(8,128)S(1)}, f32[3,16,8,128]{3,2,1,0:T(8,128)S(1)}, u32[]{:S(2)}, u32[]{:S(2)}) collective-permute-start(f32[3,16,8,128]{3,2,1,0:T(8,128)S(1)} %get-tuple-element.13), channel_id=1, source_target_pairs={{0,224},{32,0},{64,32},{96,64},{128,96},{160,128},{192,160},{224,1... | collective-permute-start | bytes 589832 | tf_op jit(solution)/shard_map/ppermute | solution.py:302
  14.5 0.0 collective-permute-start
  14.5 3.2 %collective-permute-done.1.high_ref = f32[3,16,8,128]{3,2,1,0:T(8,128)S(1)} collective-permute-done((f32[3,16,8,128]{3,2,1,0:T(8,128)S(1)}, f32[3,16,8,128]{3,2,1,0:T(8,128)S(1)}, u32[]{:S(2)}, u32[]{:S(2)}) %collective-permute-start.1) | collective-permute-done | bytes 196640 | tf_op jit(solution)/shard_map/ppermute | solution.py:302
  17.7 3.7 %collective-permute-done.low_ref = f32[3,16,8,128]{3,2,1,0:T(8,128)S(1)} collective-permute-done((f32[3,16,8,128]{3,2,1,0:T(8,128)S(1)}, f32[3,16,8,128]{3,2,1,0:T(8,128)S(1)}, u32[]{:S(2)}, u32[]{:S(2)}) %collective-permute-start) | collective-permute-done | bytes 196640 | tf_op jit(solution)/shard_map/ppermute | solution.py:301
  21.4 0.0 copy-done
  21.4 0.7 copy-done.1
  22.1 1.8 %pack_corners.1 = (f32[16,8,128]{2,1,0:T(8,128)}, f32[16,8,128]{2,1,0:T(8,128)}) custom-call(f32[3,16,8,128]{3,2,1,0:T(8,128)} %copy-done.1, f32[3,16,8,128]{3,2,1,0:T(8,128)} %copy-done), custom_call_target="tpu_custom_call" | custom-call | tf_op jit(solution)/shard_map/pack_corners/pallas_call | solution.py:313
  23.8 0.0 collective-permute-start.4
  23.8 3.9 %collective-permute-start.5 = (f32[16,8,128]{2,1,0:T(8,128)}, f32[16,8,128]{2,1,0:T(8,128)S(1)}, u32[]{:S(2)}, u32[]{:S(2)}) collective-permute-start(f32[16,8,128]{2,1,0:T(8,128)} %get-tuple-element.12), channel_id=1, source_target_pairs={{0,31},{1,0},{2,1},{3,2},{4,3},{5,4},{6,5},{7,6},{8,7},{9,8},{10,9... | collective-permute-start | bytes 196616 | tf_op jit(solution)/shard_map/ppermute | solution.py:322
  27.7 0.6 add_convert_fusion.edge_ref
  28.3 1.6 %collective-permute-done.4.top_corner_ref = f32[16,8,128]{2,1,0:T(8,128)S(1)} collective-permute-done((f32[16,8,128]{2,1,0:T(8,128)}, f32[16,8,128]{2,1,0:T(8,128)S(1)}, u32[]{:S(2)}, u32[]{:S(2)}) %collective-permute-start.4) | collective-permute-done | bytes 65568 | tf_op jit(solution)/shard_map/ppermute | solution.py:321
  29.8 0.1 collective-permute-done.5.bottom_corner_ref
  29.9 0.0 collective-permute-done.2.top_ref
  29.9 0.0 collective-permute-done.3.bottom_ref
  29.9 0.6 copy-done.11
  30.5 0.1 copy-done.12
  30.5 0.3 copy-done.2
  30.8 0.9 copy-done.3
  31.7 36.8 %render.1 = f32[8,13,2,8,128]{4,3,2,1,0:T(8,128)} custom-call(f32[4]{0:T(128)} %add_convert_fusion.edge_ref, f32[3,4]{1,0:T(4,128)} %colour_ref.1, f32[4]{0:T(128)} %opacity_ref.1, f32[4,3]{1,0:T(4,128)} %dir_ref.1, f32[4,3]{1,0:T(4,128)} %light_ref.1, f32[32,16,8,128]{3,2,1,0:T(8,128)} %bitcast.10, f32[3,16,8,128]{3,2,1,0:T(8,128)} %copy-done.1, ...), custom_call_target="tpu_custom_call" | custom-call | tf_op jit(solution)/shard_map/render/pallas_call | solution.py:325
  68.5 27.2 %all_to_all.5.parts_ref = f32[8,13,2,8,128]{4,3,2,1,0:T(8,128)} all-to-all(f32[8,13,2,8,128]{4,3,2,1,0:T(8,128)} %render.1), channel_id=1, replica_groups=mesh['depth'=8,'height'=32] {'depth'}, dimensions={0} | all-to-all | bytes 1703936 | tf_op jit(solution)/shard_map/all_to_all | solution.py:352
  95.7 1.9 %fold.1.refs_0_ = f32[13,2,8,128]{3,2,1,0:T(8,128)} custom-call(f32[8,13,2,8,128]{4,3,2,1,0:T(8,128)} %all_to_all.5.parts_ref), custom_call_target="tpu_custom_call" | custom-call | tf_op jit(solution)/shard_map/fold/pallas_call | solution.py:353
  97.6 0.6 collective-permute-start.6
  98.2 2.7 %collective-permute-start.10 = (f32[13,2,8,128]{3,2,1,0:T(8,128)}, f32[13,2,8,128]{3,2,1,0:T(8,128)S(1)}, u32[]{:S(2)}, u32[]{:S(2)}) collective-permute-start(f32[13,2,8,128]{3,2,1,0:T(8,128)} %fold.1.refs_0_), channel_id=1, source_target_pairs={{0,224},{32,0},{64,32},{96,64},{128,96},{160,128},{192,160},{224,1... | collective-permute-start | bytes 319496 | tf_op jit(solution)/shard_map/ppermute | solution.py:364
  100.8 3.8 %collective-permute-done.6.refs_1_ = f32[13,2,8,128]{3,2,1,0:T(8,128)S(1)} collective-permute-done((f32[13,2,8,128]{3,2,1,0:T(8,128)}, f32[13,2,8,128]{3,2,1,0:T(8,128)S(1)}, u32[]{:S(2)}, u32[]{:S(2)}) %collective-permute-start.6) | collective-permute-done | bytes 106528 | tf_op jit(solution)/shard_map/ppermute | solution.py:363
  104.6 0.0 collective-permute-start.7
  104.6 0.0 collective-permute-done.10.refs_5_
  104.6 0.0 copy-start.5
  104.6 3.4 %collective-permute-start.11 = (f32[13,2,8,128]{3,2,1,0:T(8,128)S(1)}, f32[13,2,8,128]{3,2,1,0:T(8,128)S(1)}, u32[]{:S(2)}, u32[]{:S(2)}) collective-permute-start(f32[13,2,8,128]{3,2,1,0:T(8,128)S(1)} %collective-permute-done.10.refs_5_), channel_id=1, source_target_pairs={{0,224},{32,0},{64,32},{96,64},{128,96},{160,128},{192,160},{224,1... | collective-permute-start | bytes 319496 | tf_op jit(solution)/shard_map/ppermute | solution.py:364
  108.1 2.7 %collective-permute-done.7.refs_2_ = f32[13,2,8,128]{3,2,1,0:T(8,128)S(1)} collective-permute-done((f32[13,2,8,128]{3,2,1,0:T(8,128)S(1)}, f32[13,2,8,128]{3,2,1,0:T(8,128)S(1)}, u32[]{:S(2)}, u32[]{:S(2)}) %collective-permute-start.7) | collective-permute-done | bytes 106528 | tf_op jit(solution)/shard_map/ppermute | solution.py:363
  110.8 0.0 collective-permute-start.8
  110.8 0.0 collective-permute-done.11.refs_6_
  110.8 0.0 copy-start.7
  110.8 3.4 %collective-permute-start.12 = (f32[13,2,8,128]{3,2,1,0:T(8,128)S(1)}, f32[13,2,8,128]{3,2,1,0:T(8,128)S(1)}, u32[]{:S(2)}, u32[]{:S(2)}) collective-permute-start(f32[13,2,8,128]{3,2,1,0:T(8,128)S(1)} %collective-permute-done.11.refs_6_), channel_id=1, source_target_pairs={{0,224},{32,0},{64,32},{96,64},{128,96},{160,128},{192,160},{224,1... | collective-permute-start | bytes 319496 | tf_op jit(solution)/shard_map/ppermute | solution.py:364
  114.2 2.5 %collective-permute-done.8.refs_3_ = f32[13,2,8,128]{3,2,1,0:T(8,128)S(1)} collective-permute-done((f32[13,2,8,128]{3,2,1,0:T(8,128)S(1)}, f32[13,2,8,128]{3,2,1,0:T(8,128)S(1)}, u32[]{:S(2)}, u32[]{:S(2)}) %collective-permute-start.8) | collective-permute-done | bytes 106528 | tf_op jit(solution)/shard_map/ppermute | solution.py:363
  116.7 0.0 collective-permute-start.9
  116.7 0.0 collective-permute-done.12.refs_7_
  116.7 0.0 copy-start.9
  116.8 5.9 %collective-permute-done.9.refs_4_ = f32[13,2,8,128]{3,2,1,0:T(8,128)S(1)} collective-permute-done((f32[13,2,8,128]{3,2,1,0:T(8,128)S(1)}, f32[13,2,8,128]{3,2,1,0:T(8,128)S(1)}, u32[]{:S(2)}, u32[]{:S(2)}) %collective-permute-start.9) | collective-permute-done | bytes 106528 | tf_op jit(solution)/shard_map/ppermute | solution.py:363
  122.7 0.0 copy-done.5
  122.7 0.0 copy-done.7
  122.7 0.0 copy-done.8
  122.7 0.0 copy-done.9
  122.7 0.6 copy-done.10
  123.3 2.2 %spread.1 = f32[13,8,2048]{2,1,0:T(8,128)} custom-call(s32[1]{0:T(128)} %bitcast.place_ref, f32[13,2,8,128]{3,2,1,0:T(8,128)} %fold.1.refs_0_, f32[13,2,8,128]{3,2,1,0:T(8,128)} %copy-done.4, f32[13,2,8,128]{3,2,1,0:T(8,128)} %copy-done.6, f32[13,2,8,128]{3,2,1,0:T(8,128)} %copy-done.8, f32[13,2,8,128]{3,2,1,0:T(8,128)} %copy-done.10, ...), custom_call_target="tpu_custom_call" | custom-call | tf_op jit(solution)/shard_map/spread/pallas_call | solution.py:366
  (12 shorter events, 0.0 us)
Async XLA Ops:
  3.6 26.3 %collective-permute-start.2 = (f32[3,16,32,128]{3,2,1,0:T(8,128)}, f32[3,16,32,128]{3,2,1,0:T(8,128)S(1)}, u32[]{:S(2)}, u32[]{:S(2)}) collective-permute-start(f32[3,16,32,128]{3,2,1,0:T(8,128)} %get-tuple-element.9), channel_id=1, source_target_pairs={{0,1},{1,2},{2,3},{3,4},{4,5},{5,6},{6,7},{7,8},{8,9},{9,10},{10,1... | collective-permute-start | bytes 2359304 | tf_op jit(solution)/shard_map/ppermute | solution.py:311
  3.6 26.3 %collective-permute-start.3 = (f32[3,16,32,128]{3,2,1,0:T(8,128)}, f32[3,16,32,128]{3,2,1,0:T(8,128)S(1)}, u32[]{:S(2)}, u32[]{:S(2)}) collective-permute-start(f32[3,16,32,128]{3,2,1,0:T(8,128)} %get-tuple-element.10), channel_id=1, source_target_pairs={{0,31},{1,0},{2,1},{3,2},{4,3},{5,4},{6,5},{7,6},{8,7},{9,8},{10,9... | collective-permute-start | bytes 2359304 | tf_op jit(solution)/shard_map/ppermute | solution.py:312
  8.5 9.1 %collective-permute-start.1 = (f32[3,16,8,128]{3,2,1,0:T(8,128)S(1)}, f32[3,16,8,128]{3,2,1,0:T(8,128)S(1)}, u32[]{:S(2)}, u32[]{:S(2)}) collective-permute-start(f32[3,16,8,128]{3,2,1,0:T(8,128)S(1)} %get-tuple-element.13), channel_id=1, source_target_pairs={{0,224},{32,0},{64,32},{96,64},{128,96},{160,128},{192,160},{224,1... | collective-permute-start | bytes 589832 | tf_op jit(solution)/shard_map/ppermute | solution.py:302
  14.5 6.9 %collective-permute-start = (f32[3,16,8,128]{3,2,1,0:T(8,128)S(1)}, f32[3,16,8,128]{3,2,1,0:T(8,128)S(1)}, u32[]{:S(2)}, u32[]{:S(2)}) collective-permute-start(f32[3,16,8,128]{3,2,1,0:T(8,128)S(1)} %get-tuple-element.14), channel_id=1, source_target_pairs={{0,32},{32,64},{64,96},{96,128},{128,160},{160,192},{192,224},{224... | collective-permute-start | bytes 589832 | tf_op jit(solution)/shard_map/ppermute | solution.py:301
  17.7 3.7 %copy-start = (f32[3,16,8,128]{3,2,1,0:T(8,128)}, f32[3,16,8,128]{3,2,1,0:T(8,128)S(1)}, u32[]{:S(2)}) copy-start(f32[3,16,8,128]{3,2,1,0:T(8,128)S(1)} %collective-permute-done.1.high_ref) | copy-start | bytes 589828
  21.4 0.7 copy-start.1
  23.8 6.0 %collective-permute-start.4 = (f32[16,8,128]{2,1,0:T(8,128)}, f32[16,8,128]{2,1,0:T(8,128)S(1)}, u32[]{:S(2)}, u32[]{:S(2)}) collective-permute-start(f32[16,8,128]{2,1,0:T(8,128)} %get-tuple-element.11), channel_id=1, source_target_pairs={{0,1},{1,2},{2,3},{3,4},{4,5},{5,6},{6,7},{7,8},{8,9},{9,10},{10,1... | collective-permute-start | bytes 196616 | tf_op jit(solution)/shard_map/ppermute | solution.py:321
  23.8 6.1 %collective-permute-start.5 = (f32[16,8,128]{2,1,0:T(8,128)}, f32[16,8,128]{2,1,0:T(8,128)S(1)}, u32[]{:S(2)}, u32[]{:S(2)}) collective-permute-start(f32[16,8,128]{2,1,0:T(8,128)} %get-tuple-element.12), channel_id=1, source_target_pairs={{0,31},{1,0},{2,1},{3,2},{4,3},{5,4},{6,5},{7,6},{8,7},{9,8},{10,9... | collective-permute-start | bytes 196616 | tf_op jit(solution)/shard_map/ppermute | solution.py:322
  29.8 0.6 copy-start.11
  29.9 0.6 copy-start.12
  29.9 0.9 copy-start.2
  30.8 0.9 copy-start.3
  97.6 7.0 %collective-permute-start.6 = (f32[13,2,8,128]{3,2,1,0:T(8,128)}, f32[13,2,8,128]{3,2,1,0:T(8,128)S(1)}, u32[]{:S(2)}, u32[]{:S(2)}) collective-permute-start(f32[13,2,8,128]{3,2,1,0:T(8,128)} %fold.1.refs_0_), channel_id=1, source_target_pairs={{0,32},{32,64},{64,96},{96,128},{128,160},{160,192},{192,224},{224... | collective-permute-start | bytes 319496 | tf_op jit(solution)/shard_map/ppermute | solution.py:363
  98.2 6.5 %collective-permute-start.10 = (f32[13,2,8,128]{3,2,1,0:T(8,128)}, f32[13,2,8,128]{3,2,1,0:T(8,128)S(1)}, u32[]{:S(2)}, u32[]{:S(2)}) collective-permute-start(f32[13,2,8,128]{3,2,1,0:T(8,128)} %fold.1.refs_0_), channel_id=1, source_target_pairs={{0,224},{32,0},{64,32},{96,64},{128,96},{160,128},{192,160},{224,1... | collective-permute-start | bytes 319496 | tf_op jit(solution)/shard_map/ppermute | solution.py:364
  104.6 18.0 %copy-start.4 = (f32[13,2,8,128]{3,2,1,0:T(8,128)}, f32[13,2,8,128]{3,2,1,0:T(8,128)S(1)}, u32[]{:S(2)}) copy-start(f32[13,2,8,128]{3,2,1,0:T(8,128)S(1)} %collective-permute-done.6.refs_1_) | copy-start | bytes 319492
  104.6 6.2 %collective-permute-start.7 = (f32[13,2,8,128]{3,2,1,0:T(8,128)S(1)}, f32[13,2,8,128]{3,2,1,0:T(8,128)S(1)}, u32[]{:S(2)}, u32[]{:S(2)}) collective-permute-start(f32[13,2,8,128]{3,2,1,0:T(8,128)S(1)} %collective-permute-done.6.refs_1_), channel_id=1, source_target_pairs={{0,32},{32,64},{64,96},{96,128},{128,160},{160,192},{192,224},{224... | collective-permute-start | bytes 319496 | tf_op jit(solution)/shard_map/ppermute | solution.py:363
  104.6 18.0 %copy-start.5 = (f32[13,2,8,128]{3,2,1,0:T(8,128)}, f32[13,2,8,128]{3,2,1,0:T(8,128)S(1)}, u32[]{:S(2)}) copy-start(f32[13,2,8,128]{3,2,1,0:T(8,128)S(1)} %collective-permute-done.10.refs_5_) | copy-start | bytes 319492
  104.6 6.2 %collective-permute-start.11 = (f32[13,2,8,128]{3,2,1,0:T(8,128)S(1)}, f32[13,2,8,128]{3,2,1,0:T(8,128)S(1)}, u32[]{:S(2)}, u32[]{:S(2)}) collective-permute-start(f32[13,2,8,128]{3,2,1,0:T(8,128)S(1)} %collective-permute-done.10.refs_5_), channel_id=1, source_target_pairs={{0,224},{32,0},{64,32},{96,64},{128,96},{160,128},{192,160},{224,1... | collective-permute-start | bytes 319496 | tf_op jit(solution)/shard_map/ppermute | solution.py:364
  110.8 11.8 %copy-start.6 = (f32[13,2,8,128]{3,2,1,0:T(8,128)}, f32[13,2,8,128]{3,2,1,0:T(8,128)S(1)}, u32[]{:S(2)}) copy-start(f32[13,2,8,128]{3,2,1,0:T(8,128)S(1)} %collective-permute-done.7.refs_2_) | copy-start | bytes 319492
  110.8 5.9 %collective-permute-start.8 = (f32[13,2,8,128]{3,2,1,0:T(8,128)S(1)}, f32[13,2,8,128]{3,2,1,0:T(8,128)S(1)}, u32[]{:S(2)}, u32[]{:S(2)}) collective-permute-start(f32[13,2,8,128]{3,2,1,0:T(8,128)S(1)} %collective-permute-done.7.refs_2_), channel_id=1, source_target_pairs={{0,32},{32,64},{64,96},{96,128},{128,160},{160,192},{192,224},{224... | collective-permute-start | bytes 319496 | tf_op jit(solution)/shard_map/ppermute | solution.py:363
  110.8 11.8 %copy-start.7 = (f32[13,2,8,128]{3,2,1,0:T(8,128)}, f32[13,2,8,128]{3,2,1,0:T(8,128)S(1)}, u32[]{:S(2)}) copy-start(f32[13,2,8,128]{3,2,1,0:T(8,128)S(1)} %collective-permute-done.11.refs_6_) | copy-start | bytes 319492
  110.8 5.9 %collective-permute-start.12 = (f32[13,2,8,128]{3,2,1,0:T(8,128)S(1)}, f32[13,2,8,128]{3,2,1,0:T(8,128)S(1)}, u32[]{:S(2)}, u32[]{:S(2)}) collective-permute-start(f32[13,2,8,128]{3,2,1,0:T(8,128)S(1)} %collective-permute-done.11.refs_6_), channel_id=1, source_target_pairs={{0,224},{32,0},{64,32},{96,64},{128,96},{160,128},{192,160},{224,1... | collective-permute-start | bytes 319496 | tf_op jit(solution)/shard_map/ppermute | solution.py:364
  116.7 5.9 %copy-start.8 = (f32[13,2,8,128]{3,2,1,0:T(8,128)}, f32[13,2,8,128]{3,2,1,0:T(8,128)S(1)}, u32[]{:S(2)}) copy-start(f32[13,2,8,128]{3,2,1,0:T(8,128)S(1)} %collective-permute-done.8.refs_3_) | copy-start | bytes 319492
  116.7 5.9 %collective-permute-start.9 = (f32[13,2,8,128]{3,2,1,0:T(8,128)S(1)}, f32[13,2,8,128]{3,2,1,0:T(8,128)S(1)}, u32[]{:S(2)}, u32[]{:S(2)}) collective-permute-start(f32[13,2,8,128]{3,2,1,0:T(8,128)S(1)} %collective-permute-done.8.refs_3_), channel_id=1, source_target_pairs={{0,32},{32,64},{64,96},{96,128},{128,160},{160,192},{192,224},{224... | collective-permute-start | bytes 319496 | tf_op jit(solution)/shard_map/ppermute | solution.py:363
  116.7 5.9 %copy-start.9 = (f32[13,2,8,128]{3,2,1,0:T(8,128)}, f32[13,2,8,128]{3,2,1,0:T(8,128)S(1)}, u32[]{:S(2)}) copy-start(f32[13,2,8,128]{3,2,1,0:T(8,128)S(1)} %collective-permute-done.12.refs_7_) | copy-start | bytes 319492
  122.7 0.6 copy-start.10

commit v2 on v1

v2 whole, which is shorter than its diff:
```python
import functools

import jax
import jax.numpy as jnp
from jax import lax
from jax.experimental import pallas as pl
from jax.experimental.pallas import tpu as pltpu
from jax.sharding import PartitionSpec as P

VMEM = pltpu.VMEM
DMA = pltpu.SemaphoreType.DMA
F32 = jnp.float32
LANES = 128
ROWS = 8
BAND = 8
OWN = 4


def inverse_of(q):
    return pltpu.reciprocal(q, approx=True)


def flux(d):
    return d * inverse_of(d * d + 1.0)


def pack(vol_ref, down_ref, up_ref, first_ref, last_ref, held, down, up, in_sem, edge_sem, out_sem):
    cells, tiles = vol_ref.shape[0], vol_ref.shape[1]
    groups = cells // 8
    loads = [
        pltpu.make_async_copy(vol_ref.at[pl.ds(8 * g, 8)], held.at[pl.ds(8 * g, 8)], in_sem.at[g])
        for g in range(groups)
    ]
    edges = [
        pltpu.make_async_copy(vol_ref.at[pl.ds(0, 3)], first_ref, edge_sem.at[0]),
        pltpu.make_async_copy(vol_ref.at[pl.ds(cells - 3, 3)], last_ref, edge_sem.at[1]),
    ]
    for copy in loads + edges:
        copy.start()
    stores = []
    for g in range(groups):
        loads[g].wait()
        for k in range(8):
            z = 8 * g + k
            for tile in range(tiles):
                up[tile, 3 * z : 3 * z + 3, :] = held[z, tile, 0:3, :]
                down[tile, 3 * z : 3 * z + 3, :] = held[z, tile, 5:8, :]
        part = pl.ds(24 * g, 24)
        for i, (ref, out_ref) in enumerate(((down, down_ref), (up, up_ref))):
            copy = pltpu.make_async_copy(
                ref.at[:, part, :], out_ref.at[:, part, :], out_sem.at[2 * g + i]
            )
            copy.start()
            stores.append(copy)
    for copy in stores + edges:
        copy.wait()


CORNERS = ((0, 1, 0), (0, 0, 0), (0, 1, 1), (1, 0, 0), (1, 1, 0), (1, 0, 1))


def pack_corners(low_ref, high_ref, down_ref, up_ref, near, sem):
    tiles = low_ref.shape[1]
    copies = [
        pltpu.make_async_copy(low_ref.at[pl.ds(1, 2)], near.at[0], sem.at[0]),
        pltpu.make_async_copy(high_ref.at[pl.ds(0, 2)], near.at[1], sem.at[1]),
    ]
    for copy in copies:
        copy.start()
    for copy in copies:
        copy.wait()
    zero = jnp.zeros((2, LANES), F32)
    for tile in range(tiles):
        for slot, (side, plane, depth) in enumerate(CORNERS):
            up_ref[tile, slot : slot + 1, :] = near[side, plane, tile, depth : depth + 1, :]
            down_ref[tile, slot : slot + 1, :] = near[side, plane, tile, 7 - depth : 8 - depth, :]
        up_ref[tile, 6:8, :] = zero
        down_ref[tile, 6:8, :] = zero


def beside(src, base, z, parity, nexts, befores):
    tiles = src.shape[1]
    lane = lax.broadcasted_iota(jnp.int32, (ROWS, LANES), 1)
    for part in range(2):
        rows = pl.ds(base + 8 * part, 8)
        now = src[z, 0, rows, :]
        lowered, raised = pltpu.roll(now, LANES - 1, 1), pltpu.roll(now, 1, 1)
        earlier = 0.0
        for tile in range(tiles):
            if tile + 1 < tiles:
                later = src[z, tile + 1, rows, :]
                later_lowered = pltpu.roll(later, LANES - 1, 1)
                later_raised = pltpu.roll(later, 1, 1)
            else:
                later_lowered, later_raised = 0.0, None
            nexts[parity, tile, part] = jnp.where(lane == LANES - 1, later_lowered, lowered)
            befores[parity, tile, part] = jnp.where(lane == 0, earlier, raised)
            earlier, lowered, raised = raised, later_lowered, later_raised


def diffuse_plane(src, base, z, parity, nexts, befores, held, dst, out, rims):
    tiles = src.shape[1]
    sub = lax.broadcasted_iota(jnp.int32, (ROWS, LANES), 0)
    for tile in range(tiles):
        below = None
        for part in range(2):
            first = base + 8 * part
            u = src[z, tile, pl.ds(first, 8), :]
            across = flux(nexts[parity, tile, part] - u) + flux(befores[parity, tile, part] - u)
            if first + 9 <= src.shape[2]:
                above = src[z, tile, pl.ds(first + 1, 8), :]
            else:
                above = pltpu.roll(u, ROWS - 1, 0)
            up = flux(above - u)
            turned = pltpu.roll(up, 1, 0)
            along = up - (turned if part == 0 else jnp.where(sub == 0, below, turned))
            below = turned
            ahead = flux(src[z + 1, tile, pl.ds(first, 8), :] - u)
            total = (across + along) + (ahead - held[tile, part])
            held[tile, part] = ahead
            dst[out, tile, pl.ds(8 * part, 8), :] = (u + 0.12 * total) * rims[part]


def width_slope(field, z, slope):
    tiles = field.shape[1]
    lane = lax.broadcasted_iota(jnp.int32, (ROWS, LANES), 1)
    rows = pl.ds(OWN, 8)
    now = field[z, 0, rows, :]
    lowered, raised = pltpu.roll(now, LANES - 1, 1), pltpu.roll(now, 1, 1)
    earlier = 0.0
    for tile in range(tiles):
        if tile + 1 < tiles:
            later = field[z, tile + 1, rows, :]
            later_lowered, later_raised = pltpu.roll(later, LANES - 1, 1), pltpu.roll(later, 1, 1)
        else:
            later_lowered, later_raised = 0.0, None
        slope[z, tile] = jnp.where(lane == LANES - 1, later_lowered, lowered) - jnp.where(
            lane == 0, earlier, raised
        )
        earlier, lowered, raised = raised, later_lowered, later_raised


def diffuse(src, base, dst, planes, nexts, befores, held, rims, slope=None):
    for tile in range(src.shape[1]):
        for part in range(2):
            rows = pl.ds(base + 8 * part, 8)
            held[tile, part] = flux(src[1, tile, rows, :] - src[0, tile, rows, :])
    beside(src, base, 1, 1, nexts, befores)

    def pair(g, carry):
        for k in range(2):
            z = 2 * g + k + 1
            beside(src, base, z + 1, k, nexts, befores)
            diffuse_plane(src, base, z, 1 - k, nexts, befores, held, dst, z - 1, rims)
            if slope is not None:
                width_slope(dst, jnp.maximum(z - 3, 0), slope)
        return carry

    lax.fori_loop(0, planes // 2, pair, 0)
    if slope is not None:
        width_slope(dst, planes - 2, slope)


def render(
    edge_ref,
    colour_ref,
    opacity_ref,
    dir_ref,
    light_ref,
    vol_ref,
    low_ref,
    high_ref,
    top_ref,
    bottom_ref,
    top_corner_ref,
    bottom_corner_ref,
    out_ref,
    field,
    once,
    twice,
    slope,
    nexts,
    befores,
    held,
    rows_in,
    corners_in,
    sem,
    alpha_top,
):
    cells, tiles = vol_ref.shape[0], vol_ref.shape[1]
    own = pl.ds(BAND, 8)
    copies = [
        pltpu.make_async_copy(low_ref, field.at[pl.ds(0, 3), :, own, :], sem.at[0]),
        pltpu.make_async_copy(high_ref, field.at[pl.ds(cells + 3, 3), :, own, :], sem.at[1]),
        pltpu.make_async_copy(top_corner_ref, corners_in.at[0], sem.at[2]),
        pltpu.make_async_copy(bottom_corner_ref, corners_in.at[1], sem.at[3]),
        pltpu.make_async_copy(top_ref, rows_in.at[0], sem.at[4]),
        pltpu.make_async_copy(bottom_ref, rows_in.at[1], sem.at[5]),
        pltpu.make_async_copy(vol_ref, field.at[pl.ds(3, cells), :, own, :], sem.at[6]),
    ]
    for copy in copies:
        copy.start()

    sub = lax.broadcasted_iota(jnp.int32, (ROWS, LANES), 0)
    keep_low, keep_high = edge_ref[0], edge_ref[1]
    keep_top, keep_bottom = edge_ref[2], edge_ref[3]
    rims = (
        jnp.where(sub < OWN, jnp.full((ROWS, LANES), keep_top), 1.0),
        jnp.where(sub >= OWN, jnp.full((ROWS, LANES), keep_bottom), 1.0),
    )

    zero = jnp.zeros((ROWS, LANES), F32)
    for k in range(3):
        for tile in range(tiles):
            for plane in (k, cells + 3 + k):
                field[plane, tile, 0:8, :] = zero
                field[plane, tile, 16:24, :] = zero
    for copy in copies[:4]:
        copy.wait()
    for k in range(3):
        for tile in range(tiles):
            field[k, tile, own, :] = field[k, tile, own, :] * keep_low
            field[cells + 3 + k, tile, own, :] = field[cells + 3 + k, tile, own, :] * keep_high
    for tile in range(tiles):
        for slot, (side, plane, away) in enumerate(CORNERS):
            at = (cells + 3 if side else 1) + plane
            keep = keep_high if side else keep_low
            field[at, tile, 7 - away : 8 - away, :] = corners_in[0, tile, slot : slot + 1, :] * (
                keep * keep_top
            )
            field[at, tile, 16 + away : 17 + away, :] = corners_in[
                1, tile, slot : slot + 1, :
            ] * (keep * keep_bottom)
    copies[4].wait()
    copies[5].wait()

    def rims_in(g, carry):
        at = pl.multiple_of(24 * g, 24)
        for tile in range(tiles):
            for k in range(8):
                field[8 * g + k + 3, tile, 5:8, :] = (
                    rows_in[0, tile, pl.ds(at + 3 * k, 3), :] * keep_top
                )
                field[8 * g + k + 3, tile, 16:19, :] = (
                    rows_in[1, tile, pl.ds(at + 3 * k, 3), :] * keep_bottom
                )
        return carry

    lax.fori_loop(0, cells // 8, rims_in, 0)
    copies[6].wait()

    diffuse(field, OWN, once, cells + 4, nexts, befores, held, rims)
    for k in range(2):
        for tile in range(tiles):
            for rows in (slice(0, 8), slice(8, 16)):
                once[k, tile, rows, :] = once[k, tile, rows, :] * keep_low
                once[cells + 2 + k, tile, rows, :] = once[cells + 2 + k, tile, rows, :] * keep_high
    diffuse(once, 0, twice, cells + 2, nexts, befores, held, rims, slope)
    own = pl.ds(OWN, 8)
    for tile in range(tiles):
        twice[0, tile, own, :] = twice[0, tile, own, :] * keep_low
        twice[cells + 1, tile, own, :] = twice[cells + 1, tile, own, :] * keep_high

    colour = [[colour_ref[c, j] for j in range(4)] for c in range(3)]
    opac = [opacity_ref[j] for j in range(4)]
    light = [[0.5 * dir_ref[l, d] for d in range(3)] for l in range(4)]

    def poly(c, v):
        return ((c[3] * v + c[2]) * v + c[1]) * v + c[0]

    def column(tile, carry):
        def cell(z, state):
            through, sums, base_sums = state
            v = twice[z + 1, tile, own, :]
            g_z = twice[z + 2, tile, own, :] - twice[z, tile, own, :]
            g_h = twice[z + 1, tile, pl.ds(OWN + 1, 8), :] - twice[z + 1, tile, pl.ds(OWN - 1, 8), :]
            g_w = slope[z + 1, tile]
            inverse = lax.rsqrt(0.25 * (g_z * g_z + g_h * g_h + g_w * g_w) + 1.0)
            p = poly(opac, v)
            s = p * p
            opacity = (alpha_top * s) * inverse_of(1.0 + s)
            weight = through * opacity
            through = through - weight
            half = 0.5 * weight
            shaded = [half + half * jnp.tanh(poly(colour[c], v)) for c in range(3)]
            base_sums = [base_sums[c] + shaded[c] for c in range(3)]
            tilted = [inverse * shaded[c] for c in range(3)]
            new = []
            for l in range(4):
                facing = jnp.abs(g_z * light[l][0] + g_h * light[l][1] + g_w * light[l][2])
                for c in range(3):
                    new.append(sums[3 * l + c] + facing * tilted[c])
            return through, new, base_sums

        state = (jnp.ones((ROWS, LANES), F32), [zero] * 12, [zero] * 3)

        def group(g, state):
            for k in range(4):
                state = cell(g * 4 + k, state)
            return state

        through, sums, base_sums = lax.fori_loop(0, cells // 4, group, state)
        for l in range(4):
            for c in range(3):
                out_ref[tile // 2, 3 * l + c, tile % 2] = light_ref[l, c] * (
                    0.2 * base_sums[c] + sums[3 * l + c]
                )
        out_ref[tile // 2, 12, tile % 2] = 1.0 - through
        return carry

    lax.fori_loop(0, tiles, column, 0)


def fold(parts_ref, out_ref):
    slabs, channels = parts_ref.shape[0], parts_ref.shape[1]
    for tile in range(parts_ref.shape[2]):
        through = 1.0 - parts_ref[0, 12, tile]
        total = [parts_ref[0, ch, tile] for ch in range(channels)]
        for slab in range(1, slabs):
            total = [total[ch] + through * parts_ref[slab, ch, tile] for ch in range(channels)]
            through = through * (1.0 - parts_ref[slab, 12, tile])
        for ch in range(channels):
            out_ref[ch, tile] = total[ch]


def spread(place_ref, *refs):
    pieces, out_ref, sem = refs[:-2], refs[-2], refs[-1]
    count = len(pieces)
    tiles = out_ref.shape[1] // count
    copies = []
    for step, ref in enumerate(pieces):
        offset = step if step <= count // 2 else count // 2 - step
        owner = lax.rem(place_ref[0] - offset + count, count)
        copies.append(
            pltpu.make_async_copy(ref, out_ref.at[:, pl.ds(owner * tiles, tiles)], sem.at[step])
        )
    for copy in copies:
        copy.start()
    for copy in copies:
        copy.wait()


def in_vmem(count):
    return [pl.BlockSpec(memory_space=VMEM)] * count


def in_smem(count):
    return [pl.BlockSpec(memory_space=pltpu.SMEM)] * count


def anywhere(count):
    return [pl.BlockSpec(memory_space=pl.ANY)] * count


def shape(*dims):
    return jax.ShapeDtypeStruct(dims, F32)


def ring(axis, by):
    count = lax.axis_size(axis)
    return [(i, (i + by) % count) for i in range(count)]


def per_device(volume, colour_coef, opacity_coef, light_dir, light_colour):
    slabs, bands = lax.axis_size("depth"), lax.axis_size("height")
    cells, rows, width = volume.shape
    tiles = width // LANES
    slab, band = lax.axis_index("depth"), lax.axis_index("height")
    limit = pltpu.CompilerParams(vmem_limit_bytes=58 << 20)
    field = volume.reshape(cells, rows, tiles, LANES).transpose(0, 2, 1, 3)

    down, up, first, last = pl.pallas_call(
        pack,
        out_shape=[shape(tiles, 3 * cells, LANES)] * 2 + [shape(3, tiles, rows, LANES)] * 2,
        in_specs=anywhere(1),
        out_specs=anywhere(4),
        scratch_shapes=[
            VMEM((cells, tiles, rows, LANES), F32),
            VMEM((tiles, 3 * cells, LANES), F32),
            VMEM((tiles, 3 * cells, LANES), F32),
            DMA((cells // 8,)),
            DMA((2,)),
            DMA((cells // 4,)),
        ],
        compiler_params=limit,
        name="pack",
    )(field)
    top = lax.ppermute(down, "height", ring("height", 1))
    bottom = lax.ppermute(up, "height", ring("height", -1))
    low = lax.ppermute(last, "depth", ring("depth", 1))
    high = lax.ppermute(first, "depth", ring("depth", -1))
    corner_down, corner_up = pl.pallas_call(
        pack_corners,
        out_shape=[shape(tiles, rows, LANES)] * 2,
        in_specs=anywhere(2),
        out_specs=in_vmem(2),
        scratch_shapes=[VMEM((2, 2, tiles, rows, LANES), F32), DMA((2,))],
        compiler_params=limit,
        name="pack_corners",
    )(low, high)
    top_corner = lax.ppermute(corner_down, "height", ring("height", 1))
    bottom_corner = lax.ppermute(corner_up, "height", ring("height", -1))

    edges = jnp.stack([slab > 0, slab < slabs - 1, band > 0, band < bands - 1]).astype(F32)
    partial = pl.pallas_call(
        functools.partial(render, alpha_top=2.0 / (cells * slabs)),
        out_shape=shape(slabs, 13, tiles // slabs, rows, LANES),
        in_specs=in_smem(5) + anywhere(7),
        out_specs=pl.BlockSpec(memory_space=VMEM),
        scratch_shapes=[
            VMEM((cells + 6, tiles, 24, LANES), F32),
            VMEM((cells + 4, tiles, 16, LANES), F32),
            VMEM((cells + 2, tiles, 16, LANES), F32),
            VMEM((cells + 1, tiles, rows, LANES), F32),
            VMEM((2, tiles, 2, rows, LANES), F32),
            VMEM((2, tiles, 2, rows, LANES), F32),
            VMEM((tiles, 2, rows, LANES), F32),
            VMEM((2, tiles, 3 * cells, LANES), F32),
            VMEM((2, tiles, rows, LANES), F32),
            DMA((7,)),
        ],
        compiler_params=limit,
        name="render",
    )(
        edges,
        colour_coef,
        opacity_coef,
        light_dir,
        light_colour,
        field,
        low,
        high,
        top,
        bottom,
        top_corner,
        bottom_corner,
    )
    exchanged = lax.all_to_all(partial, "depth", 0, 0, tiled=True)
    own = pl.pallas_call(
        fold,
        out_shape=shape(13, tiles // slabs, rows, LANES),
        in_specs=in_vmem(1),
        out_specs=pl.BlockSpec(memory_space=VMEM),
        compiler_params=limit,
        name="fold",
    )(exchanged)
    from_below, from_above = [own], [own]
    for _ in range(slabs // 2):
        from_below.append(lax.ppermute(from_below[-1], "depth", ring("depth", 1)))
        from_above.append(lax.ppermute(from_above[-1], "depth", ring("depth", -1)))
    pieces = from_below + from_above[1 : slabs // 2]
    image = pl.pallas_call(
        spread,
        out_shape=shape(13, tiles, rows, LANES),
        in_specs=in_smem(1) + anywhere(slabs),
        out_specs=pl.BlockSpec(memory_space=pl.ANY),
        scratch_shapes=[DMA((slabs,))],
        compiler_params=limit,
        name="spread",
    )(slab[None], *pieces)
    return image.transpose(0, 2, 1, 3).reshape(13, rows, width)


def solution(mesh):
    placed = (P("depth", "height", None), P(), P(), P(), P())
    return jax.shard_map(
        per_device, mesh=mesh, in_specs=placed, out_specs=P(None, "height", None), check_vma=False
    )
```

time: 126 us -> 148 us (1.17)
  the two profiles are of different devices: /device:TPU:8 before, /device:TPU:0 now
where the time goes in v2:
time: 148 us; the launch traced here: 145 us
  Pallas kernels  69.6 us (47%)
  blocking collectives  26.7 us (18%)
  starting transfers between devices  24.1 us (16%)
  waiting for transfers between devices  19.9 us (13%)
  local copies, waits for them, and re-layouts  3.81 us (3%)
    pallas_call x1, Pallas kernels, per_device(): pl.pallas_call(spread, out_shape=shape(13, tiles, rows, LANES), in_specs=...  27 us
    all_to_all x1, blocking collectives, per_device(): exchanged = lax.all_to_all(partial, 'depth', 0, 0, tiled=True)  26.7 us
    pallas_call x1, Pallas kernels, per_device(): pl.pallas_call(functools.partial(render, alpha_top=2.0 / (cells * slabs))...  25.9 us
    ppermute x4, waiting for transfers between devices, per_device(): from_below.append(lax.ppermute(from_below[-1], 'depth', ring('depth', 1)))  14.4 us
    pallas_call x1, Pallas kernels, per_device(): pl.pallas_call(pack, out_shape=[shape(tiles, 3 * cells, LANES)] * 2 + [sh...  13.1 us
    ppermute x3, starting transfers between devices, per_device(): from_above.append(lax.ppermute(from_above[-1], 'depth', ring('depth', -1)))  9.22 us
    ppermute x1, starting transfers between devices, per_device(): bottom = lax.ppermute(up, 'height', ring('height', -1))  5.05 us
    ppermute x1, starting transfers between devices, per_device(): bottom_corner = lax.ppermute(corner_up, 'height', ring('height', -1))  5.05 us
  transfers between devices with their start and end apart: 13, of which 7 were waited for; matrix products, arithmetic and copies ran while one was open for 0% of the time, Pallas kernels for 1%

profile of v2, /device:TPU:0, one launch (start us, length us, event | category | flops | bytes accessed | tf_op | source)
XLA Modules:
  0.0 144.7 jit_solution(12875211815150262868)
XLA Ops:
  0.0 13.1 %pack.1 = (f32[16,96,128]{2,1,0:T(8,128)}, f32[16,96,128]{2,1,0:T(8,128)}, f32[3,16,8,128]{3,2,1,0:T(8,128)}, f32[3,16,8,128]{3,2,1,0:T(8,128)}) custom-call(f32[32,16,8,128]{3,2,1,0:T(8,128)} %bitcast.11), custom_call_target="tpu_custom_call" | custom-call | tf_op jit(solution)/shard_map/pack/pallas_call | solution.py:372
  13.1 0.1 collective-permute-start.2
  13.2 5.1 %collective-permute-start.3 = (f32[16,96,128]{2,1,0:T(8,128)}, f32[16,96,128]{2,1,0:T(8,128)S(1)}, u32[]{:S(2)}, u32[]{:S(2)}) collective-permute-start(f32[16,96,128]{2,1,0:T(8,128)} %get-tuple-element.14), channel_id=1, source_target_pairs={{0,31},{1,0},{2,1},{3,2},{4,3},{5,4},{6,5},{7,6},{8,7},{9,8},{10,9... | collective-permute-start | bytes 2359304 | tf_op jit(solution)/shard_map/ppermute | solution.py:389
  18.3 0.2 collective-permute-start
  18.5 3.9 %collective-permute-start.1 = (f32[3,16,8,128]{3,2,1,0:T(8,128)}, f32[3,16,8,128]{3,2,1,0:T(8,128)S(1)}, u32[]{:S(2)}, u32[]{:S(2)}) collective-permute-start(f32[3,16,8,128]{3,2,1,0:T(8,128)} %get-tuple-element.12), channel_id=1, source_target_pairs={{0,224},{32,0},{64,32},{96,64},{128,96},{160,128},{192,160},{224,1... | collective-permute-start | bytes 589832 | tf_op jit(solution)/shard_map/ppermute | solution.py:391
  22.4 3.9 %collective-permute-done.low_ref = f32[3,16,8,128]{3,2,1,0:T(8,128)S(1)} collective-permute-done((f32[3,16,8,128]{3,2,1,0:T(8,128)}, f32[3,16,8,128]{3,2,1,0:T(8,128)S(1)}, u32[]{:S(2)}, u32[]{:S(2)}) %collective-permute-start) | collective-permute-done | bytes 196640 | tf_op jit(solution)/shard_map/ppermute | solution.py:390
  26.3 0.0 collective-permute-done.1.high_ref
  26.3 0.7 copy-done
  27.0 0.7 copy-done.1
  27.6 1.7 %pack_corners.1 = (f32[16,8,128]{2,1,0:T(8,128)}, f32[16,8,128]{2,1,0:T(8,128)}) custom-call(f32[3,16,8,128]{3,2,1,0:T(8,128)} %copy-done, f32[3,16,8,128]{3,2,1,0:T(8,128)} %copy-done.1), custom_call_target="tpu_custom_call" | custom-call | tf_op jit(solution)/shard_map/pack_corners/pallas_call | solution.py:392
  29.3 0.1 collective-permute-start.4
  29.4 5.1 %collective-permute-start.5 = (f32[16,8,128]{2,1,0:T(8,128)}, f32[16,8,128]{2,1,0:T(8,128)S(1)}, u32[]{:S(2)}, u32[]{:S(2)}) collective-permute-start(f32[16,8,128]{2,1,0:T(8,128)} %get-tuple-element.16), channel_id=1, source_target_pairs={{0,31},{1,0},{2,1},{3,2},{4,3},{5,4},{6,5},{7,6},{8,7},{9,8},{10,9... | collective-permute-start | bytes 196616 | tf_op jit(solution)/shard_map/ppermute | solution.py:402
  34.5 0.6 add_convert_fusion.edge_ref
  35.1 1.6 %collective-permute-done.4.top_corner_ref = f32[16,8,128]{2,1,0:T(8,128)S(1)} collective-permute-done((f32[16,8,128]{2,1,0:T(8,128)}, f32[16,8,128]{2,1,0:T(8,128)S(1)}, u32[]{:S(2)}, u32[]{:S(2)}) %collective-permute-start.4) | collective-permute-done | bytes 65568 | tf_op jit(solution)/shard_map/ppermute | solution.py:401
  36.6 0.1 collective-permute-done.5.bottom_corner_ref
  36.7 0.0 collective-permute-done.2.top_ref
  36.7 0.0 collective-permute-done.3.bottom_ref
  36.7 0.5 copy-done.11
  37.3 0.1 copy-done.12
  37.3 0.3 copy-done.2
  37.6 0.9 copy-done.3
  38.5 25.9 %render.1 = f32[8,13,2,8,128]{4,3,2,1,0:T(8,128)} custom-call(f32[4]{0:T(128)} %add_convert_fusion.edge_ref, f32[3,4]{1,0:T(4,128)} %colour_ref.1, f32[4]{0:T(128)} %opacity_ref.1, f32[4,3]{1,0:T(4,128)} %dir_ref.1, f32[4,3]{1,0:T(4,128)} %light_ref.1, f32[32,16,8,128]{3,2,1,0:T(8,128)} %bitcast.12, f32[3,16,8,128]{3,2,1,0:T(8,128)} %copy-done, ...), custom_call_target="tpu_custom_call" | custom-call | tf_op jit(solution)/shard_map/render/pallas_call | solution.py:405
  64.4 26.7 %all_to_all.5.parts_ref = f32[8,13,2,8,128]{4,3,2,1,0:T(8,128)} all-to-all(f32[8,13,2,8,128]{4,3,2,1,0:T(8,128)} %render.1), channel_id=1, replica_groups=mesh['depth'=8,'height'=32] {'depth'}, dimensions={0} | all-to-all | bytes 1703936 | tf_op jit(solution)/shard_map/all_to_all | solution.py:438
  91.1 1.9 %fold.1.refs_0_ = f32[13,2,8,128]{3,2,1,0:T(8,128)} custom-call(f32[8,13,2,8,128]{4,3,2,1,0:T(8,128)} %all_to_all.5.parts_ref), custom_call_target="tpu_custom_call" | custom-call | tf_op jit(solution)/shard_map/fold/pallas_call | solution.py:439
  92.9 0.5 collective-permute-start.6
  93.4 2.8 %collective-permute-start.10 = (f32[13,2,8,128]{3,2,1,0:T(8,128)}, f32[13,2,8,128]{3,2,1,0:T(8,128)S(1)}, u32[]{:S(2)}, u32[]{:S(2)}) collective-permute-start(f32[13,2,8,128]{3,2,1,0:T(8,128)} %fold.1.refs_0_), channel_id=1, source_target_pairs={{0,224},{32,0},{64,32},{96,64},{128,96},{160,128},{192,160},{224,1... | collective-permute-start | bytes 319496 | tf_op jit(solution)/shard_map/ppermute | solution.py:450
  96.2 2.9 %collective-permute-done.6.refs_1_ = f32[13,2,8,128]{3,2,1,0:T(8,128)S(1)} collective-permute-done((f32[13,2,8,128]{3,2,1,0:T(8,128)}, f32[13,2,8,128]{3,2,1,0:T(8,128)S(1)}, u32[]{:S(2)}, u32[]{:S(2)}) %collective-permute-start.6) | collective-permute-done | bytes 106528 | tf_op jit(solution)/shard_map/ppermute | solution.py:449
  99.1 0.0 collective-permute-start.7
  99.1 0.0 collective-permute-done.10.refs_5_
  99.1 0.0 copy-start.5
  99.1 3.2 %collective-permute-start.11 = (f32[13,2,8,128]{3,2,1,0:T(8,128)S(1)}, f32[13,2,8,128]{3,2,1,0:T(8,128)S(1)}, u32[]{:S(2)}, u32[]{:S(2)}) collective-permute-start(f32[13,2,8,128]{3,2,1,0:T(8,128)S(1)} %collective-permute-done.10.refs_5_), channel_id=1, source_target_pairs={{0,224},{32,0},{64,32},{96,64},{128,96},{160,128},{192,160},{224,1... | collective-permute-start | bytes 319496 | tf_op jit(solution)/shard_map/ppermute | solution.py:450
  102.3 2.9 %collective-permute-done.7.refs_2_ = f32[13,2,8,128]{3,2,1,0:T(8,128)S(1)} collective-permute-done((f32[13,2,8,128]{3,2,1,0:T(8,128)S(1)}, f32[13,2,8,128]{3,2,1,0:T(8,128)S(1)}, u32[]{:S(2)}, u32[]{:S(2)}) %collective-permute-start.7) | collective-permute-done | bytes 106528 | tf_op jit(solution)/shard_map/ppermute | solution.py:449
  105.2 0.0 collective-permute-start.8
  105.2 0.0 collective-permute-done.11.refs_6_
  105.2 0.0 copy-start.7
  105.3 3.2 %collective-permute-start.12 = (f32[13,2,8,128]{3,2,1,0:T(8,128)S(1)}, f32[13,2,8,128]{3,2,1,0:T(8,128)S(1)}, u32[]{:S(2)}, u32[]{:S(2)}) collective-permute-start(f32[13,2,8,128]{3,2,1,0:T(8,128)S(1)} %collective-permute-done.11.refs_6_), channel_id=1, source_target_pairs={{0,224},{32,0},{64,32},{96,64},{128,96},{160,128},{192,160},{224,1... | collective-permute-start | bytes 319496 | tf_op jit(solution)/shard_map/ppermute | solution.py:450
  108.5 2.7 %collective-permute-done.8.refs_3_ = f32[13,2,8,128]{3,2,1,0:T(8,128)S(1)} collective-permute-done((f32[13,2,8,128]{3,2,1,0:T(8,128)S(1)}, f32[13,2,8,128]{3,2,1,0:T(8,128)S(1)}, u32[]{:S(2)}, u32[]{:S(2)}) %collective-permute-start.8) | collective-permute-done | bytes 106528 | tf_op jit(solution)/shard_map/ppermute | solution.py:449
  111.2 0.0 collective-permute-start.9
  111.2 0.0 collective-permute-done.12.refs_7_
  111.2 0.0 copy-start.9
  111.2 5.9 %collective-permute-done.9.refs_4_ = f32[13,2,8,128]{3,2,1,0:T(8,128)S(1)} collective-permute-done((f32[13,2,8,128]{3,2,1,0:T(8,128)S(1)}, f32[13,2,8,128]{3,2,1,0:T(8,128)S(1)}, u32[]{:S(2)}, u32[]{:S(2)}) %collective-permute-start.9) | collective-permute-done | bytes 106528 | tf_op jit(solution)/shard_map/ppermute | solution.py:449
  117.1 0.0 copy-done.4
  117.1 0.0 copy-done.5
  117.1 0.0 copy-done.7
  117.1 0.0 copy-done.8
  117.1 0.0 copy-done.9
  117.1 0.6 copy-done.10
  117.7 27.0 %spread.1 = f32[13,16,8,128]{3,2,1,0:T(8,128)} custom-call(s32[1]{0:T(128)} %bitcast.place_ref, f32[13,2,8,128]{3,2,1,0:T(8,128)} %fold.1.refs_0_, f32[13,2,8,128]{3,2,1,0:T(8,128)} %copy-done.4, f32[13,2,8,128]{3,2,1,0:T(8,128)} %copy-done.6, f32[13,2,8,128]{3,2,1,0:T(8,128)} %copy-done.8, f32[13,2,8,128]{3,2,1,0:T(8,128)} %copy-done.10, ...), custom_call_target="tpu_custom_call" | custom-call | tf_op jit(solution)/shard_map/spread/pallas_call | solution.py:452
  (11 shorter events, 0.0 us)
Async XLA Ops:
  13.1 23.6 %collective-permute-start.2 = (f32[16,96,128]{2,1,0:T(8,128)}, f32[16,96,128]{2,1,0:T(8,128)S(1)}, u32[]{:S(2)}, u32[]{:S(2)}) collective-permute-start(f32[16,96,128]{2,1,0:T(8,128)} %get-tuple-element.13), channel_id=1, source_target_pairs={{0,1},{1,2},{2,3},{3,4},{4,5},{5,6},{6,7},{7,8},{8,9},{9,10},{10,1... | collective-permute-start | bytes 2359304 | tf_op jit(solution)/shard_map/ppermute | solution.py:388
  13.2 23.5 %collective-permute-start.3 = (f32[16,96,128]{2,1,0:T(8,128)}, f32[16,96,128]{2,1,0:T(8,128)S(1)}, u32[]{:S(2)}, u32[]{:S(2)}) collective-permute-start(f32[16,96,128]{2,1,0:T(8,128)} %get-tuple-element.14), channel_id=1, source_target_pairs={{0,31},{1,0},{2,1},{3,2},{4,3},{5,4},{6,5},{7,6},{8,7},{9,8},{10,9... | collective-permute-start | bytes 2359304 | tf_op jit(solution)/shard_map/ppermute | solution.py:389
  18.3 8.0 %collective-permute-start = (f32[3,16,8,128]{3,2,1,0:T(8,128)}, f32[3,16,8,128]{3,2,1,0:T(8,128)S(1)}, u32[]{:S(2)}, u32[]{:S(2)}) collective-permute-start(f32[3,16,8,128]{3,2,1,0:T(8,128)} %get-tuple-element.11), channel_id=1, source_target_pairs={{0,32},{32,64},{64,96},{96,128},{128,160},{160,192},{192,224},{224... | collective-permute-start | bytes 589832 | tf_op jit(solution)/shard_map/ppermute | solution.py:390
  18.5 7.8 %collective-permute-start.1 = (f32[3,16,8,128]{3,2,1,0:T(8,128)}, f32[3,16,8,128]{3,2,1,0:T(8,128)S(1)}, u32[]{:S(2)}, u32[]{:S(2)}) collective-permute-start(f32[3,16,8,128]{3,2,1,0:T(8,128)} %get-tuple-element.12), channel_id=1, source_target_pairs={{0,224},{32,0},{64,32},{96,64},{128,96},{160,128},{192,160},{224,1... | collective-permute-start | bytes 589832 | tf_op jit(solution)/shard_map/ppermute | solution.py:391
  26.3 0.7 copy-start
  26.9 0.7 copy-start.1
  29.3 7.3 %collective-permute-start.4 = (f32[16,8,128]{2,1,0:T(8,128)}, f32[16,8,128]{2,1,0:T(8,128)S(1)}, u32[]{:S(2)}, u32[]{:S(2)}) collective-permute-start(f32[16,8,128]{2,1,0:T(8,128)} %get-tuple-element.15), channel_id=1, source_target_pairs={{0,1},{1,2},{2,3},{3,4},{4,5},{5,6},{6,7},{7,8},{8,9},{9,10},{10,1... | collective-permute-start | bytes 196616 | tf_op jit(solution)/shard_map/ppermute | solution.py:401
  29.4 7.3 %collective-permute-start.5 = (f32[16,8,128]{2,1,0:T(8,128)}, f32[16,8,128]{2,1,0:T(8,128)S(1)}, u32[]{:S(2)}, u32[]{:S(2)}) collective-permute-start(f32[16,8,128]{2,1,0:T(8,128)} %get-tuple-element.16), channel_id=1, source_target_pairs={{0,31},{1,0},{2,1},{3,2},{4,3},{5,4},{6,5},{7,6},{8,7},{9,8},{10,9... | collective-permute-start | bytes 196616 | tf_op jit(solution)/shard_map/ppermute | solution.py:402
  36.6 0.6 copy-start.11
  36.7 0.6 copy-start.12
  36.7 0.9 copy-start.2
  37.6 0.9 copy-start.3
  92.9 6.1 %collective-permute-start.6 = (f32[13,2,8,128]{3,2,1,0:T(8,128)}, f32[13,2,8,128]{3,2,1,0:T(8,128)S(1)}, u32[]{:S(2)}, u32[]{:S(2)}) collective-permute-start(f32[13,2,8,128]{3,2,1,0:T(8,128)} %fold.1.refs_0_), channel_id=1, source_target_pairs={{0,32},{32,64},{64,96},{96,128},{128,160},{160,192},{192,224},{224... | collective-permute-start | bytes 319496 | tf_op jit(solution)/shard_map/ppermute | solution.py:449
  93.4 5.7 %collective-permute-start.10 = (f32[13,2,8,128]{3,2,1,0:T(8,128)}, f32[13,2,8,128]{3,2,1,0:T(8,128)S(1)}, u32[]{:S(2)}, u32[]{:S(2)}) collective-permute-start(f32[13,2,8,128]{3,2,1,0:T(8,128)} %fold.1.refs_0_), channel_id=1, source_target_pairs={{0,224},{32,0},{64,32},{96,64},{128,96},{160,128},{192,160},{224,1... | collective-permute-start | bytes 319496 | tf_op jit(solution)/shard_map/ppermute | solution.py:450
  99.1 18.0 %copy-start.4 = (f32[13,2,8,128]{3,2,1,0:T(8,128)}, f32[13,2,8,128]{3,2,1,0:T(8,128)S(1)}, u32[]{:S(2)}) copy-start(f32[13,2,8,128]{3,2,1,0:T(8,128)S(1)} %collective-permute-done.6.refs_1_) | copy-start | bytes 319492
  99.1 6.2 %collective-permute-start.7 = (f32[13,2,8,128]{3,2,1,0:T(8,128)S(1)}, f32[13,2,8,128]{3,2,1,0:T(8,128)S(1)}, u32[]{:S(2)}, u32[]{:S(2)}) collective-permute-start(f32[13,2,8,128]{3,2,1,0:T(8,128)S(1)} %collective-permute-done.6.refs_1_), channel_id=1, source_target_pairs={{0,32},{32,64},{64,96},{96,128},{128,160},{160,192},{192,224},{224... | collective-permute-start | bytes 319496 | tf_op jit(solution)/shard_map/ppermute | solution.py:449
  99.1 18.0 %copy-start.5 = (f32[13,2,8,128]{3,2,1,0:T(8,128)}, f32[13,2,8,128]{3,2,1,0:T(8,128)S(1)}, u32[]{:S(2)}) copy-start(f32[13,2,8,128]{3,2,1,0:T(8,128)S(1)} %collective-permute-done.10.refs_5_) | copy-start | bytes 319492
  99.1 6.2 %collective-permute-start.11 = (f32[13,2,8,128]{3,2,1,0:T(8,128)S(1)}, f32[13,2,8,128]{3,2,1,0:T(8,128)S(1)}, u32[]{:S(2)}, u32[]{:S(2)}) collective-permute-start(f32[13,2,8,128]{3,2,1,0:T(8,128)S(1)} %collective-permute-done.10.refs_5_), channel_id=1, source_target_pairs={{0,224},{32,0},{64,32},{96,64},{128,96},{160,128},{192,160},{224,1... | collective-permute-start | bytes 319496 | tf_op jit(solution)/shard_map/ppermute | solution.py:450
  105.2 11.8 %copy-start.6 = (f32[13,2,8,128]{3,2,1,0:T(8,128)}, f32[13,2,8,128]{3,2,1,0:T(8,128)S(1)}, u32[]{:S(2)}) copy-start(f32[13,2,8,128]{3,2,1,0:T(8,128)S(1)} %collective-permute-done.7.refs_2_) | copy-start | bytes 319492
  105.2 5.9 %collective-permute-start.8 = (f32[13,2,8,128]{3,2,1,0:T(8,128)S(1)}, f32[13,2,8,128]{3,2,1,0:T(8,128)S(1)}, u32[]{:S(2)}, u32[]{:S(2)}) collective-permute-start(f32[13,2,8,128]{3,2,1,0:T(8,128)S(1)} %collective-permute-done.7.refs_2_), channel_id=1, source_target_pairs={{0,32},{32,64},{64,96},{96,128},{128,160},{160,192},{192,224},{224... | collective-permute-start | bytes 319496 | tf_op jit(solution)/shard_map/ppermute | solution.py:449
  105.2 11.8 %copy-start.7 = (f32[13,2,8,128]{3,2,1,0:T(8,128)}, f32[13,2,8,128]{3,2,1,0:T(8,128)S(1)}, u32[]{:S(2)}) copy-start(f32[13,2,8,128]{3,2,1,0:T(8,128)S(1)} %collective-permute-done.11.refs_6_) | copy-start | bytes 319492
  105.3 5.9 %collective-permute-start.12 = (f32[13,2,8,128]{3,2,1,0:T(8,128)S(1)}, f32[13,2,8,128]{3,2,1,0:T(8,128)S(1)}, u32[]{:S(2)}, u32[]{:S(2)}) collective-permute-start(f32[13,2,8,128]{3,2,1,0:T(8,128)S(1)} %collective-permute-done.11.refs_6_), channel_id=1, source_target_pairs={{0,224},{32,0},{64,32},{96,64},{128,96},{160,128},{192,160},{224,1... | collective-permute-start | bytes 319496 | tf_op jit(solution)/shard_map/ppermute | solution.py:450
  111.2 5.9 %copy-start.8 = (f32[13,2,8,128]{3,2,1,0:T(8,128)}, f32[13,2,8,128]{3,2,1,0:T(8,128)S(1)}, u32[]{:S(2)}) copy-start(f32[13,2,8,128]{3,2,1,0:T(8,128)S(1)} %collective-permute-done.8.refs_3_) | copy-start | bytes 319492
  111.2 5.9 %collective-permute-start.9 = (f32[13,2,8,128]{3,2,1,0:T(8,128)S(1)}, f32[13,2,8,128]{3,2,1,0:T(8,128)S(1)}, u32[]{:S(2)}, u32[]{:S(2)}) collective-permute-start(f32[13,2,8,128]{3,2,1,0:T(8,128)S(1)} %collective-permute-done.8.refs_3_), channel_id=1, source_target_pairs={{0,32},{32,64},{64,96},{96,128},{128,160},{160,192},{192,224},{224... | collective-permute-start | bytes 319496 | tf_op jit(solution)/shard_map/ppermute | solution.py:449
  111.2 5.9 %copy-start.9 = (f32[13,2,8,128]{3,2,1,0:T(8,128)}, f32[13,2,8,128]{3,2,1,0:T(8,128)S(1)}, u32[]{:S(2)}) copy-start(f32[13,2,8,128]{3,2,1,0:T(8,128)S(1)} %collective-permute-done.12.refs_7_) | copy-start | bytes 319492
  117.1 0.6 copy-start.10

commit v3 on v2

--- a/solution.py
+++ b/solution.py
@@ -24,7 +24,9 @@
     return d * inverse_of(d * d + 1.0)
 
 
-def pack(vol_ref, down_ref, up_ref, first_ref, last_ref, held, down, up, in_sem, edge_sem, out_sem):
+def pack(vol_ref, *refs):
+    down_refs, up_refs, first_ref, last_ref = refs[0:2], refs[2:4], refs[4], refs[5]
+    held, down, up, in_sem, edge_sem, out_sem = refs[6:]
     cells, tiles = vol_ref.shape[0], vol_ref.shape[1]
     groups = cells // 8
     loads = [
@@ -32,26 +34,34 @@
         for g in range(groups)
     ]
     edges = [
-        pltpu.make_async_copy(vol_ref.at[pl.ds(0, 3)], first_ref, edge_sem.at[0]),
-        pltpu.make_async_copy(vol_ref.at[pl.ds(cells - 3, 3)], last_ref, edge_sem.at[1]),
+        pltpu.make_async_copy(held.at[pl.ds(0, 3)], first_ref, edge_sem.at[0]),
+        pltpu.make_async_copy(held.at[pl.ds(cells - 3, 3)], last_ref, edge_sem.at[1]),
     ]
-    for copy in loads + edges:
+    for copy in loads:
         copy.start()
     stores = []
     for g in range(groups):
         loads[g].wait()
+        if g == 0:
+            edges[0].start()
+        if g == groups - 1:
+            edges[1].start()
         for k in range(8):
             z = 8 * g + k
             for tile in range(tiles):
                 up[tile, 3 * z : 3 * z + 3, :] = held[z, tile, 0:3, :]
                 down[tile, 3 * z : 3 * z + 3, :] = held[z, tile, 5:8, :]
         part = pl.ds(24 * g, 24)
-        for i, (ref, out_ref) in enumerate(((down, down_ref), (up, up_ref))):
-            copy = pltpu.make_async_copy(
-                ref.at[:, part, :], out_ref.at[:, part, :], out_sem.at[2 * g + i]
-            )
-            copy.start()
-            stores.append(copy)
+        for half in range(2):
+            for ref, out_refs in ((down, down_refs), (up, up_refs)):
+                count = out_refs[half].shape[0]
+                copy = pltpu.make_async_copy(
+                    ref.at[pl.ds(half * (tiles - count), count), part, :],
+                    out_refs[half].at[:, part, :],
+                    out_sem.at[len(stores)],
+                )
+                copy.start()
+                stores.append(copy)
     for copy in stores + edges:
         copy.wait()
 
@@ -186,17 +196,22 @@
     corners_in,
     sem,
     alpha_top,
+    half,
 ):
-    cells, tiles = vol_ref.shape[0], vol_ref.shape[1]
-    own = pl.ds(BAND, 8)
+    cells, tiles = vol_ref.shape[0], top_ref.shape[0]
+    start = half * (vol_ref.shape[1] - tiles)
+    own, part = pl.ds(BAND, 8), pl.ds(start, tiles)
+    low, high = field.at[pl.ds(0, 3), :, own, :], field.at[pl.ds(cells + 3, 3), :, own, :]
     copies = [
-        pltpu.make_async_copy(low_ref, field.at[pl.ds(0, 3), :, own, :], sem.at[0]),
-        pltpu.make_async_copy(high_ref, field.at[pl.ds(cells + 3, 3), :, own, :], sem.at[1]),
-        pltpu.make_async_copy(top_corner_ref, corners_in.at[0], sem.at[2]),
-        pltpu.make_async_copy(bottom_corner_ref, corners_in.at[1], sem.at[3]),
+        pltpu.make_async_copy(low_ref.at[:, part], low, sem.at[0]),
+        pltpu.make_async_copy(high_ref.at[:, part], high, sem.at[1]),
+        pltpu.make_async_copy(top_corner_ref.at[part], corners_in.at[0], sem.at[2]),
+        pltpu.make_async_copy(bottom_corner_ref.at[part], corners_in.at[1], sem.at[3]),
         pltpu.make_async_copy(top_ref, rows_in.at[0], sem.at[4]),
         pltpu.make_async_copy(bottom_ref, rows_in.at[1], sem.at[5]),
-        pltpu.make_async_copy(vol_ref, field.at[pl.ds(3, cells), :, own, :], sem.at[6]),
+        pltpu.make_async_copy(
+            vol_ref.at[:, part], field.at[pl.ds(3, cells), :, own, :], sem.at[6]
+        ),
     ]
     for copy in copies:
         copy.start()
@@ -268,7 +283,9 @@
     def poly(c, v):
         return ((c[3] * v + c[2]) * v + c[1]) * v + c[0]
 
-    def column(tile, carry):
+    def column(piece, carry):
+        tile = piece + half * (tiles - out_ref.shape[0])
+
         def cell(z, state):
             through, sums, base_sums = state
             v = twice[z + 1, tile, own, :]
@@ -302,38 +319,41 @@
         through, sums, base_sums = lax.fori_loop(0, cells // 4, group, state)
         for l in range(4):
             for c in range(3):
-                out_ref[tile // 2, 3 * l + c, tile % 2] = light_ref[l, c] * (
+                out_ref[piece, 3 * l + c] = light_ref[l, c] * (
                     0.2 * base_sums[c] + sums[3 * l + c]
                 )
-        out_ref[tile // 2, 12, tile % 2] = 1.0 - through
+        out_ref[piece, 12] = 1.0 - through
         return carry
 
-    lax.fori_loop(0, tiles, column, 0)
-
-
-def fold(parts_ref, out_ref):
-    slabs, channels = parts_ref.shape[0], parts_ref.shape[1]
-    for tile in range(parts_ref.shape[2]):
-        through = 1.0 - parts_ref[0, 12, tile]
-        total = [parts_ref[0, ch, tile] for ch in range(channels)]
+    lax.fori_loop(0, out_ref.shape[0], column, 0)
+
+
+def fold(*refs):
+    out_ref = refs[-1]
+    for half, parts_ref in enumerate(refs[:-1]):
+        slabs, channels = parts_ref.shape[0], parts_ref.shape[1]
+        through = 1.0 - parts_ref[0, 12]
+        total = [parts_ref[0, ch] for ch in range(channels)]
         for slab in range(1, slabs):
-            total = [total[ch] + through * parts_ref[slab, ch, tile] for ch in range(channels)]
-            through = through * (1.0 - parts_ref[slab, 12, tile])
+            total = [total[ch] + through * parts_ref[slab, ch] for ch in range(channels)]
+            through = through * (1.0 - parts_ref[slab, 12])
         for ch in range(channels):
-            out_ref[ch, tile] = total[ch]
+            out_ref[half, ch] = total[ch]
 
 
 def spread(place_ref, *refs):
     pieces, out_ref, sem = refs[:-2], refs[-2], refs[-1]
     count = len(pieces)
-    tiles = out_ref.shape[1] // count
     copies = []
     for step, ref in enumerate(pieces):
         offset = step if step <= count // 2 else count // 2 - step
         owner = lax.rem(place_ref[0] - offset + count, count)
-        copies.append(
-            pltpu.make_async_copy(ref, out_ref.at[:, pl.ds(owner * tiles, tiles)], sem.at[step])
-        )
+        for half in range(2):
+            copies.append(
+                pltpu.make_async_copy(
+                    ref.at[half], out_ref.at[:, half * count + owner], sem.at[2 * step + half]
+                )
+            )
     for copy in copies:
         copy.start()
     for copy in copies:
@@ -369,26 +389,27 @@
     limit = pltpu.CompilerParams(vmem_limit_bytes=58 << 20)
     field = volume.reshape(cells, rows, tiles, LANES).transpose(0, 2, 1, 3)
 
-    down, up, first, last = pl.pallas_call(
+    reach = tiles // 2 + 1
+    down0, down1, up0, up1, first, last = pl.pallas_call(
         pack,
-        out_shape=[shape(tiles, 3 * cells, LANES)] * 2 + [shape(3, tiles, rows, LANES)] * 2,
+        out_shape=[shape(reach, 3 * cells, LANES)] * 4 + [shape(3, tiles, rows, LANES)] * 2,
         in_specs=anywhere(1),
-        out_specs=anywhere(4),
+        out_specs=anywhere(6),
         scratch_shapes=[
             VMEM((cells, tiles, rows, LANES), F32),
             VMEM((tiles, 3 * cells, LANES), F32),
             VMEM((tiles, 3 * cells, LANES), F32),
             DMA((cells // 8,)),
             DMA((2,)),
-            DMA((cells // 4,)),
+            DMA((cells // 2,)),
         ],
         compiler_params=limit,
         name="pack",
     )(field)
-    top = lax.ppermute(down, "height", ring("height", 1))
-    bottom = lax.ppermute(up, "height", ring("height", -1))
     low = lax.ppermute(last, "depth", ring("depth", 1))
     high = lax.ppermute(first, "depth", ring("depth", -1))
+    tops = [lax.ppermute(down, "height", ring("height", 1)) for down in (down0, down1)]
+    bottoms = [lax.ppermute(up, "height", ring("height", -1)) for up in (up0, up1)]
     corner_down, corner_up = pl.pallas_call(
         pack_corners,
         out_shape=[shape(tiles, rows, LANES)] * 2,
@@ -402,48 +423,53 @@
     bottom_corner = lax.ppermute(corner_up, "height", ring("height", -1))
 
     edges = jnp.stack([slab > 0, slab < slabs - 1, band > 0, band < bands - 1]).astype(F32)
-    partial = pl.pallas_call(
-        functools.partial(render, alpha_top=2.0 / (cells * slabs)),
-        out_shape=shape(slabs, 13, tiles // slabs, rows, LANES),
-        in_specs=in_smem(5) + anywhere(7),
-        out_specs=pl.BlockSpec(memory_space=VMEM),
-        scratch_shapes=[
-            VMEM((cells + 6, tiles, 24, LANES), F32),
-            VMEM((cells + 4, tiles, 16, LANES), F32),
-            VMEM((cells + 2, tiles, 16, LANES), F32),
-            VMEM((cells + 1, tiles, rows, LANES), F32),
-            VMEM((2, tiles, 2, rows, LANES), F32),
-            VMEM((2, tiles, 2, rows, LANES), F32),
-            VMEM((tiles, 2, rows, LANES), F32),
-            VMEM((2, tiles, 3 * cells, LANES), F32),
-            VMEM((2, tiles, rows, LANES), F32),
-            DMA((7,)),
-        ],
-        compiler_params=limit,
-        name="render",
-    )(
-        edges,
-        colour_coef,
-        opacity_coef,
-        light_dir,
-        light_colour,
-        field,
-        low,
-        high,
-        top,
-        bottom,
-        top_corner,
-        bottom_corner,
-    )
-    exchanged = lax.all_to_all(partial, "depth", 0, 0, tiled=True)
+    exchanged = []
+    for half in range(2):
+        partial = pl.pallas_call(
+            functools.partial(render, alpha_top=2.0 / (cells * slabs), half=half),
+            out_shape=shape(slabs, 13, rows, LANES),
+            in_specs=in_smem(5) + anywhere(7),
+            out_specs=pl.BlockSpec(memory_space=VMEM),
+            scratch_shapes=[
+                VMEM((cells + 6, reach, 24, LANES), F32),
+                VMEM((cells + 4, reach, 16, LANES), F32),
+                VMEM((cells + 2, reach, 16, LANES), F32),
+                VMEM((cells + 1, reach, rows, LANES), F32),
+                VMEM((2, reach, 2, rows, LANES), F32),
+                VMEM((2, reach, 2, rows, LANES), F32),
+                VMEM((reach, 2, rows, LANES), F32),
+                VMEM((2, reach, 3 * cells, LANES), F32),
+                VMEM((2, reach, rows, LANES), F32),
+                DMA((7,)),
+            ],
+            compiler_params=limit,
+            cost_estimate=pl.CostEstimate(
+                flops=400_000_000, bytes_accessed=40_000_000, transcendentals=4_000_000
+            ),
+            name="render",
+        )(
+            edges,
+            colour_coef,
+            opacity_coef,
+            light_dir,
+            light_colour,
+            field,
+            low,
+            high,
+            tops[half],
+            bottoms[half],
+            top_corner,
+            bottom_corner,
+        )
+        exchanged.append(lax.all_to_all(partial, "depth", 0, 0, tiled=True))
     own = pl.pallas_call(
         fold,
-        out_shape=shape(13, tiles // slabs, rows, LANES),
-        in_specs=in_vmem(1),
+        out_shape=shape(2, 13, rows, LANES),
+        in_specs=in_vmem(2),
         out_specs=pl.BlockSpec(memory_space=VMEM),
         compiler_params=limit,
         name="fold",
-    )(exchanged)
+    )(*exchanged)
     from_below, from_above = [own], [own]
     for _ in range(slabs // 2):
         from_below.append(lax.ppermute(from_below[-1], "depth", ring("depth", 1)))
@@ -452,9 +478,9 @@
     image = pl.pallas_call(
         spread,
         out_shape=shape(13, tiles, rows, LANES),
-        in_specs=in_smem(1) + anywhere(slabs),
+        in_specs=in_smem(1) + in_vmem(slabs),
         out_specs=pl.BlockSpec(memory_space=pl.ANY),
-        scratch_shapes=[DMA((slabs,))],
+        scratch_shapes=[DMA((2 * slabs,))],
         compiler_params=limit,
         name="spread",
     )(slab[None], *pieces)

time: 148 us -> 129 us (0.87); the launches traced: 145 us -> 129 us
  Pallas kernels: 69.6 us -> 40.5 us
  starting transfers between devices: 24.1 us -> 35.1 us
  waiting for transfers between devices: 19.9 us -> 26.7 us
  blocking collectives: 26.7 us -> 20.6 us
    pallas_call x1, Pallas kernels: 27 us -> 2.24 us  [per_device(): pl.pallas_call(spread, out_shape=shape(13, tiles, rows, LANES), in_specs=...]
    all_to_all x1, blocking collectives: 26.7 us -> 20.6 us  [per_device(): exchanged.append(lax.all_to_all(partial, 'depth', 0, 0, tiled=True))]
    ppermute x2 -> x4, waiting for transfers between devices: 0.01 us -> 5.99 us  [the longest x2 5.98 us: per_device(): lax.ppermute(down, 'height', ring('height', 1))]
    all_to_all x0 -> x1, starting transfers between devices: none -> 5.86 us  [per_device(): exchanged.append(lax.all_to_all(partial, 'depth', 0, 0, tiled=True))]
    ppermute x2 -> x4, starting transfers between devices: 5.14 us -> 10.3 us  [the longest x2 10.1 us: per_device(): lax.ppermute(up, 'height', ring('height', -1))]
    pallas_call x3 -> x4, Pallas kernels: 40.9 us -> 36.5 us  [the longest x2 32 us: per_device(): pl.pallas_call(functools.partial(render, alpha_top=2.0 / (cells * slabs),...]
    unnamed x26 -> x36, local copies, waits for them, and re-layouts: 3.81 us -> 5.03 us
  transfers between devices with their start and end apart: 13 -> 16, of which waited for: 7 -> 8; matrix products, arithmetic and copies ran while one was open for 0% -> 0% of each run, Pallas kernels for 1% -> 14%
where the time goes in v3:
time: 129 us
  Pallas kernels  40.5 us (31%)
  starting transfers between devices  35.1 us (27%)
  waiting for transfers between devices  26.7 us (21%)
  blocking collectives  20.6 us (16%)
  local copies, waits for them, and re-layouts  5.03 us (4%)
    pallas_call x2, Pallas kernels, per_device(): pl.pallas_call(functools.partial(render, alpha_top=2.0 / (cells * slabs),...  32 us
    all_to_all x1, blocking collectives, per_device(): exchanged.append(lax.all_to_all(partial, 'depth', 0, 0, tiled=True))  20.6 us
    ppermute x4, waiting for transfers between devices, per_device(): from_below.append(lax.ppermute(from_below[-1], 'depth', ring('depth', 1)))  15.2 us
    ppermute x2, starting transfers between devices, per_device(): lax.ppermute(up, 'height', ring('height', -1))  10.1 us
    ppermute x3, starting transfers between devices, per_device(): from_above.append(lax.ppermute(from_above[-1], 'depth', ring('depth', -1)))  9.02 us
    ppermute x2, waiting for transfers between devices, per_device(): lax.ppermute(down, 'height', ring('height', 1))  5.98 us
    all_to_all x1, starting transfers between devices, per_device(): exchanged.append(lax.all_to_all(partial, 'depth', 0, 0, tiled=True))  5.86 us
    ppermute x1, starting transfers between devices, per_device(): bottom_corner = lax.ppermute(corner_up, 'height', ring('height', -1))  5.05 us
  transfers between devices with their start and end apart: 16, of which 8 were waited for; matrix products, arithmetic and copies ran while one was open for 0% of the time, Pallas kernels for 14%

profile of v3, /device:TPU:0, one launch (start us, length us, event | category | flops | bytes accessed | tf_op | source)
XLA Modules:
  0.0 128.7 jit_solution(7193672763661550393)
XLA Ops:
  0.0 2.7 %pack.1 = (f32[9,96,128]{2,1,0:T(8,128)}, f32[9,96,128]{2,1,0:T(8,128)}, f32[9,96,128]{2,1,0:T(8,128)}, f32[9,96,128]{2,1,0:T(8,128)}, f32[3,16,8,128]{3,2,1,0:T(8,128)}, /*index=5*/f32[3,16,8,128]{3,2,1,0:T(8,128)}) custom-call(f32[32,16,8,128]{3,2,1,0:T(8,128)} %bitcast.11), custom_call_target="tpu_custom_call" | custom-call | tf_op jit(solution)/shard_map/pack/pallas_call | solution.py:393
  2.7 0.1 collective-permute-start.2
  2.8 5.1 %collective-permute-start.3 = (f32[9,96,128]{2,1,0:T(8,128)}, f32[9,96,128]{2,1,0:T(8,128)S(1)}, u32[]{:S(2)}, u32[]{:S(2)}) collective-permute-start(f32[9,96,128]{2,1,0:T(8,128)} %get-tuple-element.16), channel_id=1, source_target_pairs={{0,31},{1,0},{2,1},{3,2},{4,3},{5,4},{6,5},{7,6},{8,7},{9,8},{10,9... | collective-permute-start | bytes 1327112 | tf_op jit(solution)/shard_map/ppermute | solution.py:412
  7.8 0.2 collective-permute-start
  8.0 3.9 %collective-permute-start.1 = (f32[3,16,8,128]{3,2,1,0:T(8,128)}, f32[3,16,8,128]{3,2,1,0:T(8,128)S(1)}, u32[]{:S(2)}, u32[]{:S(2)}) collective-permute-start(f32[3,16,8,128]{3,2,1,0:T(8,128)} %get-tuple-element.14), channel_id=1, source_target_pairs={{0,224},{32,0},{64,32},{96,64},{128,96},{160,128},{192,160},{224,1... | collective-permute-start | bytes 589832 | tf_op jit(solution)/shard_map/ppermute | solution.py:410
  12.0 3.9 %collective-permute-done.low_ref = f32[3,16,8,128]{3,2,1,0:T(8,128)S(1)} collective-permute-done((f32[3,16,8,128]{3,2,1,0:T(8,128)}, f32[3,16,8,128]{3,2,1,0:T(8,128)S(1)}, u32[]{:S(2)}, u32[]{:S(2)}) %collective-permute-start) | collective-permute-done | bytes 196640 | tf_op jit(solution)/shard_map/ppermute | solution.py:409
  15.8 0.0 collective-permute-done.1.high_ref
  15.8 0.7 copy-done.1
  16.5 0.7 copy-done.2
  17.1 1.7 %pack_corners.1 = (f32[16,8,128]{2,1,0:T(8,128)}, f32[16,8,128]{2,1,0:T(8,128)}) custom-call(f32[3,16,8,128]{3,2,1,0:T(8,128)} %copy-done.1, f32[3,16,8,128]{3,2,1,0:T(8,128)} %copy-done.2), custom_call_target="tpu_custom_call" | custom-call | tf_op jit(solution)/shard_map/pack_corners/pallas_call | solution.py:413
  18.9 0.1 collective-permute-start.4
  19.0 5.1 %collective-permute-start.5 = (f32[16,8,128]{2,1,0:T(8,128)}, f32[16,8,128]{2,1,0:T(8,128)S(1)}, u32[]{:S(2)}, u32[]{:S(2)}) collective-permute-start(f32[16,8,128]{2,1,0:T(8,128)} %get-tuple-element.18), channel_id=1, source_target_pairs={{0,31},{1,0},{2,1},{3,2},{4,3},{5,4},{6,5},{7,6},{8,7},{9,8},{10,9... | collective-permute-start | bytes 196616 | tf_op jit(solution)/shard_map/ppermute | solution.py:423
  24.0 0.6 add_convert_fusion.edge_ref
  24.6 1.6 %collective-permute-done.4.top_corner_ref = f32[16,8,128]{2,1,0:T(8,128)S(1)} collective-permute-done((f32[16,8,128]{2,1,0:T(8,128)}, f32[16,8,128]{2,1,0:T(8,128)S(1)}, u32[]{:S(2)}, u32[]{:S(2)}) %collective-permute-start.4) | collective-permute-done | bytes 65568 | tf_op jit(solution)/shard_map/ppermute | solution.py:422
  26.2 0.1 collective-permute-done.5.bottom_corner_ref
  26.2 0.0 collective-permute-done.2.top_ref
  26.2 0.0 collective-permute-done.3.bottom_ref
  26.2 0.5 copy-done.16
  26.8 0.1 copy-done.17
  26.9 0.1 copy-done.12
  27.0 0.8 copy-done.13
  27.8 16.1 %render.2 = f32[8,13,8,128]{3,2,1,0:T(8,128)} custom-call(f32[4]{0:T(128)} %add_convert_fusion.edge_ref, f32[3,4]{1,0:T(4,128)} %colour_ref.3, f32[4]{0:T(128)} %opacity_ref.3, f32[4,3]{1,0:T(4,128)} %dir_ref.3, f32[4,3]{1,0:T(4,128)} %light_ref.3, f32[32,16,8,128]{3,2,1,0:T(8,128)} %bitcast.12, f32[3,16,8,128]{3,2,1,0:T(8,128)} %copy-done.1, ...), custom_call_target="tpu_custom_call" | custom-call | flops 400000000 | bytes 40000000 | tf_op jit(solution)/shard_map/render/pallas_call | solution.py:428
  43.8 5.9 %all-to-all-start = ((f32[8,13,8,128]{3,2,1,0:T(8,128)}), f32[8,13,8,128]{3,2,1,0:T(8,128)S(1)}, u32[]{:S(2)}, u32[]{:S(2)}) async-start(f32[8,13,8,128]{3,2,1,0:T(8,128)} %render.2), calls=%async_computation | async-start | bytes 851968 | tf_op jit(solution)/shard_map/all_to_all | solution.py:464
  49.7 0.1 collective-permute-start.6
  49.8 5.0 %collective-permute-start.7 = (f32[9,96,128]{2,1,0:T(8,128)S(1)}, f32[9,96,128]{2,1,0:T(8,128)S(1)}, u32[]{:S(2)}, u32[]{:S(2)}) collective-permute-start(f32[9,96,128]{2,1,0:T(8,128)S(1)} %copy-done.10), channel_id=1, source_target_pairs={{0,31},{1,0},{2,1},{3,2},{4,3},{5,4},{6,5},{7,6},{8,7},{9,8},{10,9... | collective-permute-start | bytes 1327112 | tf_op jit(solution)/shard_map/ppermute | solution.py:412
  54.9 6.0 %collective-permute-done.6.top_ref = f32[9,96,128]{2,1,0:T(8,128)S(1)} collective-permute-done((f32[9,96,128]{2,1,0:T(8,128)S(1)}, f32[9,96,128]{2,1,0:T(8,128)S(1)}, u32[]{:S(2)}, u32[]{:S(2)}) %collective-permute-start.6) | collective-permute-done | bytes 442400 | tf_op jit(solution)/shard_map/ppermute | solution.py:411
  60.8 0.0 collective-permute-done.7.bottom_ref
  60.8 0.8 copy-done.14
  61.6 0.8 copy-done.15
  62.4 16.0 %render.3 = f32[8,13,8,128]{3,2,1,0:T(8,128)} custom-call(f32[4]{0:T(128)} %add_convert_fusion.edge_ref, f32[3,4]{1,0:T(4,128)} %colour_ref.3, f32[4]{0:T(128)} %opacity_ref.3, f32[4,3]{1,0:T(4,128)} %dir_ref.3, f32[4,3]{1,0:T(4,128)} %light_ref.3, f32[32,16,8,128]{3,2,1,0:T(8,128)} %bitcast.13, f32[3,16,8,128]{3,2,1,0:T(8,128)} %copy-done.1, ...), custom_call_target="tpu_custom_call" | custom-call | flops 400000000 | bytes 40000000 | tf_op jit(solution)/shard_map/render/pallas_call | solution.py:428
  78.3 0.0 all-to-all-done.refs_0_
  78.4 0.0 copy-start
  78.4 20.6 %all_to_all.10.refs_1_ = f32[8,13,8,128]{3,2,1,0:T(8,128)} all-to-all(f32[8,13,8,128]{3,2,1,0:T(8,128)} %render.3), channel_id=1, replica_groups=mesh['depth'=8,'height'=32] {'depth'}, dimensions={0} | all-to-all | bytes 851968 | tf_op jit(solution)/shard_map/all_to_all | solution.py:464
  99.0 1.8 %fold.1.refs_0_ = f32[2,13,8,128]{3,2,1,0:T(8,128)} custom-call(f32[8,13,8,128]{3,2,1,0:T(8,128)} %copy-done, f32[8,13,8,128]{3,2,1,0:T(8,128)} %all_to_all.10.refs_1_), custom_call_target="tpu_custom_call" | custom-call | tf_op jit(solution)/shard_map/fold/pallas_call | solution.py:465
  100.8 0.7 collective-permute-start.8
  101.5 2.6 %collective-permute-start.12 = (f32[2,13,8,128]{3,2,1,0:T(8,128)}, f32[2,13,8,128]{3,2,1,0:T(8,128)S(1)}, u32[]{:S(2)}, u32[]{:S(2)}) collective-permute-start(f32[2,13,8,128]{3,2,1,0:T(8,128)} %fold.1.refs_0_), channel_id=1, source_target_pairs={{0,224},{32,0},{64,32},{96,64},{128,96},{160,128},{192,160},{224,1... | collective-permute-start | bytes 319496 | tf_op jit(solution)/shard_map/ppermute | solution.py:476
  104.1 3.9 %collective-permute-done.8.refs_1_ = f32[2,13,8,128]{3,2,1,0:T(8,128)S(1)} collective-permute-done((f32[2,13,8,128]{3,2,1,0:T(8,128)}, f32[2,13,8,128]{3,2,1,0:T(8,128)S(1)}, u32[]{:S(2)}, u32[]{:S(2)}) %collective-permute-start.8) | collective-permute-done | bytes 106528 | tf_op jit(solution)/shard_map/ppermute | solution.py:475
  108.0 0.0 collective-permute-start.9
  108.0 0.0 collective-permute-done.12.refs_5_
  108.0 3.2 %collective-permute-start.13 = (f32[2,13,8,128]{3,2,1,0:T(8,128)S(1)}, f32[2,13,8,128]{3,2,1,0:T(8,128)S(1)}, u32[]{:S(2)}, u32[]{:S(2)}) collective-permute-start(f32[2,13,8,128]{3,2,1,0:T(8,128)S(1)} %collective-permute-done.12.refs_5_), channel_id=1, source_target_pairs={{0,224},{32,0},{64,32},{96,64},{128,96},{160,128},{192,160},{224,1... | collective-permute-start | bytes 319496 | tf_op jit(solution)/shard_map/ppermute | solution.py:476
  111.2 2.8 %collective-permute-done.9.refs_2_ = f32[2,13,8,128]{3,2,1,0:T(8,128)S(1)} collective-permute-done((f32[2,13,8,128]{3,2,1,0:T(8,128)S(1)}, f32[2,13,8,128]{3,2,1,0:T(8,128)S(1)}, u32[]{:S(2)}, u32[]{:S(2)}) %collective-permute-start.9) | collective-permute-done | bytes 106528 | tf_op jit(solution)/shard_map/ppermute | solution.py:475
  114.0 0.0 collective-permute-start.10
  114.0 3.2 %collective-permute-start.14 = (f32[2,13,8,128]{3,2,1,0:T(8,128)S(1)}, f32[2,13,8,128]{3,2,1,0:T(8,128)S(1)}, u32[]{:S(2)}, u32[]{:S(2)}) collective-permute-start(f32[2,13,8,128]{3,2,1,0:T(8,128)S(1)} %collective-permute-done.13.refs_6_), channel_id=1, source_target_pairs={{0,224},{32,0},{64,32},{96,64},{128,96},{160,128},{192,160},{224,1... | collective-permute-start | bytes 319496 | tf_op jit(solution)/shard_map/ppermute | solution.py:476
  117.2 2.7 %collective-permute-done.10.refs_3_ = f32[2,13,8,128]{3,2,1,0:T(8,128)S(1)} collective-permute-done((f32[2,13,8,128]{3,2,1,0:T(8,128)S(1)}, f32[2,13,8,128]{3,2,1,0:T(8,128)S(1)}, u32[]{:S(2)}, u32[]{:S(2)}) %collective-permute-start.10) | collective-permute-done | bytes 106528 | tf_op jit(solution)/shard_map/ppermute | solution.py:475
  119.9 0.0 collective-permute-done.14.refs_7_
  119.9 5.9 %collective-permute-done.11.refs_4_ = f32[2,13,8,128]{3,2,1,0:T(8,128)S(1)} collective-permute-done((f32[2,13,8,128]{3,2,1,0:T(8,128)S(1)}, f32[2,13,8,128]{3,2,1,0:T(8,128)S(1)}, u32[]{:S(2)}, u32[]{:S(2)}) %collective-permute-start.11) | collective-permute-done | bytes 106528 | tf_op jit(solution)/shard_map/ppermute | solution.py:475
  125.9 0.6 copy-done.9
  126.5 2.2 %spread.1 = f32[13,16,8,128]{3,2,1,0:T(8,128)} custom-call(s32[1]{0:T(128)} %bitcast.place_ref, f32[2,13,8,128]{3,2,1,0:T(8,128)} %fold.1.refs_0_, f32[2,13,8,128]{3,2,1,0:T(8,128)} %copy-done.3, f32[2,13,8,128]{3,2,1,0:T(8,128)} %copy-done.5, f32[2,13,8,128]{3,2,1,0:T(8,128)} %copy-done.7, f32[2,13,8,128]{3,2,1,0:T(8,128)} %copy-done.9, ...), custom_call_target="tpu_custom_call" | custom-call | tf_op jit(solution)/shard_map/spread/pallas_call | solution.py:478
  (28 shorter events, 0.1 us)
Async XLA Ops:
  2.7 23.6 %collective-permute-start.2 = (f32[9,96,128]{2,1,0:T(8,128)}, f32[9,96,128]{2,1,0:T(8,128)S(1)}, u32[]{:S(2)}, u32[]{:S(2)}) collective-permute-start(f32[9,96,128]{2,1,0:T(8,128)} %get-tuple-element.15), channel_id=1, source_target_pairs={{0,1},{1,2},{2,3},{3,4},{4,5},{5,6},{6,7},{7,8},{8,9},{9,10},{10,1... | collective-permute-start | bytes 1327112 | tf_op jit(solution)/shard_map/ppermute | solution.py:411
  2.8 23.5 %collective-permute-start.3 = (f32[9,96,128]{2,1,0:T(8,128)}, f32[9,96,128]{2,1,0:T(8,128)S(1)}, u32[]{:S(2)}, u32[]{:S(2)}) collective-permute-start(f32[9,96,128]{2,1,0:T(8,128)} %get-tuple-element.16), channel_id=1, source_target_pairs={{0,31},{1,0},{2,1},{3,2},{4,3},{5,4},{6,5},{7,6},{8,7},{9,8},{10,9... | collective-permute-start | bytes 1327112 | tf_op jit(solution)/shard_map/ppermute | solution.py:412
  7.8 8.0 %collective-permute-start = (f32[3,16,8,128]{3,2,1,0:T(8,128)}, f32[3,16,8,128]{3,2,1,0:T(8,128)S(1)}, u32[]{:S(2)}, u32[]{:S(2)}) collective-permute-start(f32[3,16,8,128]{3,2,1,0:T(8,128)} %get-tuple-element.13), channel_id=1, source_target_pairs={{0,32},{32,64},{64,96},{96,128},{128,160},{160,192},{192,224},{224... | collective-permute-start | bytes 589832 | tf_op jit(solution)/shard_map/ppermute | solution.py:409
  8.0 7.8 %collective-permute-start.1 = (f32[3,16,8,128]{3,2,1,0:T(8,128)}, f32[3,16,8,128]{3,2,1,0:T(8,128)S(1)}, u32[]{:S(2)}, u32[]{:S(2)}) collective-permute-start(f32[3,16,8,128]{3,2,1,0:T(8,128)} %get-tuple-element.14), channel_id=1, source_target_pairs={{0,224},{32,0},{64,32},{96,64},{128,96},{160,128},{192,160},{224,1... | collective-permute-start | bytes 589832 | tf_op jit(solution)/shard_map/ppermute | solution.py:410
  15.8 0.7 copy-start.1
  16.5 0.7 copy-start.2
  18.9 7.3 %collective-permute-start.4 = (f32[16,8,128]{2,1,0:T(8,128)}, f32[16,8,128]{2,1,0:T(8,128)S(1)}, u32[]{:S(2)}, u32[]{:S(2)}) collective-permute-start(f32[16,8,128]{2,1,0:T(8,128)} %get-tuple-element.17), channel_id=1, source_target_pairs={{0,1},{1,2},{2,3},{3,4},{4,5},{5,6},{6,7},{7,8},{8,9},{9,10},{10,1... | collective-permute-start | bytes 196616 | tf_op jit(solution)/shard_map/ppermute | solution.py:422
  19.0 7.3 %collective-permute-start.5 = (f32[16,8,128]{2,1,0:T(8,128)}, f32[16,8,128]{2,1,0:T(8,128)S(1)}, u32[]{:S(2)}, u32[]{:S(2)}) collective-permute-start(f32[16,8,128]{2,1,0:T(8,128)} %get-tuple-element.18), channel_id=1, source_target_pairs={{0,31},{1,0},{2,1},{3,2},{4,3},{5,4},{6,5},{7,6},{8,7},{9,8},{10,9... | collective-permute-start | bytes 196616 | tf_op jit(solution)/shard_map/ppermute | solution.py:423
  24.6 25.1 %copy-start.11 = (f32[9,96,128]{2,1,0:T(8,128)S(1)}, f32[9,96,128]{2,1,0:T(8,128)}, u32[]{:S(2)}) copy-start(f32[9,96,128]{2,1,0:T(8,128)} %get-tuple-element.19) | copy-start | bytes 1327108
  24.6 25.2 %copy-start.10 = (f32[9,96,128]{2,1,0:T(8,128)S(1)}, f32[9,96,128]{2,1,0:T(8,128)}, u32[]{:S(2)}) copy-start(f32[9,96,128]{2,1,0:T(8,128)} %get-tuple-element.20) | copy-start | bytes 1327108
  26.2 0.6 copy-start.16
  26.2 0.6 copy-start.17
  26.2 0.8 copy-start.12
  27.0 0.8 copy-start.13
  43.8 34.5 %all-to-all-start = ((f32[8,13,8,128]{3,2,1,0:T(8,128)}), f32[8,13,8,128]{3,2,1,0:T(8,128)S(1)}, u32[]{:S(2)}, u32[]{:S(2)}) async-start(f32[8,13,8,128]{3,2,1,0:T(8,128)} %render.2), calls=%async_computation | async-start | bytes 851968 | tf_op jit(solution)/shard_map/all_to_all | solution.py:464
  49.7 11.1 %collective-permute-start.6 = (f32[9,96,128]{2,1,0:T(8,128)S(1)}, f32[9,96,128]{2,1,0:T(8,128)S(1)}, u32[]{:S(2)}, u32[]{:S(2)}) collective-permute-start(f32[9,96,128]{2,1,0:T(8,128)S(1)} %copy-done.11), channel_id=1, source_target_pairs={{0,1},{1,2},{2,3},{3,4},{4,5},{5,6},{6,7},{7,8},{8,9},{9,10},{10,1... | collective-permute-start | bytes 1327112 | tf_op jit(solution)/shard_map/ppermute | solution.py:411
  49.8 11.0 %collective-permute-start.7 = (f32[9,96,128]{2,1,0:T(8,128)S(1)}, f32[9,96,128]{2,1,0:T(8,128)S(1)}, u32[]{:S(2)}, u32[]{:S(2)}) collective-permute-start(f32[9,96,128]{2,1,0:T(8,128)S(1)} %copy-done.10), channel_id=1, source_target_pairs={{0,31},{1,0},{2,1},{3,2},{4,3},{5,4},{6,5},{7,6},{8,7},{9,8},{10,9... | collective-permute-start | bytes 1327112 | tf_op jit(solution)/shard_map/ppermute | solution.py:412
  60.8 0.8 copy-start.14
  61.6 0.8 copy-start.15
  78.4 20.6 %copy-start = (f32[8,13,8,128]{3,2,1,0:T(8,128)}, f32[8,13,8,128]{3,2,1,0:T(8,128)S(1)}, u32[]{:S(2)}) copy-start(f32[8,13,8,128]{3,2,1,0:T(8,128)S(1)} %all-to-all-done.refs_0_) | copy-start | bytes 1277956
  100.8 7.1 %collective-permute-start.8 = (f32[2,13,8,128]{3,2,1,0:T(8,128)}, f32[2,13,8,128]{3,2,1,0:T(8,128)S(1)}, u32[]{:S(2)}, u32[]{:S(2)}) collective-permute-start(f32[2,13,8,128]{3,2,1,0:T(8,128)} %fold.1.refs_0_), channel_id=1, source_target_pairs={{0,32},{32,64},{64,96},{96,128},{128,160},{160,192},{192,224},{224... | collective-permute-start | bytes 319496 | tf_op jit(solution)/shard_map/ppermute | solution.py:475
  101.5 6.5 %collective-permute-start.12 = (f32[2,13,8,128]{3,2,1,0:T(8,128)}, f32[2,13,8,128]{3,2,1,0:T(8,128)S(1)}, u32[]{:S(2)}, u32[]{:S(2)}) collective-permute-start(f32[2,13,8,128]{3,2,1,0:T(8,128)} %fold.1.refs_0_), channel_id=1, source_target_pairs={{0,224},{32,0},{64,32},{96,64},{128,96},{160,128},{192,160},{224,1... | collective-permute-start | bytes 319496 | tf_op jit(solution)/shard_map/ppermute | solution.py:476
  108.0 17.9 %copy-start.3 = (f32[2,13,8,128]{3,2,1,0:T(8,128)}, f32[2,13,8,128]{3,2,1,0:T(8,128)S(1)}, u32[]{:S(2)}) copy-start(f32[2,13,8,128]{3,2,1,0:T(8,128)S(1)} %collective-permute-done.8.refs_1_) | copy-start | bytes 319492
  108.0 6.0 %collective-permute-start.9 = (f32[2,13,8,128]{3,2,1,0:T(8,128)S(1)}, f32[2,13,8,128]{3,2,1,0:T(8,128)S(1)}, u32[]{:S(2)}, u32[]{:S(2)}) collective-permute-start(f32[2,13,8,128]{3,2,1,0:T(8,128)S(1)} %collective-permute-done.8.refs_1_), channel_id=1, source_target_pairs={{0,32},{32,64},{64,96},{96,128},{128,160},{160,192},{192,224},{224... | collective-permute-start | bytes 319496 | tf_op jit(solution)/shard_map/ppermute | solution.py:475
  108.0 17.9 %copy-start.4 = (f32[2,13,8,128]{3,2,1,0:T(8,128)}, f32[2,13,8,128]{3,2,1,0:T(8,128)S(1)}, u32[]{:S(2)}) copy-start(f32[2,13,8,128]{3,2,1,0:T(8,128)S(1)} %collective-permute-done.12.refs_5_) | copy-start | bytes 319492
  108.0 6.0 %collective-permute-start.13 = (f32[2,13,8,128]{3,2,1,0:T(8,128)S(1)}, f32[2,13,8,128]{3,2,1,0:T(8,128)S(1)}, u32[]{:S(2)}, u32[]{:S(2)}) collective-permute-start(f32[2,13,8,128]{3,2,1,0:T(8,128)S(1)} %collective-permute-done.12.refs_5_), channel_id=1, source_target_pairs={{0,224},{32,0},{64,32},{96,64},{128,96},{160,128},{192,160},{224,1... | collective-permute-start | bytes 319496 | tf_op jit(solution)/shard_map/ppermute | solution.py:476
  114.0 11.8 %copy-start.5 = (f32[2,13,8,128]{3,2,1,0:T(8,128)}, f32[2,13,8,128]{3,2,1,0:T(8,128)S(1)}, u32[]{:S(2)}) copy-start(f32[2,13,8,128]{3,2,1,0:T(8,128)S(1)} %collective-permute-done.9.refs_2_) | copy-start | bytes 319492
  114.0 5.9 %collective-permute-start.10 = (f32[2,13,8,128]{3,2,1,0:T(8,128)S(1)}, f32[2,13,8,128]{3,2,1,0:T(8,128)S(1)}, u32[]{:S(2)}, u32[]{:S(2)}) collective-permute-start(f32[2,13,8,128]{3,2,1,0:T(8,128)S(1)} %collective-permute-done.9.refs_2_), channel_id=1, source_target_pairs={{0,32},{32,64},{64,96},{96,128},{128,160},{160,192},{192,224},{224... | collective-permute-start | bytes 319496 | tf_op jit(solution)/shard_map/ppermute | solution.py:475
  114.0 11.8 %copy-start.6 = (f32[2,13,8,128]{3,2,1,0:T(8,128)}, f32[2,13,8,128]{3,2,1,0:T(8,128)S(1)}, u32[]{:S(2)}) copy-start(f32[2,13,8,128]{3,2,1,0:T(8,128)S(1)} %collective-permute-done.13.refs_6_) | copy-start | bytes 319492
  114.0 5.9 %collective-permute-start.14 = (f32[2,13,8,128]{3,2,1,0:T(8,128)S(1)}, f32[2,13,8,128]{3,2,1,0:T(8,128)S(1)}, u32[]{:S(2)}, u32[]{:S(2)}) collective-permute-start(f32[2,13,8,128]{3,2,1,0:T(8,128)S(1)} %collective-permute-done.13.refs_6_), channel_id=1, source_target_pairs={{0,224},{32,0},{64,32},{96,64},{128,96},{160,128},{192,160},{224,1... | collective-permute-start | bytes 319496 | tf_op jit(solution)/shard_map/ppermute | solution.py:476
  119.9 5.9 %copy-start.7 = (f32[2,13,8,128]{3,2,1,0:T(8,128)}, f32[2,13,8,128]{3,2,1,0:T(8,128)S(1)}, u32[]{:S(2)}) copy-start(f32[2,13,8,128]{3,2,1,0:T(8,128)S(1)} %collective-permute-done.10.refs_3_) | copy-start | bytes 319492
  119.9 5.9 %collective-permute-start.11 = (f32[2,13,8,128]{3,2,1,0:T(8,128)S(1)}, f32[2,13,8,128]{3,2,1,0:T(8,128)S(1)}, u32[]{:S(2)}, u32[]{:S(2)}) collective-permute-start(f32[2,13,8,128]{3,2,1,0:T(8,128)S(1)} %collective-permute-done.10.refs_3_), channel_id=1, source_target_pairs={{0,32},{32,64},{64,96},{96,128},{128,160},{160,192},{192,224},{224... | collective-permute-start | bytes 319496 | tf_op jit(solution)/shard_map/ppermute | solution.py:475
  119.9 5.9 %copy-start.8 = (f32[2,13,8,128]{3,2,1,0:T(8,128)}, f32[2,13,8,128]{3,2,1,0:T(8,128)S(1)}, u32[]{:S(2)}) copy-start(f32[2,13,8,128]{3,2,1,0:T(8,128)S(1)} %collective-permute-done.14.refs_7_) | copy-start | bytes 319492
  125.8 0.6 copy-start.9

commit v4 on v2

--- a/solution.py
+++ b/solution.py
@@ -24,21 +24,32 @@
     return d * inverse_of(d * d + 1.0)
 
 
-def pack(vol_ref, down_ref, up_ref, first_ref, last_ref, held, down, up, in_sem, edge_sem, out_sem):
+CORNERS = ((0, 0), (1, 0), (0, 1))
+
+
+def pack(vol_ref, down_ref, up_ref, first_ref, last_ref, *refs):
+    corner_refs = refs[0:4]
+    held, down, up, corners, in_sem, edge_sem, out_sem = refs[4:]
     cells, tiles = vol_ref.shape[0], vol_ref.shape[1]
     groups = cells // 8
-    loads = [
-        pltpu.make_async_copy(vol_ref.at[pl.ds(8 * g, 8)], held.at[pl.ds(8 * g, 8)], in_sem.at[g])
-        for g in range(groups)
+    order = [0, groups - 1] + list(range(1, groups - 1))
+    loads = {
+        g: pltpu.make_async_copy(
+            vol_ref.at[pl.ds(8 * g, 8)], held.at[pl.ds(8 * g, 8)], in_sem.at[g]
+        )
+        for g in order
+    }
+    edges = [
+        pltpu.make_async_copy(held.at[pl.ds(0, 3)], first_ref, edge_sem.at[0]),
+        pltpu.make_async_copy(held.at[pl.ds(cells - 3, 3)], last_ref, edge_sem.at[1]),
     ]
-    edges = [
-        pltpu.make_async_copy(vol_ref.at[pl.ds(0, 3)], first_ref, edge_sem.at[0]),
-        pltpu.make_async_copy(vol_ref.at[pl.ds(cells - 3, 3)], last_ref, edge_sem.at[1]),
+    edges += [
+        pltpu.make_async_copy(corners.at[i], corner_refs[i], edge_sem.at[2 + i]) for i in range(4)
     ]
-    for copy in loads + edges:
-        copy.start()
+    for g in order:
+        loads[g].start()
     stores = []
-    for g in range(groups):
+    for g in order:
         loads[g].wait()
         for k in range(8):
             z = 8 * g + k
@@ -52,30 +63,18 @@
             )
             copy.start()
             stores.append(copy)
+        if g == groups - 1:
+            for i, (z_far, row_far) in enumerate(((1, 1), (1, 0), (0, 1), (0, 0))):
+                for tile in range(tiles):
+                    for slot, (depth, row) in enumerate(CORNERS):
+                        z = cells - 1 - depth if z_far else depth
+                        r = ROWS - 1 - row if row_far else row
+                        corners[i, tile, slot : slot + 1, :] = held[z, tile, r : r + 1, :]
+                    corners[i, tile, 3:8, :] = jnp.zeros((5, LANES), F32)
+            for copy in edges:
+                copy.start()
     for copy in stores + edges:
         copy.wait()
-
-
-CORNERS = ((0, 1, 0), (0, 0, 0), (0, 1, 1), (1, 0, 0), (1, 1, 0), (1, 0, 1))
-
-
-def pack_corners(low_ref, high_ref, down_ref, up_ref, near, sem):
-    tiles = low_ref.shape[1]
-    copies = [
-        pltpu.make_async_copy(low_ref.at[pl.ds(1, 2)], near.at[0], sem.at[0]),
-        pltpu.make_async_copy(high_ref.at[pl.ds(0, 2)], near.at[1], sem.at[1]),
-    ]
-    for copy in copies:
-        copy.start()
-    for copy in copies:
-        copy.wait()
-    zero = jnp.zeros((2, LANES), F32)
-    for tile in range(tiles):
-        for slot, (side, plane, depth) in enumerate(CORNERS):
-            up_ref[tile, slot : slot + 1, :] = near[side, plane, tile, depth : depth + 1, :]
-            down_ref[tile, slot : slot + 1, :] = near[side, plane, tile, 7 - depth : 8 - depth, :]
-        up_ref[tile, 6:8, :] = zero
-        down_ref[tile, 6:8, :] = zero
 
 
 def beside(src, base, z, parity, nexts, befores):
@@ -172,9 +171,13 @@
     high_ref,
     top_ref,
     bottom_ref,
-    top_corner_ref,
-    bottom_corner_ref,
+    low_top_ref,
+    low_bottom_ref,
+    high_top_ref,
+    high_bottom_ref,
     out_ref,
+    twice_ref,
+    slope_ref,
     field,
     once,
     twice,
@@ -185,6 +188,7 @@
     rows_in,
     corners_in,
     sem,
+    later_sem,
     alpha_top,
 ):
     cells, tiles = vol_ref.shape[0], vol_ref.shape[1]
@@ -192,11 +196,13 @@
     copies = [
         pltpu.make_async_copy(low_ref, field.at[pl.ds(0, 3), :, own, :], sem.at[0]),
         pltpu.make_async_copy(high_ref, field.at[pl.ds(cells + 3, 3), :, own, :], sem.at[1]),
-        pltpu.make_async_copy(top_corner_ref, corners_in.at[0], sem.at[2]),
-        pltpu.make_async_copy(bottom_corner_ref, corners_in.at[1], sem.at[3]),
-        pltpu.make_async_copy(top_ref, rows_in.at[0], sem.at[4]),
-        pltpu.make_async_copy(bottom_ref, rows_in.at[1], sem.at[5]),
-        pltpu.make_async_copy(vol_ref, field.at[pl.ds(3, cells), :, own, :], sem.at[6]),
+        pltpu.make_async_copy(low_top_ref, corners_in.at[0], sem.at[2]),
+        pltpu.make_async_copy(low_bottom_ref, corners_in.at[1], sem.at[3]),
+        pltpu.make_async_copy(high_top_ref, corners_in.at[2], sem.at[4]),
+        pltpu.make_async_copy(high_bottom_ref, corners_in.at[3], sem.at[5]),
+        pltpu.make_async_copy(top_ref, rows_in.at[0], sem.at[6]),
+        pltpu.make_async_copy(bottom_ref, rows_in.at[1], sem.at[7]),
+        pltpu.make_async_copy(vol_ref, field.at[pl.ds(3, cells), :, own, :], sem.at[8]),
     ]
     for copy in copies:
         copy.start()
@@ -215,24 +221,21 @@
             for plane in (k, cells + 3 + k):
                 field[plane, tile, 0:8, :] = zero
                 field[plane, tile, 16:24, :] = zero
-    for copy in copies[:4]:
+    for copy in copies[:6]:
         copy.wait()
     for k in range(3):
         for tile in range(tiles):
             field[k, tile, own, :] = field[k, tile, own, :] * keep_low
             field[cells + 3 + k, tile, own, :] = field[cells + 3 + k, tile, own, :] * keep_high
-    for tile in range(tiles):
-        for slot, (side, plane, away) in enumerate(CORNERS):
-            at = (cells + 3 if side else 1) + plane
-            keep = keep_high if side else keep_low
-            field[at, tile, 7 - away : 8 - away, :] = corners_in[0, tile, slot : slot + 1, :] * (
-                keep * keep_top
-            )
-            field[at, tile, 16 + away : 17 + away, :] = corners_in[
-                1, tile, slot : slot + 1, :
-            ] * (keep * keep_bottom)
-    copies[4].wait()
-    copies[5].wait()
+    for i in range(4):
+        keep = (keep_high if i // 2 else keep_low) * (keep_bottom if i % 2 else keep_top)
+        for tile in range(tiles):
+            for slot, (depth, row) in enumerate(CORNERS):
+                at = cells + 3 + depth if i // 2 else 2 - depth
+                r = 16 + row if i % 2 else 7 - row
+                field[at, tile, r : r + 1, :] = corners_in[i, tile, slot : slot + 1, :] * keep
+    copies[6].wait()
+    copies[7].wait()
 
     def rims_in(g, carry):
         at = pl.multiple_of(24 * g, 24)
@@ -247,7 +250,7 @@
         return carry
 
     lax.fori_loop(0, cells // 8, rims_in, 0)
-    copies[6].wait()
+    copies[8].wait()
 
     diffuse(field, OWN, once, cells + 4, nexts, befores, held, rims)
     for k in range(2):
@@ -261,6 +264,54 @@
         twice[0, tile, own, :] = twice[0, tile, own, :] * keep_low
         twice[cells + 1, tile, own, :] = twice[cells + 1, tile, own, :] * keep_high
 
+    half = out_ref.shape[0]
+    later = [
+        pltpu.make_async_copy(twice.at[:, pl.ds(half, half)], twice_ref, later_sem.at[0]),
+        pltpu.make_async_copy(slope.at[:, pl.ds(half, half)], slope_ref, later_sem.at[1]),
+    ]
+    for copy in later:
+        copy.start()
+    shade(colour_ref, opacity_ref, dir_ref, light_ref, twice, slope, out_ref, alpha_top)
+    for copy in later:
+        copy.wait()
+
+
+def render_rest(
+    colour_ref,
+    opacity_ref,
+    dir_ref,
+    light_ref,
+    twice_ref,
+    slope_ref,
+    out_ref,
+    twice,
+    slope,
+    sem,
+    alpha_top,
+):
+    def load(tile):
+        return [
+            pltpu.make_async_copy(twice_ref.at[:, tile], twice.at[:, tile], sem.at[0, tile]),
+            pltpu.make_async_copy(slope_ref.at[:, tile], slope.at[:, tile], sem.at[1, tile]),
+        ]
+
+    for tile in range(out_ref.shape[0]):
+        for copy in load(tile):
+            copy.start()
+
+    def ready(tile):
+        for copy in load(tile):
+            copy.wait()
+
+    shade(colour_ref, opacity_ref, dir_ref, light_ref, twice, slope, out_ref, alpha_top, ready)
+
+
+def shade(
+    colour_ref, opacity_ref, dir_ref, light_ref, twice, slope, out_ref, alpha_top, ready=None
+):
+    cells = slope.shape[0] - 1
+    own = pl.ds(OWN, 8)
+    zero = jnp.zeros((ROWS, LANES), F32)
     colour = [[colour_ref[c, j] for j in range(4)] for c in range(3)]
     opac = [opacity_ref[j] for j in range(4)]
     light = [[0.5 * dir_ref[l, d] for d in range(3)] for l in range(4)]
@@ -269,6 +320,9 @@
         return ((c[3] * v + c[2]) * v + c[1]) * v + c[0]
 
     def column(tile, carry):
+        if ready is not None:
+            ready(tile)
+
         def cell(z, state):
             through, sums, base_sums = state
             v = twice[z + 1, tile, own, :]
@@ -295,45 +349,50 @@
         state = (jnp.ones((ROWS, LANES), F32), [zero] * 12, [zero] * 3)
 
         def group(g, state):
-            for k in range(4):
-                state = cell(g * 4 + k, state)
+            for k in range(8):
+                state = cell(g * 8 + k, state)
             return state
 
-        through, sums, base_sums = lax.fori_loop(0, cells // 4, group, state)
+        through, sums, base_sums = lax.fori_loop(0, cells // 8, group, state)
         for l in range(4):
             for c in range(3):
-                out_ref[tile // 2, 3 * l + c, tile % 2] = light_ref[l, c] * (
+                out_ref[tile, 3 * l + c] = light_ref[l, c] * (
                     0.2 * base_sums[c] + sums[3 * l + c]
                 )
-        out_ref[tile // 2, 12, tile % 2] = 1.0 - through
+        out_ref[tile, 12] = 1.0 - through
         return carry
 
-    lax.fori_loop(0, tiles, column, 0)
-
-
-def fold(parts_ref, out_ref):
+    lax.fori_loop(0, out_ref.shape[0], column, 0)
+
+
+def fold(parts_ref, *refs):
+    if len(refs) > 1:
+        first_ref, both_ref = refs
+        both_ref[0] = first_ref[...]
+        out_ref = both_ref.at[1]
+    else:
+        (out_ref,) = refs
     slabs, channels = parts_ref.shape[0], parts_ref.shape[1]
-    for tile in range(parts_ref.shape[2]):
-        through = 1.0 - parts_ref[0, 12, tile]
-        total = [parts_ref[0, ch, tile] for ch in range(channels)]
-        for slab in range(1, slabs):
-            total = [total[ch] + through * parts_ref[slab, ch, tile] for ch in range(channels)]
-            through = through * (1.0 - parts_ref[slab, 12, tile])
-        for ch in range(channels):
-            out_ref[ch, tile] = total[ch]
-
-
-def spread(place_ref, *refs):
-    pieces, out_ref, sem = refs[:-2], refs[-2], refs[-1]
-    count = len(pieces)
-    tiles = out_ref.shape[1] // count
+    through = 1.0 - parts_ref[0, 12]
+    total = [parts_ref[0, ch] for ch in range(channels)]
+    for slab in range(1, slabs):
+        total = [total[ch] + through * parts_ref[slab, ch] for ch in range(channels)]
+        through = through * (1.0 - parts_ref[slab, 12])
+    for ch in range(channels):
+        out_ref[ch] = total[ch]
+
+
+def spread(count, offsets, place_ref, *refs):
+    pieces, out_ref, sem = refs[: len(offsets)], refs[-2], refs[-1]
     copies = []
-    for step, ref in enumerate(pieces):
-        offset = step if step <= count // 2 else count // 2 - step
-        owner = lax.rem(place_ref[0] - offset + count, count)
-        copies.append(
-            pltpu.make_async_copy(ref, out_ref.at[:, pl.ds(owner * tiles, tiles)], sem.at[step])
-        )
+    for i, ref in enumerate(pieces):
+        owner = lax.rem(place_ref[0] - offsets[i] + count, count)
+        for half in range(2):
+            copies.append(
+                pltpu.make_async_copy(
+                    ref.at[half], out_ref.at[:, half * count + owner], sem.at[2 * i + half]
+                )
+            )
     for copy in copies:
         copy.start()
     for copy in copies:
@@ -369,44 +428,51 @@
     limit = pltpu.CompilerParams(vmem_limit_bytes=58 << 20)
     field = volume.reshape(cells, rows, tiles, LANES).transpose(0, 2, 1, 3)
 
-    down, up, first, last = pl.pallas_call(
+    packed = pl.pallas_call(
         pack,
-        out_shape=[shape(tiles, 3 * cells, LANES)] * 2 + [shape(3, tiles, rows, LANES)] * 2,
+        out_shape=[shape(tiles, 3 * cells, LANES)] * 2
+        + [shape(3, tiles, rows, LANES)] * 2
+        + [shape(tiles, rows, LANES)] * 4,
         in_specs=anywhere(1),
-        out_specs=anywhere(4),
+        out_specs=anywhere(8),
         scratch_shapes=[
             VMEM((cells, tiles, rows, LANES), F32),
             VMEM((tiles, 3 * cells, LANES), F32),
             VMEM((tiles, 3 * cells, LANES), F32),
+            VMEM((4, tiles, rows, LANES), F32),
             DMA((cells // 8,)),
-            DMA((2,)),
+            DMA((6,)),
             DMA((cells // 4,)),
         ],
         compiler_params=limit,
         name="pack",
     )(field)
+    down, up, first, last = packed[:4]
     top = lax.ppermute(down, "height", ring("height", 1))
     bottom = lax.ppermute(up, "height", ring("height", -1))
     low = lax.ppermute(last, "depth", ring("depth", 1))
     high = lax.ppermute(first, "depth", ring("depth", -1))
-    corner_down, corner_up = pl.pallas_call(
-        pack_corners,
-        out_shape=[shape(tiles, rows, LANES)] * 2,
-        in_specs=anywhere(2),
-        out_specs=in_vmem(2),
-        scratch_shapes=[VMEM((2, 2, tiles, rows, LANES), F32), DMA((2,))],
-        compiler_params=limit,
-        name="pack_corners",
-    )(low, high)
-    top_corner = lax.ppermute(corner_down, "height", ring("height", 1))
-    bottom_corner = lax.ppermute(corner_up, "height", ring("height", -1))
+    corners = []
+    for i, (dz, dh) in enumerate(((1, 1), (1, -1), (-1, 1), (-1, -1))):
+        pairs = [
+            (z * bands + h, (z + dz) % slabs * bands + (h + dh) % bands)
+            for z in range(slabs)
+            for h in range(bands)
+        ]
+        corners.append(lax.ppermute(packed[4 + i], ("depth", "height"), pairs))
 
     edges = jnp.stack([slab > 0, slab < slabs - 1, band > 0, band < bands - 1]).astype(F32)
-    partial = pl.pallas_call(
-        functools.partial(render, alpha_top=2.0 / (cells * slabs)),
-        out_shape=shape(slabs, 13, tiles // slabs, rows, LANES),
-        in_specs=in_smem(5) + anywhere(7),
-        out_specs=pl.BlockSpec(memory_space=VMEM),
+    half = tiles // 2
+    alpha_top = 2.0 / (cells * slabs)
+    partial, twice, slope = pl.pallas_call(
+        functools.partial(render, alpha_top=alpha_top),
+        out_shape=[
+            shape(half, 13, rows, LANES),
+            shape(cells + 2, half, 16, LANES),
+            shape(cells + 1, half, rows, LANES),
+        ],
+        in_specs=in_smem(5) + anywhere(9),
+        out_specs=in_vmem(1) + anywhere(2),
         scratch_shapes=[
             VMEM((cells + 6, tiles, 24, LANES), F32),
             VMEM((cells + 4, tiles, 16, LANES), F32),
@@ -416,10 +482,14 @@
             VMEM((2, tiles, 2, rows, LANES), F32),
             VMEM((tiles, 2, rows, LANES), F32),
             VMEM((2, tiles, 3 * cells, LANES), F32),
-            VMEM((2, tiles, rows, LANES), F32),
-            DMA((7,)),
+            VMEM((4, tiles, rows, LANES), F32),
+            DMA((9,)),
+            DMA((2,)),
         ],
         compiler_params=limit,
+        cost_estimate=pl.CostEstimate(
+            flops=400_000_000, bytes_accessed=40_000_000, transcendentals=4_000_000
+        ),
         name="render",
     )(
         edges,
@@ -432,29 +502,54 @@
         high,
         top,
         bottom,
-        top_corner,
-        bottom_corner,
+        *corners,
     )
-    exchanged = lax.all_to_all(partial, "depth", 0, 0, tiled=True)
-    own = pl.pallas_call(
-        fold,
-        out_shape=shape(13, tiles // slabs, rows, LANES),
-        in_specs=in_vmem(1),
+    partial_rest = pl.pallas_call(
+        functools.partial(render_rest, alpha_top=alpha_top),
+        out_shape=shape(half, 13, rows, LANES),
+        in_specs=in_smem(4) + anywhere(2),
         out_specs=pl.BlockSpec(memory_space=VMEM),
+        scratch_shapes=[
+            VMEM((cells + 2, half, 16, LANES), F32),
+            VMEM((cells + 1, half, rows, LANES), F32),
+            DMA((2, half)),
+        ],
         compiler_params=limit,
-        name="fold",
-    )(exchanged)
-    from_below, from_above = [own], [own]
-    for _ in range(slabs // 2):
+        cost_estimate=pl.CostEstimate(
+            flops=50_000_000, bytes_accessed=10_000_000, transcendentals=1_000_000
+        ),
+        name="render_rest",
+    )(colour_coef, opacity_coef, light_dir, light_colour, twice, slope)
+    count = slabs // 2
+    own = []
+    for value in (partial, partial_rest):
+        exchanged = lax.all_to_all(value, "depth", 0, 0, tiled=True)
+        image_shape = (2,) * len(own) + (13, rows, LANES)
+        own = [
+            pl.pallas_call(
+                fold,
+                out_shape=shape(*image_shape),
+                in_specs=in_vmem(1 + len(own)),
+                out_specs=pl.BlockSpec(memory_space=VMEM),
+                compiler_params=limit,
+                cost_estimate=pl.CostEstimate(
+                    flops=10_000_000, bytes_accessed=2_000_000, transcendentals=0
+                ),
+                name="fold",
+            )(exchanged, *own)
+        ]
+    (both,) = own
+    from_below, from_above = [both], [both]
+    for _ in range(count):
         from_below.append(lax.ppermute(from_below[-1], "depth", ring("depth", 1)))
         from_above.append(lax.ppermute(from_above[-1], "depth", ring("depth", -1)))
-    pieces = from_below + from_above[1 : slabs // 2]
+    pieces = from_below + from_above[1:count]
     image = pl.pallas_call(
-        spread,
+        functools.partial(spread, slabs, [k for k in range(count + 1)] + [-k for k in range(1, count)]),
         out_shape=shape(13, tiles, rows, LANES),
-        in_specs=in_smem(1) + anywhere(slabs),
+        in_specs=in_smem(1) + in_vmem(slabs),
         out_specs=pl.BlockSpec(memory_space=pl.ANY),
-        scratch_shapes=[DMA((slabs,))],
+        scratch_shapes=[DMA((2 * slabs,))],
         compiler_params=limit,
         name="spread",
     )(slab[None], *pieces)

time: 148 us -> 123 us (0.83); the launches traced: 145 us -> 122 us
  Pallas kernels: 69.6 us -> 35.9 us
  waiting for transfers between devices: 19.9 us -> 48.5 us
  blocking collectives: 26.7 us -> 0 us
  starting transfers between devices: 24.1 us -> 34 us
    all_to_all x1 -> x0, blocking collectives: 26.7 us -> none  [per_device(): exchanged = lax.all_to_all(partial, 'depth', 0, 0, tiled=True)]
    pallas_call x4 -> x5, Pallas kernels: 56.4 us -> 33.1 us  [the longest x1 20.9 us: per_device(): pl.pallas_call(functools.partial(render, alpha_top=alpha_top), out_shape=...]
    all_to_all x0 -> x2, waiting for transfers between devices: none -> 19.9 us  [per_device(): exchanged = lax.all_to_all(value, 'depth', 0, 0, tiled=True)]
    ppermute x2 -> x4, waiting for transfers between devices: 1.62 us -> 13.8 us  [per_device(): corners.append(lax.ppermute(packed[4 + i], ('depth', 'height'), pairs))]
    pallas_call x1, Pallas kernels: 13.1 us -> 2.72 us  [per_device(): pl.pallas_call(pack, out_shape=[shape(tiles, 3 * cells, LANES)] * 2 + [sh...]
    all_to_all x0 -> x2, starting transfers between devices: none -> 7.9 us  [per_device(): exchanged = lax.all_to_all(value, 'depth', 0, 0, tiled=True)]
    ppermute x1, waiting for transfers between devices: 3.85 us -> 0.01 us  [per_device(): low = lax.ppermute(last, 'depth', ring('depth', 1))]
    ppermute x1, starting transfers between devices: 0.18 us -> 1.92 us  [per_device(): low = lax.ppermute(last, 'depth', ring('depth', 1))]
  transfers between devices with their start and end apart: 13 -> 17, of which waited for: 7 -> 9; matrix products, arithmetic and copies ran while one was open for 0% -> 0% of each run, Pallas kernels for 1% -> 7%
where the time goes in v4:
time: 123 us; the launch traced here: 122 us
  waiting for transfers between devices  48.5 us (39%)
  Pallas kernels  35.9 us (29%)
  starting transfers between devices  34 us (28%)
  local copies, waits for them, and re-layouts  3.23 us (3%)
    pallas_call x1, Pallas kernels, per_device(): pl.pallas_call(functools.partial(render, alpha_top=alpha_top), out_shape=...  20.9 us
    all_to_all x2, waiting for transfers between devices, per_device(): exchanged = lax.all_to_all(value, 'depth', 0, 0, tiled=True)  19.9 us
    ppermute x4, waiting for transfers between devices, per_device(): from_below.append(lax.ppermute(from_below[-1], 'depth', ring('depth', 1)))  14.8 us
    ppermute x4, waiting for transfers between devices, per_device(): corners.append(lax.ppermute(packed[4 + i], ('depth', 'height'), pairs))  13.8 us
    ppermute x3, starting transfers between devices, per_device(): from_above.append(lax.ppermute(from_above[-1], 'depth', ring('depth', -1)))  9.61 us
    all_to_all x2, starting transfers between devices, per_device(): exchanged = lax.all_to_all(value, 'depth', 0, 0, tiled=True)  7.9 us
    pallas_call x1, Pallas kernels, per_device(): pl.pallas_call(functools.partial(render_rest, alpha_top=alpha_top), out_s...  6.66 us
    ppermute x4, starting transfers between devices, per_device(): corners.append(lax.ppermute(packed[4 + i], ('depth', 'height'), pairs))  6.04 us
  transfers between devices with their start and end apart: 17, of which 9 were waited for; matrix products, arithmetic and copies ran while one was open for 0% of the time, Pallas kernels for 7%

profile of v4, /device:TPU:0, one launch (start us, length us, event | category | flops | bytes accessed | tf_op | source)
XLA Modules:
  0.0 122.4 jit_solution(1044620481316241243)
XLA Ops:
  0.0 2.7 %pack.1 = (f32[16,96,128]{2,1,0:T(8,128)}, f32[16,96,128]{2,1,0:T(8,128)}, f32[3,16,8,128]{3,2,1,0:T(8,128)}, f32[3,16,8,128]{3,2,1,0:T(8,128)}, f32[16,8,128]{2...) custom-call(f32[32,16,8,128]{3,2,1,0:T(8,128)} %bitcast.11), custom_call_target="tpu_custom_call" | custom-call | tf_op jit(solution)/shard_map/pack/pallas_call | solution.py:431
  2.7 0.1 collective-permute-start.2
  2.8 5.1 %collective-permute-start.3 = (f32[16,96,128]{2,1,0:T(8,128)}, f32[16,96,128]{2,1,0:T(8,128)S(1)}, u32[]{:S(2)}, u32[]{:S(2)}) collective-permute-start(f32[16,96,128]{2,1,0:T(8,128)} %get-tuple-element.19), channel_id=1, source_target_pairs={{0,31},{1,0},{2,1},{3,2},{4,3},{5,4},{6,5},{7,6},{8,7},{9,8},{10,9... | collective-permute-start | bytes 2359304 | tf_op jit(solution)/shard_map/ppermute | solution.py:452
  7.9 0.0 collective-permute-start.4
  7.9 6.0 %collective-permute-start.5 = (f32[16,8,128]{2,1,0:T(8,128)}, f32[16,8,128]{2,1,0:T(8,128)S(1)}, u32[]{:S(2)}, u32[]{:S(2)}) collective-permute-start(f32[16,8,128]{2,1,0:T(8,128)} %get-tuple-element.21), channel_id=1, source_target_pairs={{0,63},{1,32},{2,33},{3,34},{4,35},{5,36},{6,37},{7,38},{8,39},{9,... | collective-permute-start | bytes 196616 | tf_op jit(solution)/shard_map/ppermute | solution.py:462
  13.9 1.9 %collective-permute-start = (f32[3,16,8,128]{3,2,1,0:T(8,128)}, f32[3,16,8,128]{3,2,1,0:T(8,128)S(1)}, u32[]{:S(2)}, u32[]{:S(2)}) collective-permute-start(f32[3,16,8,128]{3,2,1,0:T(8,128)} %get-tuple-element.16), channel_id=1, source_target_pairs={{0,32},{32,64},{64,96},{96,128},{128,160},{160,192},{192,224},{224... | collective-permute-start | bytes 589832 | tf_op jit(solution)/shard_map/ppermute | solution.py:453
  15.8 1.8 %collective-permute-done.4.low_top_ref = f32[16,8,128]{2,1,0:T(8,128)S(1)} collective-permute-done((f32[16,8,128]{2,1,0:T(8,128)}, f32[16,8,128]{2,1,0:T(8,128)S(1)}, u32[]{:S(2)}, u32[]{:S(2)}) %collective-permute-start.4) | collective-permute-done | bytes 65568 | tf_op jit(solution)/shard_map/ppermute | solution.py:462
  17.6 2.8 %collective-permute-start.1 = (f32[3,16,8,128]{3,2,1,0:T(8,128)}, f32[3,16,8,128]{3,2,1,0:T(8,128)S(1)}, u32[]{:S(2)}, u32[]{:S(2)}) collective-permute-start(f32[3,16,8,128]{3,2,1,0:T(8,128)} %get-tuple-element.17), channel_id=1, source_target_pairs={{0,224},{32,0},{64,32},{96,64},{128,96},{160,128},{192,160},{224,1... | collective-permute-start | bytes 589832 | tf_op jit(solution)/shard_map/ppermute | solution.py:454
  20.4 0.0 collective-permute-done.5.low_bottom_ref
  20.4 0.0 collective-permute-start.6
  20.4 8.8 %collective-permute-done.6.high_top_ref = f32[16,8,128]{2,1,0:T(8,128)S(1)} collective-permute-done((f32[16,8,128]{2,1,0:T(8,128)}, f32[16,8,128]{2,1,0:T(8,128)S(1)}, u32[]{:S(2)}, u32[]{:S(2)}) %collective-permute-start.6) | collective-permute-done | bytes 65568 | tf_op jit(solution)/shard_map/ppermute | solution.py:462
  29.2 0.0 collective-permute-start.7
  29.2 0.6 add_convert_fusion.edge_ref
  29.8 3.3 %collective-permute-done.7.high_bottom_ref = f32[16,8,128]{2,1,0:T(8,128)S(1)} collective-permute-done((f32[16,8,128]{2,1,0:T(8,128)}, f32[16,8,128]{2,1,0:T(8,128)S(1)}, u32[]{:S(2)}, u32[]{:S(2)}) %collective-permute-start.7) | collective-permute-done | bytes 65568 | tf_op jit(solution)/shard_map/ppermute | solution.py:462
  33.1 0.0 collective-permute-done.low_ref
  33.1 0.0 collective-permute-done.1.high_ref
  33.1 0.0 collective-permute-done.2.top_ref
  33.1 0.0 copy-start.9
  33.1 0.0 collective-permute-done.3.bottom_ref
  33.2 0.5 copy-done.16
  33.7 0.1 copy-done.11
  33.8 0.1 copy-done.12
  33.9 0.2 copy-done.9
  34.1 0.9 copy-done.10
  35.0 20.9 %render.1 = (f32[8,13,8,128]{3,2,1,0:T(8,128)}, f32[34,8,16,128]{3,2,1,0:T(8,128)}, f32[33,8,8,128]{3,2,1,0:T(8,128)}) custom-call(f32[4]{0:T(128)} %add_convert_fusion.edge_ref, f32[3,4]{1,0:T(4,128)} %colour_ref.3, f32[4]{0:T(128)} %opacity_ref.3, f32[4,3]{1,0:T(4,128)} %dir_ref.3, f32[4,3]{1,0:T(4,128)} %light_ref.3, f32[32,16,8,128]{3,2,1,0:T(8,128)} %bitcast.12, ...), custom_call_target="tpu_custom_call" | custom-call | flops 400000000 | bytes 40000000 | tf_op jit(solution)/shard_map/render/pallas_call | solution.py:467
  55.9 4.4 %all-to-all-start.1 = ((f32[8,13,8,128]{3,2,1,0:T(8,128)}), f32[8,13,8,128]{3,2,1,0:T(8,128)S(1)}, u32[]{:S(2)}, u32[]{:S(2)}) async-start(f32[8,13,8,128]{3,2,1,0:T(8,128)} %get-tuple-element.26), calls=%async_computation.1 | async-start | bytes 851968 | tf_op jit(solution)/shard_map/all_to_all | solution.py:526
  60.3 6.7 %render_rest.1 = f32[8,13,8,128]{3,2,1,0:T(8,128)} custom-call(f32[3,4]{1,0:T(4,128)} %colour_ref.3, f32[4]{0:T(128)} %opacity_ref.3, f32[4,3]{1,0:T(4,128)} %dir_ref.3, f32[4,3]{1,0:T(4,128)} %light_ref.3, f32[34,8,16,128]{3,2,1,0:T(8,128)} %get-tuple-element.24.twice_ref, f32[33,8,8,128]{3,2,1,0:T(8,128)} %get-tuple-element.25.slope_ref), custom_call_target="tpu_custom_call" | custom-call | flops 50000000 | bytes 10000000 | tf_op jit(solution)/shard_map/render_rest/pallas_call | solution.py:507
  67.0 7.9 %all-to-all-done.1.parts_ref = f32[8,13,8,128]{3,2,1,0:T(8,128)S(1)} async-done(((f32[8,13,8,128]{3,2,1,0:T(8,128)}), f32[8,13,8,128]{3,2,1,0:T(8,128)S(1)}, u32[]{:S(2)}, u32[]{:S(2)}) %all-to-all-start.1) | async-done | bytes 426016 | tf_op jit(solution)/shard_map/all_to_all | solution.py:526
  74.9 3.5 %all-to-all-start = ((f32[8,13,8,128]{3,2,1,0:T(8,128)}), f32[8,13,8,128]{3,2,1,0:T(8,128)S(1)}, u32[]{:S(2)}, u32[]{:S(2)}) async-start(f32[8,13,8,128]{3,2,1,0:T(8,128)} %render_rest.1), calls=%async_computation | async-start | bytes 851968 | tf_op jit(solution)/shard_map/all_to_all | solution.py:526
  78.4 1.7 %fold.2.refs_0_ = f32[13,8,128]{2,1,0:T(8,128)} custom-call(f32[8,13,8,128]{3,2,1,0:T(8,128)} %copy-done), custom_call_target="tpu_custom_call" | custom-call | flops 10000000 | bytes 2000000 | tf_op jit(solution)/shard_map/fold/pallas_call | solution.py:529
  80.1 12.0 %all-to-all-done.parts_ref = f32[8,13,8,128]{3,2,1,0:T(8,128)S(1)} async-done(((f32[8,13,8,128]{3,2,1,0:T(8,128)}), f32[8,13,8,128]{3,2,1,0:T(8,128)S(1)}, u32[]{:S(2)}, u32[]{:S(2)}) %all-to-all-start) | async-done | bytes 426016 | tf_op jit(solution)/shard_map/all_to_all | solution.py:526
  92.1 0.8 copy-done.1
  92.8 1.7 %fold.3.refs_0_ = f32[2,13,8,128]{3,2,1,0:T(8,128)} custom-call(f32[8,13,8,128]{3,2,1,0:T(8,128)} %copy-done.1, f32[13,8,128]{2,1,0:T(8,128)} %fold.2.refs_0_), custom_call_target="tpu_custom_call" | custom-call | flops 10000000 | bytes 2000000 | tf_op jit(solution)/shard_map/fold/pallas_call | solution.py:529
  94.5 0.6 collective-permute-start.8
  95.1 2.7 %collective-permute-start.12 = (f32[2,13,8,128]{3,2,1,0:T(8,128)}, f32[2,13,8,128]{3,2,1,0:T(8,128)S(1)}, u32[]{:S(2)}, u32[]{:S(2)}) collective-permute-start(f32[2,13,8,128]{3,2,1,0:T(8,128)} %fold.3.refs_0_), channel_id=1, source_target_pairs={{0,224},{32,0},{64,32},{96,64},{128,96},{160,128},{192,160},{224,1... | collective-permute-start | bytes 319496 | tf_op jit(solution)/shard_map/ppermute | solution.py:545
  97.7 3.7 %collective-permute-done.8.refs_1_ = f32[2,13,8,128]{3,2,1,0:T(8,128)S(1)} collective-permute-done((f32[2,13,8,128]{3,2,1,0:T(8,128)}, f32[2,13,8,128]{3,2,1,0:T(8,128)S(1)}, u32[]{:S(2)}, u32[]{:S(2)}) %collective-permute-start.8) | collective-permute-done | bytes 106528 | tf_op jit(solution)/shard_map/ppermute | solution.py:544
  101.4 0.0 collective-permute-start.9
  101.4 0.0 collective-permute-done.12.refs_5_
  101.5 3.5 %collective-permute-start.13 = (f32[2,13,8,128]{3,2,1,0:T(8,128)S(1)}, f32[2,13,8,128]{3,2,1,0:T(8,128)S(1)}, u32[]{:S(2)}, u32[]{:S(2)}) collective-permute-start(f32[2,13,8,128]{3,2,1,0:T(8,128)S(1)} %collective-permute-done.12.refs_5_), channel_id=1, source_target_pairs={{0,224},{32,0},{64,32},{96,64},{128,96},{160,128},{192,160},{224,1... | collective-permute-start | bytes 319496 | tf_op jit(solution)/shard_map/ppermute | solution.py:545
  104.9 2.7 %collective-permute-done.9.refs_2_ = f32[2,13,8,128]{3,2,1,0:T(8,128)S(1)} collective-permute-done((f32[2,13,8,128]{3,2,1,0:T(8,128)S(1)}, f32[2,13,8,128]{3,2,1,0:T(8,128)S(1)}, u32[]{:S(2)}, u32[]{:S(2)}) %collective-permute-start.9) | collective-permute-done | bytes 106528 | tf_op jit(solution)/shard_map/ppermute | solution.py:544
  107.7 0.0 collective-permute-start.10
  107.7 0.0 collective-permute-done.13.refs_6_
  107.7 3.5 %collective-permute-start.14 = (f32[2,13,8,128]{3,2,1,0:T(8,128)S(1)}, f32[2,13,8,128]{3,2,1,0:T(8,128)S(1)}, u32[]{:S(2)}, u32[]{:S(2)}) collective-permute-start(f32[2,13,8,128]{3,2,1,0:T(8,128)S(1)} %collective-permute-done.13.refs_6_), channel_id=1, source_target_pairs={{0,224},{32,0},{64,32},{96,64},{128,96},{160,128},{192,160},{224,1... | collective-permute-start | bytes 319496 | tf_op jit(solution)/shard_map/ppermute | solution.py:545
  111.2 2.4 %collective-permute-done.10.refs_3_ = f32[2,13,8,128]{3,2,1,0:T(8,128)S(1)} collective-permute-done((f32[2,13,8,128]{3,2,1,0:T(8,128)S(1)}, f32[2,13,8,128]{3,2,1,0:T(8,128)S(1)}, u32[]{:S(2)}, u32[]{:S(2)}) %collective-permute-start.10) | collective-permute-done | bytes 106528 | tf_op jit(solution)/shard_map/ppermute | solution.py:544
  113.6 0.0 collective-permute-start.11
  113.6 5.9 %collective-permute-done.11.refs_4_ = f32[2,13,8,128]{3,2,1,0:T(8,128)S(1)} collective-permute-done((f32[2,13,8,128]{3,2,1,0:T(8,128)S(1)}, f32[2,13,8,128]{3,2,1,0:T(8,128)S(1)}, u32[]{:S(2)}, u32[]{:S(2)}) %collective-permute-start.11) | collective-permute-done | bytes 106528 | tf_op jit(solution)/shard_map/ppermute | solution.py:544
  119.5 0.6 copy-done.8
  120.2 2.2 %spread.1 = f32[13,16,8,128]{3,2,1,0:T(8,128)} custom-call(s32[1]{0:T(128)} %bitcast.place_ref, f32[2,13,8,128]{3,2,1,0:T(8,128)} %fold.3.refs_0_, f32[2,13,8,128]{3,2,1,0:T(8,128)} %copy-done.2, f32[2,13,8,128]{3,2,1,0:T(8,128)} %copy-done.4, f32[2,13,8,128]{3,2,1,0:T(8,128)} %copy-done.6, f32[2,13,8,128]{3,2,1,0:T(8,128)} %copy-done.8, ...), custom_call_target="tpu_custom_call" | custom-call | tf_op jit(solution)/shard_map/spread/pallas_call | solution.py:547
  (27 shorter events, 0.1 us)
Async XLA Ops:
  2.7 30.4 %collective-permute-start.2 = (f32[16,96,128]{2,1,0:T(8,128)}, f32[16,96,128]{2,1,0:T(8,128)S(1)}, u32[]{:S(2)}, u32[]{:S(2)}) collective-permute-start(f32[16,96,128]{2,1,0:T(8,128)} %get-tuple-element.18), channel_id=1, source_target_pairs={{0,1},{1,2},{2,3},{3,4},{4,5},{5,6},{6,7},{7,8},{8,9},{9,10},{10,1... | collective-permute-start | bytes 2359304 | tf_op jit(solution)/shard_map/ppermute | solution.py:451
  2.8 30.3 %collective-permute-start.3 = (f32[16,96,128]{2,1,0:T(8,128)}, f32[16,96,128]{2,1,0:T(8,128)S(1)}, u32[]{:S(2)}, u32[]{:S(2)}) collective-permute-start(f32[16,96,128]{2,1,0:T(8,128)} %get-tuple-element.19), channel_id=1, source_target_pairs={{0,31},{1,0},{2,1},{3,2},{4,3},{5,4},{6,5},{7,6},{8,7},{9,8},{10,9... | collective-permute-start | bytes 2359304 | tf_op jit(solution)/shard_map/ppermute | solution.py:452
  7.9 9.7 %collective-permute-start.4 = (f32[16,8,128]{2,1,0:T(8,128)}, f32[16,8,128]{2,1,0:T(8,128)S(1)}, u32[]{:S(2)}, u32[]{:S(2)}) collective-permute-start(f32[16,8,128]{2,1,0:T(8,128)} %get-tuple-element.20), channel_id=1, source_target_pairs={{0,33},{1,34},{2,35},{3,36},{4,37},{5,38},{6,39},{7,40},{8,41},{9,... | collective-permute-start | bytes 196616 | tf_op jit(solution)/shard_map/ppermute | solution.py:462
  7.9 12.5 %collective-permute-start.5 = (f32[16,8,128]{2,1,0:T(8,128)}, f32[16,8,128]{2,1,0:T(8,128)S(1)}, u32[]{:S(2)}, u32[]{:S(2)}) collective-permute-start(f32[16,8,128]{2,1,0:T(8,128)} %get-tuple-element.21), channel_id=1, source_target_pairs={{0,63},{1,32},{2,33},{3,34},{4,35},{5,36},{6,37},{7,38},{8,39},{9,... | collective-permute-start | bytes 196616 | tf_op jit(solution)/shard_map/ppermute | solution.py:462
  13.9 19.2 %collective-permute-start = (f32[3,16,8,128]{3,2,1,0:T(8,128)}, f32[3,16,8,128]{3,2,1,0:T(8,128)S(1)}, u32[]{:S(2)}, u32[]{:S(2)}) collective-permute-start(f32[3,16,8,128]{3,2,1,0:T(8,128)} %get-tuple-element.16), channel_id=1, source_target_pairs={{0,32},{32,64},{64,96},{96,128},{128,160},{160,192},{192,224},{224... | collective-permute-start | bytes 589832 | tf_op jit(solution)/shard_map/ppermute | solution.py:453
  17.6 15.5 %copy-start.13 = (f32[16,8,128]{2,1,0:T(8,128)}, f32[16,8,128]{2,1,0:T(8,128)S(1)}, u32[]{:S(2)}) copy-start(f32[16,8,128]{2,1,0:T(8,128)S(1)} %collective-permute-done.4.low_top_ref) | copy-start | bytes 196612
  17.6 15.5 %collective-permute-start.1 = (f32[3,16,8,128]{3,2,1,0:T(8,128)}, f32[3,16,8,128]{3,2,1,0:T(8,128)S(1)}, u32[]{:S(2)}, u32[]{:S(2)}) collective-permute-start(f32[3,16,8,128]{3,2,1,0:T(8,128)} %get-tuple-element.17), channel_id=1, source_target_pairs={{0,224},{32,0},{64,32},{96,64},{128,96},{160,128},{192,160},{224,1... | collective-permute-start | bytes 589832 | tf_op jit(solution)/shard_map/ppermute | solution.py:454
  20.4 12.8 %copy-start.14 = (f32[16,8,128]{2,1,0:T(8,128)}, f32[16,8,128]{2,1,0:T(8,128)S(1)}, u32[]{:S(2)}) copy-start(f32[16,8,128]{2,1,0:T(8,128)S(1)} %collective-permute-done.5.low_bottom_ref) | copy-start | bytes 196612
  20.4 8.8 %collective-permute-start.6 = (f32[16,8,128]{2,1,0:T(8,128)}, f32[16,8,128]{2,1,0:T(8,128)S(1)}, u32[]{:S(2)}, u32[]{:S(2)}) collective-permute-start(f32[16,8,128]{2,1,0:T(8,128)} %get-tuple-element.22), channel_id=1, source_target_pairs={{0,225},{1,226},{2,227},{3,228},{4,229},{5,230},{6,231},{7,232},{8... | collective-permute-start | bytes 196616 | tf_op jit(solution)/shard_map/ppermute | solution.py:462
  29.2 4.0 %copy-start.15 = (f32[16,8,128]{2,1,0:T(8,128)}, f32[16,8,128]{2,1,0:T(8,128)S(1)}, u32[]{:S(2)}) copy-start(f32[16,8,128]{2,1,0:T(8,128)S(1)} %collective-permute-done.6.high_top_ref) | copy-start | bytes 196612
  29.2 3.9 %collective-permute-start.7 = (f32[16,8,128]{2,1,0:T(8,128)}, f32[16,8,128]{2,1,0:T(8,128)S(1)}, u32[]{:S(2)}, u32[]{:S(2)}) collective-permute-start(f32[16,8,128]{2,1,0:T(8,128)} %get-tuple-element.23), channel_id=1, source_target_pairs={{0,255},{1,224},{2,225},{3,226},{4,227},{5,228},{6,229},{7,230},{8... | collective-permute-start | bytes 196616 | tf_op jit(solution)/shard_map/ppermute | solution.py:462
  33.1 0.6 copy-start.16
  33.1 0.7 copy-start.11
  33.1 0.8 copy-start.12
  33.1 1.0 copy-start.9
  34.1 0.9 copy-start.10
  55.9 19.0 %all-to-all-start.1 = ((f32[8,13,8,128]{3,2,1,0:T(8,128)}), f32[8,13,8,128]{3,2,1,0:T(8,128)S(1)}, u32[]{:S(2)}, u32[]{:S(2)}) async-start(f32[8,13,8,128]{3,2,1,0:T(8,128)} %get-tuple-element.26), calls=%async_computation.1 | async-start | bytes 851968 | tf_op jit(solution)/shard_map/all_to_all | solution.py:526
  74.9 3.5 %copy-start = (f32[8,13,8,128]{3,2,1,0:T(8,128)}, f32[8,13,8,128]{3,2,1,0:T(8,128)S(1)}, u32[]{:S(2)}) copy-start(f32[8,13,8,128]{3,2,1,0:T(8,128)S(1)} %all-to-all-done.1.parts_ref) | copy-start | bytes 1277956
  74.9 17.1 %all-to-all-start = ((f32[8,13,8,128]{3,2,1,0:T(8,128)}), f32[8,13,8,128]{3,2,1,0:T(8,128)S(1)}, u32[]{:S(2)}, u32[]{:S(2)}) async-start(f32[8,13,8,128]{3,2,1,0:T(8,128)} %render_rest.1), calls=%async_computation | async-start | bytes 851968 | tf_op jit(solution)/shard_map/all_to_all | solution.py:526
  92.1 0.8 copy-start.1
  94.5 6.9 %collective-permute-start.8 = (f32[2,13,8,128]{3,2,1,0:T(8,128)}, f32[2,13,8,128]{3,2,1,0:T(8,128)S(1)}, u32[]{:S(2)}, u32[]{:S(2)}) collective-permute-start(f32[2,13,8,128]{3,2,1,0:T(8,128)} %fold.3.refs_0_), channel_id=1, source_target_pairs={{0,32},{32,64},{64,96},{96,128},{128,160},{160,192},{192,224},{224... | collective-permute-start | bytes 319496 | tf_op jit(solution)/shard_map/ppermute | solution.py:544
  95.1 6.4 %collective-permute-start.12 = (f32[2,13,8,128]{3,2,1,0:T(8,128)}, f32[2,13,8,128]{3,2,1,0:T(8,128)S(1)}, u32[]{:S(2)}, u32[]{:S(2)}) collective-permute-start(f32[2,13,8,128]{3,2,1,0:T(8,128)} %fold.3.refs_0_), channel_id=1, source_target_pairs={{0,224},{32,0},{64,32},{96,64},{128,96},{160,128},{192,160},{224,1... | collective-permute-start | bytes 319496 | tf_op jit(solution)/shard_map/ppermute | solution.py:545
  101.4 18.1 %copy-start.2 = (f32[2,13,8,128]{3,2,1,0:T(8,128)}, f32[2,13,8,128]{3,2,1,0:T(8,128)S(1)}, u32[]{:S(2)}) copy-start(f32[2,13,8,128]{3,2,1,0:T(8,128)S(1)} %collective-permute-done.8.refs_1_) | copy-start | bytes 319492
  101.4 6.2 %collective-permute-start.9 = (f32[2,13,8,128]{3,2,1,0:T(8,128)S(1)}, f32[2,13,8,128]{3,2,1,0:T(8,128)S(1)}, u32[]{:S(2)}, u32[]{:S(2)}) collective-permute-start(f32[2,13,8,128]{3,2,1,0:T(8,128)S(1)} %collective-permute-done.8.refs_1_), channel_id=1, source_target_pairs={{0,32},{32,64},{64,96},{96,128},{128,160},{160,192},{192,224},{224... | collective-permute-start | bytes 319496 | tf_op jit(solution)/shard_map/ppermute | solution.py:544
  101.4 18.1 %copy-start.3 = (f32[2,13,8,128]{3,2,1,0:T(8,128)}, f32[2,13,8,128]{3,2,1,0:T(8,128)S(1)}, u32[]{:S(2)}) copy-start(f32[2,13,8,128]{3,2,1,0:T(8,128)S(1)} %collective-permute-done.12.refs_5_) | copy-start | bytes 319492
  101.5 6.2 %collective-permute-start.13 = (f32[2,13,8,128]{3,2,1,0:T(8,128)S(1)}, f32[2,13,8,128]{3,2,1,0:T(8,128)S(1)}, u32[]{:S(2)}, u32[]{:S(2)}) collective-permute-start(f32[2,13,8,128]{3,2,1,0:T(8,128)S(1)} %collective-permute-done.12.refs_5_), channel_id=1, source_target_pairs={{0,224},{32,0},{64,32},{96,64},{128,96},{160,128},{192,160},{224,1... | collective-permute-start | bytes 319496 | tf_op jit(solution)/shard_map/ppermute | solution.py:545
  107.7 11.8 %copy-start.4 = (f32[2,13,8,128]{3,2,1,0:T(8,128)}, f32[2,13,8,128]{3,2,1,0:T(8,128)S(1)}, u32[]{:S(2)}) copy-start(f32[2,13,8,128]{3,2,1,0:T(8,128)S(1)} %collective-permute-done.9.refs_2_) | copy-start | bytes 319492
  107.7 5.9 %collective-permute-start.10 = (f32[2,13,8,128]{3,2,1,0:T(8,128)S(1)}, f32[2,13,8,128]{3,2,1,0:T(8,128)S(1)}, u32[]{:S(2)}, u32[]{:S(2)}) collective-permute-start(f32[2,13,8,128]{3,2,1,0:T(8,128)S(1)} %collective-permute-done.9.refs_2_), channel_id=1, source_target_pairs={{0,32},{32,64},{64,96},{96,128},{128,160},{160,192},{192,224},{224... | collective-permute-start | bytes 319496 | tf_op jit(solution)/shard_map/ppermute | solution.py:544
  107.7 11.8 %copy-start.5 = (f32[2,13,8,128]{3,2,1,0:T(8,128)}, f32[2,13,8,128]{3,2,1,0:T(8,128)S(1)}, u32[]{:S(2)}) copy-start(f32[2,13,8,128]{3,2,1,0:T(8,128)S(1)} %collective-permute-done.13.refs_6_) | copy-start | bytes 319492
  107.7 5.9 %collective-permute-start.14 = (f32[2,13,8,128]{3,2,1,0:T(8,128)S(1)}, f32[2,13,8,128]{3,2,1,0:T(8,128)S(1)}, u32[]{:S(2)}, u32[]{:S(2)}) collective-permute-start(f32[2,13,8,128]{3,2,1,0:T(8,128)S(1)} %collective-permute-done.13.refs_6_), channel_id=1, source_target_pairs={{0,224},{32,0},{64,32},{96,64},{128,96},{160,128},{192,160},{224,1... | collective-permute-start | bytes 319496 | tf_op jit(solution)/shard_map/ppermute | solution.py:545
  113.6 5.9 %copy-start.6 = (f32[2,13,8,128]{3,2,1,0:T(8,128)}, f32[2,13,8,128]{3,2,1,0:T(8,128)S(1)}, u32[]{:S(2)}) copy-start(f32[2,13,8,128]{3,2,1,0:T(8,128)S(1)} %collective-permute-done.10.refs_3_) | copy-start | bytes 319492
  113.6 5.9 %collective-permute-start.11 = (f32[2,13,8,128]{3,2,1,0:T(8,128)S(1)}, f32[2,13,8,128]{3,2,1,0:T(8,128)S(1)}, u32[]{:S(2)}, u32[]{:S(2)}) collective-permute-start(f32[2,13,8,128]{3,2,1,0:T(8,128)S(1)} %collective-permute-done.10.refs_3_), channel_id=1, source_target_pairs={{0,32},{32,64},{64,96},{96,128},{128,160},{160,192},{192,224},{224... | collective-permute-start | bytes 319496 | tf_op jit(solution)/shard_map/ppermute | solution.py:544
  113.6 5.9 %copy-start.7 = (f32[2,13,8,128]{3,2,1,0:T(8,128)}, f32[2,13,8,128]{3,2,1,0:T(8,128)S(1)}, u32[]{:S(2)}) copy-start(f32[2,13,8,128]{3,2,1,0:T(8,128)S(1)} %collective-permute-done.14.refs_7_) | copy-start | bytes 319492
  119.5 0.6 copy-start.8

commit v5 on v2

--- a/solution.py
+++ b/solution.py
@@ -32,14 +32,18 @@
         for g in range(groups)
     ]
     edges = [
-        pltpu.make_async_copy(vol_ref.at[pl.ds(0, 3)], first_ref, edge_sem.at[0]),
-        pltpu.make_async_copy(vol_ref.at[pl.ds(cells - 3, 3)], last_ref, edge_sem.at[1]),
+        pltpu.make_async_copy(held.at[pl.ds(0, 3)], first_ref, edge_sem.at[0]),
+        pltpu.make_async_copy(held.at[pl.ds(cells - 3, 3)], last_ref, edge_sem.at[1]),
     ]
-    for copy in loads + edges:
+    for copy in loads:
         copy.start()
     stores = []
     for g in range(groups):
         loads[g].wait()
+        if g == 0:
+            edges[0].start()
+        if g == groups - 1:
+            edges[1].start()
         for k in range(8):
             z = 8 * g + k
             for tile in range(tiles):
@@ -295,11 +299,11 @@
         state = (jnp.ones((ROWS, LANES), F32), [zero] * 12, [zero] * 3)
 
         def group(g, state):
-            for k in range(4):
-                state = cell(g * 4 + k, state)
+            for k in range(8):
+                state = cell(g * 8 + k, state)
             return state
 
-        through, sums, base_sums = lax.fori_loop(0, cells // 4, group, state)
+        through, sums, base_sums = lax.fori_loop(0, cells // 8, group, state)
         for l in range(4):
             for c in range(3):
                 out_ref[tile // 2, 3 * l + c, tile % 2] = light_ref[l, c] * (
@@ -323,16 +327,14 @@
             out_ref[ch, tile] = total[ch]
 
 
-def spread(place_ref, *refs):
-    pieces, out_ref, sem = refs[:-2], refs[-2], refs[-1]
-    count = len(pieces)
+def spread(count, offsets, place_ref, *refs):
+    pieces, out_ref, sem = refs[: len(offsets)], refs[-2], refs[-1]
     tiles = out_ref.shape[1] // count
     copies = []
-    for step, ref in enumerate(pieces):
-        offset = step if step <= count // 2 else count // 2 - step
-        owner = lax.rem(place_ref[0] - offset + count, count)
+    for i, ref in enumerate(pieces):
+        owner = lax.rem(place_ref[0] - offsets[i] + count, count)
         copies.append(
-            pltpu.make_async_copy(ref, out_ref.at[:, pl.ds(owner * tiles, tiles)], sem.at[step])
+            pltpu.make_async_copy(ref, out_ref.at[:, pl.ds(owner * tiles, tiles)], sem.at[i])
         )
     for copy in copies:
         copy.start()
@@ -366,7 +368,7 @@
     cells, rows, width = volume.shape
     tiles = width // LANES
     slab, band = lax.axis_index("depth"), lax.axis_index("height")
-    limit = pltpu.CompilerParams(vmem_limit_bytes=58 << 20)
+    limit = pltpu.CompilerParams(vmem_limit_bytes=63 << 20)
     field = volume.reshape(cells, rows, tiles, LANES).transpose(0, 2, 1, 3)
 
     down, up, first, last = pl.pallas_call(
@@ -385,10 +387,10 @@
         compiler_params=limit,
         name="pack",
     )(field)
+    low = lax.ppermute(last, "depth", ring("depth", 1))
+    high = lax.ppermute(first, "depth", ring("depth", -1))
     top = lax.ppermute(down, "height", ring("height", 1))
     bottom = lax.ppermute(up, "height", ring("height", -1))
-    low = lax.ppermute(last, "depth", ring("depth", 1))
-    high = lax.ppermute(first, "depth", ring("depth", -1))
     corner_down, corner_up = pl.pallas_call(
         pack_corners,
         out_shape=[shape(tiles, rows, LANES)] * 2,
@@ -396,6 +398,9 @@
         out_specs=in_vmem(2),
         scratch_shapes=[VMEM((2, 2, tiles, rows, LANES), F32), DMA((2,))],
         compiler_params=limit,
+        cost_estimate=pl.CostEstimate(
+            flops=400_000_000, bytes_accessed=80_000_000, transcendentals=0
+        ),
         name="pack_corners",
     )(low, high)
     top_corner = lax.ppermute(corner_down, "height", ring("height", 1))
@@ -448,16 +453,29 @@
     for _ in range(slabs // 2):
         from_below.append(lax.ppermute(from_below[-1], "depth", ring("depth", 1)))
         from_above.append(lax.ppermute(from_above[-1], "depth", ring("depth", -1)))
-    pieces = from_below + from_above[1 : slabs // 2]
-    image = pl.pallas_call(
-        spread,
-        out_shape=shape(13, tiles, rows, LANES),
-        in_specs=in_smem(1) + anywhere(slabs),
-        out_specs=pl.BlockSpec(memory_space=pl.ANY),
-        scratch_shapes=[DMA((slabs,))],
-        compiler_params=limit,
-        name="spread",
-    )(slab[None], *pieces)
+    count = slabs // 2
+    early = list(range(1 - count // 2, 1 + count // 2))
+    late = [k for k in range(1 - count, 1 + count) if k not in early]
+    image = []
+    for offsets in (early, late):
+        aliases = {1 + len(offsets): 0} if image else {}
+        image = [
+            pl.pallas_call(
+                functools.partial(spread, slabs, offsets),
+                out_shape=shape(13, tiles, rows, LANES),
+                in_specs=in_smem(1) + in_vmem(len(offsets)) + anywhere(len(image)),
+                out_specs=pl.BlockSpec(memory_space=pl.ANY),
+                scratch_shapes=[DMA((len(offsets),))],
+                input_output_aliases=aliases,
+                compiler_params=limit,
+                name="spread",
+            )(
+                slab[None],
+                *[from_below[k] if k >= 0 else from_above[-k] for k in offsets],
+                *image,
+            )
+        ]
+    (image,) = image
     return image.transpose(0, 2, 1, 3).reshape(13, rows, width)
 
 

time: 148 us -> 110 us (0.74)
  the two profiles are of different devices: /device:TPU:0 before, /device:TPU:8 now
where the time goes in v5:
time: 110 us; the launch traced here: 109 us
  Pallas kernels  34.9 us (32%)
  blocking collectives  29 us (26%)
  starting transfers between devices  23.5 us (21%)
  waiting for transfers between devices  18.9 us (17%)
  local copies, waits for them, and re-layouts  2.24 us (2%)
    all_to_all x1, blocking collectives, per_device(): exchanged = lax.all_to_all(partial, 'depth', 0, 0, tiled=True)  29 us
    pallas_call x1, Pallas kernels, per_device(): pl.pallas_call(functools.partial(render, alpha_top=2.0 / (cells * slabs))...  25.1 us
    ppermute x4, waiting for transfers between devices, per_device(): from_below.append(lax.ppermute(from_below[-1], 'depth', ring('depth', 1)))  13.4 us
    ppermute x3, starting transfers between devices, per_device(): from_above.append(lax.ppermute(from_above[-1], 'depth', ring('depth', -1)))  9.21 us
    ppermute x1, starting transfers between devices, per_device(): high = lax.ppermute(first, 'depth', ring('depth', -1))  3.94 us
    ppermute x1, waiting for transfers between devices, per_device(): low = lax.ppermute(last, 'depth', ring('depth', 1))  3.85 us
    ppermute x1, starting transfers between devices, per_device(): bottom_corner = lax.ppermute(corner_up, 'height', ring('height', -1))  3.84 us
    ppermute x1, starting transfers between devices, per_device(): bottom = lax.ppermute(up, 'height', ring('height', -1))  3.84 us
  transfers between devices with their start and end apart: 13, of which 7 were waited for; matrix products, arithmetic and copies ran while one was open for 1% of the time, Pallas kernels for 3%

profile of v5, /device:TPU:8, one launch (start us, length us, event | category | flops | bytes accessed | tf_op | source)
XLA Modules:
  0.0 109.2 jit_solution(12319118670876829399)
XLA Ops:
  0.0 2.6 %pack.1 = (f32[16,96,128]{2,1,0:T(8,128)}, f32[16,96,128]{2,1,0:T(8,128)}, f32[3,16,8,128]{3,2,1,0:T(8,128)}, f32[3,16,8,128]{3,2,1,0:T(8,128)}) custom-call(f32[32,16,8,128]{3,2,1,0:T(8,128)} %bitcast.11), custom_call_target="tpu_custom_call" | custom-call | tf_op jit(solution)/shard_map/pack/pallas_call | solution.py:374
  2.6 0.1 collective-permute-start.2
  2.7 3.8 %collective-permute-start.3 = (f32[16,96,128]{2,1,0:T(8,128)}, f32[16,96,128]{2,1,0:T(8,128)}, u32[]{:S(2)}, u32[]{:S(2)}) collective-permute-start(f32[16,96,128]{2,1,0:T(8,128)} %get-tuple-element.14), channel_id=1, source_target_pairs={{0,31},{1,0},{2,1},{3,2},{4,3},{5,4},{6,5},{7,6},{8,7},{9,8},{10,9... | collective-permute-start | bytes 2359304 | tf_op jit(solution)/shard_map/ppermute | solution.py:393
  6.5 1.9 %collective-permute-start = (f32[3,16,8,128]{3,2,1,0:T(8,128)}, f32[3,16,8,128]{3,2,1,0:T(8,128)S(1)}, u32[]{:S(2)}, u32[]{:S(2)}) collective-permute-start(f32[3,16,8,128]{3,2,1,0:T(8,128)} %get-tuple-element.11), channel_id=1, source_target_pairs={{0,32},{32,64},{64,96},{96,128},{128,160},{160,192},{192,224},{224... | collective-permute-start | bytes 589832 | tf_op jit(solution)/shard_map/ppermute | solution.py:390
  8.4 3.9 %collective-permute-start.1 = (f32[3,16,8,128]{3,2,1,0:T(8,128)}, f32[3,16,8,128]{3,2,1,0:T(8,128)}, u32[]{:S(2)}, u32[]{:S(2)}) collective-permute-start(f32[3,16,8,128]{3,2,1,0:T(8,128)} %get-tuple-element.12), channel_id=1, source_target_pairs={{0,224},{32,0},{64,32},{96,64},{128,96},{160,128},{192,160},{224,1... | collective-permute-start | bytes 589832 | tf_op jit(solution)/shard_map/ppermute | solution.py:391
  12.4 3.9 %collective-permute-done.low_ref = f32[3,16,8,128]{3,2,1,0:T(8,128)S(1)} collective-permute-done((f32[3,16,8,128]{3,2,1,0:T(8,128)}, f32[3,16,8,128]{3,2,1,0:T(8,128)S(1)}, u32[]{:S(2)}, u32[]{:S(2)}) %collective-permute-start) | collective-permute-done | bytes 196640 | tf_op jit(solution)/shard_map/ppermute | solution.py:390
  16.2 0.0 collective-permute-done.1.high_ref
  16.2 0.7 copy-done.1
  16.9 1.7 %pack_corners.1 = (f32[16,8,128]{2,1,0:T(8,128)}, f32[16,8,128]{2,1,0:T(8,128)}) custom-call(f32[3,16,8,128]{3,2,1,0:T(8,128)} %copy-done.1, f32[3,16,8,128]{3,2,1,0:T(8,128)} %collective-permute-done.1.high_ref), custom_call_target="tpu_custom_call" | custom-call | flops 400000000 | bytes 80000000 | tf_op jit(solution)/shard_map/pack_corners/pallas_call | solution.py:394
  18.6 0.1 collective-permute-start.4
  18.7 3.8 %collective-permute-start.5 = (f32[16,8,128]{2,1,0:T(8,128)}, f32[16,8,128]{2,1,0:T(8,128)S(1)}, u32[]{:S(2)}, u32[]{:S(2)}) collective-permute-start(f32[16,8,128]{2,1,0:T(8,128)} %get-tuple-element.16), channel_id=1, source_target_pairs={{0,31},{1,0},{2,1},{3,2},{4,3},{5,4},{6,5},{7,6},{8,7},{9,8},{10,9... | collective-permute-start | bytes 196616 | tf_op jit(solution)/shard_map/ppermute | solution.py:407
  22.6 0.6 add_convert_fusion.edge_ref
  23.2 1.6 %collective-permute-done.4.top_corner_ref = f32[16,8,128]{2,1,0:T(8,128)S(1)} collective-permute-done((f32[16,8,128]{2,1,0:T(8,128)}, f32[16,8,128]{2,1,0:T(8,128)S(1)}, u32[]{:S(2)}, u32[]{:S(2)}) %collective-permute-start.4) | collective-permute-done | bytes 65568 | tf_op jit(solution)/shard_map/ppermute | solution.py:406
  24.7 0.1 collective-permute-done.5.bottom_corner_ref
  24.8 0.0 collective-permute-done.2.top_ref
  24.8 0.0 collective-permute-done.3.bottom_ref
  24.8 0.5 copy-done.9
  25.3 0.1 copy-done.10
  25.4 0.3 copy-done
  25.7 25.1 %render.1 = f32[8,13,2,8,128]{4,3,2,1,0:T(8,128)} custom-call(f32[4]{0:T(128)} %add_convert_fusion.edge_ref, f32[3,4]{1,0:T(4,128)} %colour_ref.1, f32[4]{0:T(128)} %opacity_ref.1, f32[4,3]{1,0:T(4,128)} %dir_ref.1, f32[4,3]{1,0:T(4,128)} %light_ref.1, f32[32,16,8,128]{3,2,1,0:T(8,128)} %bitcast.12, f32[3,16,8,128]{3,2,1,0:T(8,128)} %copy-done.1, ...), custom_call_target="tpu_custom_call" | custom-call | tf_op jit(solution)/shard_map/render/pallas_call | solution.py:410
  50.8 29.0 %all_to_all.5.parts_ref = f32[8,13,2,8,128]{4,3,2,1,0:T(8,128)} all-to-all(f32[8,13,2,8,128]{4,3,2,1,0:T(8,128)} %render.1), channel_id=1, replica_groups=mesh['depth'=8,'height'=32] {'depth'}, dimensions={0} | all-to-all | bytes 1703936 | tf_op jit(solution)/shard_map/all_to_all | solution.py:443
  79.7 1.8 %fold.1.refs_1_ = f32[13,2,8,128]{3,2,1,0:T(8,128)} custom-call(f32[8,13,2,8,128]{4,3,2,1,0:T(8,128)} %all_to_all.5.parts_ref), custom_call_target="tpu_custom_call" | custom-call | tf_op jit(solution)/shard_map/fold/pallas_call | solution.py:444
  81.6 0.6 collective-permute-start.9
  82.1 2.7 %collective-permute-start.6 = (f32[13,2,8,128]{3,2,1,0:T(8,128)}, f32[13,2,8,128]{3,2,1,0:T(8,128)S(1)}, u32[]{:S(2)}, u32[]{:S(2)}) collective-permute-start(f32[13,2,8,128]{3,2,1,0:T(8,128)} %fold.1.refs_1_), channel_id=1, source_target_pairs={{0,224},{32,0},{64,32},{96,64},{128,96},{160,128},{192,160},{224,1... | collective-permute-start | bytes 319496 | tf_op jit(solution)/shard_map/ppermute | solution.py:455
  84.8 3.8 %collective-permute-done.9.refs_2_ = f32[13,2,8,128]{3,2,1,0:T(8,128)S(1)} collective-permute-done((f32[13,2,8,128]{3,2,1,0:T(8,128)}, f32[13,2,8,128]{3,2,1,0:T(8,128)S(1)}, u32[]{:S(2)}, u32[]{:S(2)}) %collective-permute-start.9) | collective-permute-done | bytes 106528 | tf_op jit(solution)/shard_map/ppermute | solution.py:454
  88.7 0.0 collective-permute-start.10
  88.7 0.0 collective-permute-done.6.refs_0_
  88.7 0.0 copy-start.3
  88.7 3.3 %collective-permute-start.7 = (f32[13,2,8,128]{3,2,1,0:T(8,128)S(1)}, f32[13,2,8,128]{3,2,1,0:T(8,128)S(1)}, u32[]{:S(2)}, u32[]{:S(2)}) collective-permute-start(f32[13,2,8,128]{3,2,1,0:T(8,128)S(1)} %collective-permute-done.6.refs_0_), channel_id=1, source_target_pairs={{0,224},{32,0},{64,32},{96,64},{128,96},{160,128},{192,160},{224,1... | collective-permute-start | bytes 319496 | tf_op jit(solution)/shard_map/ppermute | solution.py:455
  92.0 2.9 %collective-permute-done.10.refs_3_ = f32[13,2,8,128]{3,2,1,0:T(8,128)S(1)} collective-permute-done((f32[13,2,8,128]{3,2,1,0:T(8,128)S(1)}, f32[13,2,8,128]{3,2,1,0:T(8,128)S(1)}, u32[]{:S(2)}, u32[]{:S(2)}) %collective-permute-start.10) | collective-permute-done | bytes 106528 | tf_op jit(solution)/shard_map/ppermute | solution.py:454
  94.9 0.0 collective-permute-start.11
  94.9 0.0 collective-permute-done.7.refs_1_
  94.9 0.0 copy-start.5
  94.9 3.2 %collective-permute-start.8 = (f32[13,2,8,128]{3,2,1,0:T(8,128)S(1)}, f32[13,2,8,128]{3,2,1,0:T(8,128)S(1)}, u32[]{:S(2)}, u32[]{:S(2)}) collective-permute-start(f32[13,2,8,128]{3,2,1,0:T(8,128)S(1)} %collective-permute-done.7.refs_1_), channel_id=1, source_target_pairs={{0,224},{32,0},{64,32},{96,64},{128,96},{160,128},{192,160},{224,1... | collective-permute-start | bytes 319496 | tf_op jit(solution)/shard_map/ppermute | solution.py:455
  98.1 2.7 %collective-permute-done.11.refs_2_ = f32[13,2,8,128]{3,2,1,0:T(8,128)S(1)} collective-permute-done((f32[13,2,8,128]{3,2,1,0:T(8,128)S(1)}, f32[13,2,8,128]{3,2,1,0:T(8,128)S(1)}, u32[]{:S(2)}, u32[]{:S(2)}) %collective-permute-start.11) | collective-permute-done | bytes 106528 | tf_op jit(solution)/shard_map/ppermute | solution.py:454
  100.8 0.0 collective-permute-start.12
  100.8 0.0 copy-done.2
  100.8 0.0 copy-done.3
  100.8 0.0 copy-done.4
  100.8 1.9 %spread.2.refs_4_ = f32[13,16,8,128]{3,2,1,0:T(8,128)} custom-call(s32[1]{0:T(128)} %bitcast.place_ref, f32[13,2,8,128]{3,2,1,0:T(8,128)} %copy-done.3, f32[13,2,8,128]{3,2,1,0:T(8,128)} %fold.1.refs_1_, f32[13,2,8,128]{3,2,1,0:T(8,128)} %copy-done.2, f32[13,2,8,128]{3,2,1,0:T(8,128)} %copy-done.4), custom_call_target="tpu_custom_call" | custom-call | tf_op jit(solution)/shard_map/spread/pallas_call | solution.py:463
  102.7 0.0 collective-permute-done.8.refs_0_
  102.7 0.0 copy-start.7
  102.7 4.0 %collective-permute-done.12.refs_3_ = f32[13,2,8,128]{3,2,1,0:T(8,128)S(1)} collective-permute-done((f32[13,2,8,128]{3,2,1,0:T(8,128)S(1)}, f32[13,2,8,128]{3,2,1,0:T(8,128)S(1)}, u32[]{:S(2)}, u32[]{:S(2)}) %collective-permute-start.12) | collective-permute-done | bytes 106528 | tf_op jit(solution)/shard_map/ppermute | solution.py:454
  106.7 0.0 copy-done.5
  106.7 0.0 copy-done.6
  106.7 0.0 copy-done.7
  106.7 0.6 copy-done.8
  107.3 1.8 %spread.3 = f32[13,16,8,128]{3,2,1,0:T(8,128)} custom-call(s32[1]{0:T(128)} %bitcast.place_ref, f32[13,2,8,128]{3,2,1,0:T(8,128)} %copy-done.7, f32[13,2,8,128]{3,2,1,0:T(8,128)} %copy-done.5, f32[13,2,8,128]{3,2,1,0:T(8,128)} %copy-done.6, f32[13,2,8,128]{3,2,1,0:T(8,128)} %copy-done.8, ...), custom_call_target="tpu_custom_call", output_to_operand_aliasing={{}: (5, {})} | custom-call | tf_op jit(solution)/shard_map/spread/pallas_call | solution.py:463
  (8 shorter events, 0.0 us)
Async XLA Ops:
  2.6 22.2 %collective-permute-start.2 = (f32[16,96,128]{2,1,0:T(8,128)}, f32[16,96,128]{2,1,0:T(8,128)S(1)}, u32[]{:S(2)}, u32[]{:S(2)}) collective-permute-start(f32[16,96,128]{2,1,0:T(8,128)} %get-tuple-element.13), channel_id=1, source_target_pairs={{0,1},{1,2},{2,3},{3,4},{4,5},{5,6},{6,7},{7,8},{8,9},{9,10},{10,1... | collective-permute-start | bytes 2359304 | tf_op jit(solution)/shard_map/ppermute | solution.py:392
  2.7 22.1 %collective-permute-start.3 = (f32[16,96,128]{2,1,0:T(8,128)}, f32[16,96,128]{2,1,0:T(8,128)}, u32[]{:S(2)}, u32[]{:S(2)}) collective-permute-start(f32[16,96,128]{2,1,0:T(8,128)} %get-tuple-element.14), channel_id=1, source_target_pairs={{0,31},{1,0},{2,1},{3,2},{4,3},{5,4},{6,5},{7,6},{8,7},{9,8},{10,9... | collective-permute-start | bytes 2359304 | tf_op jit(solution)/shard_map/ppermute | solution.py:393
  6.5 9.7 %collective-permute-start = (f32[3,16,8,128]{3,2,1,0:T(8,128)}, f32[3,16,8,128]{3,2,1,0:T(8,128)S(1)}, u32[]{:S(2)}, u32[]{:S(2)}) collective-permute-start(f32[3,16,8,128]{3,2,1,0:T(8,128)} %get-tuple-element.11), channel_id=1, source_target_pairs={{0,32},{32,64},{64,96},{96,128},{128,160},{160,192},{192,224},{224... | collective-permute-start | bytes 589832 | tf_op jit(solution)/shard_map/ppermute | solution.py:390
  8.4 7.8 %collective-permute-start.1 = (f32[3,16,8,128]{3,2,1,0:T(8,128)}, f32[3,16,8,128]{3,2,1,0:T(8,128)}, u32[]{:S(2)}, u32[]{:S(2)}) collective-permute-start(f32[3,16,8,128]{3,2,1,0:T(8,128)} %get-tuple-element.12), channel_id=1, source_target_pairs={{0,224},{32,0},{64,32},{96,64},{128,96},{160,128},{192,160},{224,1... | collective-permute-start | bytes 589832 | tf_op jit(solution)/shard_map/ppermute | solution.py:391
  16.2 0.7 copy-start.1
  18.6 6.1 %collective-permute-start.4 = (f32[16,8,128]{2,1,0:T(8,128)}, f32[16,8,128]{2,1,0:T(8,128)S(1)}, u32[]{:S(2)}, u32[]{:S(2)}) collective-permute-start(f32[16,8,128]{2,1,0:T(8,128)} %get-tuple-element.15), channel_id=1, source_target_pairs={{0,1},{1,2},{2,3},{3,4},{4,5},{5,6},{6,7},{7,8},{8,9},{9,10},{10,1... | collective-permute-start | bytes 196616 | tf_op jit(solution)/shard_map/ppermute | solution.py:406
  18.7 6.1 %collective-permute-start.5 = (f32[16,8,128]{2,1,0:T(8,128)}, f32[16,8,128]{2,1,0:T(8,128)S(1)}, u32[]{:S(2)}, u32[]{:S(2)}) collective-permute-start(f32[16,8,128]{2,1,0:T(8,128)} %get-tuple-element.16), channel_id=1, source_target_pairs={{0,31},{1,0},{2,1},{3,2},{4,3},{5,4},{6,5},{7,6},{8,7},{9,8},{10,9... | collective-permute-start | bytes 196616 | tf_op jit(solution)/shard_map/ppermute | solution.py:407
  24.7 0.6 copy-start.9
  24.8 0.6 copy-start.10
  24.8 0.9 copy-start
  81.6 7.1 %collective-permute-start.9 = (f32[13,2,8,128]{3,2,1,0:T(8,128)}, f32[13,2,8,128]{3,2,1,0:T(8,128)S(1)}, u32[]{:S(2)}, u32[]{:S(2)}) collective-permute-start(f32[13,2,8,128]{3,2,1,0:T(8,128)} %fold.1.refs_1_), channel_id=1, source_target_pairs={{0,32},{32,64},{64,96},{96,128},{128,160},{160,192},{192,224},{224... | collective-permute-start | bytes 319496 | tf_op jit(solution)/shard_map/ppermute | solution.py:454
  82.1 6.5 %collective-permute-start.6 = (f32[13,2,8,128]{3,2,1,0:T(8,128)}, f32[13,2,8,128]{3,2,1,0:T(8,128)S(1)}, u32[]{:S(2)}, u32[]{:S(2)}) collective-permute-start(f32[13,2,8,128]{3,2,1,0:T(8,128)} %fold.1.refs_1_), channel_id=1, source_target_pairs={{0,224},{32,0},{64,32},{96,64},{128,96},{160,128},{192,160},{224,1... | collective-permute-start | bytes 319496 | tf_op jit(solution)/shard_map/ppermute | solution.py:455
  88.7 12.1 %copy-start.2 = (f32[13,2,8,128]{3,2,1,0:T(8,128)}, f32[13,2,8,128]{3,2,1,0:T(8,128)S(1)}, u32[]{:S(2)}) copy-start(f32[13,2,8,128]{3,2,1,0:T(8,128)S(1)} %collective-permute-done.9.refs_2_) | copy-start | bytes 319492
  88.7 6.2 %collective-permute-start.10 = (f32[13,2,8,128]{3,2,1,0:T(8,128)S(1)}, f32[13,2,8,128]{3,2,1,0:T(8,128)S(1)}, u32[]{:S(2)}, u32[]{:S(2)}) collective-permute-start(f32[13,2,8,128]{3,2,1,0:T(8,128)S(1)} %collective-permute-done.9.refs_2_), channel_id=1, source_target_pairs={{0,32},{32,64},{64,96},{96,128},{128,160},{160,192},{192,224},{224... | collective-permute-start | bytes 319496 | tf_op jit(solution)/shard_map/ppermute | solution.py:454
  88.7 12.1 %copy-start.3 = (f32[13,2,8,128]{3,2,1,0:T(8,128)}, f32[13,2,8,128]{3,2,1,0:T(8,128)S(1)}, u32[]{:S(2)}) copy-start(f32[13,2,8,128]{3,2,1,0:T(8,128)S(1)} %collective-permute-done.6.refs_0_) | copy-start | bytes 319492
  88.7 6.2 %collective-permute-start.7 = (f32[13,2,8,128]{3,2,1,0:T(8,128)S(1)}, f32[13,2,8,128]{3,2,1,0:T(8,128)S(1)}, u32[]{:S(2)}, u32[]{:S(2)}) collective-permute-start(f32[13,2,8,128]{3,2,1,0:T(8,128)S(1)} %collective-permute-done.6.refs_0_), channel_id=1, source_target_pairs={{0,224},{32,0},{64,32},{96,64},{128,96},{160,128},{192,160},{224,1... | collective-permute-start | bytes 319496 | tf_op jit(solution)/shard_map/ppermute | solution.py:455
  94.9 5.9 %copy-start.4 = (f32[13,2,8,128]{3,2,1,0:T(8,128)}, f32[13,2,8,128]{3,2,1,0:T(8,128)S(1)}, u32[]{:S(2)}) copy-start(f32[13,2,8,128]{3,2,1,0:T(8,128)S(1)} %collective-permute-done.10.refs_3_) | copy-start | bytes 319492
  94.9 5.9 %collective-permute-start.11 = (f32[13,2,8,128]{3,2,1,0:T(8,128)S(1)}, f32[13,2,8,128]{3,2,1,0:T(8,128)S(1)}, u32[]{:S(2)}, u32[]{:S(2)}) collective-permute-start(f32[13,2,8,128]{3,2,1,0:T(8,128)S(1)} %collective-permute-done.10.refs_3_), channel_id=1, source_target_pairs={{0,32},{32,64},{64,96},{96,128},{128,160},{160,192},{192,224},{224... | collective-permute-start | bytes 319496 | tf_op jit(solution)/shard_map/ppermute | solution.py:454
  94.9 11.8 %copy-start.5 = (f32[13,2,8,128]{3,2,1,0:T(8,128)}, f32[13,2,8,128]{3,2,1,0:T(8,128)S(1)}, u32[]{:S(2)}) copy-start(f32[13,2,8,128]{3,2,1,0:T(8,128)S(1)} %collective-permute-done.7.refs_1_) | copy-start | bytes 319492
  94.9 7.8 %collective-permute-start.8 = (f32[13,2,8,128]{3,2,1,0:T(8,128)S(1)}, f32[13,2,8,128]{3,2,1,0:T(8,128)S(1)}, u32[]{:S(2)}, u32[]{:S(2)}) collective-permute-start(f32[13,2,8,128]{3,2,1,0:T(8,128)S(1)} %collective-permute-done.7.refs_1_), channel_id=1, source_target_pairs={{0,224},{32,0},{64,32},{96,64},{128,96},{160,128},{192,160},{224,1... | collective-permute-start | bytes 319496 | tf_op jit(solution)/shard_map/ppermute | solution.py:455
  100.8 5.9 %copy-start.6 = (f32[13,2,8,128]{3,2,1,0:T(8,128)}, f32[13,2,8,128]{3,2,1,0:T(8,128)S(1)}, u32[]{:S(2)}) copy-start(f32[13,2,8,128]{3,2,1,0:T(8,128)S(1)} %collective-permute-done.11.refs_2_) | copy-start | bytes 319492
  100.8 5.9 %collective-permute-start.12 = (f32[13,2,8,128]{3,2,1,0:T(8,128)S(1)}, f32[13,2,8,128]{3,2,1,0:T(8,128)S(1)}, u32[]{:S(2)}, u32[]{:S(2)}) collective-permute-start(f32[13,2,8,128]{3,2,1,0:T(8,128)S(1)} %collective-permute-done.11.refs_2_), channel_id=1, source_target_pairs={{0,32},{32,64},{64,96},{96,128},{128,160},{160,192},{192,224},{224... | collective-permute-start | bytes 319496 | tf_op jit(solution)/shard_map/ppermute | solution.py:454
  102.7 4.0 %copy-start.7 = (f32[13,2,8,128]{3,2,1,0:T(8,128)}, f32[13,2,8,128]{3,2,1,0:T(8,128)S(1)}, u32[]{:S(2)}) copy-start(f32[13,2,8,128]{3,2,1,0:T(8,128)S(1)} %collective-permute-done.8.refs_0_) | copy-start | bytes 319492
  106.7 0.6 copy-start.8

commit v6 on v5

--- a/solution.py
+++ b/solution.py
@@ -165,8 +165,13 @@
         width_slope(dst, planes - 2, slope)
 
 
+SHIFTS = (4, 3, 5, 2, 6, 1, 7, 0)
+FAR = 3
+
+
 def render(
     edge_ref,
+    tile_ref,
     colour_ref,
     opacity_ref,
     dir_ref,
@@ -178,19 +183,12 @@
     bottom_ref,
     top_corner_ref,
     bottom_corner_ref,
-    out_ref,
-    field,
-    once,
-    twice,
-    slope,
-    nexts,
-    befores,
-    held,
-    rows_in,
-    corners_in,
-    sem,
+    *refs,
     alpha_top,
 ):
+    out_refs, twice_ref, slope_ref = refs[:FAR], refs[FAR], refs[FAR + 1]
+    (field, once, twice, slope, nexts, befores, held, rows_in, corners_in, images) = refs[FAR + 2 : -3]
+    sem, later_sem, out_sem = refs[-3:]
     cells, tiles = vol_ref.shape[0], vol_ref.shape[1]
     own = pl.ds(BAND, 8)
     copies = [
@@ -265,6 +263,74 @@
         twice[0, tile, own, :] = twice[0, tile, own, :] * keep_low
         twice[cells + 1, tile, own, :] = twice[cells + 1, tile, own, :] * keep_high
 
+    each = tiles // len(SHIFTS)
+    ahead = FAR * each
+    later = []
+    for k in range(tiles - ahead):
+        tile = tile_ref[ahead + k]
+        later += [
+            pltpu.make_async_copy(twice.at[:, tile], twice_ref.at[k], later_sem.at[0, k]),
+            pltpu.make_async_copy(slope.at[:, tile], slope_ref.at[k], later_sem.at[1, k]),
+        ]
+    for copy in later:
+        copy.start()
+
+    def smooth(k, z, row):
+        return twice[z, tile_ref[k], pl.ds(row, 8), :]
+
+    def across(k, z):
+        return slope[z, tile_ref[k]]
+
+    coefs = (colour_ref, opacity_ref, dir_ref, light_ref)
+    shade(coefs, cells, ahead, smooth, across, images, alpha_top)
+    send(images, out_refs, out_sem)
+    for copy in later:
+        copy.wait()
+
+
+def render_rest(colour_ref, opacity_ref, dir_ref, light_ref, twice_ref, slope_ref, *refs, alpha_top):
+    out_refs, (twice, slope, images, sem, out_sem) = refs[:-5], refs[-5:]
+    count, cells = slope.shape[0], slope.shape[1] - 1
+
+    def load(k):
+        return [
+            pltpu.make_async_copy(twice_ref.at[k], twice.at[k], sem.at[0, k]),
+            pltpu.make_async_copy(slope_ref.at[k], slope.at[k], sem.at[1, k]),
+        ]
+
+    for k in range(count):
+        for copy in load(k):
+            copy.start()
+
+    def ready(k):
+        for copy in load(k):
+            copy.wait()
+
+    def smooth(k, z, row):
+        return twice[k, z, pl.ds(row, 8), :]
+
+    def across(k, z):
+        return slope[k, z]
+
+    coefs = (colour_ref, opacity_ref, dir_ref, light_ref)
+    shade(coefs, cells, count, smooth, across, images, alpha_top, ready)
+    send(images, out_refs, out_sem)
+
+
+def send(images, out_refs, sem):
+    copies = [
+        pltpu.make_async_copy(images.at[k], ref, sem.at[k]) for k, ref in enumerate(out_refs)
+    ]
+    for copy in copies:
+        copy.start()
+    for copy in copies:
+        copy.wait()
+
+
+def shade(coefs, cells, count, smooth, across, images, alpha_top, ready=None):
+    colour_ref, opacity_ref, dir_ref, light_ref = coefs
+    each = images.shape[2]
+    zero = jnp.zeros((ROWS, LANES), F32)
     colour = [[colour_ref[c, j] for j in range(4)] for c in range(3)]
     opac = [opacity_ref[j] for j in range(4)]
     light = [[0.5 * dir_ref[l, d] for d in range(3)] for l in range(4)]
@@ -272,13 +338,16 @@
     def poly(c, v):
         return ((c[3] * v + c[2]) * v + c[1]) * v + c[0]
 
-    def column(tile, carry):
+    def column(k, carry):
+        if ready is not None:
+            ready(k)
+
         def cell(z, state):
             through, sums, base_sums = state
-            v = twice[z + 1, tile, own, :]
-            g_z = twice[z + 2, tile, own, :] - twice[z, tile, own, :]
-            g_h = twice[z + 1, tile, pl.ds(OWN + 1, 8), :] - twice[z + 1, tile, pl.ds(OWN - 1, 8), :]
-            g_w = slope[z + 1, tile]
+            v = smooth(k, z + 1, OWN)
+            g_z = smooth(k, z + 2, OWN) - smooth(k, z, OWN)
+            g_h = smooth(k, z + 1, OWN + 1) - smooth(k, z + 1, OWN - 1)
+            g_w = across(k, z + 1)
             inverse = lax.rsqrt(0.25 * (g_z * g_z + g_h * g_h + g_w * g_w) + 1.0)
             p = poly(opac, v)
             s = p * p
@@ -299,30 +368,39 @@
         state = (jnp.ones((ROWS, LANES), F32), [zero] * 12, [zero] * 3)
 
         def group(g, state):
-            for k in range(8):
-                state = cell(g * 8 + k, state)
+            for i in range(8):
+                state = cell(g * 8 + i, state)
             return state
 
         through, sums, base_sums = lax.fori_loop(0, cells // 8, group, state)
         for l in range(4):
             for c in range(3):
-                out_ref[tile // 2, 3 * l + c, tile % 2] = light_ref[l, c] * (
+                images[k // each, 3 * l + c, k % each] = light_ref[l, c] * (
                     0.2 * base_sums[c] + sums[3 * l + c]
                 )
-        out_ref[tile // 2, 12, tile % 2] = 1.0 - through
+        images[k // each, 12, k % each] = 1.0 - through
         return carry
 
-    lax.fori_loop(0, tiles, column, 0)
-
-
-def fold(parts_ref, out_ref):
-    slabs, channels = parts_ref.shape[0], parts_ref.shape[1]
-    for tile in range(parts_ref.shape[2]):
-        through = 1.0 - parts_ref[0, 12, tile]
-        total = [parts_ref[0, ch, tile] for ch in range(channels)]
+    lax.fori_loop(0, count, column, 0)
+
+
+def fold(place_ref, *refs):
+    pieces, (out_ref, parts, sem) = refs[:-3], refs[-3:]
+    slabs, channels = parts.shape[0], parts.shape[1]
+    copies = []
+    for i, ref in enumerate(pieces):
+        slab = lax.rem(place_ref[0] - SHIFTS[i] + slabs, slabs)
+        copies.append(pltpu.make_async_copy(ref, parts.at[slab], sem.at[i]))
+    for copy in copies:
+        copy.start()
+    for copy in copies:
+        copy.wait()
+    for tile in range(parts.shape[2]):
+        through = 1.0 - parts[0, 12, tile]
+        total = [parts[0, ch, tile] for ch in range(channels)]
         for slab in range(1, slabs):
-            total = [total[ch] + through * parts_ref[slab, ch, tile] for ch in range(channels)]
-            through = through * (1.0 - parts_ref[slab, 12, tile])
+            total = [total[ch] + through * parts[slab, ch, tile] for ch in range(channels)]
+            through = through * (1.0 - parts[slab, 12, tile])
         for ch in range(channels):
             out_ref[ch, tile] = total[ch]
 
@@ -407,11 +485,17 @@
     bottom_corner = lax.ppermute(corner_up, "height", ring("height", -1))
 
     edges = jnp.stack([slab > 0, slab < slabs - 1, band > 0, band < bands - 1]).astype(F32)
-    partial = pl.pallas_call(
-        functools.partial(render, alpha_top=2.0 / (cells * slabs)),
-        out_shape=shape(slabs, 13, tiles // slabs, rows, LANES),
-        in_specs=in_smem(5) + anywhere(7),
-        out_specs=pl.BlockSpec(memory_space=VMEM),
+    each = tiles // slabs
+    rest = tiles - FAR * each
+    alpha_top = 2.0 / (cells * slabs)
+    piece = shape(13, each, rows, LANES)
+    order = [(slab + by) % slabs * each + k for by in SHIFTS for k in range(each)]
+    *pieces, twice, slope = pl.pallas_call(
+        functools.partial(render, alpha_top=alpha_top),
+        out_shape=[piece] * FAR
+        + [shape(rest, cells + 2, 16, LANES), shape(rest, cells + 1, rows, LANES)],
+        in_specs=in_smem(6) + anywhere(7),
+        out_specs=anywhere(FAR + 2),
         scratch_shapes=[
             VMEM((cells + 6, tiles, 24, LANES), F32),
             VMEM((cells + 4, tiles, 16, LANES), F32),
@@ -422,12 +506,16 @@
             VMEM((tiles, 2, rows, LANES), F32),
             VMEM((2, tiles, 3 * cells, LANES), F32),
             VMEM((2, tiles, rows, LANES), F32),
+            VMEM((FAR, 13, each, rows, LANES), F32),
             DMA((7,)),
+            DMA((2, rest)),
+            DMA((FAR,)),
         ],
         compiler_params=limit,
         name="render",
     )(
         edges,
+        jnp.stack(order).astype(jnp.int32),
         colour_coef,
         opacity_coef,
         light_dir,
@@ -440,15 +528,37 @@
         top_corner,
         bottom_corner,
     )
-    exchanged = lax.all_to_all(partial, "depth", 0, 0, tiled=True)
+    pieces += pl.pallas_call(
+        functools.partial(render_rest, alpha_top=alpha_top),
+        out_shape=[piece] * (slabs - FAR),
+        in_specs=in_smem(4) + anywhere(2),
+        out_specs=anywhere(slabs - FAR),
+        scratch_shapes=[
+            VMEM((rest, cells + 2, 16, LANES), F32),
+            VMEM((rest, cells + 1, rows, LANES), F32),
+            VMEM((slabs - FAR, 13, each, rows, LANES), F32),
+            DMA((2, rest)),
+            DMA((slabs - FAR,)),
+        ],
+        compiler_params=limit,
+        cost_estimate=pl.CostEstimate(
+            flops=50_000_000, bytes_accessed=20_000_000, transcendentals=1_000_000
+        ),
+        name="render_rest",
+    )(colour_coef, opacity_coef, light_dir, light_colour, twice, slope)
+    arrived = [
+        lax.ppermute(value, "depth", ring("depth", by)) if by else value
+        for value, by in zip(pieces, SHIFTS)
+    ]
     own = pl.pallas_call(
         fold,
-        out_shape=shape(13, tiles // slabs, rows, LANES),
-        in_specs=in_vmem(1),
+        out_shape=piece,
+        in_specs=in_smem(1) + anywhere(slabs),
         out_specs=pl.BlockSpec(memory_space=VMEM),
+        scratch_shapes=[VMEM((slabs, 13, each, rows, LANES), F32), DMA((slabs,))],
         compiler_params=limit,
         name="fold",
-    )(exchanged)
+    )(slab[None], *arrived)
     from_below, from_above = [own], [own]
     for _ in range(slabs // 2):
         from_below.append(lax.ppermute(from_below[-1], "depth", ring("depth", 1)))

time: 110 us -> 104 us (0.945)
  the two profiles are of different devices: /device:TPU:8 before, /device:TPU:0 now
where the time goes in v6:
time: 104 us
  starting transfers between devices  41.4 us (40%)
  Pallas kernels  37.9 us (36%)
  waiting for transfers between devices  20.1 us (19%)
  local copies, waits for them, and re-layouts  3.6 us (3%)
    pallas_call x1, Pallas kernels, per_device(): pl.pallas_call(functools.partial(render, alpha_top=alpha_top), out_shape=...  20.2 us
    ppermute x7, starting transfers between devices, per_device(): lax.ppermute(value, 'depth', ring('depth', by))  17.1 us
    ppermute x4, waiting for transfers between devices, per_device(): from_below.append(lax.ppermute(from_below[-1], 'depth', ring('depth', 1)))  12.5 us
    ppermute x3, starting transfers between devices, per_device(): from_above.append(lax.ppermute(from_above[-1], 'depth', ring('depth', -1)))  9.73 us
    pallas_call x1, Pallas kernels, per_device(): pl.pallas_call(functools.partial(render_rest, alpha_top=alpha_top), out_s...  7.81 us
    ppermute x1, starting transfers between devices, per_device(): bottom = lax.ppermute(up, 'height', ring('height', -1))  5.05 us
    ppermute x1, starting transfers between devices, per_device(): bottom_corner = lax.ppermute(corner_up, 'height', ring('height', -1))  5.05 us
    ppermute x1, starting transfers between devices, per_device(): high = lax.ppermute(first, 'depth', ring('depth', -1))  3.94 us
  transfers between devices with their start and end apart: 20, of which 9 were waited for; matrix products, arithmetic and copies ran while one was open for 1% of the time, Pallas kernels for 11%

profile of v6, /device:TPU:0, one launch (start us, length us, event | category | flops | bytes accessed | tf_op | source)
XLA Modules:
  0.0 104.0 jit_solution(17363097092353713976)
XLA Ops:
  0.0 2.6 %pack.1 = (f32[16,96,128]{2,1,0:T(8,128)}, f32[16,96,128]{2,1,0:T(8,128)}, f32[3,16,8,128]{3,2,1,0:T(8,128)}, f32[3,16,8,128]{3,2,1,0:T(8,128)}) custom-call(f32[32,16,8,128]{3,2,1,0:T(8,128)} %bitcast.27), custom_call_target="tpu_custom_call" | custom-call | tf_op jit(solution)/shard_map/pack/pallas_call | solution.py:452
  2.6 0.1 collective-permute-start.2
  2.7 5.1 %collective-permute-start.3 = (f32[16,96,128]{2,1,0:T(8,128)}, f32[16,96,128]{2,1,0:T(8,128)}, u32[]{:S(2)}, u32[]{:S(2)}) collective-permute-start(f32[16,96,128]{2,1,0:T(8,128)} %get-tuple-element.24), channel_id=1, source_target_pairs={{0,31},{1,0},{2,1},{3,2},{4,3},{5,4},{6,5},{7,6},{8,7},{9,8},{10,9... | collective-permute-start | bytes 2359304 | tf_op jit(solution)/shard_map/ppermute | solution.py:471
  7.7 0.2 collective-permute-start
  7.9 3.9 %collective-permute-start.1 = (f32[3,16,8,128]{3,2,1,0:T(8,128)}, f32[3,16,8,128]{3,2,1,0:T(8,128)}, u32[]{:S(2)}, u32[]{:S(2)}) collective-permute-start(f32[3,16,8,128]{3,2,1,0:T(8,128)} %get-tuple-element.22), channel_id=1, source_target_pairs={{0,224},{32,0},{64,32},{96,64},{128,96},{160,128},{192,160},{224,1... | collective-permute-start | bytes 589832 | tf_op jit(solution)/shard_map/ppermute | solution.py:469
  11.8 0.7 stack.87.tile_ref
  12.5 3.2 %collective-permute-done.low_ref = f32[3,16,8,128]{3,2,1,0:T(8,128)S(1)} collective-permute-done((f32[3,16,8,128]{3,2,1,0:T(8,128)}, f32[3,16,8,128]{3,2,1,0:T(8,128)S(1)}, u32[]{:S(2)}, u32[]{:S(2)}) %collective-permute-start) | collective-permute-done | bytes 196640 | tf_op jit(solution)/shard_map/ppermute | solution.py:468
  15.7 0.7 copy-done.1
  16.4 1.7 %pack_corners.1 = (f32[16,8,128]{2,1,0:T(8,128)}, f32[16,8,128]{2,1,0:T(8,128)}) custom-call(f32[3,16,8,128]{3,2,1,0:T(8,128)} %copy-done.1, f32[3,16,8,128]{3,2,1,0:T(8,128)} %collective-permute-done.1.high_ref), custom_call_target="tpu_custom_call" | custom-call | flops 400000000 | bytes 80000000 | tf_op jit(solution)/shard_map/pack_corners/pallas_call | solution.py:472
  18.1 0.1 collective-permute-start.4
  18.2 5.1 %collective-permute-start.5 = (f32[16,8,128]{2,1,0:T(8,128)}, f32[16,8,128]{2,1,0:T(8,128)S(1)}, u32[]{:S(2)}, u32[]{:S(2)}) collective-permute-start(f32[16,8,128]{2,1,0:T(8,128)} %get-tuple-element.26), channel_id=1, source_target_pairs={{0,31},{1,0},{2,1},{3,2},{4,3},{5,4},{6,5},{7,6},{8,7},{9,8},{10,9... | collective-permute-start | bytes 196616 | tf_op jit(solution)/shard_map/ppermute | solution.py:485
  23.3 0.7 add_convert_fusion.edge_ref
  23.9 1.5 %collective-permute-done.4.top_corner_ref = f32[16,8,128]{2,1,0:T(8,128)S(1)} collective-permute-done((f32[16,8,128]{2,1,0:T(8,128)}, f32[16,8,128]{2,1,0:T(8,128)S(1)}, u32[]{:S(2)}, u32[]{:S(2)}) %collective-permute-start.4) | collective-permute-done | bytes 65568 | tf_op jit(solution)/shard_map/ppermute | solution.py:484
  25.4 0.1 collective-permute-done.5.bottom_corner_ref
  25.5 0.0 collective-permute-done.2.top_ref
  25.5 0.5 copy-done.16
  26.0 0.1 copy-done.17
  26.1 0.3 copy-done
  26.4 20.2 %render.1 = (f32[13,2,8,128]{3,2,1,0:T(8,128)}, f32[13,2,8,128]{3,2,1,0:T(8,128)}, f32[13,2,8,128]{3,2,1,0:T(8,128)}, f32[10,34,16,128]{3,2,1,0:T(8,128)}, f32[10,33,8,128]{3,2,1,0:T(8,128)}) custom-call(f32[4]{0:T(128)} %add_convert_fusion.edge_ref, s32[16]{0:T(128)} %stack.87.tile_ref, f32[3,4]{1,0:T(4,128)} %colour_ref.3, f32[4]{0:T(128)} %opacity_ref.3, ...), custom_call_target="tpu_custom_call" | custom-call | tf_op jit(solution)/shard_map/render/pallas_call | solution.py:493
  46.6 4.7 %collective-permute-start.6 = (f32[13,2,8,128]{3,2,1,0:T(8,128)}, f32[13,2,8,128]{3,2,1,0:T(8,128)S(1)}, u32[]{:S(2)}, u32[]{:S(2)}) collective-permute-start(f32[13,2,8,128]{3,2,1,0:T(8,128)} %get-tuple-element.27), channel_id=1, source_target_pairs={{0,128},{32,160},{64,192},{96,224},{128,0},{160,32},{192,64},{224,... | collective-permute-start | bytes 319496 | tf_op jit(solution)/shard_map/ppermute | solution.py:550
  51.2 1.4 %collective-permute-start.7 = (f32[13,2,8,128]{3,2,1,0:T(8,128)}, f32[13,2,8,128]{3,2,1,0:T(8,128)S(1)}, u32[]{:S(2)}, u32[]{:S(2)}) collective-permute-start(f32[13,2,8,128]{3,2,1,0:T(8,128)} %get-tuple-element.28), channel_id=1, source_target_pairs={{0,96},{32,128},{64,160},{96,192},{128,224},{160,0},{192,32},{224,... | collective-permute-start | bytes 319496 | tf_op jit(solution)/shard_map/ppermute | solution.py:550
  52.6 3.7 %collective-permute-start.8 = (f32[13,2,8,128]{3,2,1,0:T(8,128)}, f32[13,2,8,128]{3,2,1,0:T(8,128)S(1)}, u32[]{:S(2)}, u32[]{:S(2)}) collective-permute-start(f32[13,2,8,128]{3,2,1,0:T(8,128)} %get-tuple-element.29), channel_id=1, source_target_pairs={{0,160},{32,192},{64,224},{96,0},{128,32},{160,64},{192,96},{224,1... | collective-permute-start | bytes 319496 | tf_op jit(solution)/shard_map/ppermute | solution.py:550
  56.3 7.8 %render_rest.1 = (f32[13,2,8,128]{3,2,1,0:T(8,128)}, f32[13,2,8,128]{3,2,1,0:T(8,128)}, f32[13,2,8,128]{3,2,1,0:T(8,128)}, f32[13,2,8,128]{3,2,1,0:T(8,128)}, f32[13,2,8,128]{3,2,1,0:T(8,128)}) custom-call(f32[3,4]{1,0:T(4,128)} %colour_ref.3, f32[4]{0:T(128)} %opacity_ref.3, f32[4,3]{1,0:T(4,128)} %dir_ref.3, f32[4,3]{1,0:T(4,128)} %light_ref.3, ...), custom_call_target="tpu_custom_call" | custom-call | flops 50000000 | bytes 20000000 | tf_op jit(solution)/shard_map/render_rest/pallas_call | solution.py:531
  64.1 0.8 collective-permute-start.9
  64.8 3.4 %collective-permute-start.10 = (f32[13,2,8,128]{3,2,1,0:T(8,128)}, f32[13,2,8,128]{3,2,1,0:T(8,128)S(1)}, u32[]{:S(2)}, u32[]{:S(2)}) collective-permute-start(f32[13,2,8,128]{3,2,1,0:T(8,128)} %get-tuple-element.33), channel_id=1, source_target_pairs={{0,192},{32,224},{64,0},{96,32},{128,64},{160,96},{192,128},{224,1... | collective-permute-start | bytes 319496 | tf_op jit(solution)/shard_map/ppermute | solution.py:550
  68.3 0.3 collective-permute-start.11
  68.5 0.0 collective-permute-done.7.refs_1_
  68.5 3.0 %collective-permute-start.12 = (f32[13,2,8,128]{3,2,1,0:T(8,128)}, f32[13,2,8,128]{3,2,1,0:T(8,128)S(1)}, u32[]{:S(2)}, u32[]{:S(2)}) collective-permute-start(f32[13,2,8,128]{3,2,1,0:T(8,128)} %get-tuple-element.35), channel_id=1, source_target_pairs={{0,224},{32,0},{64,32},{96,64},{128,96},{160,128},{192,160},{224,1... | collective-permute-start | bytes 319496 | tf_op jit(solution)/shard_map/ppermute | solution.py:550
  71.5 0.0 collective-permute-done.8.refs_2_
  71.5 0.5 collective-permute-done.9.refs_3_
  72.0 0.0 collective-permute-done.10.refs_4_
  72.0 2.4 %collective-permute-done.11.refs_5_ = f32[13,2,8,128]{3,2,1,0:T(8,128)S(1)} collective-permute-done((f32[13,2,8,128]{3,2,1,0:T(8,128)}, f32[13,2,8,128]{3,2,1,0:T(8,128)S(1)}, u32[]{:S(2)}, u32[]{:S(2)}) %collective-permute-start.11) | collective-permute-done | bytes 106528 | tf_op jit(solution)/shard_map/ppermute | solution.py:550
  74.4 0.0 collective-permute-done.12.refs_6_
  74.5 0.6 copy-done.9
  75.1 0.1 copy-done.11
  75.1 2.0 %fold.1.refs_1_ = f32[13,2,8,128]{3,2,1,0:T(8,128)} custom-call(s32[1]{0:T(128)} %bitcast.place_ref, f32[13,2,8,128]{3,2,1,0:T(8,128)} %copy-done.2, f32[13,2,8,128]{3,2,1,0:T(8,128)} %copy-done.3, f32[13,2,8,128]{3,2,1,0:T(8,128)} %copy-done.4, f32[13,2,8,128]{3,2,1,0:T(8,128)} %copy-done.5, f32[13,2,8,128]{3,2,1,0:T(8,128)} %copy-done.6, ...), custom_call_target="tpu_custom_call" | custom-call | tf_op jit(solution)/shard_map/fold/pallas_call | solution.py:553
  77.1 0.1 collective-permute-start.16
  77.2 3.3 %collective-permute-start.13 = (f32[13,2,8,128]{3,2,1,0:T(8,128)}, f32[13,2,8,128]{3,2,1,0:T(8,128)S(1)}, u32[]{:S(2)}, u32[]{:S(2)}) collective-permute-start(f32[13,2,8,128]{3,2,1,0:T(8,128)} %fold.1.refs_1_), channel_id=1, source_target_pairs={{0,224},{32,0},{64,32},{96,64},{128,96},{160,128},{192,160},{224,1... | collective-permute-start | bytes 319496 | tf_op jit(solution)/shard_map/ppermute | solution.py:565
  80.5 2.9 %collective-permute-done.16.refs_2_ = f32[13,2,8,128]{3,2,1,0:T(8,128)S(1)} collective-permute-done((f32[13,2,8,128]{3,2,1,0:T(8,128)}, f32[13,2,8,128]{3,2,1,0:T(8,128)S(1)}, u32[]{:S(2)}, u32[]{:S(2)}) %collective-permute-start.16) | collective-permute-done | bytes 106528 | tf_op jit(solution)/shard_map/ppermute | solution.py:564
  83.3 0.0 collective-permute-start.17
  83.4 3.3 %collective-permute-start.14 = (f32[13,2,8,128]{3,2,1,0:T(8,128)S(1)}, f32[13,2,8,128]{3,2,1,0:T(8,128)S(1)}, u32[]{:S(2)}, u32[]{:S(2)}) collective-permute-start(f32[13,2,8,128]{3,2,1,0:T(8,128)S(1)} %collective-permute-done.13.refs_0_), channel_id=1, source_target_pairs={{0,224},{32,0},{64,32},{96,64},{128,96},{160,128},{192,160},{224,1... | collective-permute-start | bytes 319496 | tf_op jit(solution)/shard_map/ppermute | solution.py:565
  86.6 2.9 %collective-permute-done.17.refs_3_ = f32[13,2,8,128]{3,2,1,0:T(8,128)S(1)} collective-permute-done((f32[13,2,8,128]{3,2,1,0:T(8,128)S(1)}, f32[13,2,8,128]{3,2,1,0:T(8,128)S(1)}, u32[]{:S(2)}, u32[]{:S(2)}) %collective-permute-start.17) | collective-permute-done | bytes 106528 | tf_op jit(solution)/shard_map/ppermute | solution.py:564
  89.6 3.2 %collective-permute-start.15 = (f32[13,2,8,128]{3,2,1,0:T(8,128)S(1)}, f32[13,2,8,128]{3,2,1,0:T(8,128)S(1)}, u32[]{:S(2)}, u32[]{:S(2)}) collective-permute-start(f32[13,2,8,128]{3,2,1,0:T(8,128)S(1)} %collective-permute-done.14.refs_1_), channel_id=1, source_target_pairs={{0,224},{32,0},{64,32},{96,64},{128,96},{160,128},{192,160},{224,1... | collective-permute-start | bytes 319496 | tf_op jit(solution)/shard_map/ppermute | solution.py:565
  92.8 2.7 %collective-permute-done.18.refs_2_ = f32[13,2,8,128]{3,2,1,0:T(8,128)S(1)} collective-permute-done((f32[13,2,8,128]{3,2,1,0:T(8,128)S(1)}, f32[13,2,8,128]{3,2,1,0:T(8,128)S(1)}, u32[]{:S(2)}, u32[]{:S(2)}) %collective-permute-start.18) | collective-permute-done | bytes 106528 | tf_op jit(solution)/shard_map/ppermute | solution.py:564
  95.5 1.9 %spread.2.refs_4_ = f32[13,16,8,128]{3,2,1,0:T(8,128)} custom-call(s32[1]{0:T(128)} %bitcast.place_ref, f32[13,2,8,128]{3,2,1,0:T(8,128)} %copy-done.8, f32[13,2,8,128]{3,2,1,0:T(8,128)} %fold.1.refs_1_, f32[13,2,8,128]{3,2,1,0:T(8,128)} %copy-done.7, f32[13,2,8,128]{3,2,1,0:T(8,128)} %copy-done.10), custom_call_target="tpu_custom_call" | custom-call | tf_op jit(solution)/shard_map/spread/pallas_call | solution.py:573
  97.4 4.0 %collective-permute-done.19.refs_3_ = f32[13,2,8,128]{3,2,1,0:T(8,128)S(1)} collective-permute-done((f32[13,2,8,128]{3,2,1,0:T(8,128)S(1)}, f32[13,2,8,128]{3,2,1,0:T(8,128)S(1)}, u32[]{:S(2)}, u32[]{:S(2)}) %collective-permute-start.19) | collective-permute-done | bytes 106528 | tf_op jit(solution)/shard_map/ppermute | solution.py:564
  101.4 0.6 copy-done.15
  102.0 1.8 %spread.3 = f32[13,16,8,128]{3,2,1,0:T(8,128)} custom-call(s32[1]{0:T(128)} %bitcast.place_ref, f32[13,2,8,128]{3,2,1,0:T(8,128)} %copy-done.14, f32[13,2,8,128]{3,2,1,0:T(8,128)} %copy-done.12, f32[13,2,8,128]{3,2,1,0:T(8,128)} %copy-done.13, f32[13,2,8,128]{3,2,1,0:T(8,128)} %copy-done.15, ...), custom_call_target="tpu_custom_call", output_to_operand_aliasing={{}: (5, {})} | custom-call | tf_op jit(solution)/shard_map/spread/pallas_call | solution.py:573
  (37 shorter events, 0.1 us)
Async XLA Ops:
  2.6 22.9 %collective-permute-start.2 = (f32[16,96,128]{2,1,0:T(8,128)}, f32[16,96,128]{2,1,0:T(8,128)S(1)}, u32[]{:S(2)}, u32[]{:S(2)}) collective-permute-start(f32[16,96,128]{2,1,0:T(8,128)} %get-tuple-element.23), channel_id=1, source_target_pairs={{0,1},{1,2},{2,3},{3,4},{4,5},{5,6},{6,7},{7,8},{8,9},{9,10},{10,1... | collective-permute-start | bytes 2359304 | tf_op jit(solution)/shard_map/ppermute | solution.py:470
  2.7 22.8 %collective-permute-start.3 = (f32[16,96,128]{2,1,0:T(8,128)}, f32[16,96,128]{2,1,0:T(8,128)}, u32[]{:S(2)}, u32[]{:S(2)}) collective-permute-start(f32[16,96,128]{2,1,0:T(8,128)} %get-tuple-element.24), channel_id=1, source_target_pairs={{0,31},{1,0},{2,1},{3,2},{4,3},{5,4},{6,5},{7,6},{8,7},{9,8},{10,9... | collective-permute-start | bytes 2359304 | tf_op jit(solution)/shard_map/ppermute | solution.py:471
  7.7 8.0 %collective-permute-start = (f32[3,16,8,128]{3,2,1,0:T(8,128)}, f32[3,16,8,128]{3,2,1,0:T(8,128)S(1)}, u32[]{:S(2)}, u32[]{:S(2)}) collective-permute-start(f32[3,16,8,128]{3,2,1,0:T(8,128)} %get-tuple-element.21), channel_id=1, source_target_pairs={{0,32},{32,64},{64,96},{96,128},{128,160},{160,192},{192,224},{224... | collective-permute-start | bytes 589832 | tf_op jit(solution)/shard_map/ppermute | solution.py:468
  7.9 7.8 %collective-permute-start.1 = (f32[3,16,8,128]{3,2,1,0:T(8,128)}, f32[3,16,8,128]{3,2,1,0:T(8,128)}, u32[]{:S(2)}, u32[]{:S(2)}) collective-permute-start(f32[3,16,8,128]{3,2,1,0:T(8,128)} %get-tuple-element.22), channel_id=1, source_target_pairs={{0,224},{32,0},{64,32},{96,64},{128,96},{160,128},{192,160},{224,1... | collective-permute-start | bytes 589832 | tf_op jit(solution)/shard_map/ppermute | solution.py:469
  15.7 0.7 copy-start.1
  18.1 7.3 %collective-permute-start.4 = (f32[16,8,128]{2,1,0:T(8,128)}, f32[16,8,128]{2,1,0:T(8,128)S(1)}, u32[]{:S(2)}, u32[]{:S(2)}) collective-permute-start(f32[16,8,128]{2,1,0:T(8,128)} %get-tuple-element.25), channel_id=1, source_target_pairs={{0,1},{1,2},{2,3},{3,4},{4,5},{5,6},{6,7},{7,8},{8,9},{9,10},{10,1... | collective-permute-start | bytes 196616 | tf_op jit(solution)/shard_map/ppermute | solution.py:484
  18.2 7.3 %collective-permute-start.5 = (f32[16,8,128]{2,1,0:T(8,128)}, f32[16,8,128]{2,1,0:T(8,128)S(1)}, u32[]{:S(2)}, u32[]{:S(2)}) collective-permute-start(f32[16,8,128]{2,1,0:T(8,128)} %get-tuple-element.26), channel_id=1, source_target_pairs={{0,31},{1,0},{2,1},{3,2},{4,3},{5,4},{6,5},{7,6},{8,7},{9,8},{10,9... | collective-permute-start | bytes 196616 | tf_op jit(solution)/shard_map/ppermute | solution.py:485
  25.4 0.6 copy-start.16
  25.5 0.6 copy-start.17
  25.5 0.9 copy-start
  46.6 21.7 %collective-permute-start.6 = (f32[13,2,8,128]{3,2,1,0:T(8,128)}, f32[13,2,8,128]{3,2,1,0:T(8,128)S(1)}, u32[]{:S(2)}, u32[]{:S(2)}) collective-permute-start(f32[13,2,8,128]{3,2,1,0:T(8,128)} %get-tuple-element.27), channel_id=1, source_target_pairs={{0,128},{32,160},{64,192},{96,224},{128,0},{160,32},{192,64},{224,... | collective-permute-start | bytes 319496 | tf_op jit(solution)/shard_map/ppermute | solution.py:550
  51.2 17.3 %collective-permute-start.7 = (f32[13,2,8,128]{3,2,1,0:T(8,128)}, f32[13,2,8,128]{3,2,1,0:T(8,128)S(1)}, u32[]{:S(2)}, u32[]{:S(2)}) collective-permute-start(f32[13,2,8,128]{3,2,1,0:T(8,128)} %get-tuple-element.28), channel_id=1, source_target_pairs={{0,96},{32,128},{64,160},{96,192},{128,224},{160,0},{192,32},{224,... | collective-permute-start | bytes 319496 | tf_op jit(solution)/shard_map/ppermute | solution.py:550
  52.6 19.0 %collective-permute-start.8 = (f32[13,2,8,128]{3,2,1,0:T(8,128)}, f32[13,2,8,128]{3,2,1,0:T(8,128)S(1)}, u32[]{:S(2)}, u32[]{:S(2)}) collective-permute-start(f32[13,2,8,128]{3,2,1,0:T(8,128)} %get-tuple-element.29), channel_id=1, source_target_pairs={{0,160},{32,192},{64,224},{96,0},{128,32},{160,64},{192,96},{224,1... | collective-permute-start | bytes 319496 | tf_op jit(solution)/shard_map/ppermute | solution.py:550
  64.1 7.9 %collective-permute-start.9 = (f32[13,2,8,128]{3,2,1,0:T(8,128)}, f32[13,2,8,128]{3,2,1,0:T(8,128)S(1)}, u32[]{:S(2)}, u32[]{:S(2)}) collective-permute-start(f32[13,2,8,128]{3,2,1,0:T(8,128)} %get-tuple-element.32), channel_id=1, source_target_pairs={{0,64},{32,96},{64,128},{96,160},{128,192},{160,224},{192,0},{224,... | collective-permute-start | bytes 319496 | tf_op jit(solution)/shard_map/ppermute | solution.py:550
  64.8 7.2 %collective-permute-start.10 = (f32[13,2,8,128]{3,2,1,0:T(8,128)}, f32[13,2,8,128]{3,2,1,0:T(8,128)S(1)}, u32[]{:S(2)}, u32[]{:S(2)}) collective-permute-start(f32[13,2,8,128]{3,2,1,0:T(8,128)} %get-tuple-element.33), channel_id=1, source_target_pairs={{0,192},{32,224},{64,0},{96,32},{128,64},{160,96},{192,128},{224,1... | collective-permute-start | bytes 319496 | tf_op jit(solution)/shard_map/ppermute | solution.py:550
  68.3 6.1 %copy-start.2 = (f32[13,2,8,128]{3,2,1,0:T(8,128)}, f32[13,2,8,128]{3,2,1,0:T(8,128)S(1)}, u32[]{:S(2)}) copy-start(f32[13,2,8,128]{3,2,1,0:T(8,128)S(1)} %collective-permute-done.6.refs_0_) | copy-start | bytes 319492
  68.3 6.1 %collective-permute-start.11 = (f32[13,2,8,128]{3,2,1,0:T(8,128)}, f32[13,2,8,128]{3,2,1,0:T(8,128)S(1)}, u32[]{:S(2)}, u32[]{:S(2)}) collective-permute-start(f32[13,2,8,128]{3,2,1,0:T(8,128)} %get-tuple-element.34), channel_id=1, source_target_pairs={{0,32},{32,64},{64,96},{96,128},{128,160},{160,192},{192,224},{224... | collective-permute-start | bytes 319496 | tf_op jit(solution)/shard_map/ppermute | solution.py:550
  68.5 5.9 %copy-start.3 = (f32[13,2,8,128]{3,2,1,0:T(8,128)}, f32[13,2,8,128]{3,2,1,0:T(8,128)S(1)}, u32[]{:S(2)}) copy-start(f32[13,2,8,128]{3,2,1,0:T(8,128)S(1)} %collective-permute-done.7.refs_1_) | copy-start | bytes 319492
  68.5 5.9 %collective-permute-start.12 = (f32[13,2,8,128]{3,2,1,0:T(8,128)}, f32[13,2,8,128]{3,2,1,0:T(8,128)S(1)}, u32[]{:S(2)}, u32[]{:S(2)}) collective-permute-start(f32[13,2,8,128]{3,2,1,0:T(8,128)} %get-tuple-element.35), channel_id=1, source_target_pairs={{0,224},{32,0},{64,32},{96,64},{128,96},{160,128},{192,160},{224,1... | collective-permute-start | bytes 319496 | tf_op jit(solution)/shard_map/ppermute | solution.py:550
  71.5 2.9 %copy-start.4 = (f32[13,2,8,128]{3,2,1,0:T(8,128)}, f32[13,2,8,128]{3,2,1,0:T(8,128)S(1)}, u32[]{:S(2)}) copy-start(f32[13,2,8,128]{3,2,1,0:T(8,128)S(1)} %collective-permute-done.8.refs_2_) | copy-start | bytes 319492
  72.0 2.5 %copy-start.5 = (f32[13,2,8,128]{3,2,1,0:T(8,128)}, f32[13,2,8,128]{3,2,1,0:T(8,128)S(1)}, u32[]{:S(2)}) copy-start(f32[13,2,8,128]{3,2,1,0:T(8,128)S(1)} %collective-permute-done.9.refs_3_) | copy-start | bytes 319492
  72.0 2.5 %copy-start.6 = (f32[13,2,8,128]{3,2,1,0:T(8,128)}, f32[13,2,8,128]{3,2,1,0:T(8,128)S(1)}, u32[]{:S(2)}) copy-start(f32[13,2,8,128]{3,2,1,0:T(8,128)S(1)} %collective-permute-done.10.refs_4_) | copy-start | bytes 319492
  74.4 0.7 copy-start.9
  74.4 0.7 copy-start.11
  77.1 6.2 %collective-permute-start.16 = (f32[13,2,8,128]{3,2,1,0:T(8,128)}, f32[13,2,8,128]{3,2,1,0:T(8,128)S(1)}, u32[]{:S(2)}, u32[]{:S(2)}) collective-permute-start(f32[13,2,8,128]{3,2,1,0:T(8,128)} %fold.1.refs_1_), channel_id=1, source_target_pairs={{0,32},{32,64},{64,96},{96,128},{128,160},{160,192},{192,224},{224... | collective-permute-start | bytes 319496 | tf_op jit(solution)/shard_map/ppermute | solution.py:564
  77.2 6.1 %collective-permute-start.13 = (f32[13,2,8,128]{3,2,1,0:T(8,128)}, f32[13,2,8,128]{3,2,1,0:T(8,128)S(1)}, u32[]{:S(2)}, u32[]{:S(2)}) collective-permute-start(f32[13,2,8,128]{3,2,1,0:T(8,128)} %fold.1.refs_1_), channel_id=1, source_target_pairs={{0,224},{32,0},{64,32},{96,64},{128,96},{160,128},{192,160},{224,1... | collective-permute-start | bytes 319496 | tf_op jit(solution)/shard_map/ppermute | solution.py:565
  83.3 12.1 %copy-start.7 = (f32[13,2,8,128]{3,2,1,0:T(8,128)}, f32[13,2,8,128]{3,2,1,0:T(8,128)S(1)}, u32[]{:S(2)}) copy-start(f32[13,2,8,128]{3,2,1,0:T(8,128)S(1)} %collective-permute-done.16.refs_2_) | copy-start | bytes 319492
  83.3 6.2 %collective-permute-start.17 = (f32[13,2,8,128]{3,2,1,0:T(8,128)S(1)}, f32[13,2,8,128]{3,2,1,0:T(8,128)S(1)}, u32[]{:S(2)}, u32[]{:S(2)}) collective-permute-start(f32[13,2,8,128]{3,2,1,0:T(8,128)S(1)} %collective-permute-done.16.refs_2_), channel_id=1, source_target_pairs={{0,32},{32,64},{64,96},{96,128},{128,160},{160,192},{192,224},{224... | collective-permute-start | bytes 319496 | tf_op jit(solution)/shard_map/ppermute | solution.py:564
  83.3 12.1 %copy-start.8 = (f32[13,2,8,128]{3,2,1,0:T(8,128)}, f32[13,2,8,128]{3,2,1,0:T(8,128)S(1)}, u32[]{:S(2)}) copy-start(f32[13,2,8,128]{3,2,1,0:T(8,128)S(1)} %collective-permute-done.13.refs_0_) | copy-start | bytes 319492
  83.4 6.2 %collective-permute-start.14 = (f32[13,2,8,128]{3,2,1,0:T(8,128)S(1)}, f32[13,2,8,128]{3,2,1,0:T(8,128)S(1)}, u32[]{:S(2)}, u32[]{:S(2)}) collective-permute-start(f32[13,2,8,128]{3,2,1,0:T(8,128)S(1)} %collective-permute-done.13.refs_0_), channel_id=1, source_target_pairs={{0,224},{32,0},{64,32},{96,64},{128,96},{160,128},{192,160},{224,1... | collective-permute-start | bytes 319496 | tf_op jit(solution)/shard_map/ppermute | solution.py:565
  89.6 5.9 %copy-start.10 = (f32[13,2,8,128]{3,2,1,0:T(8,128)}, f32[13,2,8,128]{3,2,1,0:T(8,128)S(1)}, u32[]{:S(2)}) copy-start(f32[13,2,8,128]{3,2,1,0:T(8,128)S(1)} %collective-permute-done.17.refs_3_) | copy-start | bytes 319492
  89.6 5.9 %collective-permute-start.18 = (f32[13,2,8,128]{3,2,1,0:T(8,128)S(1)}, f32[13,2,8,128]{3,2,1,0:T(8,128)S(1)}, u32[]{:S(2)}, u32[]{:S(2)}) collective-permute-start(f32[13,2,8,128]{3,2,1,0:T(8,128)S(1)} %collective-permute-done.17.refs_3_), channel_id=1, source_target_pairs={{0,32},{32,64},{64,96},{96,128},{128,160},{160,192},{192,224},{224... | collective-permute-start | bytes 319496 | tf_op jit(solution)/shard_map/ppermute | solution.py:564
  89.6 11.8 %copy-start.12 = (f32[13,2,8,128]{3,2,1,0:T(8,128)}, f32[13,2,8,128]{3,2,1,0:T(8,128)S(1)}, u32[]{:S(2)}) copy-start(f32[13,2,8,128]{3,2,1,0:T(8,128)S(1)} %collective-permute-done.14.refs_1_) | copy-start | bytes 319492
  89.6 7.8 %collective-permute-start.15 = (f32[13,2,8,128]{3,2,1,0:T(8,128)S(1)}, f32[13,2,8,128]{3,2,1,0:T(8,128)S(1)}, u32[]{:S(2)}, u32[]{:S(2)}) collective-permute-start(f32[13,2,8,128]{3,2,1,0:T(8,128)S(1)} %collective-permute-done.14.refs_1_), channel_id=1, source_target_pairs={{0,224},{32,0},{64,32},{96,64},{128,96},{160,128},{192,160},{224,1... | collective-permute-start | bytes 319496 | tf_op jit(solution)/shard_map/ppermute | solution.py:565
  95.5 5.9 %copy-start.13 = (f32[13,2,8,128]{3,2,1,0:T(8,128)}, f32[13,2,8,128]{3,2,1,0:T(8,128)S(1)}, u32[]{:S(2)}) copy-start(f32[13,2,8,128]{3,2,1,0:T(8,128)S(1)} %collective-permute-done.18.refs_2_) | copy-start | bytes 319492
  95.5 5.9 %collective-permute-start.19 = (f32[13,2,8,128]{3,2,1,0:T(8,128)S(1)}, f32[13,2,8,128]{3,2,1,0:T(8,128)S(1)}, u32[]{:S(2)}, u32[]{:S(2)}) collective-permute-start(f32[13,2,8,128]{3,2,1,0:T(8,128)S(1)} %collective-permute-done.18.refs_2_), channel_id=1, source_target_pairs={{0,32},{32,64},{64,96},{96,128},{128,160},{160,192},{192,224},{224... | collective-permute-start | bytes 319496 | tf_op jit(solution)/shard_map/ppermute | solution.py:564
  97.4 4.0 %copy-start.14 = (f32[13,2,8,128]{3,2,1,0:T(8,128)}, f32[13,2,8,128]{3,2,1,0:T(8,128)S(1)}, u32[]{:S(2)}) copy-start(f32[13,2,8,128]{3,2,1,0:T(8,128)S(1)} %collective-permute-done.15.refs_0_) | copy-start | bytes 319492
  101.4 0.6 copy-start.15

commit v7 on v6

--- a/solution.py
+++ b/solution.py
@@ -559,13 +559,13 @@
         compiler_params=limit,
         name="fold",
     )(slab[None], *arrived)
-    from_below, from_above = [own], [own]
-    for _ in range(slabs // 2):
-        from_below.append(lax.ppermute(from_below[-1], "depth", ring("depth", 1)))
-        from_above.append(lax.ppermute(from_above[-1], "depth", ring("depth", -1)))
-    count = slabs // 2
-    early = list(range(1 - count // 2, 1 + count // 2))
-    late = [k for k in range(1 - count, 1 + count) if k not in early]
+    known = {0: own}
+    for by in (1, -1, 2, -2):
+        known[by] = lax.ppermute(own, "depth", ring("depth", by))
+    early = list(known)
+    for held, by in ((2, 1), (-2, -1), (2, 2)):
+        known[held + by] = lax.ppermute(known[held], "depth", ring("depth", by))
+    late = [by for by in known if by not in early]
     image = []
     for offsets in (early, late):
         aliases = {1 + len(offsets): 0} if image else {}
@@ -581,7 +581,7 @@
                 name="spread",
             )(
                 slab[None],
-                *[from_below[k] if k >= 0 else from_above[-k] for k in offsets],
+                *[known[by] for by in offsets],
                 *image,
             )
         ]

time: 104 us -> 103 us (level); the launches traced: 104 us -> 102 us
  waiting for transfers between devices: 20.1 us -> 12.8 us
  starting transfers between devices: 41.4 us -> 45.1 us
  local copies, waits for them, and re-layouts: 3.6 us -> 4.85 us
    ppermute x7, waiting for transfers between devices: 12.5 us -> 5.2 us  [the longest x3 3.84 us: per_device(): known[held + by] = lax.ppermute(known[held], 'depth', ring('depth', by))]
    ppermute x7, starting transfers between devices: 9.83 us -> 13.5 us  [the longest x4 7.68 us: per_device(): known[by] = lax.ppermute(own, 'depth', ring('depth', by))]
    unnamed x36, local copies, waits for them, and re-layouts: 2.92 us -> 4.17 us
  transfers between devices with their start and end apart: 20 -> 20, of which waited for: 9 -> 8; matrix products, arithmetic and copies ran while one was open for 1% -> 1% of each run, Pallas kernels for 11% -> 11%
where the time goes in v7:
time: 103 us; the launch traced here: 102 us
  starting transfers between devices  45.1 us (44%)
  Pallas kernels  37.9 us (37%)
  waiting for transfers between devices  12.8 us (12%)
  local copies, waits for them, and re-layouts  4.85 us (5%)
    pallas_call x1, Pallas kernels, per_device(): pl.pallas_call(functools.partial(render, alpha_top=alpha_top), out_shape=...  20.2 us
    ppermute x7, starting transfers between devices, per_device(): lax.ppermute(value, 'depth', ring('depth', by))  17.1 us
    pallas_call x1, Pallas kernels, per_device(): pl.pallas_call(functools.partial(render_rest, alpha_top=alpha_top), out_s...  7.81 us
    ppermute x4, starting transfers between devices, per_device(): known[by] = lax.ppermute(own, 'depth', ring('depth', by))  7.68 us
    ppermute x3, starting transfers between devices, per_device(): known[held + by] = lax.ppermute(known[held], 'depth', ring('depth', by))  5.86 us
    ppermute x1, starting transfers between devices, per_device(): bottom = lax.ppermute(up, 'height', ring('height', -1))  5.05 us
    ppermute x1, starting transfers between devices, per_device(): bottom_corner = lax.ppermute(corner_up, 'height', ring('height', -1))  5.05 us
    unnamed x36, local copies, waits for them, and re-layouts  4.17 us
  transfers between devices with their start and end apart: 20, of which 8 were waited for; matrix products, arithmetic and copies ran while one was open for 1% of the time, Pallas kernels for 11%

profile of v7, /device:TPU:0, one launch (start us, length us, event | category | flops | bytes accessed | tf_op | source)
XLA Modules:
  0.0 101.7 jit_solution(4777919710926619202)
XLA Ops:
  0.0 2.6 %pack.1 = (f32[16,96,128]{2,1,0:T(8,128)}, f32[16,96,128]{2,1,0:T(8,128)}, f32[3,16,8,128]{3,2,1,0:T(8,128)}, f32[3,16,8,128]{3,2,1,0:T(8,128)}) custom-call(f32[32,16,8,128]{3,2,1,0:T(8,128)} %bitcast.27), custom_call_target="tpu_custom_call" | custom-call | tf_op jit(solution)/shard_map/pack/pallas_call | solution.py:452
  2.6 0.1 collective-permute-start.2
  2.7 5.1 %collective-permute-start.3 = (f32[16,96,128]{2,1,0:T(8,128)}, f32[16,96,128]{2,1,0:T(8,128)}, u32[]{:S(2)}, u32[]{:S(2)}) collective-permute-start(f32[16,96,128]{2,1,0:T(8,128)} %get-tuple-element.24), channel_id=1, source_target_pairs={{0,31},{1,0},{2,1},{3,2},{4,3},{5,4},{6,5},{7,6},{8,7},{9,8},{10,9... | collective-permute-start | bytes 2359304 | tf_op jit(solution)/shard_map/ppermute | solution.py:471
  7.7 0.2 collective-permute-start
  7.9 3.9 %collective-permute-start.1 = (f32[3,16,8,128]{3,2,1,0:T(8,128)}, f32[3,16,8,128]{3,2,1,0:T(8,128)}, u32[]{:S(2)}, u32[]{:S(2)}) collective-permute-start(f32[3,16,8,128]{3,2,1,0:T(8,128)} %get-tuple-element.22), channel_id=1, source_target_pairs={{0,224},{32,0},{64,32},{96,64},{128,96},{160,128},{192,160},{224,1... | collective-permute-start | bytes 589832 | tf_op jit(solution)/shard_map/ppermute | solution.py:469
  11.8 0.7 stack.87.tile_ref
  12.5 3.2 %collective-permute-done.low_ref = f32[3,16,8,128]{3,2,1,0:T(8,128)S(1)} collective-permute-done((f32[3,16,8,128]{3,2,1,0:T(8,128)}, f32[3,16,8,128]{3,2,1,0:T(8,128)S(1)}, u32[]{:S(2)}, u32[]{:S(2)}) %collective-permute-start) | collective-permute-done | bytes 196640 | tf_op jit(solution)/shard_map/ppermute | solution.py:468
  15.7 0.7 copy-done.1
  16.4 1.7 %pack_corners.1 = (f32[16,8,128]{2,1,0:T(8,128)}, f32[16,8,128]{2,1,0:T(8,128)}) custom-call(f32[3,16,8,128]{3,2,1,0:T(8,128)} %copy-done.1, f32[3,16,8,128]{3,2,1,0:T(8,128)} %collective-permute-done.1.high_ref), custom_call_target="tpu_custom_call" | custom-call | flops 400000000 | bytes 80000000 | tf_op jit(solution)/shard_map/pack_corners/pallas_call | solution.py:472
  18.1 0.1 collective-permute-start.4
  18.2 5.1 %collective-permute-start.5 = (f32[16,8,128]{2,1,0:T(8,128)}, f32[16,8,128]{2,1,0:T(8,128)S(1)}, u32[]{:S(2)}, u32[]{:S(2)}) collective-permute-start(f32[16,8,128]{2,1,0:T(8,128)} %get-tuple-element.26), channel_id=1, source_target_pairs={{0,31},{1,0},{2,1},{3,2},{4,3},{5,4},{6,5},{7,6},{8,7},{9,8},{10,9... | collective-permute-start | bytes 196616 | tf_op jit(solution)/shard_map/ppermute | solution.py:485
  23.3 0.7 add_convert_fusion.edge_ref
  23.9 1.5 %collective-permute-done.4.top_corner_ref = f32[16,8,128]{2,1,0:T(8,128)S(1)} collective-permute-done((f32[16,8,128]{2,1,0:T(8,128)}, f32[16,8,128]{2,1,0:T(8,128)S(1)}, u32[]{:S(2)}, u32[]{:S(2)}) %collective-permute-start.4) | collective-permute-done | bytes 65568 | tf_op jit(solution)/shard_map/ppermute | solution.py:484
  25.4 0.1 collective-permute-done.5.bottom_corner_ref
  25.5 0.0 collective-permute-done.2.top_ref
  25.5 0.5 copy-done.16
  26.0 0.1 copy-done.17
  26.1 0.3 copy-done
  26.4 20.2 %render.1 = (f32[13,2,8,128]{3,2,1,0:T(8,128)}, f32[13,2,8,128]{3,2,1,0:T(8,128)}, f32[13,2,8,128]{3,2,1,0:T(8,128)}, f32[10,34,16,128]{3,2,1,0:T(8,128)}, f32[10,33,8,128]{3,2,1,0:T(8,128)}) custom-call(f32[4]{0:T(128)} %add_convert_fusion.edge_ref, s32[16]{0:T(128)} %stack.87.tile_ref, f32[3,4]{1,0:T(4,128)} %colour_ref.3, f32[4]{0:T(128)} %opacity_ref.3, ...), custom_call_target="tpu_custom_call" | custom-call | tf_op jit(solution)/shard_map/render/pallas_call | solution.py:493
  46.6 4.7 %collective-permute-start.6 = (f32[13,2,8,128]{3,2,1,0:T(8,128)}, f32[13,2,8,128]{3,2,1,0:T(8,128)S(1)}, u32[]{:S(2)}, u32[]{:S(2)}) collective-permute-start(f32[13,2,8,128]{3,2,1,0:T(8,128)} %get-tuple-element.27), channel_id=1, source_target_pairs={{0,128},{32,160},{64,192},{96,224},{128,0},{160,32},{192,64},{224,... | collective-permute-start | bytes 319496 | tf_op jit(solution)/shard_map/ppermute | solution.py:550
  51.2 1.4 %collective-permute-start.7 = (f32[13,2,8,128]{3,2,1,0:T(8,128)}, f32[13,2,8,128]{3,2,1,0:T(8,128)S(1)}, u32[]{:S(2)}, u32[]{:S(2)}) collective-permute-start(f32[13,2,8,128]{3,2,1,0:T(8,128)} %get-tuple-element.28), channel_id=1, source_target_pairs={{0,96},{32,128},{64,160},{96,192},{128,224},{160,0},{192,32},{224,... | collective-permute-start | bytes 319496 | tf_op jit(solution)/shard_map/ppermute | solution.py:550
  52.6 3.7 %collective-permute-start.8 = (f32[13,2,8,128]{3,2,1,0:T(8,128)}, f32[13,2,8,128]{3,2,1,0:T(8,128)S(1)}, u32[]{:S(2)}, u32[]{:S(2)}) collective-permute-start(f32[13,2,8,128]{3,2,1,0:T(8,128)} %get-tuple-element.29), channel_id=1, source_target_pairs={{0,160},{32,192},{64,224},{96,0},{128,32},{160,64},{192,96},{224,1... | collective-permute-start | bytes 319496 | tf_op jit(solution)/shard_map/ppermute | solution.py:550
  56.3 7.8 %render_rest.1 = (f32[13,2,8,128]{3,2,1,0:T(8,128)}, f32[13,2,8,128]{3,2,1,0:T(8,128)}, f32[13,2,8,128]{3,2,1,0:T(8,128)}, f32[13,2,8,128]{3,2,1,0:T(8,128)}, f32[13,2,8,128]{3,2,1,0:T(8,128)}) custom-call(f32[3,4]{1,0:T(4,128)} %colour_ref.3, f32[4]{0:T(128)} %opacity_ref.3, f32[4,3]{1,0:T(4,128)} %dir_ref.3, f32[4,3]{1,0:T(4,128)} %light_ref.3, ...), custom_call_target="tpu_custom_call" | custom-call | flops 50000000 | bytes 20000000 | tf_op jit(solution)/shard_map/render_rest/pallas_call | solution.py:531
  64.1 0.8 collective-permute-start.9
  64.8 3.4 %collective-permute-start.10 = (f32[13,2,8,128]{3,2,1,0:T(8,128)}, f32[13,2,8,128]{3,2,1,0:T(8,128)S(1)}, u32[]{:S(2)}, u32[]{:S(2)}) collective-permute-start(f32[13,2,8,128]{3,2,1,0:T(8,128)} %get-tuple-element.33), channel_id=1, source_target_pairs={{0,192},{32,224},{64,0},{96,32},{128,64},{160,96},{192,128},{224,1... | collective-permute-start | bytes 319496 | tf_op jit(solution)/shard_map/ppermute | solution.py:550
  68.3 0.3 collective-permute-start.11
  68.5 0.0 collective-permute-done.7.refs_1_
  68.5 3.0 %collective-permute-start.12 = (f32[13,2,8,128]{3,2,1,0:T(8,128)}, f32[13,2,8,128]{3,2,1,0:T(8,128)S(1)}, u32[]{:S(2)}, u32[]{:S(2)}) collective-permute-start(f32[13,2,8,128]{3,2,1,0:T(8,128)} %get-tuple-element.35), channel_id=1, source_target_pairs={{0,224},{32,0},{64,32},{96,64},{128,96},{160,128},{192,160},{224,1... | collective-permute-start | bytes 319496 | tf_op jit(solution)/shard_map/ppermute | solution.py:550
  71.5 0.0 collective-permute-done.8.refs_2_
  71.5 0.5 collective-permute-done.9.refs_3_
  72.0 0.0 collective-permute-done.10.refs_4_
  72.0 2.4 %collective-permute-done.11.refs_5_ = f32[13,2,8,128]{3,2,1,0:T(8,128)S(1)} collective-permute-done((f32[13,2,8,128]{3,2,1,0:T(8,128)}, f32[13,2,8,128]{3,2,1,0:T(8,128)S(1)}, u32[]{:S(2)}, u32[]{:S(2)}) %collective-permute-start.11) | collective-permute-done | bytes 106528 | tf_op jit(solution)/shard_map/ppermute | solution.py:550
  74.5 0.6 copy-done.9
  75.1 0.1 copy-done.11
  75.1 2.0 %fold.1.refs_0_ = f32[13,2,8,128]{3,2,1,0:T(8,128)} custom-call(s32[1]{0:T(128)} %bitcast.place_ref, f32[13,2,8,128]{3,2,1,0:T(8,128)} %copy-done.2, f32[13,2,8,128]{3,2,1,0:T(8,128)} %copy-done.3, f32[13,2,8,128]{3,2,1,0:T(8,128)} %copy-done.4, f32[13,2,8,128]{3,2,1,0:T(8,128)} %copy-done.5, f32[13,2,8,128]{3,2,1,0:T(8,128)} %copy-done.6, ...), custom_call_target="tpu_custom_call" | custom-call | tf_op jit(solution)/shard_map/fold/pallas_call | solution.py:553
  77.1 2.2 %collective-permute-start.15 = (f32[13,2,8,128]{3,2,1,0:T(8,128)}, f32[13,2,8,128]{3,2,1,0:T(8,128)S(1)}, u32[]{:S(2)}, u32[]{:S(2)}) collective-permute-start(f32[13,2,8,128]{3,2,1,0:T(8,128)} %fold.1.refs_0_), channel_id=1, source_target_pairs={{0,192},{32,224},{64,0},{96,32},{128,64},{160,96},{192,128},{224,1... | collective-permute-start | bytes 319496 | tf_op jit(solution)/shard_map/ppermute | solution.py:564
  79.3 0.8 collective-permute-start.13
  80.1 4.7 %collective-permute-start.19 = (f32[13,2,8,128]{3,2,1,0:T(8,128)}, f32[13,2,8,128]{3,2,1,0:T(8,128)S(1)}, u32[]{:S(2)}, u32[]{:S(2)}) collective-permute-start(f32[13,2,8,128]{3,2,1,0:T(8,128)} %fold.1.refs_0_), channel_id=1, source_target_pairs={{0,224},{32,0},{64,32},{96,64},{128,96},{160,128},{192,160},{224,1... | collective-permute-start | bytes 319496 | tf_op jit(solution)/shard_map/ppermute | solution.py:564
  84.8 3.2 %collective-permute-start.16 = (f32[13,2,8,128]{3,2,1,0:T(8,128)S(1)}, f32[13,2,8,128]{3,2,1,0:T(8,128)S(1)}, u32[]{:S(2)}, u32[]{:S(2)}) collective-permute-start(f32[13,2,8,128]{3,2,1,0:T(8,128)S(1)} %collective-permute-done.15.refs_4_), channel_id=1, source_target_pairs={{0,224},{32,0},{64,32},{96,64},{128,96},{160,128},{192,160},{224,1... | collective-permute-start | bytes 319496 | tf_op jit(solution)/shard_map/ppermute | solution.py:567
  88.1 1.4 %collective-permute-done.13.refs_3_ = f32[13,2,8,128]{3,2,1,0:T(8,128)S(1)} collective-permute-done((f32[13,2,8,128]{3,2,1,0:T(8,128)}, f32[13,2,8,128]{3,2,1,0:T(8,128)S(1)}, u32[]{:S(2)}, u32[]{:S(2)}) %collective-permute-start.13) | collective-permute-done | bytes 106528 | tf_op jit(solution)/shard_map/ppermute | solution.py:564
  89.4 2.6 %collective-permute-start.14 = (f32[13,2,8,128]{3,2,1,0:T(8,128)S(1)}, f32[13,2,8,128]{3,2,1,0:T(8,128)S(1)}, u32[]{:S(2)}, u32[]{:S(2)}) collective-permute-start(f32[13,2,8,128]{3,2,1,0:T(8,128)S(1)} %collective-permute-done.13.refs_3_), channel_id=1, source_target_pairs={{0,32},{32,64},{64,96},{96,128},{128,160},{160,192},{192,224},{224... | collective-permute-start | bytes 319496 | tf_op jit(solution)/shard_map/ppermute | solution.py:567
  92.1 0.6 copy-done.10
  92.7 0.6 copy-done.12
  93.3 1.9 %spread.2.refs_3_ = f32[13,16,8,128]{3,2,1,0:T(8,128)} custom-call(s32[1]{0:T(128)} %bitcast.place_ref, f32[13,2,8,128]{3,2,1,0:T(8,128)} %fold.1.refs_0_, f32[13,2,8,128]{3,2,1,0:T(8,128)} %copy-done.12, f32[13,2,8,128]{3,2,1,0:T(8,128)} %copy-done.10, f32[13,2,8,128]{3,2,1,0:T(8,128)} %copy-done.7, f32[13,2,8,128]{3,2,1,0:T(8,128)} %copy-done.8), custom_call_target="tpu_custom_call" | custom-call | tf_op jit(solution)/shard_map/spread/pallas_call | solution.py:573
  95.3 1.6 %collective-permute-done.17.refs_2_ = f32[13,2,8,128]{3,2,1,0:T(8,128)S(1)} collective-permute-done((f32[13,2,8,128]{3,2,1,0:T(8,128)S(1)}, f32[13,2,8,128]{3,2,1,0:T(8,128)S(1)}, u32[]{:S(2)}, u32[]{:S(2)}) %collective-permute-start.17) | collective-permute-done | bytes 106528 | tf_op jit(solution)/shard_map/ppermute | solution.py:567
  96.9 2.2 %collective-permute-done.14.refs_0_ = f32[13,2,8,128]{3,2,1,0:T(8,128)S(1)} collective-permute-done((f32[13,2,8,128]{3,2,1,0:T(8,128)S(1)}, f32[13,2,8,128]{3,2,1,0:T(8,128)S(1)}, u32[]{:S(2)}, u32[]{:S(2)}) %collective-permute-start.14) | collective-permute-done | bytes 106528 | tf_op jit(solution)/shard_map/ppermute | solution.py:567
  99.1 0.6 copy-done.15
  99.8 1.7 %spread.3 = f32[13,16,8,128]{3,2,1,0:T(8,128)} custom-call(s32[1]{0:T(128)} %bitcast.place_ref, f32[13,2,8,128]{3,2,1,0:T(8,128)} %copy-done.15, f32[13,2,8,128]{3,2,1,0:T(8,128)} %copy-done.13, f32[13,2,8,128]{3,2,1,0:T(8,128)} %copy-done.14, f32[13,16,8,128]{3,2,1,0:T(8,128)} %spread.2.refs_3_), custom_call_target="tpu_custom_call", output_to_operand_aliasing={{}: (4, {})} | custom-call | tf_op jit(solution)/shard_map/spread/pallas_call | solution.py:573
  (37 shorter events, 0.1 us)
Async XLA Ops:
  2.6 22.9 %collective-permute-start.2 = (f32[16,96,128]{2,1,0:T(8,128)}, f32[16,96,128]{2,1,0:T(8,128)S(1)}, u32[]{:S(2)}, u32[]{:S(2)}) collective-permute-start(f32[16,96,128]{2,1,0:T(8,128)} %get-tuple-element.23), channel_id=1, source_target_pairs={{0,1},{1,2},{2,3},{3,4},{4,5},{5,6},{6,7},{7,8},{8,9},{9,10},{10,1... | collective-permute-start | bytes 2359304 | tf_op jit(solution)/shard_map/ppermute | solution.py:470
  2.7 22.8 %collective-permute-start.3 = (f32[16,96,128]{2,1,0:T(8,128)}, f32[16,96,128]{2,1,0:T(8,128)}, u32[]{:S(2)}, u32[]{:S(2)}) collective-permute-start(f32[16,96,128]{2,1,0:T(8,128)} %get-tuple-element.24), channel_id=1, source_target_pairs={{0,31},{1,0},{2,1},{3,2},{4,3},{5,4},{6,5},{7,6},{8,7},{9,8},{10,9... | collective-permute-start | bytes 2359304 | tf_op jit(solution)/shard_map/ppermute | solution.py:471
  7.7 8.0 %collective-permute-start = (f32[3,16,8,128]{3,2,1,0:T(8,128)}, f32[3,16,8,128]{3,2,1,0:T(8,128)S(1)}, u32[]{:S(2)}, u32[]{:S(2)}) collective-permute-start(f32[3,16,8,128]{3,2,1,0:T(8,128)} %get-tuple-element.21), channel_id=1, source_target_pairs={{0,32},{32,64},{64,96},{96,128},{128,160},{160,192},{192,224},{224... | collective-permute-start | bytes 589832 | tf_op jit(solution)/shard_map/ppermute | solution.py:468
  7.9 7.8 %collective-permute-start.1 = (f32[3,16,8,128]{3,2,1,0:T(8,128)}, f32[3,16,8,128]{3,2,1,0:T(8,128)}, u32[]{:S(2)}, u32[]{:S(2)}) collective-permute-start(f32[3,16,8,128]{3,2,1,0:T(8,128)} %get-tuple-element.22), channel_id=1, source_target_pairs={{0,224},{32,0},{64,32},{96,64},{128,96},{160,128},{192,160},{224,1... | collective-permute-start | bytes 589832 | tf_op jit(solution)/shard_map/ppermute | solution.py:469
  15.7 0.7 copy-start.1
  18.1 7.3 %collective-permute-start.4 = (f32[16,8,128]{2,1,0:T(8,128)}, f32[16,8,128]{2,1,0:T(8,128)S(1)}, u32[]{:S(2)}, u32[]{:S(2)}) collective-permute-start(f32[16,8,128]{2,1,0:T(8,128)} %get-tuple-element.25), channel_id=1, source_target_pairs={{0,1},{1,2},{2,3},{3,4},{4,5},{5,6},{6,7},{7,8},{8,9},{9,10},{10,1... | collective-permute-start | bytes 196616 | tf_op jit(solution)/shard_map/ppermute | solution.py:484
  18.2 7.3 %collective-permute-start.5 = (f32[16,8,128]{2,1,0:T(8,128)}, f32[16,8,128]{2,1,0:T(8,128)S(1)}, u32[]{:S(2)}, u32[]{:S(2)}) collective-permute-start(f32[16,8,128]{2,1,0:T(8,128)} %get-tuple-element.26), channel_id=1, source_target_pairs={{0,31},{1,0},{2,1},{3,2},{4,3},{5,4},{6,5},{7,6},{8,7},{9,8},{10,9... | collective-permute-start | bytes 196616 | tf_op jit(solution)/shard_map/ppermute | solution.py:485
  25.4 0.6 copy-start.16
  25.5 0.6 copy-start.17
  25.5 0.9 copy-start
  46.6 21.7 %collective-permute-start.6 = (f32[13,2,8,128]{3,2,1,0:T(8,128)}, f32[13,2,8,128]{3,2,1,0:T(8,128)S(1)}, u32[]{:S(2)}, u32[]{:S(2)}) collective-permute-start(f32[13,2,8,128]{3,2,1,0:T(8,128)} %get-tuple-element.27), channel_id=1, source_target_pairs={{0,128},{32,160},{64,192},{96,224},{128,0},{160,32},{192,64},{224,... | collective-permute-start | bytes 319496 | tf_op jit(solution)/shard_map/ppermute | solution.py:550
  51.2 17.3 %collective-permute-start.7 = (f32[13,2,8,128]{3,2,1,0:T(8,128)}, f32[13,2,8,128]{3,2,1,0:T(8,128)S(1)}, u32[]{:S(2)}, u32[]{:S(2)}) collective-permute-start(f32[13,2,8,128]{3,2,1,0:T(8,128)} %get-tuple-element.28), channel_id=1, source_target_pairs={{0,96},{32,128},{64,160},{96,192},{128,224},{160,0},{192,32},{224,... | collective-permute-start | bytes 319496 | tf_op jit(solution)/shard_map/ppermute | solution.py:550
  52.6 19.0 %collective-permute-start.8 = (f32[13,2,8,128]{3,2,1,0:T(8,128)}, f32[13,2,8,128]{3,2,1,0:T(8,128)S(1)}, u32[]{:S(2)}, u32[]{:S(2)}) collective-permute-start(f32[13,2,8,128]{3,2,1,0:T(8,128)} %get-tuple-element.29), channel_id=1, source_target_pairs={{0,160},{32,192},{64,224},{96,0},{128,32},{160,64},{192,96},{224,1... | collective-permute-start | bytes 319496 | tf_op jit(solution)/shard_map/ppermute | solution.py:550
  64.1 7.9 %collective-permute-start.9 = (f32[13,2,8,128]{3,2,1,0:T(8,128)}, f32[13,2,8,128]{3,2,1,0:T(8,128)S(1)}, u32[]{:S(2)}, u32[]{:S(2)}) collective-permute-start(f32[13,2,8,128]{3,2,1,0:T(8,128)} %get-tuple-element.32), channel_id=1, source_target_pairs={{0,64},{32,96},{64,128},{96,160},{128,192},{160,224},{192,0},{224,... | collective-permute-start | bytes 319496 | tf_op jit(solution)/shard_map/ppermute | solution.py:550
  64.8 7.2 %collective-permute-start.10 = (f32[13,2,8,128]{3,2,1,0:T(8,128)}, f32[13,2,8,128]{3,2,1,0:T(8,128)S(1)}, u32[]{:S(2)}, u32[]{:S(2)}) collective-permute-start(f32[13,2,8,128]{3,2,1,0:T(8,128)} %get-tuple-element.33), channel_id=1, source_target_pairs={{0,192},{32,224},{64,0},{96,32},{128,64},{160,96},{192,128},{224,1... | collective-permute-start | bytes 319496 | tf_op jit(solution)/shard_map/ppermute | solution.py:550
  68.3 6.1 %copy-start.2 = (f32[13,2,8,128]{3,2,1,0:T(8,128)}, f32[13,2,8,128]{3,2,1,0:T(8,128)S(1)}, u32[]{:S(2)}) copy-start(f32[13,2,8,128]{3,2,1,0:T(8,128)S(1)} %collective-permute-done.6.refs_0_) | copy-start | bytes 319492
  68.3 6.1 %collective-permute-start.11 = (f32[13,2,8,128]{3,2,1,0:T(8,128)}, f32[13,2,8,128]{3,2,1,0:T(8,128)S(1)}, u32[]{:S(2)}, u32[]{:S(2)}) collective-permute-start(f32[13,2,8,128]{3,2,1,0:T(8,128)} %get-tuple-element.34), channel_id=1, source_target_pairs={{0,32},{32,64},{64,96},{96,128},{128,160},{160,192},{192,224},{224... | collective-permute-start | bytes 319496 | tf_op jit(solution)/shard_map/ppermute | solution.py:550
  68.5 5.9 %copy-start.3 = (f32[13,2,8,128]{3,2,1,0:T(8,128)}, f32[13,2,8,128]{3,2,1,0:T(8,128)S(1)}, u32[]{:S(2)}) copy-start(f32[13,2,8,128]{3,2,1,0:T(8,128)S(1)} %collective-permute-done.7.refs_1_) | copy-start | bytes 319492
  68.5 5.9 %collective-permute-start.12 = (f32[13,2,8,128]{3,2,1,0:T(8,128)}, f32[13,2,8,128]{3,2,1,0:T(8,128)S(1)}, u32[]{:S(2)}, u32[]{:S(2)}) collective-permute-start(f32[13,2,8,128]{3,2,1,0:T(8,128)} %get-tuple-element.35), channel_id=1, source_target_pairs={{0,224},{32,0},{64,32},{96,64},{128,96},{160,128},{192,160},{224,1... | collective-permute-start | bytes 319496 | tf_op jit(solution)/shard_map/ppermute | solution.py:550
  71.5 2.9 %copy-start.4 = (f32[13,2,8,128]{3,2,1,0:T(8,128)}, f32[13,2,8,128]{3,2,1,0:T(8,128)S(1)}, u32[]{:S(2)}) copy-start(f32[13,2,8,128]{3,2,1,0:T(8,128)S(1)} %collective-permute-done.8.refs_2_) | copy-start | bytes 319492
  72.0 2.5 %copy-start.5 = (f32[13,2,8,128]{3,2,1,0:T(8,128)}, f32[13,2,8,128]{3,2,1,0:T(8,128)S(1)}, u32[]{:S(2)}) copy-start(f32[13,2,8,128]{3,2,1,0:T(8,128)S(1)} %collective-permute-done.9.refs_3_) | copy-start | bytes 319492
  72.0 2.5 %copy-start.6 = (f32[13,2,8,128]{3,2,1,0:T(8,128)}, f32[13,2,8,128]{3,2,1,0:T(8,128)S(1)}, u32[]{:S(2)}) copy-start(f32[13,2,8,128]{3,2,1,0:T(8,128)S(1)} %collective-permute-done.10.refs_4_) | copy-start | bytes 319492
  74.4 0.7 copy-start.9
  74.4 0.7 copy-start.11
  77.1 7.7 %collective-permute-start.15 = (f32[13,2,8,128]{3,2,1,0:T(8,128)}, f32[13,2,8,128]{3,2,1,0:T(8,128)S(1)}, u32[]{:S(2)}, u32[]{:S(2)}) collective-permute-start(f32[13,2,8,128]{3,2,1,0:T(8,128)} %fold.1.refs_0_), channel_id=1, source_target_pairs={{0,192},{32,224},{64,0},{96,32},{128,64},{160,96},{192,128},{224,1... | collective-permute-start | bytes 319496 | tf_op jit(solution)/shard_map/ppermute | solution.py:564
  79.3 10.1 %collective-permute-start.13 = (f32[13,2,8,128]{3,2,1,0:T(8,128)}, f32[13,2,8,128]{3,2,1,0:T(8,128)S(1)}, u32[]{:S(2)}, u32[]{:S(2)}) collective-permute-start(f32[13,2,8,128]{3,2,1,0:T(8,128)} %fold.1.refs_0_), channel_id=1, source_target_pairs={{0,64},{32,96},{64,128},{96,160},{128,192},{160,224},{192,0},{224,... | collective-permute-start | bytes 319496 | tf_op jit(solution)/shard_map/ppermute | solution.py:564
  80.1 11.9 %collective-permute-start.19 = (f32[13,2,8,128]{3,2,1,0:T(8,128)}, f32[13,2,8,128]{3,2,1,0:T(8,128)S(1)}, u32[]{:S(2)}, u32[]{:S(2)}) collective-permute-start(f32[13,2,8,128]{3,2,1,0:T(8,128)} %fold.1.refs_0_), channel_id=1, source_target_pairs={{0,224},{32,0},{64,32},{96,64},{128,96},{160,128},{192,160},{224,1... | collective-permute-start | bytes 319496 | tf_op jit(solution)/shard_map/ppermute | solution.py:564
  84.8 7.2 %collective-permute-start.18 = (f32[13,2,8,128]{3,2,1,0:T(8,128)}, f32[13,2,8,128]{3,2,1,0:T(8,128)S(1)}, u32[]{:S(2)}, u32[]{:S(2)}) collective-permute-start(f32[13,2,8,128]{3,2,1,0:T(8,128)} %fold.1.refs_0_), channel_id=1, source_target_pairs={{0,32},{32,64},{64,96},{96,128},{128,160},{160,192},{192,224},{224... | collective-permute-start | bytes 319496 | tf_op jit(solution)/shard_map/ppermute | solution.py:564
  84.8 7.2 %copy-start.8 = (f32[13,2,8,128]{3,2,1,0:T(8,128)}, f32[13,2,8,128]{3,2,1,0:T(8,128)S(1)}, u32[]{:S(2)}) copy-start(f32[13,2,8,128]{3,2,1,0:T(8,128)S(1)} %collective-permute-done.15.refs_4_) | copy-start | bytes 319492
  84.8 10.4 %collective-permute-start.16 = (f32[13,2,8,128]{3,2,1,0:T(8,128)S(1)}, f32[13,2,8,128]{3,2,1,0:T(8,128)S(1)}, u32[]{:S(2)}, u32[]{:S(2)}) collective-permute-start(f32[13,2,8,128]{3,2,1,0:T(8,128)S(1)} %collective-permute-done.15.refs_4_), channel_id=1, source_target_pairs={{0,224},{32,0},{64,32},{96,64},{128,96},{160,128},{192,160},{224,1... | collective-permute-start | bytes 319496 | tf_op jit(solution)/shard_map/ppermute | solution.py:567
  89.4 2.6 %copy-start.7 = (f32[13,2,8,128]{3,2,1,0:T(8,128)}, f32[13,2,8,128]{3,2,1,0:T(8,128)S(1)}, u32[]{:S(2)}) copy-start(f32[13,2,8,128]{3,2,1,0:T(8,128)S(1)} %collective-permute-done.13.refs_3_) | copy-start | bytes 319492
  89.4 7.5 %collective-permute-start.17 = (f32[13,2,8,128]{3,2,1,0:T(8,128)S(1)}, f32[13,2,8,128]{3,2,1,0:T(8,128)S(1)}, u32[]{:S(2)}, u32[]{:S(2)}) collective-permute-start(f32[13,2,8,128]{3,2,1,0:T(8,128)S(1)} %collective-permute-done.13.refs_3_), channel_id=1, source_target_pairs={{0,64},{32,96},{64,128},{96,160},{128,192},{160,224},{192,0},{224,... | collective-permute-start | bytes 319496 | tf_op jit(solution)/shard_map/ppermute | solution.py:567
  89.4 9.7 %collective-permute-start.14 = (f32[13,2,8,128]{3,2,1,0:T(8,128)S(1)}, f32[13,2,8,128]{3,2,1,0:T(8,128)S(1)}, u32[]{:S(2)}, u32[]{:S(2)}) collective-permute-start(f32[13,2,8,128]{3,2,1,0:T(8,128)S(1)} %collective-permute-done.13.refs_3_), channel_id=1, source_target_pairs={{0,32},{32,64},{64,96},{96,128},{128,160},{160,192},{192,224},{224... | collective-permute-start | bytes 319496 | tf_op jit(solution)/shard_map/ppermute | solution.py:567
  92.0 0.6 copy-start.10
  92.7 0.6 copy-start.12
  95.3 3.9 %copy-start.13 = (f32[13,2,8,128]{3,2,1,0:T(8,128)}, f32[13,2,8,128]{3,2,1,0:T(8,128)S(1)}, u32[]{:S(2)}) copy-start(f32[13,2,8,128]{3,2,1,0:T(8,128)S(1)} %collective-permute-done.16.refs_1_) | copy-start | bytes 319492
  96.9 2.2 %copy-start.14 = (f32[13,2,8,128]{3,2,1,0:T(8,128)}, f32[13,2,8,128]{3,2,1,0:T(8,128)S(1)}, u32[]{:S(2)}) copy-start(f32[13,2,8,128]{3,2,1,0:T(8,128)S(1)} %collective-permute-done.17.refs_2_) | copy-start | bytes 319492
  99.1 0.6 copy-start.15

commit v8 on v7

--- a/solution.py
+++ b/solution.py
@@ -82,27 +82,33 @@
         down_ref[tile, 6:8, :] = zero
 
 
-def beside(src, base, z, parity, nexts, befores):
+def beside(src, base, z, parity, nexts):
     tiles = src.shape[1]
     lane = lax.broadcasted_iota(jnp.int32, (ROWS, LANES), 1)
     for part in range(2):
         rows = pl.ds(base + 8 * part, 8)
-        now = src[z, 0, rows, :]
-        lowered, raised = pltpu.roll(now, LANES - 1, 1), pltpu.roll(now, 1, 1)
-        earlier = 0.0
+        turned = [pltpu.roll(src[z, tile, rows, :], LANES - 1, 1) for tile in range(tiles)]
         for tile in range(tiles):
-            if tile + 1 < tiles:
-                later = src[z, tile + 1, rows, :]
-                later_lowered = pltpu.roll(later, LANES - 1, 1)
-                later_raised = pltpu.roll(later, 1, 1)
-            else:
-                later_lowered, later_raised = 0.0, None
-            nexts[parity, tile, part] = jnp.where(lane == LANES - 1, later_lowered, lowered)
-            befores[parity, tile, part] = jnp.where(lane == 0, earlier, raised)
-            earlier, lowered, raised = raised, later_lowered, later_raised
-
-
-def diffuse_plane(src, base, z, parity, nexts, befores, held, dst, out, rims):
+            later = turned[tile + 1] if tile + 1 < tiles else 0.0
+            nexts[parity, tile, part] = jnp.where(lane == LANES - 1, later, turned[tile])
+
+
+def width_flux(src, base, z, parity, nexts, nets):
+    tiles = src.shape[1]
+    lane = lax.broadcasted_iota(jnp.int32, (ROWS, LANES), 1)
+    for part in range(2):
+        rows = pl.ds(base + 8 * part, 8)
+        earlier = None
+        for tile in range(tiles):
+            u = src[z, tile, rows, :]
+            across = flux(nexts[parity, tile, part] - u)
+            turned = pltpu.roll(across, 1, 1)
+            behind = flux(u) if earlier is None else earlier
+            nets[parity, tile, part] = across - jnp.where(lane == 0, behind, turned)
+            earlier = turned
+
+
+def diffuse_plane(src, base, z, parity, nets, held, dst, out, rims):
     tiles = src.shape[1]
     sub = lax.broadcasted_iota(jnp.int32, (ROWS, LANES), 0)
     for tile in range(tiles):
@@ -110,7 +116,6 @@
         for part in range(2):
             first = base + 8 * part
             u = src[z, tile, pl.ds(first, 8), :]
-            across = flux(nexts[parity, tile, part] - u) + flux(befores[parity, tile, part] - u)
             if first + 9 <= src.shape[2]:
                 above = src[z, tile, pl.ds(first + 1, 8), :]
             else:
@@ -120,7 +125,7 @@
             along = up - (turned if part == 0 else jnp.where(sub == 0, below, turned))
             below = turned
             ahead = flux(src[z + 1, tile, pl.ds(first, 8), :] - u)
-            total = (across + along) + (ahead - held[tile, part])
+            total = (nets[parity, tile, part] + along) + (ahead - held[tile, part])
             held[tile, part] = ahead
             dst[out, tile, pl.ds(8 * part, 8), :] = (u + 0.12 * total) * rims[part]
 
@@ -144,18 +149,21 @@
         earlier, lowered, raised = raised, later_lowered, later_raised
 
 
-def diffuse(src, base, dst, planes, nexts, befores, held, rims, slope=None):
+def diffuse(src, base, dst, planes, nexts, nets, held, rims, slope=None):
     for tile in range(src.shape[1]):
         for part in range(2):
             rows = pl.ds(base + 8 * part, 8)
             held[tile, part] = flux(src[1, tile, rows, :] - src[0, tile, rows, :])
-    beside(src, base, 1, 1, nexts, befores)
+    beside(src, base, 1, 1, nexts)
+    width_flux(src, base, 1, 1, nexts, nets)
+    beside(src, base, 2, 0, nexts)
 
     def pair(g, carry):
         for k in range(2):
             z = 2 * g + k + 1
-            beside(src, base, z + 1, k, nexts, befores)
-            diffuse_plane(src, base, z, 1 - k, nexts, befores, held, dst, z - 1, rims)
+            beside(src, base, jnp.minimum(z + 2, planes + 1), 1 - k, nexts)
+            width_flux(src, base, z + 1, k, nexts, nets)
+            diffuse_plane(src, base, z, 1 - k, nets, held, dst, z - 1, rims)
             if slope is not None:
                 width_slope(dst, jnp.maximum(z - 3, 0), slope)
         return carry
@@ -187,7 +195,7 @@
     alpha_top,
 ):
     out_refs, twice_ref, slope_ref = refs[:FAR], refs[FAR], refs[FAR + 1]
-    (field, once, twice, slope, nexts, befores, held, rows_in, corners_in, images) = refs[FAR + 2 : -3]
+    (field, once, twice, slope, nexts, nets, held, rows_in, corners_in, images) = refs[FAR + 2 : -3]
     sem, later_sem, out_sem = refs[-3:]
     cells, tiles = vol_ref.shape[0], vol_ref.shape[1]
     own = pl.ds(BAND, 8)
@@ -251,13 +259,13 @@
     lax.fori_loop(0, cells // 8, rims_in, 0)
     copies[6].wait()
 
-    diffuse(field, OWN, once, cells + 4, nexts, befores, held, rims)
+    diffuse(field, OWN, once, cells + 4, nexts, nets, held, rims)
     for k in range(2):
         for tile in range(tiles):
             for rows in (slice(0, 8), slice(8, 16)):
                 once[k, tile, rows, :] = once[k, tile, rows, :] * keep_low
                 once[cells + 2 + k, tile, rows, :] = once[cells + 2 + k, tile, rows, :] * keep_high
-    diffuse(once, 0, twice, cells + 2, nexts, befores, held, rims, slope)
+    diffuse(once, 0, twice, cells + 2, nexts, nets, held, rims, slope)
     own = pl.ds(OWN, 8)
     for tile in range(tiles):
         twice[0, tile, own, :] = twice[0, tile, own, :] * keep_low
@@ -405,8 +413,9 @@
             out_ref[ch, tile] = total[ch]
 
 
-def spread(count, offsets, place_ref, *refs):
-    pieces, out_ref, sem = refs[: len(offsets)], refs[-2], refs[-1]
+def spread(offsets, place_ref, *refs):
+    pieces, out_ref, sem = refs[:-2], refs[-2], refs[-1]
+    count = len(pieces)
     tiles = out_ref.shape[1] // count
     copies = []
     for i, ref in enumerate(pieces):
@@ -562,30 +571,17 @@
     known = {0: own}
     for by in (1, -1, 2, -2):
         known[by] = lax.ppermute(own, "depth", ring("depth", by))
-    early = list(known)
     for held, by in ((2, 1), (-2, -1), (2, 2)):
         known[held + by] = lax.ppermute(known[held], "depth", ring("depth", by))
-    late = [by for by in known if by not in early]
-    image = []
-    for offsets in (early, late):
-        aliases = {1 + len(offsets): 0} if image else {}
-        image = [
-            pl.pallas_call(
-                functools.partial(spread, slabs, offsets),
-                out_shape=shape(13, tiles, rows, LANES),
-                in_specs=in_smem(1) + in_vmem(len(offsets)) + anywhere(len(image)),
-                out_specs=pl.BlockSpec(memory_space=pl.ANY),
-                scratch_shapes=[DMA((len(offsets),))],
-                input_output_aliases=aliases,
-                compiler_params=limit,
-                name="spread",
-            )(
-                slab[None],
-                *[known[by] for by in offsets],
-                *image,
-            )
-        ]
-    (image,) = image
+    image = pl.pallas_call(
+        functools.partial(spread, list(known)),
+        out_shape=shape(13, tiles, rows, LANES),
+        in_specs=in_smem(1) + anywhere(slabs),
+        out_specs=pl.BlockSpec(memory_space=VMEM),
+        scratch_shapes=[DMA((slabs,))],
+        compiler_params=limit,
+        name="spread",
+    )(slab[None], *known.values())
     return image.transpose(0, 2, 1, 3).reshape(13, rows, width)
 
 

time: 103 us -> 101 us (0.981)
  Pallas kernels: 37.9 us -> 34.6 us
  waiting for transfers between devices: 12.8 us -> 16 us
  local copies, waits for them, and re-layouts: 4.85 us -> 3.56 us
    ppermute x3, waiting for transfers between devices: 3.84 us -> 7.04 us  [per_device(): known[held + by] = lax.ppermute(known[held], 'depth', ring('depth', by))]
    pallas_call x1, Pallas kernels: 20.2 us -> 18.4 us  [per_device(): pl.pallas_call(functools.partial(render, alpha_top=alpha_top), out_shape=...]
    pallas_call x2 -> x1, Pallas kernels: 3.66 us -> 2.19 us  [per_device(): pl.pallas_call(functools.partial(spread, list(known)), out_shape=shape(13...]
    unnamed x36, local copies, waits for them, and re-layouts: 4.17 us -> 2.88 us
  transfers between devices with their start and end apart: 20 -> 20, of which waited for: 8 -> 8; matrix products, arithmetic and copies ran while one was open for 1% -> 1% of each run, Pallas kernels for 11% -> 10%
where the time goes in v8:
time: 101 us; the launch traced here: 100 us
  starting transfers between devices  45.1 us (45%)
  Pallas kernels  34.6 us (34%)
  waiting for transfers between devices  16 us (16%)
  local copies, waits for them, and re-layouts  3.56 us (4%)
    pallas_call x1, Pallas kernels, per_device(): pl.pallas_call(functools.partial(render, alpha_top=alpha_top), out_shape=...  18.4 us
    ppermute x7, starting transfers between devices, per_device(): lax.ppermute(value, 'depth', ring('depth', by))  17.1 us
    pallas_call x1, Pallas kernels, per_device(): pl.pallas_call(functools.partial(render_rest, alpha_top=alpha_top), out_s...  7.81 us
    ppermute x4, starting transfers between devices, per_device(): known[by] = lax.ppermute(own, 'depth', ring('depth', by))  7.71 us
    ppermute x3, waiting for transfers between devices, per_device(): known[held + by] = lax.ppermute(known[held], 'depth', ring('depth', by))  7.04 us
    ppermute x3, starting transfers between devices, per_device(): known[held + by] = lax.ppermute(known[held], 'depth', ring('depth', by))  5.85 us
    ppermute x1, starting transfers between devices, per_device(): bottom = lax.ppermute(up, 'height', ring('height', -1))  5.05 us
    ppermute x1, starting transfers between devices, per_device(): bottom_corner = lax.ppermute(corner_up, 'height', ring('height', -1))  5.05 us
  transfers between devices with their start and end apart: 20, of which 8 were waited for; matrix products, arithmetic and copies ran while one was open for 1% of the time, Pallas kernels for 10%

profile of v8, /device:TPU:0, one launch (start us, length us, event | category | flops | bytes accessed | tf_op | source)
XLA Modules:
  0.0 100.3 jit_solution(15444502392510650630)
XLA Ops:
  0.0 2.6 %pack.1 = (f32[16,96,128]{2,1,0:T(8,128)}, f32[16,96,128]{2,1,0:T(8,128)}, f32[3,16,8,128]{3,2,1,0:T(8,128)}, f32[3,16,8,128]{3,2,1,0:T(8,128)}) custom-call(f32[32,16,8,128]{3,2,1,0:T(8,128)} %bitcast.27), custom_call_target="tpu_custom_call" | custom-call | tf_op jit(solution)/shard_map/pack/pallas_call | solution.py:461
  2.6 0.1 collective-permute-start.2
  2.7 5.1 %collective-permute-start.3 = (f32[16,96,128]{2,1,0:T(8,128)}, f32[16,96,128]{2,1,0:T(8,128)}, u32[]{:S(2)}, u32[]{:S(2)}) collective-permute-start(f32[16,96,128]{2,1,0:T(8,128)} %get-tuple-element.24), channel_id=1, source_target_pairs={{0,31},{1,0},{2,1},{3,2},{4,3},{5,4},{6,5},{7,6},{8,7},{9,8},{10,9... | collective-permute-start | bytes 2359304 | tf_op jit(solution)/shard_map/ppermute | solution.py:480
  7.7 0.2 collective-permute-start
  7.9 3.9 %collective-permute-start.1 = (f32[3,16,8,128]{3,2,1,0:T(8,128)}, f32[3,16,8,128]{3,2,1,0:T(8,128)}, u32[]{:S(2)}, u32[]{:S(2)}) collective-permute-start(f32[3,16,8,128]{3,2,1,0:T(8,128)} %get-tuple-element.22), channel_id=1, source_target_pairs={{0,224},{32,0},{64,32},{96,64},{128,96},{160,128},{192,160},{224,1... | collective-permute-start | bytes 589832 | tf_op jit(solution)/shard_map/ppermute | solution.py:478
  11.8 0.7 stack.87.tile_ref
  12.5 3.2 %collective-permute-done.low_ref = f32[3,16,8,128]{3,2,1,0:T(8,128)S(1)} collective-permute-done((f32[3,16,8,128]{3,2,1,0:T(8,128)}, f32[3,16,8,128]{3,2,1,0:T(8,128)S(1)}, u32[]{:S(2)}, u32[]{:S(2)}) %collective-permute-start) | collective-permute-done | bytes 196640 | tf_op jit(solution)/shard_map/ppermute | solution.py:477
  15.7 0.7 copy-done.1
  16.4 1.7 %pack_corners.1 = (f32[16,8,128]{2,1,0:T(8,128)}, f32[16,8,128]{2,1,0:T(8,128)}) custom-call(f32[3,16,8,128]{3,2,1,0:T(8,128)} %copy-done.1, f32[3,16,8,128]{3,2,1,0:T(8,128)} %collective-permute-done.1.high_ref), custom_call_target="tpu_custom_call" | custom-call | flops 400000000 | bytes 80000000 | tf_op jit(solution)/shard_map/pack_corners/pallas_call | solution.py:481
  18.1 0.1 collective-permute-start.4
  18.2 5.1 %collective-permute-start.5 = (f32[16,8,128]{2,1,0:T(8,128)}, f32[16,8,128]{2,1,0:T(8,128)S(1)}, u32[]{:S(2)}, u32[]{:S(2)}) collective-permute-start(f32[16,8,128]{2,1,0:T(8,128)} %get-tuple-element.26), channel_id=1, source_target_pairs={{0,31},{1,0},{2,1},{3,2},{4,3},{5,4},{6,5},{7,6},{8,7},{9,8},{10,9... | collective-permute-start | bytes 196616 | tf_op jit(solution)/shard_map/ppermute | solution.py:494
  23.3 0.7 add_convert_fusion.edge_ref
  23.9 1.5 %collective-permute-done.4.top_corner_ref = f32[16,8,128]{2,1,0:T(8,128)S(1)} collective-permute-done((f32[16,8,128]{2,1,0:T(8,128)}, f32[16,8,128]{2,1,0:T(8,128)S(1)}, u32[]{:S(2)}, u32[]{:S(2)}) %collective-permute-start.4) | collective-permute-done | bytes 65568 | tf_op jit(solution)/shard_map/ppermute | solution.py:493
  25.4 0.1 collective-permute-done.5.bottom_corner_ref
  25.5 0.0 collective-permute-done.2.top_ref
  25.5 0.5 copy-done.16
  26.0 0.1 copy-done.17
  26.1 0.3 copy-done
  26.4 18.4 %render.1 = (f32[13,2,8,128]{3,2,1,0:T(8,128)}, f32[13,2,8,128]{3,2,1,0:T(8,128)}, f32[13,2,8,128]{3,2,1,0:T(8,128)}, f32[10,34,16,128]{3,2,1,0:T(8,128)}, f32[10,33,8,128]{3,2,1,0:T(8,128)}) custom-call(f32[4]{0:T(128)} %add_convert_fusion.edge_ref, s32[16]{0:T(128)} %stack.87.tile_ref, f32[3,4]{1,0:T(4,128)} %colour_ref.3, f32[4]{0:T(128)} %opacity_ref.3, ...), custom_call_target="tpu_custom_call" | custom-call | tf_op jit(solution)/shard_map/render/pallas_call | solution.py:502
  44.8 4.7 %collective-permute-start.6 = (f32[13,2,8,128]{3,2,1,0:T(8,128)}, f32[13,2,8,128]{3,2,1,0:T(8,128)S(1)}, u32[]{:S(2)}, u32[]{:S(2)}) collective-permute-start(f32[13,2,8,128]{3,2,1,0:T(8,128)} %get-tuple-element.27), channel_id=1, source_target_pairs={{0,128},{32,160},{64,192},{96,224},{128,0},{160,32},{192,64},{224,... | collective-permute-start | bytes 319496 | tf_op jit(solution)/shard_map/ppermute | solution.py:559
  49.4 1.4 %collective-permute-start.7 = (f32[13,2,8,128]{3,2,1,0:T(8,128)}, f32[13,2,8,128]{3,2,1,0:T(8,128)S(1)}, u32[]{:S(2)}, u32[]{:S(2)}) collective-permute-start(f32[13,2,8,128]{3,2,1,0:T(8,128)} %get-tuple-element.28), channel_id=1, source_target_pairs={{0,96},{32,128},{64,160},{96,192},{128,224},{160,0},{192,32},{224,... | collective-permute-start | bytes 319496 | tf_op jit(solution)/shard_map/ppermute | solution.py:559
  50.8 3.7 %collective-permute-start.8 = (f32[13,2,8,128]{3,2,1,0:T(8,128)}, f32[13,2,8,128]{3,2,1,0:T(8,128)S(1)}, u32[]{:S(2)}, u32[]{:S(2)}) collective-permute-start(f32[13,2,8,128]{3,2,1,0:T(8,128)} %get-tuple-element.29), channel_id=1, source_target_pairs={{0,160},{32,192},{64,224},{96,0},{128,32},{160,64},{192,96},{224,1... | collective-permute-start | bytes 319496 | tf_op jit(solution)/shard_map/ppermute | solution.py:559
  54.5 7.8 %render_rest.1 = (f32[13,2,8,128]{3,2,1,0:T(8,128)}, f32[13,2,8,128]{3,2,1,0:T(8,128)}, f32[13,2,8,128]{3,2,1,0:T(8,128)}, f32[13,2,8,128]{3,2,1,0:T(8,128)}, f32[13,2,8,128]{3,2,1,0:T(8,128)}) custom-call(f32[3,4]{1,0:T(4,128)} %colour_ref.3, f32[4]{0:T(128)} %opacity_ref.3, f32[4,3]{1,0:T(4,128)} %dir_ref.3, f32[4,3]{1,0:T(4,128)} %light_ref.3, ...), custom_call_target="tpu_custom_call" | custom-call | flops 50000000 | bytes 20000000 | tf_op jit(solution)/shard_map/render_rest/pallas_call | solution.py:540
  62.3 0.8 collective-permute-start.9
  63.1 3.4 %collective-permute-start.10 = (f32[13,2,8,128]{3,2,1,0:T(8,128)}, f32[13,2,8,128]{3,2,1,0:T(8,128)S(1)}, u32[]{:S(2)}, u32[]{:S(2)}) collective-permute-start(f32[13,2,8,128]{3,2,1,0:T(8,128)} %get-tuple-element.33), channel_id=1, source_target_pairs={{0,192},{32,224},{64,0},{96,32},{128,64},{160,96},{192,128},{224,1... | collective-permute-start | bytes 319496 | tf_op jit(solution)/shard_map/ppermute | solution.py:559
  66.5 0.0 collective-permute-done.6.refs_0_
  66.5 0.3 collective-permute-start.11
  66.7 0.0 collective-permute-done.7.refs_1_
  66.8 3.0 %collective-permute-start.12 = (f32[13,2,8,128]{3,2,1,0:T(8,128)}, f32[13,2,8,128]{3,2,1,0:T(8,128)S(1)}, u32[]{:S(2)}, u32[]{:S(2)}) collective-permute-start(f32[13,2,8,128]{3,2,1,0:T(8,128)} %get-tuple-element.35), channel_id=1, source_target_pairs={{0,224},{32,0},{64,32},{96,64},{128,96},{160,128},{192,160},{224,1... | collective-permute-start | bytes 319496 | tf_op jit(solution)/shard_map/ppermute | solution.py:559
  69.7 0.0 collective-permute-done.8.refs_2_
  69.7 0.4 collective-permute-done.9.refs_3_
  70.2 0.0 collective-permute-done.10.refs_4_
  70.2 2.4 %collective-permute-done.11.refs_5_ = f32[13,2,8,128]{3,2,1,0:T(8,128)S(1)} collective-permute-done((f32[13,2,8,128]{3,2,1,0:T(8,128)}, f32[13,2,8,128]{3,2,1,0:T(8,128)S(1)}, u32[]{:S(2)}, u32[]{:S(2)}) %collective-permute-start.11) | collective-permute-done | bytes 106528 | tf_op jit(solution)/shard_map/ppermute | solution.py:559
  72.7 0.6 copy-done.11
  73.3 0.0 copy-done.13
  73.3 2.0 %fold.1.refs_0_ = f32[13,2,8,128]{3,2,1,0:T(8,128)} custom-call(s32[1]{0:T(128)} %bitcast.place_ref, f32[13,2,8,128]{3,2,1,0:T(8,128)} %copy-done.2, f32[13,2,8,128]{3,2,1,0:T(8,128)} %copy-done.3, f32[13,2,8,128]{3,2,1,0:T(8,128)} %copy-done.4, f32[13,2,8,128]{3,2,1,0:T(8,128)} %copy-done.6, f32[13,2,8,128]{3,2,1,0:T(8,128)} %copy-done.8, ...), custom_call_target="tpu_custom_call" | custom-call | tf_op jit(solution)/shard_map/fold/pallas_call | solution.py:562
  75.3 2.2 %collective-permute-start.16 = (f32[13,2,8,128]{3,2,1,0:T(8,128)}, f32[13,2,8,128]{3,2,1,0:T(8,128)S(1)}, u32[]{:S(2)}, u32[]{:S(2)}) collective-permute-start(f32[13,2,8,128]{3,2,1,0:T(8,128)} %fold.1.refs_0_), channel_id=1, source_target_pairs={{0,192},{32,224},{64,0},{96,32},{128,64},{160,96},{192,128},{224,1... | collective-permute-start | bytes 319496 | tf_op jit(solution)/shard_map/ppermute | solution.py:573
  77.6 0.8 collective-permute-start.15
  78.3 4.7 %collective-permute-start.14 = (f32[13,2,8,128]{3,2,1,0:T(8,128)}, f32[13,2,8,128]{3,2,1,0:T(8,128)S(1)}, u32[]{:S(2)}, u32[]{:S(2)}) collective-permute-start(f32[13,2,8,128]{3,2,1,0:T(8,128)} %fold.1.refs_0_), channel_id=1, source_target_pairs={{0,224},{32,0},{64,32},{96,64},{128,96},{160,128},{192,160},{224,1... | collective-permute-start | bytes 319496 | tf_op jit(solution)/shard_map/ppermute | solution.py:573
  83.0 0.0 collective-permute-start.13
  83.0 0.0 collective-permute-done.16.refs_4_
  83.0 3.2 %collective-permute-start.18 = (f32[13,2,8,128]{3,2,1,0:T(8,128)S(1)}, f32[13,2,8,128]{3,2,1,0:T(8,128)S(1)}, u32[]{:S(2)}, u32[]{:S(2)}) collective-permute-start(f32[13,2,8,128]{3,2,1,0:T(8,128)S(1)} %collective-permute-done.16.refs_4_), channel_id=1, source_target_pairs={{0,224},{32,0},{64,32},{96,64},{128,96},{160,128},{192,160},{224,1... | collective-permute-start | bytes 319496 | tf_op jit(solution)/shard_map/ppermute | solution.py:575
  86.3 1.4 %collective-permute-done.15.refs_3_ = f32[13,2,8,128]{3,2,1,0:T(8,128)S(1)} collective-permute-done((f32[13,2,8,128]{3,2,1,0:T(8,128)}, f32[13,2,8,128]{3,2,1,0:T(8,128)S(1)}, u32[]{:S(2)}, u32[]{:S(2)}) %collective-permute-start.15) | collective-permute-done | bytes 106528 | tf_op jit(solution)/shard_map/ppermute | solution.py:573
  87.6 2.6 %collective-permute-start.17 = (f32[13,2,8,128]{3,2,1,0:T(8,128)S(1)}, f32[13,2,8,128]{3,2,1,0:T(8,128)S(1)}, u32[]{:S(2)}, u32[]{:S(2)}) collective-permute-start(f32[13,2,8,128]{3,2,1,0:T(8,128)S(1)} %collective-permute-done.15.refs_3_), channel_id=1, source_target_pairs={{0,32},{32,64},{64,96},{96,128},{128,160},{160,192},{192,224},{224... | collective-permute-start | bytes 319496 | tf_op jit(solution)/shard_map/ppermute | solution.py:575
  90.3 4.8 %collective-permute-done.19.refs_7_ = f32[13,2,8,128]{3,2,1,0:T(8,128)S(1)} collective-permute-done((f32[13,2,8,128]{3,2,1,0:T(8,128)S(1)}, f32[13,2,8,128]{3,2,1,0:T(8,128)S(1)}, u32[]{:S(2)}, u32[]{:S(2)}) %collective-permute-start.19) | collective-permute-done | bytes 106528 | tf_op jit(solution)/shard_map/ppermute | solution.py:575
  95.1 2.2 %collective-permute-done.17.refs_5_ = f32[13,2,8,128]{3,2,1,0:T(8,128)S(1)} collective-permute-done((f32[13,2,8,128]{3,2,1,0:T(8,128)S(1)}, f32[13,2,8,128]{3,2,1,0:T(8,128)S(1)}, u32[]{:S(2)}, u32[]{:S(2)}) %collective-permute-start.17) | collective-permute-done | bytes 106528 | tf_op jit(solution)/shard_map/ppermute | solution.py:575
  97.4 0.6 copy-done.15
  98.0 2.2 %spread.1 = f32[13,16,8,128]{3,2,1,0:T(8,128)} custom-call(s32[1]{0:T(128)} %bitcast.place_ref, f32[13,2,8,128]{3,2,1,0:T(8,128)} %fold.1.refs_0_, f32[13,2,8,128]{3,2,1,0:T(8,128)} %copy-done.10, f32[13,2,8,128]{3,2,1,0:T(8,128)} %copy-done.9, f32[13,2,8,128]{3,2,1,0:T(8,128)} %copy-done.7, f32[13,2,8,128]{3,2,1,0:T(8,128)} %copy-done.5, ...), custom_call_target="tpu_custom_call" | custom-call | tf_op jit(solution)/shard_map/spread/pallas_call | solution.py:576
  (36 shorter events, 0.1 us)
Async XLA Ops:
  2.6 22.9 %collective-permute-start.2 = (f32[16,96,128]{2,1,0:T(8,128)}, f32[16,96,128]{2,1,0:T(8,128)S(1)}, u32[]{:S(2)}, u32[]{:S(2)}) collective-permute-start(f32[16,96,128]{2,1,0:T(8,128)} %get-tuple-element.23), channel_id=1, source_target_pairs={{0,1},{1,2},{2,3},{3,4},{4,5},{5,6},{6,7},{7,8},{8,9},{9,10},{10,1... | collective-permute-start | bytes 2359304 | tf_op jit(solution)/shard_map/ppermute | solution.py:479
  2.7 22.8 %collective-permute-start.3 = (f32[16,96,128]{2,1,0:T(8,128)}, f32[16,96,128]{2,1,0:T(8,128)}, u32[]{:S(2)}, u32[]{:S(2)}) collective-permute-start(f32[16,96,128]{2,1,0:T(8,128)} %get-tuple-element.24), channel_id=1, source_target_pairs={{0,31},{1,0},{2,1},{3,2},{4,3},{5,4},{6,5},{7,6},{8,7},{9,8},{10,9... | collective-permute-start | bytes 2359304 | tf_op jit(solution)/shard_map/ppermute | solution.py:480
  7.7 8.0 %collective-permute-start = (f32[3,16,8,128]{3,2,1,0:T(8,128)}, f32[3,16,8,128]{3,2,1,0:T(8,128)S(1)}, u32[]{:S(2)}, u32[]{:S(2)}) collective-permute-start(f32[3,16,8,128]{3,2,1,0:T(8,128)} %get-tuple-element.21), channel_id=1, source_target_pairs={{0,32},{32,64},{64,96},{96,128},{128,160},{160,192},{192,224},{224... | collective-permute-start | bytes 589832 | tf_op jit(solution)/shard_map/ppermute | solution.py:477
  7.9 7.8 %collective-permute-start.1 = (f32[3,16,8,128]{3,2,1,0:T(8,128)}, f32[3,16,8,128]{3,2,1,0:T(8,128)}, u32[]{:S(2)}, u32[]{:S(2)}) collective-permute-start(f32[3,16,8,128]{3,2,1,0:T(8,128)} %get-tuple-element.22), channel_id=1, source_target_pairs={{0,224},{32,0},{64,32},{96,64},{128,96},{160,128},{192,160},{224,1... | collective-permute-start | bytes 589832 | tf_op jit(solution)/shard_map/ppermute | solution.py:478
  15.7 0.7 copy-start.1
  18.1 7.3 %collective-permute-start.4 = (f32[16,8,128]{2,1,0:T(8,128)}, f32[16,8,128]{2,1,0:T(8,128)S(1)}, u32[]{:S(2)}, u32[]{:S(2)}) collective-permute-start(f32[16,8,128]{2,1,0:T(8,128)} %get-tuple-element.25), channel_id=1, source_target_pairs={{0,1},{1,2},{2,3},{3,4},{4,5},{5,6},{6,7},{7,8},{8,9},{9,10},{10,1... | collective-permute-start | bytes 196616 | tf_op jit(solution)/shard_map/ppermute | solution.py:493
  18.2 7.3 %collective-permute-start.5 = (f32[16,8,128]{2,1,0:T(8,128)}, f32[16,8,128]{2,1,0:T(8,128)S(1)}, u32[]{:S(2)}, u32[]{:S(2)}) collective-permute-start(f32[16,8,128]{2,1,0:T(8,128)} %get-tuple-element.26), channel_id=1, source_target_pairs={{0,31},{1,0},{2,1},{3,2},{4,3},{5,4},{6,5},{7,6},{8,7},{9,8},{10,9... | collective-permute-start | bytes 196616 | tf_op jit(solution)/shard_map/ppermute | solution.py:494
  25.4 0.6 copy-start.16
  25.5 0.6 copy-start.17
  25.5 0.9 copy-start
  44.8 21.7 %collective-permute-start.6 = (f32[13,2,8,128]{3,2,1,0:T(8,128)}, f32[13,2,8,128]{3,2,1,0:T(8,128)S(1)}, u32[]{:S(2)}, u32[]{:S(2)}) collective-permute-start(f32[13,2,8,128]{3,2,1,0:T(8,128)} %get-tuple-element.27), channel_id=1, source_target_pairs={{0,128},{32,160},{64,192},{96,224},{128,0},{160,32},{192,64},{224,... | collective-permute-start | bytes 319496 | tf_op jit(solution)/shard_map/ppermute | solution.py:559
  49.4 17.3 %collective-permute-start.7 = (f32[13,2,8,128]{3,2,1,0:T(8,128)}, f32[13,2,8,128]{3,2,1,0:T(8,128)S(1)}, u32[]{:S(2)}, u32[]{:S(2)}) collective-permute-start(f32[13,2,8,128]{3,2,1,0:T(8,128)} %get-tuple-element.28), channel_id=1, source_target_pairs={{0,96},{32,128},{64,160},{96,192},{128,224},{160,0},{192,32},{224,... | collective-permute-start | bytes 319496 | tf_op jit(solution)/shard_map/ppermute | solution.py:559
  50.8 19.0 %collective-permute-start.8 = (f32[13,2,8,128]{3,2,1,0:T(8,128)}, f32[13,2,8,128]{3,2,1,0:T(8,128)S(1)}, u32[]{:S(2)}, u32[]{:S(2)}) collective-permute-start(f32[13,2,8,128]{3,2,1,0:T(8,128)} %get-tuple-element.29), channel_id=1, source_target_pairs={{0,160},{32,192},{64,224},{96,0},{128,32},{160,64},{192,96},{224,1... | collective-permute-start | bytes 319496 | tf_op jit(solution)/shard_map/ppermute | solution.py:559
  62.3 7.9 %collective-permute-start.9 = (f32[13,2,8,128]{3,2,1,0:T(8,128)}, f32[13,2,8,128]{3,2,1,0:T(8,128)S(1)}, u32[]{:S(2)}, u32[]{:S(2)}) collective-permute-start(f32[13,2,8,128]{3,2,1,0:T(8,128)} %get-tuple-element.32), channel_id=1, source_target_pairs={{0,64},{32,96},{64,128},{96,160},{128,192},{160,224},{192,0},{224,... | collective-permute-start | bytes 319496 | tf_op jit(solution)/shard_map/ppermute | solution.py:559
  63.1 7.2 %collective-permute-start.10 = (f32[13,2,8,128]{3,2,1,0:T(8,128)}, f32[13,2,8,128]{3,2,1,0:T(8,128)S(1)}, u32[]{:S(2)}, u32[]{:S(2)}) collective-permute-start(f32[13,2,8,128]{3,2,1,0:T(8,128)} %get-tuple-element.33), channel_id=1, source_target_pairs={{0,192},{32,224},{64,0},{96,32},{128,64},{160,96},{192,128},{224,1... | collective-permute-start | bytes 319496 | tf_op jit(solution)/shard_map/ppermute | solution.py:559
  66.5 6.1 %copy-start.2 = (f32[13,2,8,128]{3,2,1,0:T(8,128)}, f32[13,2,8,128]{3,2,1,0:T(8,128)S(1)}, u32[]{:S(2)}) copy-start(f32[13,2,8,128]{3,2,1,0:T(8,128)S(1)} %collective-permute-done.6.refs_0_) | copy-start | bytes 319492
  66.5 6.1 %collective-permute-start.11 = (f32[13,2,8,128]{3,2,1,0:T(8,128)}, f32[13,2,8,128]{3,2,1,0:T(8,128)S(1)}, u32[]{:S(2)}, u32[]{:S(2)}) collective-permute-start(f32[13,2,8,128]{3,2,1,0:T(8,128)} %get-tuple-element.34), channel_id=1, source_target_pairs={{0,32},{32,64},{64,96},{96,128},{128,160},{160,192},{192,224},{224... | collective-permute-start | bytes 319496 | tf_op jit(solution)/shard_map/ppermute | solution.py:559
  66.8 5.9 %copy-start.3 = (f32[13,2,8,128]{3,2,1,0:T(8,128)}, f32[13,2,8,128]{3,2,1,0:T(8,128)S(1)}, u32[]{:S(2)}) copy-start(f32[13,2,8,128]{3,2,1,0:T(8,128)S(1)} %collective-permute-done.7.refs_1_) | copy-start | bytes 319492
  66.8 5.9 %collective-permute-start.12 = (f32[13,2,8,128]{3,2,1,0:T(8,128)}, f32[13,2,8,128]{3,2,1,0:T(8,128)S(1)}, u32[]{:S(2)}, u32[]{:S(2)}) collective-permute-start(f32[13,2,8,128]{3,2,1,0:T(8,128)} %get-tuple-element.35), channel_id=1, source_target_pairs={{0,224},{32,0},{64,32},{96,64},{128,96},{160,128},{192,160},{224,1... | collective-permute-start | bytes 319496 | tf_op jit(solution)/shard_map/ppermute | solution.py:559
  69.7 2.9 %copy-start.4 = (f32[13,2,8,128]{3,2,1,0:T(8,128)}, f32[13,2,8,128]{3,2,1,0:T(8,128)S(1)}, u32[]{:S(2)}) copy-start(f32[13,2,8,128]{3,2,1,0:T(8,128)S(1)} %collective-permute-done.8.refs_2_) | copy-start | bytes 319492
  70.2 2.5 %copy-start.6 = (f32[13,2,8,128]{3,2,1,0:T(8,128)}, f32[13,2,8,128]{3,2,1,0:T(8,128)S(1)}, u32[]{:S(2)}) copy-start(f32[13,2,8,128]{3,2,1,0:T(8,128)S(1)} %collective-permute-done.9.refs_3_) | copy-start | bytes 319492
  70.2 2.5 %copy-start.8 = (f32[13,2,8,128]{3,2,1,0:T(8,128)}, f32[13,2,8,128]{3,2,1,0:T(8,128)S(1)}, u32[]{:S(2)}) copy-start(f32[13,2,8,128]{3,2,1,0:T(8,128)S(1)} %collective-permute-done.10.refs_4_) | copy-start | bytes 319492
  72.6 0.7 copy-start.11
  72.6 0.7 copy-start.13
  75.3 7.7 %collective-permute-start.16 = (f32[13,2,8,128]{3,2,1,0:T(8,128)}, f32[13,2,8,128]{3,2,1,0:T(8,128)S(1)}, u32[]{:S(2)}, u32[]{:S(2)}) collective-permute-start(f32[13,2,8,128]{3,2,1,0:T(8,128)} %fold.1.refs_0_), channel_id=1, source_target_pairs={{0,192},{32,224},{64,0},{96,32},{128,64},{160,96},{192,128},{224,1... | collective-permute-start | bytes 319496 | tf_op jit(solution)/shard_map/ppermute | solution.py:573
  77.6 10.1 %collective-permute-start.15 = (f32[13,2,8,128]{3,2,1,0:T(8,128)}, f32[13,2,8,128]{3,2,1,0:T(8,128)S(1)}, u32[]{:S(2)}, u32[]{:S(2)}) collective-permute-start(f32[13,2,8,128]{3,2,1,0:T(8,128)} %fold.1.refs_0_), channel_id=1, source_target_pairs={{0,64},{32,96},{64,128},{96,160},{128,192},{160,224},{192,0},{224,... | collective-permute-start | bytes 319496 | tf_op jit(solution)/shard_map/ppermute | solution.py:573
  78.3 11.9 %collective-permute-start.14 = (f32[13,2,8,128]{3,2,1,0:T(8,128)}, f32[13,2,8,128]{3,2,1,0:T(8,128)S(1)}, u32[]{:S(2)}, u32[]{:S(2)}) collective-permute-start(f32[13,2,8,128]{3,2,1,0:T(8,128)} %fold.1.refs_0_), channel_id=1, source_target_pairs={{0,224},{32,0},{64,32},{96,64},{128,96},{160,128},{192,160},{224,1... | collective-permute-start | bytes 319496 | tf_op jit(solution)/shard_map/ppermute | solution.py:573
  83.0 7.2 %collective-permute-start.13 = (f32[13,2,8,128]{3,2,1,0:T(8,128)}, f32[13,2,8,128]{3,2,1,0:T(8,128)S(1)}, u32[]{:S(2)}, u32[]{:S(2)}) collective-permute-start(f32[13,2,8,128]{3,2,1,0:T(8,128)} %fold.1.refs_0_), channel_id=1, source_target_pairs={{0,32},{32,64},{64,96},{96,128},{128,160},{160,192},{192,224},{224... | collective-permute-start | bytes 319496 | tf_op jit(solution)/shard_map/ppermute | solution.py:573
  83.0 14.3 %copy-start.5 = (f32[13,2,8,128]{3,2,1,0:T(8,128)}, f32[13,2,8,128]{3,2,1,0:T(8,128)S(1)}, u32[]{:S(2)}) copy-start(f32[13,2,8,128]{3,2,1,0:T(8,128)S(1)} %collective-permute-done.16.refs_4_) | copy-start | bytes 319492
  83.0 7.2 %collective-permute-start.18 = (f32[13,2,8,128]{3,2,1,0:T(8,128)S(1)}, f32[13,2,8,128]{3,2,1,0:T(8,128)S(1)}, u32[]{:S(2)}, u32[]{:S(2)}) collective-permute-start(f32[13,2,8,128]{3,2,1,0:T(8,128)S(1)} %collective-permute-done.16.refs_4_), channel_id=1, source_target_pairs={{0,224},{32,0},{64,32},{96,64},{128,96},{160,128},{192,160},{224,1... | collective-permute-start | bytes 319496 | tf_op jit(solution)/shard_map/ppermute | solution.py:575
  87.6 9.7 %copy-start.7 = (f32[13,2,8,128]{3,2,1,0:T(8,128)}, f32[13,2,8,128]{3,2,1,0:T(8,128)S(1)}, u32[]{:S(2)}) copy-start(f32[13,2,8,128]{3,2,1,0:T(8,128)S(1)} %collective-permute-done.15.refs_3_) | copy-start | bytes 319492
  87.6 7.5 %collective-permute-start.19 = (f32[13,2,8,128]{3,2,1,0:T(8,128)S(1)}, f32[13,2,8,128]{3,2,1,0:T(8,128)S(1)}, u32[]{:S(2)}, u32[]{:S(2)}) collective-permute-start(f32[13,2,8,128]{3,2,1,0:T(8,128)S(1)} %collective-permute-done.15.refs_3_), channel_id=1, source_target_pairs={{0,64},{32,96},{64,128},{96,160},{128,192},{160,224},{192,0},{224,... | collective-permute-start | bytes 319496 | tf_op jit(solution)/shard_map/ppermute | solution.py:575
  87.6 9.7 %collective-permute-start.17 = (f32[13,2,8,128]{3,2,1,0:T(8,128)S(1)}, f32[13,2,8,128]{3,2,1,0:T(8,128)S(1)}, u32[]{:S(2)}, u32[]{:S(2)}) collective-permute-start(f32[13,2,8,128]{3,2,1,0:T(8,128)S(1)} %collective-permute-done.15.refs_3_), channel_id=1, source_target_pairs={{0,32},{32,64},{64,96},{96,128},{128,160},{160,192},{192,224},{224... | collective-permute-start | bytes 319496 | tf_op jit(solution)/shard_map/ppermute | solution.py:575
  90.2 7.1 %copy-start.9 = (f32[13,2,8,128]{3,2,1,0:T(8,128)}, f32[13,2,8,128]{3,2,1,0:T(8,128)S(1)}, u32[]{:S(2)}) copy-start(f32[13,2,8,128]{3,2,1,0:T(8,128)S(1)} %collective-permute-done.14.refs_2_) | copy-start | bytes 319492
  90.3 7.1 %copy-start.10 = (f32[13,2,8,128]{3,2,1,0:T(8,128)}, f32[13,2,8,128]{3,2,1,0:T(8,128)S(1)}, u32[]{:S(2)}) copy-start(f32[13,2,8,128]{3,2,1,0:T(8,128)S(1)} %collective-permute-done.13.refs_1_) | copy-start | bytes 319492
  90.3 7.1 %copy-start.12 = (f32[13,2,8,128]{3,2,1,0:T(8,128)}, f32[13,2,8,128]{3,2,1,0:T(8,128)S(1)}, u32[]{:S(2)}) copy-start(f32[13,2,8,128]{3,2,1,0:T(8,128)S(1)} %collective-permute-done.18.refs_6_) | copy-start | bytes 319492
  95.1 2.3 %copy-start.14 = (f32[13,2,8,128]{3,2,1,0:T(8,128)}, f32[13,2,8,128]{3,2,1,0:T(8,128)S(1)}, u32[]{:S(2)}) copy-start(f32[13,2,8,128]{3,2,1,0:T(8,128)S(1)} %collective-permute-done.19.refs_7_) | copy-start | bytes 319492
  97.4 0.6 copy-start.15

commit v9 on v8

--- a/solution.py
+++ b/solution.py
@@ -290,8 +290,7 @@
         return slope[z, tile_ref[k]]
 
     coefs = (colour_ref, opacity_ref, dir_ref, light_ref)
-    shade(coefs, cells, ahead, smooth, across, images, alpha_top)
-    send(images, out_refs, out_sem)
+    shade(coefs, cells, ahead, smooth, across, images, out_refs, out_sem, alpha_top)
     for copy in later:
         copy.wait()
 
@@ -321,23 +320,17 @@
         return slope[k, z]
 
     coefs = (colour_ref, opacity_ref, dir_ref, light_ref)
-    shade(coefs, cells, count, smooth, across, images, alpha_top, ready)
-    send(images, out_refs, out_sem)
-
-
-def send(images, out_refs, sem):
-    copies = [
-        pltpu.make_async_copy(images.at[k], ref, sem.at[k]) for k, ref in enumerate(out_refs)
-    ]
-    for copy in copies:
-        copy.start()
-    for copy in copies:
-        copy.wait()
-
-
-def shade(coefs, cells, count, smooth, across, images, alpha_top, ready=None):
+    shade(coefs, cells, count, smooth, across, images, out_refs, out_sem, alpha_top, ready)
+
+
+def shade(
+    coefs, cells, count, smooth, across, images, out_refs, out_sem, alpha_top, ready=None
+):
     colour_ref, opacity_ref, dir_ref, light_ref = coefs
     each = images.shape[2]
+    copies = [
+        pltpu.make_async_copy(images.at[i], ref, out_sem.at[i]) for i, ref in enumerate(out_refs)
+    ]
     zero = jnp.zeros((ROWS, LANES), F32)
     colour = [[colour_ref[c, j] for j in range(4)] for c in range(3)]
     opac = [opacity_ref[j] for j in range(4)]
@@ -387,30 +380,32 @@
                     0.2 * base_sums[c] + sums[3 * l + c]
                 )
         images[k // each, 12, k % each] = 1.0 - through
+        for i, copy in enumerate(copies):
+            pl.when(k == (i + 1) * each - 1)(copy.start)
         return carry
 
     lax.fori_loop(0, count, column, 0)
-
-
-def fold(place_ref, *refs):
-    pieces, (out_ref, parts, sem) = refs[:-3], refs[-3:]
-    slabs, channels = parts.shape[0], parts.shape[1]
-    copies = []
-    for i, ref in enumerate(pieces):
-        slab = lax.rem(place_ref[0] - SHIFTS[i] + slabs, slabs)
-        copies.append(pltpu.make_async_copy(ref, parts.at[slab], sem.at[i]))
-    for copy in copies:
-        copy.start()
     for copy in copies:
         copy.wait()
-    for tile in range(parts.shape[2]):
-        through = 1.0 - parts[0, 12, tile]
-        total = [parts[0, ch, tile] for ch in range(channels)]
-        for slab in range(1, slabs):
-            total = [total[ch] + through * parts[slab, ch, tile] for ch in range(channels)]
-            through = through * (1.0 - parts[slab, 12, tile])
+
+
+def fold(place_ref, *refs):
+    pieces, out_ref = refs[:-1], refs[-1]
+    slabs = len(pieces)
+    channels, tiles = out_ref.shape[0], out_ref.shape[1]
+    owner = [lax.rem(place_ref[0] - by + slabs, slabs) for by in SHIFTS]
+    for tile in range(tiles):
+        through = [1.0 - ref[12, tile] for ref in pieces]
+        weight = []
+        for i in range(slabs):
+            product = None
+            for j in range(slabs):
+                if j != i:
+                    factor = jnp.where(owner[j] < owner[i], through[j], 1.0)
+                    product = factor if product is None else product * factor
+            weight.append(product)
         for ch in range(channels):
-            out_ref[ch, tile] = total[ch]
+            out_ref[ch, tile] = sum(weight[i] * pieces[i][ch, tile] for i in range(slabs))
 
 
 def spread(offsets, place_ref, *refs):
@@ -562,9 +557,8 @@
     own = pl.pallas_call(
         fold,
         out_shape=piece,
-        in_specs=in_smem(1) + anywhere(slabs),
+        in_specs=in_smem(1) + in_vmem(slabs),
         out_specs=pl.BlockSpec(memory_space=VMEM),
-        scratch_shapes=[VMEM((slabs, 13, each, rows, LANES), F32), DMA((slabs,))],
         compiler_params=limit,
         name="fold",
     )(slab[None], *arrived)

time: 101 us -> 101 us (level)
  transfers between devices with their start and end apart: 20 -> 20, of which waited for: 8 -> 8; matrix products, arithmetic and copies ran while one was open for 1% -> 1% of each run, Pallas kernels for 10% -> 9%
where the time goes in v9:
time: 101 us; the launch traced here: 100 us
  starting transfers between devices  45.1 us (45%)
  Pallas kernels  34.5 us (34%)
  waiting for transfers between devices  15.9 us (16%)
  local copies, waits for them, and re-layouts  3.54 us (4%)
    pallas_call x1, Pallas kernels, per_device(): pl.pallas_call(functools.partial(render, alpha_top=alpha_top), out_shape=...  18.3 us
    ppermute x7, starting transfers between devices, per_device(): lax.ppermute(value, 'depth', ring('depth', by))  17.1 us
    ppermute x4, starting transfers between devices, per_device(): known[by] = lax.ppermute(own, 'depth', ring('depth', by))  7.72 us
    pallas_call x1, Pallas kernels, per_device(): pl.pallas_call(functools.partial(render_rest, alpha_top=alpha_top), out_s...  7.71 us
    ppermute x3, waiting for transfers between devices, per_device(): known[held + by] = lax.ppermute(known[held], 'depth', ring('depth', by))  6.99 us
    ppermute x3, starting transfers between devices, per_device(): known[held + by] = lax.ppermute(known[held], 'depth', ring('depth', by))  5.79 us
    ppermute x1, starting transfers between devices, per_device(): bottom = lax.ppermute(up, 'height', ring('height', -1))  5.05 us
    ppermute x1, starting transfers between devices, per_device(): bottom_corner = lax.ppermute(corner_up, 'height', ring('height', -1))  5.05 us
  transfers between devices with their start and end apart: 20, of which 8 were waited for; matrix products, arithmetic and copies ran while one was open for 1% of the time, Pallas kernels for 9%

profile of v9, /device:TPU:0, one launch (start us, length us, event | category | flops | bytes accessed | tf_op | source)
XLA Modules:
  0.0 100.0 jit_solution(10203375950125940374)
XLA Ops:
  0.0 2.6 %pack.1 = (f32[16,96,128]{2,1,0:T(8,128)}, f32[16,96,128]{2,1,0:T(8,128)}, f32[3,16,8,128]{3,2,1,0:T(8,128)}, f32[3,16,8,128]{3,2,1,0:T(8,128)}) custom-call(f32[32,16,8,128]{3,2,1,0:T(8,128)} %bitcast.27), custom_call_target="tpu_custom_call" | custom-call | tf_op jit(solution)/shard_map/pack/pallas_call | solution.py:456
  2.6 0.1 collective-permute-start.2
  2.7 5.1 %collective-permute-start.3 = (f32[16,96,128]{2,1,0:T(8,128)}, f32[16,96,128]{2,1,0:T(8,128)}, u32[]{:S(2)}, u32[]{:S(2)}) collective-permute-start(f32[16,96,128]{2,1,0:T(8,128)} %get-tuple-element.24), channel_id=1, source_target_pairs={{0,31},{1,0},{2,1},{3,2},{4,3},{5,4},{6,5},{7,6},{8,7},{9,8},{10,9... | collective-permute-start | bytes 2359304 | tf_op jit(solution)/shard_map/ppermute | solution.py:475
  7.7 0.2 collective-permute-start
  7.9 3.9 %collective-permute-start.1 = (f32[3,16,8,128]{3,2,1,0:T(8,128)}, f32[3,16,8,128]{3,2,1,0:T(8,128)}, u32[]{:S(2)}, u32[]{:S(2)}) collective-permute-start(f32[3,16,8,128]{3,2,1,0:T(8,128)} %get-tuple-element.22), channel_id=1, source_target_pairs={{0,224},{32,0},{64,32},{96,64},{128,96},{160,128},{192,160},{224,1... | collective-permute-start | bytes 589832 | tf_op jit(solution)/shard_map/ppermute | solution.py:473
  11.8 0.7 stack.87.tile_ref
  12.5 3.2 %collective-permute-done.low_ref = f32[3,16,8,128]{3,2,1,0:T(8,128)S(1)} collective-permute-done((f32[3,16,8,128]{3,2,1,0:T(8,128)}, f32[3,16,8,128]{3,2,1,0:T(8,128)S(1)}, u32[]{:S(2)}, u32[]{:S(2)}) %collective-permute-start) | collective-permute-done | bytes 196640 | tf_op jit(solution)/shard_map/ppermute | solution.py:472
  15.7 0.7 copy-done.1
  16.4 1.7 %pack_corners.1 = (f32[16,8,128]{2,1,0:T(8,128)}, f32[16,8,128]{2,1,0:T(8,128)}) custom-call(f32[3,16,8,128]{3,2,1,0:T(8,128)} %copy-done.1, f32[3,16,8,128]{3,2,1,0:T(8,128)} %collective-permute-done.1.high_ref), custom_call_target="tpu_custom_call" | custom-call | flops 400000000 | bytes 80000000 | tf_op jit(solution)/shard_map/pack_corners/pallas_call | solution.py:476
  18.1 0.1 collective-permute-start.4
  18.2 5.1 %collective-permute-start.5 = (f32[16,8,128]{2,1,0:T(8,128)}, f32[16,8,128]{2,1,0:T(8,128)S(1)}, u32[]{:S(2)}, u32[]{:S(2)}) collective-permute-start(f32[16,8,128]{2,1,0:T(8,128)} %get-tuple-element.26), channel_id=1, source_target_pairs={{0,31},{1,0},{2,1},{3,2},{4,3},{5,4},{6,5},{7,6},{8,7},{9,8},{10,9... | collective-permute-start | bytes 196616 | tf_op jit(solution)/shard_map/ppermute | solution.py:489
  23.3 0.7 add_convert_fusion.edge_ref
  23.9 1.5 %collective-permute-done.4.top_corner_ref = f32[16,8,128]{2,1,0:T(8,128)S(1)} collective-permute-done((f32[16,8,128]{2,1,0:T(8,128)}, f32[16,8,128]{2,1,0:T(8,128)S(1)}, u32[]{:S(2)}, u32[]{:S(2)}) %collective-permute-start.4) | collective-permute-done | bytes 65568 | tf_op jit(solution)/shard_map/ppermute | solution.py:488
  25.4 0.1 collective-permute-done.5.bottom_corner_ref
  25.5 0.0 collective-permute-done.2.top_ref
  25.5 0.5 copy-done.16
  26.0 0.1 copy-done.17
  26.1 0.3 copy-done
  26.4 18.3 %render.1 = (f32[13,2,8,128]{3,2,1,0:T(8,128)}, f32[13,2,8,128]{3,2,1,0:T(8,128)}, f32[13,2,8,128]{3,2,1,0:T(8,128)}, f32[10,34,16,128]{3,2,1,0:T(8,128)}, f32[10,33,8,128]{3,2,1,0:T(8,128)}) custom-call(f32[4]{0:T(128)} %add_convert_fusion.edge_ref, s32[16]{0:T(128)} %stack.87.tile_ref, f32[3,4]{1,0:T(4,128)} %colour_ref.3, f32[4]{0:T(128)} %opacity_ref.3, ...), custom_call_target="tpu_custom_call" | custom-call | tf_op jit(solution)/shard_map/render/pallas_call | solution.py:497
  44.7 4.7 %collective-permute-start.6 = (f32[13,2,8,128]{3,2,1,0:T(8,128)}, f32[13,2,8,128]{3,2,1,0:T(8,128)S(1)}, u32[]{:S(2)}, u32[]{:S(2)}) collective-permute-start(f32[13,2,8,128]{3,2,1,0:T(8,128)} %get-tuple-element.27), channel_id=1, source_target_pairs={{0,128},{32,160},{64,192},{96,224},{128,0},{160,32},{192,64},{224,... | collective-permute-start | bytes 319496 | tf_op jit(solution)/shard_map/ppermute | solution.py:554
  49.4 1.4 %collective-permute-start.7 = (f32[13,2,8,128]{3,2,1,0:T(8,128)}, f32[13,2,8,128]{3,2,1,0:T(8,128)S(1)}, u32[]{:S(2)}, u32[]{:S(2)}) collective-permute-start(f32[13,2,8,128]{3,2,1,0:T(8,128)} %get-tuple-element.28), channel_id=1, source_target_pairs={{0,96},{32,128},{64,160},{96,192},{128,224},{160,0},{192,32},{224,... | collective-permute-start | bytes 319496 | tf_op jit(solution)/shard_map/ppermute | solution.py:554
  50.7 3.7 %collective-permute-start.8 = (f32[13,2,8,128]{3,2,1,0:T(8,128)}, f32[13,2,8,128]{3,2,1,0:T(8,128)S(1)}, u32[]{:S(2)}, u32[]{:S(2)}) collective-permute-start(f32[13,2,8,128]{3,2,1,0:T(8,128)} %get-tuple-element.29), channel_id=1, source_target_pairs={{0,160},{32,192},{64,224},{96,0},{128,32},{160,64},{192,96},{224,1... | collective-permute-start | bytes 319496 | tf_op jit(solution)/shard_map/ppermute | solution.py:554
  54.4 7.7 %render_rest.1 = (f32[13,2,8,128]{3,2,1,0:T(8,128)}, f32[13,2,8,128]{3,2,1,0:T(8,128)}, f32[13,2,8,128]{3,2,1,0:T(8,128)}, f32[13,2,8,128]{3,2,1,0:T(8,128)}, f32[13,2,8,128]{3,2,1,0:T(8,128)}) custom-call(f32[3,4]{1,0:T(4,128)} %colour_ref.3, f32[4]{0:T(128)} %opacity_ref.3, f32[4,3]{1,0:T(4,128)} %dir_ref.3, f32[4,3]{1,0:T(4,128)} %light_ref.3, ...), custom_call_target="tpu_custom_call" | custom-call | flops 50000000 | bytes 20000000 | tf_op jit(solution)/shard_map/render_rest/pallas_call | solution.py:535
  62.1 0.8 collective-permute-start.9
  62.9 3.4 %collective-permute-start.10 = (f32[13,2,8,128]{3,2,1,0:T(8,128)}, f32[13,2,8,128]{3,2,1,0:T(8,128)S(1)}, u32[]{:S(2)}, u32[]{:S(2)}) collective-permute-start(f32[13,2,8,128]{3,2,1,0:T(8,128)} %get-tuple-element.33), channel_id=1, source_target_pairs={{0,192},{32,224},{64,0},{96,32},{128,64},{160,96},{192,128},{224,1... | collective-permute-start | bytes 319496 | tf_op jit(solution)/shard_map/ppermute | solution.py:554
  66.3 0.2 collective-permute-start.11
  66.6 3.0 %collective-permute-start.12 = (f32[13,2,8,128]{3,2,1,0:T(8,128)}, f32[13,2,8,128]{3,2,1,0:T(8,128)S(1)}, u32[]{:S(2)}, u32[]{:S(2)}) collective-permute-start(f32[13,2,8,128]{3,2,1,0:T(8,128)} %get-tuple-element.35), channel_id=1, source_target_pairs={{0,224},{32,0},{64,32},{96,64},{128,96},{160,128},{192,160},{224,1... | collective-permute-start | bytes 319496 | tf_op jit(solution)/shard_map/ppermute | solution.py:554
  69.6 0.0 collective-permute-done.8.refs_2_
  69.6 0.4 collective-permute-done.9.refs_3_
  70.0 0.0 collective-permute-done.10.refs_4_
  70.0 2.4 %collective-permute-done.11.refs_5_ = f32[13,2,8,128]{3,2,1,0:T(8,128)S(1)} collective-permute-done((f32[13,2,8,128]{3,2,1,0:T(8,128)}, f32[13,2,8,128]{3,2,1,0:T(8,128)S(1)}, u32[]{:S(2)}, u32[]{:S(2)}) %collective-permute-start.11) | collective-permute-done | bytes 106528 | tf_op jit(solution)/shard_map/ppermute | solution.py:554
  72.5 0.0 collective-permute-done.12.refs_6_
  72.5 0.6 copy-done.11
  73.1 0.0 copy-done.13
  73.2 2.0 %fold.1.refs_0_ = f32[13,2,8,128]{3,2,1,0:T(8,128)} custom-call(s32[1]{0:T(128)} %bitcast.place_ref, f32[13,2,8,128]{3,2,1,0:T(8,128)} %copy-done.2, f32[13,2,8,128]{3,2,1,0:T(8,128)} %copy-done.3, f32[13,2,8,128]{3,2,1,0:T(8,128)} %copy-done.4, f32[13,2,8,128]{3,2,1,0:T(8,128)} %copy-done.6, f32[13,2,8,128]{3,2,1,0:T(8,128)} %copy-done.8, ...), custom_call_target="tpu_custom_call" | custom-call | tf_op jit(solution)/shard_map/fold/pallas_call | solution.py:557
  75.1 2.2 %collective-permute-start.16 = (f32[13,2,8,128]{3,2,1,0:T(8,128)}, f32[13,2,8,128]{3,2,1,0:T(8,128)S(1)}, u32[]{:S(2)}, u32[]{:S(2)}) collective-permute-start(f32[13,2,8,128]{3,2,1,0:T(8,128)} %fold.1.refs_0_), channel_id=1, source_target_pairs={{0,192},{32,224},{64,0},{96,32},{128,64},{160,96},{192,128},{224,1... | collective-permute-start | bytes 319496 | tf_op jit(solution)/shard_map/ppermute | solution.py:567
  77.3 0.8 collective-permute-start.15
  78.1 4.8 %collective-permute-start.14 = (f32[13,2,8,128]{3,2,1,0:T(8,128)}, f32[13,2,8,128]{3,2,1,0:T(8,128)S(1)}, u32[]{:S(2)}, u32[]{:S(2)}) collective-permute-start(f32[13,2,8,128]{3,2,1,0:T(8,128)} %fold.1.refs_0_), channel_id=1, source_target_pairs={{0,224},{32,0},{64,32},{96,64},{128,96},{160,128},{192,160},{224,1... | collective-permute-start | bytes 319496 | tf_op jit(solution)/shard_map/ppermute | solution.py:567
  82.9 0.0 collective-permute-start.13
  82.9 0.0 collective-permute-done.16.refs_4_
  82.9 3.2 %collective-permute-start.18 = (f32[13,2,8,128]{3,2,1,0:T(8,128)S(1)}, f32[13,2,8,128]{3,2,1,0:T(8,128)S(1)}, u32[]{:S(2)}, u32[]{:S(2)}) collective-permute-start(f32[13,2,8,128]{3,2,1,0:T(8,128)S(1)} %collective-permute-done.16.refs_4_), channel_id=1, source_target_pairs={{0,224},{32,0},{64,32},{96,64},{128,96},{160,128},{192,160},{224,1... | collective-permute-start | bytes 319496 | tf_op jit(solution)/shard_map/ppermute | solution.py:569
  86.1 1.3 %collective-permute-done.15.refs_3_ = f32[13,2,8,128]{3,2,1,0:T(8,128)S(1)} collective-permute-done((f32[13,2,8,128]{3,2,1,0:T(8,128)}, f32[13,2,8,128]{3,2,1,0:T(8,128)S(1)}, u32[]{:S(2)}, u32[]{:S(2)}) %collective-permute-start.15) | collective-permute-done | bytes 106528 | tf_op jit(solution)/shard_map/ppermute | solution.py:567
  87.4 2.6 %collective-permute-start.17 = (f32[13,2,8,128]{3,2,1,0:T(8,128)S(1)}, f32[13,2,8,128]{3,2,1,0:T(8,128)S(1)}, u32[]{:S(2)}, u32[]{:S(2)}) collective-permute-start(f32[13,2,8,128]{3,2,1,0:T(8,128)S(1)} %collective-permute-done.15.refs_3_), channel_id=1, source_target_pairs={{0,32},{32,64},{64,96},{96,128},{128,160},{160,192},{192,224},{224... | collective-permute-start | bytes 319496 | tf_op jit(solution)/shard_map/ppermute | solution.py:569
  89.9 0.0 collective-permute-done.14.refs_2_
  90.0 4.8 %collective-permute-done.19.refs_7_ = f32[13,2,8,128]{3,2,1,0:T(8,128)S(1)} collective-permute-done((f32[13,2,8,128]{3,2,1,0:T(8,128)S(1)}, f32[13,2,8,128]{3,2,1,0:T(8,128)S(1)}, u32[]{:S(2)}, u32[]{:S(2)}) %collective-permute-start.19) | collective-permute-done | bytes 106528 | tf_op jit(solution)/shard_map/ppermute | solution.py:569
  94.7 2.2 %collective-permute-done.17.refs_5_ = f32[13,2,8,128]{3,2,1,0:T(8,128)S(1)} collective-permute-done((f32[13,2,8,128]{3,2,1,0:T(8,128)S(1)}, f32[13,2,8,128]{3,2,1,0:T(8,128)S(1)}, u32[]{:S(2)}, u32[]{:S(2)}) %collective-permute-start.17) | collective-permute-done | bytes 106528 | tf_op jit(solution)/shard_map/ppermute | solution.py:569
  97.0 0.6 copy-done.15
  97.6 2.2 %spread.1 = f32[13,16,8,128]{3,2,1,0:T(8,128)} custom-call(s32[1]{0:T(128)} %bitcast.place_ref, f32[13,2,8,128]{3,2,1,0:T(8,128)} %fold.1.refs_0_, f32[13,2,8,128]{3,2,1,0:T(8,128)} %copy-done.10, f32[13,2,8,128]{3,2,1,0:T(8,128)} %copy-done.9, f32[13,2,8,128]{3,2,1,0:T(8,128)} %copy-done.7, f32[13,2,8,128]{3,2,1,0:T(8,128)} %copy-done.5, ...), custom_call_target="tpu_custom_call" | custom-call | tf_op jit(solution)/shard_map/spread/pallas_call | solution.py:570
  (36 shorter events, 0.1 us)
Async XLA Ops:
  2.6 22.9 %collective-permute-start.2 = (f32[16,96,128]{2,1,0:T(8,128)}, f32[16,96,128]{2,1,0:T(8,128)S(1)}, u32[]{:S(2)}, u32[]{:S(2)}) collective-permute-start(f32[16,96,128]{2,1,0:T(8,128)} %get-tuple-element.23), channel_id=1, source_target_pairs={{0,1},{1,2},{2,3},{3,4},{4,5},{5,6},{6,7},{7,8},{8,9},{9,10},{10,1... | collective-permute-start | bytes 2359304 | tf_op jit(solution)/shard_map/ppermute | solution.py:474
  2.7 22.8 %collective-permute-start.3 = (f32[16,96,128]{2,1,0:T(8,128)}, f32[16,96,128]{2,1,0:T(8,128)}, u32[]{:S(2)}, u32[]{:S(2)}) collective-permute-start(f32[16,96,128]{2,1,0:T(8,128)} %get-tuple-element.24), channel_id=1, source_target_pairs={{0,31},{1,0},{2,1},{3,2},{4,3},{5,4},{6,5},{7,6},{8,7},{9,8},{10,9... | collective-permute-start | bytes 2359304 | tf_op jit(solution)/shard_map/ppermute | solution.py:475
  7.7 8.0 %collective-permute-start = (f32[3,16,8,128]{3,2,1,0:T(8,128)}, f32[3,16,8,128]{3,2,1,0:T(8,128)S(1)}, u32[]{:S(2)}, u32[]{:S(2)}) collective-permute-start(f32[3,16,8,128]{3,2,1,0:T(8,128)} %get-tuple-element.21), channel_id=1, source_target_pairs={{0,32},{32,64},{64,96},{96,128},{128,160},{160,192},{192,224},{224... | collective-permute-start | bytes 589832 | tf_op jit(solution)/shard_map/ppermute | solution.py:472
  7.9 7.8 %collective-permute-start.1 = (f32[3,16,8,128]{3,2,1,0:T(8,128)}, f32[3,16,8,128]{3,2,1,0:T(8,128)}, u32[]{:S(2)}, u32[]{:S(2)}) collective-permute-start(f32[3,16,8,128]{3,2,1,0:T(8,128)} %get-tuple-element.22), channel_id=1, source_target_pairs={{0,224},{32,0},{64,32},{96,64},{128,96},{160,128},{192,160},{224,1... | collective-permute-start | bytes 589832 | tf_op jit(solution)/shard_map/ppermute | solution.py:473
  15.7 0.7 copy-start.1
  18.1 7.3 %collective-permute-start.4 = (f32[16,8,128]{2,1,0:T(8,128)}, f32[16,8,128]{2,1,0:T(8,128)S(1)}, u32[]{:S(2)}, u32[]{:S(2)}) collective-permute-start(f32[16,8,128]{2,1,0:T(8,128)} %get-tuple-element.25), channel_id=1, source_target_pairs={{0,1},{1,2},{2,3},{3,4},{4,5},{5,6},{6,7},{7,8},{8,9},{9,10},{10,1... | collective-permute-start | bytes 196616 | tf_op jit(solution)/shard_map/ppermute | solution.py:488
  18.2 7.3 %collective-permute-start.5 = (f32[16,8,128]{2,1,0:T(8,128)}, f32[16,8,128]{2,1,0:T(8,128)S(1)}, u32[]{:S(2)}, u32[]{:S(2)}) collective-permute-start(f32[16,8,128]{2,1,0:T(8,128)} %get-tuple-element.26), channel_id=1, source_target_pairs={{0,31},{1,0},{2,1},{3,2},{4,3},{5,4},{6,5},{7,6},{8,7},{9,8},{10,9... | collective-permute-start | bytes 196616 | tf_op jit(solution)/shard_map/ppermute | solution.py:489
  25.4 0.6 copy-start.16
  25.5 0.6 copy-start.17
  25.5 0.9 copy-start
  44.7 21.6 %collective-permute-start.6 = (f32[13,2,8,128]{3,2,1,0:T(8,128)}, f32[13,2,8,128]{3,2,1,0:T(8,128)S(1)}, u32[]{:S(2)}, u32[]{:S(2)}) collective-permute-start(f32[13,2,8,128]{3,2,1,0:T(8,128)} %get-tuple-element.27), channel_id=1, source_target_pairs={{0,128},{32,160},{64,192},{96,224},{128,0},{160,32},{192,64},{224,... | collective-permute-start | bytes 319496 | tf_op jit(solution)/shard_map/ppermute | solution.py:554
  49.4 17.2 %collective-permute-start.7 = (f32[13,2,8,128]{3,2,1,0:T(8,128)}, f32[13,2,8,128]{3,2,1,0:T(8,128)S(1)}, u32[]{:S(2)}, u32[]{:S(2)}) collective-permute-start(f32[13,2,8,128]{3,2,1,0:T(8,128)} %get-tuple-element.28), channel_id=1, source_target_pairs={{0,96},{32,128},{64,160},{96,192},{128,224},{160,0},{192,32},{224,... | collective-permute-start | bytes 319496 | tf_op jit(solution)/shard_map/ppermute | solution.py:554
  50.7 18.9 %collective-permute-start.8 = (f32[13,2,8,128]{3,2,1,0:T(8,128)}, f32[13,2,8,128]{3,2,1,0:T(8,128)S(1)}, u32[]{:S(2)}, u32[]{:S(2)}) collective-permute-start(f32[13,2,8,128]{3,2,1,0:T(8,128)} %get-tuple-element.29), channel_id=1, source_target_pairs={{0,160},{32,192},{64,224},{96,0},{128,32},{160,64},{192,96},{224,1... | collective-permute-start | bytes 319496 | tf_op jit(solution)/shard_map/ppermute | solution.py:554
  62.1 7.9 %collective-permute-start.9 = (f32[13,2,8,128]{3,2,1,0:T(8,128)}, f32[13,2,8,128]{3,2,1,0:T(8,128)S(1)}, u32[]{:S(2)}, u32[]{:S(2)}) collective-permute-start(f32[13,2,8,128]{3,2,1,0:T(8,128)} %get-tuple-element.32), channel_id=1, source_target_pairs={{0,64},{32,96},{64,128},{96,160},{128,192},{160,224},{192,0},{224,... | collective-permute-start | bytes 319496 | tf_op jit(solution)/shard_map/ppermute | solution.py:554
  62.9 7.1 %collective-permute-start.10 = (f32[13,2,8,128]{3,2,1,0:T(8,128)}, f32[13,2,8,128]{3,2,1,0:T(8,128)S(1)}, u32[]{:S(2)}, u32[]{:S(2)}) collective-permute-start(f32[13,2,8,128]{3,2,1,0:T(8,128)} %get-tuple-element.33), channel_id=1, source_target_pairs={{0,192},{32,224},{64,0},{96,32},{128,64},{160,96},{192,128},{224,1... | collective-permute-start | bytes 319496 | tf_op jit(solution)/shard_map/ppermute | solution.py:554
  66.3 6.2 %copy-start.2 = (f32[13,2,8,128]{3,2,1,0:T(8,128)}, f32[13,2,8,128]{3,2,1,0:T(8,128)S(1)}, u32[]{:S(2)}) copy-start(f32[13,2,8,128]{3,2,1,0:T(8,128)S(1)} %collective-permute-done.6.refs_0_) | copy-start | bytes 319492
  66.3 6.1 %collective-permute-start.11 = (f32[13,2,8,128]{3,2,1,0:T(8,128)}, f32[13,2,8,128]{3,2,1,0:T(8,128)S(1)}, u32[]{:S(2)}, u32[]{:S(2)}) collective-permute-start(f32[13,2,8,128]{3,2,1,0:T(8,128)} %get-tuple-element.34), channel_id=1, source_target_pairs={{0,32},{32,64},{64,96},{96,128},{128,160},{160,192},{192,224},{224... | collective-permute-start | bytes 319496 | tf_op jit(solution)/shard_map/ppermute | solution.py:554
  66.6 5.9 %copy-start.3 = (f32[13,2,8,128]{3,2,1,0:T(8,128)}, f32[13,2,8,128]{3,2,1,0:T(8,128)S(1)}, u32[]{:S(2)}) copy-start(f32[13,2,8,128]{3,2,1,0:T(8,128)S(1)} %collective-permute-done.7.refs_1_) | copy-start | bytes 319492
  66.6 5.9 %collective-permute-start.12 = (f32[13,2,8,128]{3,2,1,0:T(8,128)}, f32[13,2,8,128]{3,2,1,0:T(8,128)S(1)}, u32[]{:S(2)}, u32[]{:S(2)}) collective-permute-start(f32[13,2,8,128]{3,2,1,0:T(8,128)} %get-tuple-element.35), channel_id=1, source_target_pairs={{0,224},{32,0},{64,32},{96,64},{128,96},{160,128},{192,160},{224,1... | collective-permute-start | bytes 319496 | tf_op jit(solution)/shard_map/ppermute | solution.py:554
  69.6 2.9 %copy-start.4 = (f32[13,2,8,128]{3,2,1,0:T(8,128)}, f32[13,2,8,128]{3,2,1,0:T(8,128)S(1)}, u32[]{:S(2)}) copy-start(f32[13,2,8,128]{3,2,1,0:T(8,128)S(1)} %collective-permute-done.8.refs_2_) | copy-start | bytes 319492
  70.0 2.5 %copy-start.6 = (f32[13,2,8,128]{3,2,1,0:T(8,128)}, f32[13,2,8,128]{3,2,1,0:T(8,128)S(1)}, u32[]{:S(2)}) copy-start(f32[13,2,8,128]{3,2,1,0:T(8,128)S(1)} %collective-permute-done.9.refs_3_) | copy-start | bytes 319492
  70.0 2.5 %copy-start.8 = (f32[13,2,8,128]{3,2,1,0:T(8,128)}, f32[13,2,8,128]{3,2,1,0:T(8,128)S(1)}, u32[]{:S(2)}) copy-start(f32[13,2,8,128]{3,2,1,0:T(8,128)S(1)} %collective-permute-done.10.refs_4_) | copy-start | bytes 319492
  72.5 0.7 copy-start.11
  72.5 0.7 copy-start.13
  75.1 7.7 %collective-permute-start.16 = (f32[13,2,8,128]{3,2,1,0:T(8,128)}, f32[13,2,8,128]{3,2,1,0:T(8,128)S(1)}, u32[]{:S(2)}, u32[]{:S(2)}) collective-permute-start(f32[13,2,8,128]{3,2,1,0:T(8,128)} %fold.1.refs_0_), channel_id=1, source_target_pairs={{0,192},{32,224},{64,0},{96,32},{128,64},{160,96},{192,128},{224,1... | collective-permute-start | bytes 319496 | tf_op jit(solution)/shard_map/ppermute | solution.py:567
  77.3 10.1 %collective-permute-start.15 = (f32[13,2,8,128]{3,2,1,0:T(8,128)}, f32[13,2,8,128]{3,2,1,0:T(8,128)S(1)}, u32[]{:S(2)}, u32[]{:S(2)}) collective-permute-start(f32[13,2,8,128]{3,2,1,0:T(8,128)} %fold.1.refs_0_), channel_id=1, source_target_pairs={{0,64},{32,96},{64,128},{96,160},{128,192},{160,224},{192,0},{224,... | collective-permute-start | bytes 319496 | tf_op jit(solution)/shard_map/ppermute | solution.py:567
  78.1 11.9 %collective-permute-start.14 = (f32[13,2,8,128]{3,2,1,0:T(8,128)}, f32[13,2,8,128]{3,2,1,0:T(8,128)S(1)}, u32[]{:S(2)}, u32[]{:S(2)}) collective-permute-start(f32[13,2,8,128]{3,2,1,0:T(8,128)} %fold.1.refs_0_), channel_id=1, source_target_pairs={{0,224},{32,0},{64,32},{96,64},{128,96},{160,128},{192,160},{224,1... | collective-permute-start | bytes 319496 | tf_op jit(solution)/shard_map/ppermute | solution.py:567
  82.9 7.1 %collective-permute-start.13 = (f32[13,2,8,128]{3,2,1,0:T(8,128)}, f32[13,2,8,128]{3,2,1,0:T(8,128)S(1)}, u32[]{:S(2)}, u32[]{:S(2)}) collective-permute-start(f32[13,2,8,128]{3,2,1,0:T(8,128)} %fold.1.refs_0_), channel_id=1, source_target_pairs={{0,32},{32,64},{64,96},{96,128},{128,160},{160,192},{192,224},{224... | collective-permute-start | bytes 319496 | tf_op jit(solution)/shard_map/ppermute | solution.py:567
  82.9 14.1 %copy-start.5 = (f32[13,2,8,128]{3,2,1,0:T(8,128)}, f32[13,2,8,128]{3,2,1,0:T(8,128)S(1)}, u32[]{:S(2)}) copy-start(f32[13,2,8,128]{3,2,1,0:T(8,128)S(1)} %collective-permute-done.16.refs_4_) | copy-start | bytes 319492
  82.9 7.1 %collective-permute-start.18 = (f32[13,2,8,128]{3,2,1,0:T(8,128)S(1)}, f32[13,2,8,128]{3,2,1,0:T(8,128)S(1)}, u32[]{:S(2)}, u32[]{:S(2)}) collective-permute-start(f32[13,2,8,128]{3,2,1,0:T(8,128)S(1)} %collective-permute-done.16.refs_4_), channel_id=1, source_target_pairs={{0,224},{32,0},{64,32},{96,64},{128,96},{160,128},{192,160},{224,1... | collective-permute-start | bytes 319496 | tf_op jit(solution)/shard_map/ppermute | solution.py:569
  87.4 9.6 %copy-start.7 = (f32[13,2,8,128]{3,2,1,0:T(8,128)}, f32[13,2,8,128]{3,2,1,0:T(8,128)S(1)}, u32[]{:S(2)}) copy-start(f32[13,2,8,128]{3,2,1,0:T(8,128)S(1)} %collective-permute-done.15.refs_3_) | copy-start | bytes 319492
  87.4 7.4 %collective-permute-start.19 = (f32[13,2,8,128]{3,2,1,0:T(8,128)S(1)}, f32[13,2,8,128]{3,2,1,0:T(8,128)S(1)}, u32[]{:S(2)}, u32[]{:S(2)}) collective-permute-start(f32[13,2,8,128]{3,2,1,0:T(8,128)S(1)} %collective-permute-done.15.refs_3_), channel_id=1, source_target_pairs={{0,64},{32,96},{64,128},{96,160},{128,192},{160,224},{192,0},{224,... | collective-permute-start | bytes 319496 | tf_op jit(solution)/shard_map/ppermute | solution.py:569
  87.4 9.6 %collective-permute-start.17 = (f32[13,2,8,128]{3,2,1,0:T(8,128)S(1)}, f32[13,2,8,128]{3,2,1,0:T(8,128)S(1)}, u32[]{:S(2)}, u32[]{:S(2)}) collective-permute-start(f32[13,2,8,128]{3,2,1,0:T(8,128)S(1)} %collective-permute-done.15.refs_3_), channel_id=1, source_target_pairs={{0,32},{32,64},{64,96},{96,128},{128,160},{160,192},{192,224},{224... | collective-permute-start | bytes 319496 | tf_op jit(solution)/shard_map/ppermute | solution.py:569
  89.9 7.0 %copy-start.9 = (f32[13,2,8,128]{3,2,1,0:T(8,128)}, f32[13,2,8,128]{3,2,1,0:T(8,128)S(1)}, u32[]{:S(2)}) copy-start(f32[13,2,8,128]{3,2,1,0:T(8,128)S(1)} %collective-permute-done.14.refs_2_) | copy-start | bytes 319492
  89.9 7.0 %copy-start.10 = (f32[13,2,8,128]{3,2,1,0:T(8,128)}, f32[13,2,8,128]{3,2,1,0:T(8,128)S(1)}, u32[]{:S(2)}) copy-start(f32[13,2,8,128]{3,2,1,0:T(8,128)S(1)} %collective-permute-done.13.refs_1_) | copy-start | bytes 319492
  90.0 7.0 %copy-start.12 = (f32[13,2,8,128]{3,2,1,0:T(8,128)}, f32[13,2,8,128]{3,2,1,0:T(8,128)S(1)}, u32[]{:S(2)}) copy-start(f32[13,2,8,128]{3,2,1,0:T(8,128)S(1)} %collective-permute-done.18.refs_6_) | copy-start | bytes 319492
  94.7 2.3 %copy-start.14 = (f32[13,2,8,128]{3,2,1,0:T(8,128)}, f32[13,2,8,128]{3,2,1,0:T(8,128)S(1)}, u32[]{:S(2)}) copy-start(f32[13,2,8,128]{3,2,1,0:T(8,128)S(1)} %collective-permute-done.19.refs_7_) | copy-start | bytes 319492
  97.0 0.6 copy-start.15

commit v10 on v9

--- a/solution.py
+++ b/solution.py
@@ -450,7 +450,7 @@
     cells, rows, width = volume.shape
     tiles = width // LANES
     slab, band = lax.axis_index("depth"), lax.axis_index("height")
-    limit = pltpu.CompilerParams(vmem_limit_bytes=63 << 20)
+    limit = pltpu.CompilerParams(vmem_limit_bytes=(64 << 20) - (32 << 10))
     field = volume.reshape(cells, rows, tiles, LANES).transpose(0, 2, 1, 3)
 
     down, up, first, last = pl.pallas_call(

time: 101 us -> 99.2 us (0.982)
  local copies, waits for them, and re-layouts: 3.54 us -> 1.93 us
    unnamed x36 -> x12, local copies, waits for them, and re-layouts: 2.87 us -> 1.29 us
    ppermute x4, starting transfers between devices: 7.72 us -> 8.85 us  [per_device(): known[by] = lax.ppermute(own, 'depth', ring('depth', by))]
  transfers between devices with their start and end apart: 20 -> 20, of which waited for: 8 -> 11; matrix products, arithmetic and copies ran while one was open for 1% -> 1% of each run, Pallas kernels for 9% -> 10%
where the time goes in v10:
time: 99.2 us; the launch traced here: 98.2 us
  starting transfers between devices  45.2 us (46%)
  Pallas kernels  34.5 us (35%)
  waiting for transfers between devices  15.7 us (16%)
  local copies, waits for them, and re-layouts  1.93 us (2%)
    pallas_call x1, Pallas kernels, per_device(): pl.pallas_call(functools.partial(render, alpha_top=alpha_top), out_shape=...  18.3 us
    ppermute x7, starting transfers between devices, per_device(): lax.ppermute(value, 'depth', ring('depth', by))  17.1 us
    ppermute x4, starting transfers between devices, per_device(): known[by] = lax.ppermute(own, 'depth', ring('depth', by))  8.85 us
    pallas_call x1, Pallas kernels, per_device(): pl.pallas_call(functools.partial(render_rest, alpha_top=alpha_top), out_s...  7.72 us
    ppermute x3, waiting for transfers between devices, per_device(): known[held + by] = lax.ppermute(known[held], 'depth', ring('depth', by))  6.53 us
    ppermute x1, starting transfers between devices, per_device(): bottom_corner = lax.ppermute(corner_up, 'height', ring('height', -1))  5.05 us
    ppermute x1, starting transfers between devices, per_device(): bottom = lax.ppermute(up, 'height', ring('height', -1))  5.05 us
    ppermute x3, starting transfers between devices, per_device(): known[held + by] = lax.ppermute(known[held], 'depth', ring('depth', by))  4.86 us
  transfers between devices with their start and end apart: 20, of which 11 were waited for; matrix products, arithmetic and copies ran while one was open for 1% of the time, Pallas kernels for 10%

profile of v10, /device:TPU:0, one launch (start us, length us, event | category | flops | bytes accessed | tf_op | source)
XLA Modules:
  0.0 98.2 jit_solution(7833995576354190683)
XLA Ops:
  0.0 2.6 %pack.1 = (f32[16,96,128]{2,1,0:T(8,128)}, f32[16,96,128]{2,1,0:T(8,128)}, f32[3,16,8,128]{3,2,1,0:T(8,128)}, f32[3,16,8,128]{3,2,1,0:T(8,128)}) custom-call(f32[32,16,8,128]{3,2,1,0:T(8,128)} %bitcast.27), custom_call_target="tpu_custom_call" | custom-call | tf_op jit(solution)/shard_map/pack/pallas_call | solution.py:456
  2.6 0.1 collective-permute-start.2
  2.7 5.1 %collective-permute-start.3 = (f32[16,96,128]{2,1,0:T(8,128)}, f32[16,96,128]{2,1,0:T(8,128)}, u32[]{:S(2)}, u32[]{:S(2)}) collective-permute-start(f32[16,96,128]{2,1,0:T(8,128)} %get-tuple-element.24), channel_id=1, source_target_pairs={{0,31},{1,0},{2,1},{3,2},{4,3},{5,4},{6,5},{7,6},{8,7},{9,8},{10,9... | collective-permute-start | bytes 2359304 | tf_op jit(solution)/shard_map/ppermute | solution.py:475
  7.7 0.2 collective-permute-start
  7.9 3.9 %collective-permute-start.1 = (f32[3,16,8,128]{3,2,1,0:T(8,128)}, f32[3,16,8,128]{3,2,1,0:T(8,128)}, u32[]{:S(2)}, u32[]{:S(2)}) collective-permute-start(f32[3,16,8,128]{3,2,1,0:T(8,128)} %get-tuple-element.22), channel_id=1, source_target_pairs={{0,224},{32,0},{64,32},{96,64},{128,96},{160,128},{192,160},{224,1... | collective-permute-start | bytes 589832 | tf_op jit(solution)/shard_map/ppermute | solution.py:473
  11.8 0.6 stack.87.tile_ref
  12.5 3.3 %collective-permute-done.low_ref = f32[3,16,8,128]{3,2,1,0:T(8,128)} collective-permute-done((f32[3,16,8,128]{3,2,1,0:T(8,128)}, f32[3,16,8,128]{3,2,1,0:T(8,128)}, u32[]{:S(2)}, u32[]{:S(2)}) %collective-permute-start) | collective-permute-done | bytes 196640 | tf_op jit(solution)/shard_map/ppermute | solution.py:472
  15.8 0.0 collective-permute-done.1.high_ref
  15.8 1.7 %pack_corners.1 = (f32[16,8,128]{2,1,0:T(8,128)}, f32[16,8,128]{2,1,0:T(8,128)}) custom-call(f32[3,16,8,128]{3,2,1,0:T(8,128)} %collective-permute-done.low_ref, f32[3,16,8,128]{3,2,1,0:T(8,128)} %collective-permute-done.1.high_ref), custom_call_target="tpu_custom_call" | custom-call | flops 400000000 | bytes 80000000 | tf_op jit(solution)/shard_map/pack_corners/pallas_call | solution.py:476
  17.5 0.1 collective-permute-start.4
  17.6 5.1 %collective-permute-start.5 = (f32[16,8,128]{2,1,0:T(8,128)}, f32[16,8,128]{2,1,0:T(8,128)}, u32[]{:S(2)}, u32[]{:S(2)}) collective-permute-start(f32[16,8,128]{2,1,0:T(8,128)} %get-tuple-element.26), channel_id=1, source_target_pairs={{0,31},{1,0},{2,1},{3,2},{4,3},{5,4},{6,5},{7,6},{8,7},{9,8},{10,9... | collective-permute-start | bytes 196616 | tf_op jit(solution)/shard_map/ppermute | solution.py:489
  22.7 0.7 add_convert_fusion.edge_ref
  23.3 1.6 %collective-permute-done.4.top_corner_ref = f32[16,8,128]{2,1,0:T(8,128)} collective-permute-done((f32[16,8,128]{2,1,0:T(8,128)}, f32[16,8,128]{2,1,0:T(8,128)}, u32[]{:S(2)}, u32[]{:S(2)}) %collective-permute-start.4) | collective-permute-done | bytes 65568 | tf_op jit(solution)/shard_map/ppermute | solution.py:488
  24.9 0.0 collective-permute-done.2.top_ref
  24.9 0.0 collective-permute-done.3.bottom_ref
  24.9 18.3 %render.1 = (f32[13,2,8,128]{3,2,1,0:T(8,128)}, f32[13,2,8,128]{3,2,1,0:T(8,128)}, f32[13,2,8,128]{3,2,1,0:T(8,128)}, f32[10,34,16,128]{3,2,1,0:T(8,128)}, f32[10,33,8,128]{3,2,1,0:T(8,128)}) custom-call(f32[4]{0:T(128)} %add_convert_fusion.edge_ref, s32[16]{0:T(128)} %stack.87.tile_ref, f32[3,4]{1,0:T(4,128)} %colour_ref.3, f32[4]{0:T(128)} %opacity_ref.3, ...), custom_call_target="tpu_custom_call" | custom-call | tf_op jit(solution)/shard_map/render/pallas_call | solution.py:497
  43.3 4.7 %collective-permute-start.6 = (f32[13,2,8,128]{3,2,1,0:T(8,128)}, f32[13,2,8,128]{3,2,1,0:T(8,128)}, u32[]{:S(2)}, u32[]{:S(2)}) collective-permute-start(f32[13,2,8,128]{3,2,1,0:T(8,128)} %get-tuple-element.27), channel_id=1, source_target_pairs={{0,128},{32,160},{64,192},{96,224},{128,0},{160,32},{192,64},{224,... | collective-permute-start | bytes 319496 | tf_op jit(solution)/shard_map/ppermute | solution.py:554
  47.9 1.9 %collective-permute-start.7 = (f32[13,2,8,128]{3,2,1,0:T(8,128)}, f32[13,2,8,128]{3,2,1,0:T(8,128)}, u32[]{:S(2)}, u32[]{:S(2)}) collective-permute-start(f32[13,2,8,128]{3,2,1,0:T(8,128)} %get-tuple-element.28), channel_id=1, source_target_pairs={{0,96},{32,128},{64,160},{96,192},{128,224},{160,0},{192,32},{224,... | collective-permute-start | bytes 319496 | tf_op jit(solution)/shard_map/ppermute | solution.py:554
  49.8 3.1 %collective-permute-start.8 = (f32[13,2,8,128]{3,2,1,0:T(8,128)}, f32[13,2,8,128]{3,2,1,0:T(8,128)}, u32[]{:S(2)}, u32[]{:S(2)}) collective-permute-start(f32[13,2,8,128]{3,2,1,0:T(8,128)} %get-tuple-element.29), channel_id=1, source_target_pairs={{0,160},{32,192},{64,224},{96,0},{128,32},{160,64},{192,96},{224,1... | collective-permute-start | bytes 319496 | tf_op jit(solution)/shard_map/ppermute | solution.py:554
  53.0 7.7 %render_rest.1 = (f32[13,2,8,128]{3,2,1,0:T(8,128)}, f32[13,2,8,128]{3,2,1,0:T(8,128)}, f32[13,2,8,128]{3,2,1,0:T(8,128)}, f32[13,2,8,128]{3,2,1,0:T(8,128)}, f32[13,2,8,128]{3,2,1,0:T(8,128)}) custom-call(f32[3,4]{1,0:T(4,128)} %colour_ref.3, f32[4]{0:T(128)} %opacity_ref.3, f32[4,3]{1,0:T(4,128)} %dir_ref.3, f32[4,3]{1,0:T(4,128)} %light_ref.3, ...), custom_call_target="tpu_custom_call" | custom-call | flops 50000000 | bytes 20000000 | tf_op jit(solution)/shard_map/render_rest/pallas_call | solution.py:535
  60.7 1.4 %collective-permute-start.9 = (f32[13,2,8,128]{3,2,1,0:T(8,128)}, f32[13,2,8,128]{3,2,1,0:T(8,128)}, u32[]{:S(2)}, u32[]{:S(2)}) collective-permute-start(f32[13,2,8,128]{3,2,1,0:T(8,128)} %get-tuple-element.32), channel_id=1, source_target_pairs={{0,64},{32,96},{64,128},{96,160},{128,192},{160,224},{192,0},{224,... | collective-permute-start | bytes 319496 | tf_op jit(solution)/shard_map/ppermute | solution.py:554
  62.0 2.9 %collective-permute-start.10 = (f32[13,2,8,128]{3,2,1,0:T(8,128)}, f32[13,2,8,128]{3,2,1,0:T(8,128)}, u32[]{:S(2)}, u32[]{:S(2)}) collective-permute-start(f32[13,2,8,128]{3,2,1,0:T(8,128)} %get-tuple-element.33), channel_id=1, source_target_pairs={{0,192},{32,224},{64,0},{96,32},{128,64},{160,96},{192,128},{224,1... | collective-permute-start | bytes 319496 | tf_op jit(solution)/shard_map/ppermute | solution.py:554
  64.9 0.0 collective-permute-done.6.refs_0_
  64.9 0.8 collective-permute-start.11
  65.7 0.0 collective-permute-done.7.refs_1_
  65.7 2.4 %collective-permute-start.12 = (f32[13,2,8,128]{3,2,1,0:T(8,128)}, f32[13,2,8,128]{3,2,1,0:T(8,128)}, u32[]{:S(2)}, u32[]{:S(2)}) collective-permute-start(f32[13,2,8,128]{3,2,1,0:T(8,128)} %get-tuple-element.35), channel_id=1, source_target_pairs={{0,224},{32,0},{64,32},{96,64},{128,96},{160,128},{192,160},{224,1... | collective-permute-start | bytes 319496 | tf_op jit(solution)/shard_map/ppermute | solution.py:554
  68.1 0.0 collective-permute-done.8.refs_2_
  68.1 0.2 collective-permute-done.9.refs_3_
  68.4 0.3 collective-permute-done.10.refs_4_
  68.6 2.5 %collective-permute-done.11.refs_5_ = f32[13,2,8,128]{3,2,1,0:T(8,128)} collective-permute-done((f32[13,2,8,128]{3,2,1,0:T(8,128)}, f32[13,2,8,128]{3,2,1,0:T(8,128)}, u32[]{:S(2)}, u32[]{:S(2)}) %collective-permute-start.11) | collective-permute-done | bytes 106528 | tf_op jit(solution)/shard_map/ppermute | solution.py:554
  71.1 0.6 collective-permute-done.12.refs_6_
  71.7 2.0 %fold.1.refs_0_ = f32[13,2,8,128]{3,2,1,0:T(8,128)} custom-call(s32[1]{0:T(128)} %bitcast.place_ref, f32[13,2,8,128]{3,2,1,0:T(8,128)} %collective-permute-done.6.refs_0_, f32[13,2,8,128]{3,2,1,0:T(8,128)} %collective-permute-done.7.refs_1_, f32[13,2,8,128]{3,2,1,0:T(8,128)} %collective-permute-done.8.refs_2_, ...), custom_call_target="tpu_custom_call" | custom-call | tf_op jit(solution)/shard_map/fold/pallas_call | solution.py:557
  73.7 2.5 %collective-permute-start.16 = (f32[13,2,8,128]{3,2,1,0:T(8,128)}, f32[13,2,8,128]{3,2,1,0:T(8,128)S(1)}, u32[]{:S(2)}, u32[]{:S(2)}) collective-permute-start(f32[13,2,8,128]{3,2,1,0:T(8,128)} %fold.1.refs_0_), channel_id=1, source_target_pairs={{0,192},{32,224},{64,0},{96,32},{128,64},{160,96},{192,128},{224,1... | collective-permute-start | bytes 319496 | tf_op jit(solution)/shard_map/ppermute | solution.py:567
  76.3 0.4 collective-permute-start.15
  76.6 5.9 %collective-permute-start.14 = (f32[13,2,8,128]{3,2,1,0:T(8,128)}, f32[13,2,8,128]{3,2,1,0:T(8,128)S(1)}, u32[]{:S(2)}, u32[]{:S(2)}) collective-permute-start(f32[13,2,8,128]{3,2,1,0:T(8,128)} %fold.1.refs_0_), channel_id=1, source_target_pairs={{0,224},{32,0},{64,32},{96,64},{128,96},{160,128},{192,160},{224,1... | collective-permute-start | bytes 319496 | tf_op jit(solution)/shard_map/ppermute | solution.py:567
  82.6 0.0 collective-permute-start.13
  82.6 0.0 collective-permute-done.16.refs_4_
  82.6 0.6 copy-done
  83.2 3.2 %collective-permute-start.18 = (f32[13,2,8,128]{3,2,1,0:T(8,128)S(1)}, f32[13,2,8,128]{3,2,1,0:T(8,128)S(1)}, u32[]{:S(2)}, u32[]{:S(2)}) collective-permute-start(f32[13,2,8,128]{3,2,1,0:T(8,128)S(1)} %collective-permute-done.16.refs_4_), channel_id=1, source_target_pairs={{0,224},{32,0},{64,32},{96,64},{128,96},{160,128},{192,160},{224,1... | collective-permute-start | bytes 319496 | tf_op jit(solution)/shard_map/ppermute | solution.py:569
  86.5 0.1 collective-permute-done.15.refs_3_
  86.5 1.6 %collective-permute-start.17 = (f32[13,2,8,128]{3,2,1,0:T(8,128)S(1)}, f32[13,2,8,128]{3,2,1,0:T(8,128)}, u32[]{:S(2)}, u32[]{:S(2)}) collective-permute-start(f32[13,2,8,128]{3,2,1,0:T(8,128)S(1)} %collective-permute-done.15.refs_3_), channel_id=1, source_target_pairs={{0,32},{32,64},{64,96},{96,128},{128,160},{160,192},{192,224},{224... | collective-permute-start | bytes 319496 | tf_op jit(solution)/shard_map/ppermute | solution.py:569
  88.1 0.0 collective-permute-done.14.refs_2_
  88.2 0.5 collective-permute-done.13.refs_1_
  88.7 0.1 collective-permute-done.18.refs_6_
  88.8 4.8 %collective-permute-done.19.refs_7_ = f32[13,2,8,128]{3,2,1,0:T(8,128)S(1)} collective-permute-done((f32[13,2,8,128]{3,2,1,0:T(8,128)S(1)}, f32[13,2,8,128]{3,2,1,0:T(8,128)S(1)}, u32[]{:S(2)}, u32[]{:S(2)}) %collective-permute-start.19) | collective-permute-done | bytes 106528 | tf_op jit(solution)/shard_map/ppermute | solution.py:569
  93.6 0.6 copy-done.5
  94.2 1.6 %collective-permute-done.17.refs_5_ = f32[13,2,8,128]{3,2,1,0:T(8,128)} collective-permute-done((f32[13,2,8,128]{3,2,1,0:T(8,128)S(1)}, f32[13,2,8,128]{3,2,1,0:T(8,128)}, u32[]{:S(2)}, u32[]{:S(2)}) %collective-permute-start.17) | collective-permute-done | bytes 106528 | tf_op jit(solution)/shard_map/ppermute | solution.py:569
  95.9 2.2 %spread.1 = f32[13,16,8,128]{3,2,1,0:T(8,128)} custom-call(s32[1]{0:T(128)} %bitcast.place_ref, f32[13,2,8,128]{3,2,1,0:T(8,128)} %fold.1.refs_0_, f32[13,2,8,128]{3,2,1,0:T(8,128)} %copy-done.3, f32[13,2,8,128]{3,2,1,0:T(8,128)} %copy-done.2, f32[13,2,8,128]{3,2,1,0:T(8,128)} %copy-done.1, f32[13,2,8,128]{3,2,1,0:T(8,128)} %copy-done, ...), custom_call_target="tpu_custom_call" | custom-call | tf_op jit(solution)/shard_map/spread/pallas_call | solution.py:570
  (12 shorter events, 0.0 us)
Async XLA Ops:
  2.6 22.4 %collective-permute-start.2 = (f32[16,96,128]{2,1,0:T(8,128)}, f32[16,96,128]{2,1,0:T(8,128)}, u32[]{:S(2)}, u32[]{:S(2)}) collective-permute-start(f32[16,96,128]{2,1,0:T(8,128)} %get-tuple-element.23), channel_id=1, source_target_pairs={{0,1},{1,2},{2,3},{3,4},{4,5},{5,6},{6,7},{7,8},{8,9},{9,10},{10,1... | collective-permute-start | bytes 2359304 | tf_op jit(solution)/shard_map/ppermute | solution.py:474
  2.7 22.3 %collective-permute-start.3 = (f32[16,96,128]{2,1,0:T(8,128)}, f32[16,96,128]{2,1,0:T(8,128)}, u32[]{:S(2)}, u32[]{:S(2)}) collective-permute-start(f32[16,96,128]{2,1,0:T(8,128)} %get-tuple-element.24), channel_id=1, source_target_pairs={{0,31},{1,0},{2,1},{3,2},{4,3},{5,4},{6,5},{7,6},{8,7},{9,8},{10,9... | collective-permute-start | bytes 2359304 | tf_op jit(solution)/shard_map/ppermute | solution.py:475
  7.7 8.1 %collective-permute-start = (f32[3,16,8,128]{3,2,1,0:T(8,128)}, f32[3,16,8,128]{3,2,1,0:T(8,128)}, u32[]{:S(2)}, u32[]{:S(2)}) collective-permute-start(f32[3,16,8,128]{3,2,1,0:T(8,128)} %get-tuple-element.21), channel_id=1, source_target_pairs={{0,32},{32,64},{64,96},{96,128},{128,160},{160,192},{192,224},{224... | collective-permute-start | bytes 589832 | tf_op jit(solution)/shard_map/ppermute | solution.py:472
  7.9 7.9 %collective-permute-start.1 = (f32[3,16,8,128]{3,2,1,0:T(8,128)}, f32[3,16,8,128]{3,2,1,0:T(8,128)}, u32[]{:S(2)}, u32[]{:S(2)}) collective-permute-start(f32[3,16,8,128]{3,2,1,0:T(8,128)} %get-tuple-element.22), channel_id=1, source_target_pairs={{0,224},{32,0},{64,32},{96,64},{128,96},{160,128},{192,160},{224,1... | collective-permute-start | bytes 589832 | tf_op jit(solution)/shard_map/ppermute | solution.py:473
  17.5 7.4 %collective-permute-start.4 = (f32[16,8,128]{2,1,0:T(8,128)}, f32[16,8,128]{2,1,0:T(8,128)}, u32[]{:S(2)}, u32[]{:S(2)}) collective-permute-start(f32[16,8,128]{2,1,0:T(8,128)} %get-tuple-element.25), channel_id=1, source_target_pairs={{0,1},{1,2},{2,3},{3,4},{4,5},{5,6},{6,7},{7,8},{8,9},{9,10},{10,1... | collective-permute-start | bytes 196616 | tf_op jit(solution)/shard_map/ppermute | solution.py:488
  17.6 7.3 %collective-permute-start.5 = (f32[16,8,128]{2,1,0:T(8,128)}, f32[16,8,128]{2,1,0:T(8,128)}, u32[]{:S(2)}, u32[]{:S(2)}) collective-permute-start(f32[16,8,128]{2,1,0:T(8,128)} %get-tuple-element.26), channel_id=1, source_target_pairs={{0,31},{1,0},{2,1},{3,2},{4,3},{5,4},{6,5},{7,6},{8,7},{9,8},{10,9... | collective-permute-start | bytes 196616 | tf_op jit(solution)/shard_map/ppermute | solution.py:489
  43.3 21.6 %collective-permute-start.6 = (f32[13,2,8,128]{3,2,1,0:T(8,128)}, f32[13,2,8,128]{3,2,1,0:T(8,128)}, u32[]{:S(2)}, u32[]{:S(2)}) collective-permute-start(f32[13,2,8,128]{3,2,1,0:T(8,128)} %get-tuple-element.27), channel_id=1, source_target_pairs={{0,128},{32,160},{64,192},{96,224},{128,0},{160,32},{192,64},{224,... | collective-permute-start | bytes 319496 | tf_op jit(solution)/shard_map/ppermute | solution.py:554
  47.9 17.8 %collective-permute-start.7 = (f32[13,2,8,128]{3,2,1,0:T(8,128)}, f32[13,2,8,128]{3,2,1,0:T(8,128)}, u32[]{:S(2)}, u32[]{:S(2)}) collective-permute-start(f32[13,2,8,128]{3,2,1,0:T(8,128)} %get-tuple-element.28), channel_id=1, source_target_pairs={{0,96},{32,128},{64,160},{96,192},{128,224},{160,0},{192,32},{224,... | collective-permute-start | bytes 319496 | tf_op jit(solution)/shard_map/ppermute | solution.py:554
  49.8 18.3 %collective-permute-start.8 = (f32[13,2,8,128]{3,2,1,0:T(8,128)}, f32[13,2,8,128]{3,2,1,0:T(8,128)}, u32[]{:S(2)}, u32[]{:S(2)}) collective-permute-start(f32[13,2,8,128]{3,2,1,0:T(8,128)} %get-tuple-element.29), channel_id=1, source_target_pairs={{0,160},{32,192},{64,224},{96,0},{128,32},{160,64},{192,96},{224,1... | collective-permute-start | bytes 319496 | tf_op jit(solution)/shard_map/ppermute | solution.py:554
  60.7 7.7 %collective-permute-start.9 = (f32[13,2,8,128]{3,2,1,0:T(8,128)}, f32[13,2,8,128]{3,2,1,0:T(8,128)}, u32[]{:S(2)}, u32[]{:S(2)}) collective-permute-start(f32[13,2,8,128]{3,2,1,0:T(8,128)} %get-tuple-element.32), channel_id=1, source_target_pairs={{0,64},{32,96},{64,128},{96,160},{128,192},{160,224},{192,0},{224,... | collective-permute-start | bytes 319496 | tf_op jit(solution)/shard_map/ppermute | solution.py:554
  62.0 6.6 %collective-permute-start.10 = (f32[13,2,8,128]{3,2,1,0:T(8,128)}, f32[13,2,8,128]{3,2,1,0:T(8,128)}, u32[]{:S(2)}, u32[]{:S(2)}) collective-permute-start(f32[13,2,8,128]{3,2,1,0:T(8,128)} %get-tuple-element.33), channel_id=1, source_target_pairs={{0,192},{32,224},{64,0},{96,32},{128,64},{160,96},{192,128},{224,1... | collective-permute-start | bytes 319496 | tf_op jit(solution)/shard_map/ppermute | solution.py:554
  64.9 6.2 %collective-permute-start.11 = (f32[13,2,8,128]{3,2,1,0:T(8,128)}, f32[13,2,8,128]{3,2,1,0:T(8,128)}, u32[]{:S(2)}, u32[]{:S(2)}) collective-permute-start(f32[13,2,8,128]{3,2,1,0:T(8,128)} %get-tuple-element.34), channel_id=1, source_target_pairs={{0,32},{32,64},{64,96},{96,128},{128,160},{160,192},{192,224},{224... | collective-permute-start | bytes 319496 | tf_op jit(solution)/shard_map/ppermute | solution.py:554
  65.7 6.0 %collective-permute-start.12 = (f32[13,2,8,128]{3,2,1,0:T(8,128)}, f32[13,2,8,128]{3,2,1,0:T(8,128)}, u32[]{:S(2)}, u32[]{:S(2)}) collective-permute-start(f32[13,2,8,128]{3,2,1,0:T(8,128)} %get-tuple-element.35), channel_id=1, source_target_pairs={{0,224},{32,0},{64,32},{96,64},{128,96},{160,128},{192,160},{224,1... | collective-permute-start | bytes 319496 | tf_op jit(solution)/shard_map/ppermute | solution.py:554
  73.7 8.9 %collective-permute-start.16 = (f32[13,2,8,128]{3,2,1,0:T(8,128)}, f32[13,2,8,128]{3,2,1,0:T(8,128)S(1)}, u32[]{:S(2)}, u32[]{:S(2)}) collective-permute-start(f32[13,2,8,128]{3,2,1,0:T(8,128)} %fold.1.refs_0_), channel_id=1, source_target_pairs={{0,192},{32,224},{64,0},{96,32},{128,64},{160,96},{192,128},{224,1... | collective-permute-start | bytes 319496 | tf_op jit(solution)/shard_map/ppermute | solution.py:567
  76.3 10.3 %collective-permute-start.15 = (f32[13,2,8,128]{3,2,1,0:T(8,128)}, f32[13,2,8,128]{3,2,1,0:T(8,128)S(1)}, u32[]{:S(2)}, u32[]{:S(2)}) collective-permute-start(f32[13,2,8,128]{3,2,1,0:T(8,128)} %fold.1.refs_0_), channel_id=1, source_target_pairs={{0,64},{32,96},{64,128},{96,160},{128,192},{160,224},{192,0},{224,... | collective-permute-start | bytes 319496 | tf_op jit(solution)/shard_map/ppermute | solution.py:567
  76.6 11.5 %collective-permute-start.14 = (f32[13,2,8,128]{3,2,1,0:T(8,128)}, f32[13,2,8,128]{3,2,1,0:T(8,128)S(1)}, u32[]{:S(2)}, u32[]{:S(2)}) collective-permute-start(f32[13,2,8,128]{3,2,1,0:T(8,128)} %fold.1.refs_0_), channel_id=1, source_target_pairs={{0,224},{32,0},{64,32},{96,64},{128,96},{160,128},{192,160},{224,1... | collective-permute-start | bytes 319496 | tf_op jit(solution)/shard_map/ppermute | solution.py:567
  82.6 6.1 %collective-permute-start.13 = (f32[13,2,8,128]{3,2,1,0:T(8,128)}, f32[13,2,8,128]{3,2,1,0:T(8,128)S(1)}, u32[]{:S(2)}, u32[]{:S(2)}) collective-permute-start(f32[13,2,8,128]{3,2,1,0:T(8,128)} %fold.1.refs_0_), channel_id=1, source_target_pairs={{0,32},{32,64},{64,96},{96,128},{128,160},{160,192},{192,224},{224... | collective-permute-start | bytes 319496 | tf_op jit(solution)/shard_map/ppermute | solution.py:567
  82.6 0.7 copy-start
  83.2 5.5 %collective-permute-start.18 = (f32[13,2,8,128]{3,2,1,0:T(8,128)S(1)}, f32[13,2,8,128]{3,2,1,0:T(8,128)S(1)}, u32[]{:S(2)}, u32[]{:S(2)}) collective-permute-start(f32[13,2,8,128]{3,2,1,0:T(8,128)S(1)} %collective-permute-done.16.refs_4_), channel_id=1, source_target_pairs={{0,224},{32,0},{64,32},{96,64},{128,96},{160,128},{192,160},{224,1... | collective-permute-start | bytes 319496 | tf_op jit(solution)/shard_map/ppermute | solution.py:569
  86.5 2.2 %copy-start.1 = (f32[13,2,8,128]{3,2,1,0:T(8,128)}, f32[13,2,8,128]{3,2,1,0:T(8,128)S(1)}, u32[]{:S(2)}) copy-start(f32[13,2,8,128]{3,2,1,0:T(8,128)S(1)} %collective-permute-done.15.refs_3_) | copy-start | bytes 319492
  86.5 7.1 %collective-permute-start.19 = (f32[13,2,8,128]{3,2,1,0:T(8,128)S(1)}, f32[13,2,8,128]{3,2,1,0:T(8,128)S(1)}, u32[]{:S(2)}, u32[]{:S(2)}) collective-permute-start(f32[13,2,8,128]{3,2,1,0:T(8,128)S(1)} %collective-permute-done.15.refs_3_), channel_id=1, source_target_pairs={{0,64},{32,96},{64,128},{96,160},{128,192},{160,224},{192,0},{224,... | collective-permute-start | bytes 319496 | tf_op jit(solution)/shard_map/ppermute | solution.py:569
  86.5 9.3 %collective-permute-start.17 = (f32[13,2,8,128]{3,2,1,0:T(8,128)S(1)}, f32[13,2,8,128]{3,2,1,0:T(8,128)}, u32[]{:S(2)}, u32[]{:S(2)}) collective-permute-start(f32[13,2,8,128]{3,2,1,0:T(8,128)S(1)} %collective-permute-done.15.refs_3_), channel_id=1, source_target_pairs={{0,32},{32,64},{64,96},{96,128},{128,160},{160,192},{192,224},{224... | collective-permute-start | bytes 319496 | tf_op jit(solution)/shard_map/ppermute | solution.py:569
  88.1 5.4 %copy-start.2 = (f32[13,2,8,128]{3,2,1,0:T(8,128)}, f32[13,2,8,128]{3,2,1,0:T(8,128)S(1)}, u32[]{:S(2)}) copy-start(f32[13,2,8,128]{3,2,1,0:T(8,128)S(1)} %collective-permute-done.14.refs_2_) | copy-start | bytes 319492
  88.7 4.9 %copy-start.3 = (f32[13,2,8,128]{3,2,1,0:T(8,128)}, f32[13,2,8,128]{3,2,1,0:T(8,128)S(1)}, u32[]{:S(2)}) copy-start(f32[13,2,8,128]{3,2,1,0:T(8,128)S(1)} %collective-permute-done.13.refs_1_) | copy-start | bytes 319492
  88.7 4.8 %copy-start.4 = (f32[13,2,8,128]{3,2,1,0:T(8,128)}, f32[13,2,8,128]{3,2,1,0:T(8,128)S(1)}, u32[]{:S(2)}) copy-start(f32[13,2,8,128]{3,2,1,0:T(8,128)S(1)} %collective-permute-done.18.refs_6_) | copy-start | bytes 319492
  93.6 0.6 copy-start.5

commit v11 on v10

--- a/solution.py
+++ b/solution.py
@@ -173,7 +173,7 @@
         width_slope(dst, planes - 2, slope)
 
 
-SHIFTS = (4, 3, 5, 2, 6, 1, 7, 0)
+SHIFTS = (3, 5, 4, 2, 6, 1, 7, 0)
 FAR = 3
 
 

time: 99.2 us -> 99.2 us (level)
  no operation moved by 1% of the time
where the time goes in v11:
time: 99.2 us; the launch traced here: 98.2 us
  starting transfers between devices  45.3 us (46%)
  Pallas kernels  34.5 us (35%)
  waiting for transfers between devices  15.6 us (16%)
  local copies, waits for them, and re-layouts  1.93 us (2%)
    pallas_call x1, Pallas kernels, per_device(): pl.pallas_call(functools.partial(render, alpha_top=alpha_top), out_shape=...  18.3 us
    ppermute x7, starting transfers between devices, per_device(): lax.ppermute(value, 'depth', ring('depth', by))  17.1 us
    ppermute x4, starting transfers between devices, per_device(): known[by] = lax.ppermute(own, 'depth', ring('depth', by))  8.91 us
    pallas_call x1, Pallas kernels, per_device(): pl.pallas_call(functools.partial(render_rest, alpha_top=alpha_top), out_s...  7.72 us
    ppermute x3, waiting for transfers between devices, per_device(): known[held + by] = lax.ppermute(known[held], 'depth', ring('depth', by))  6.61 us
    ppermute x1, starting transfers between devices, per_device(): bottom_corner = lax.ppermute(corner_up, 'height', ring('height', -1))  5.05 us
    ppermute x1, starting transfers between devices, per_device(): bottom = lax.ppermute(up, 'height', ring('height', -1))  5.05 us
    ppermute x3, starting transfers between devices, per_device(): known[held + by] = lax.ppermute(known[held], 'depth', ring('depth', by))  4.85 us
  transfers between devices with their start and end apart: 20, of which 11 were waited for; matrix products, arithmetic and copies ran while one was open for 1% of the time, Pallas kernels for 10%

profile of v11, /device:TPU:0, one launch (start us, length us, event | category | flops | bytes accessed | tf_op | source)
XLA Modules:
  0.0 98.2 jit_solution(2545156025668556791)
XLA Ops:
  0.0 2.6 %pack.1 = (f32[16,96,128]{2,1,0:T(8,128)}, f32[16,96,128]{2,1,0:T(8,128)}, f32[3,16,8,128]{3,2,1,0:T(8,128)}, f32[3,16,8,128]{3,2,1,0:T(8,128)}) custom-call(f32[32,16,8,128]{3,2,1,0:T(8,128)} %bitcast.27), custom_call_target="tpu_custom_call" | custom-call | tf_op jit(solution)/shard_map/pack/pallas_call | solution.py:456
  2.6 0.1 collective-permute-start.2
  2.7 5.1 %collective-permute-start.3 = (f32[16,96,128]{2,1,0:T(8,128)}, f32[16,96,128]{2,1,0:T(8,128)}, u32[]{:S(2)}, u32[]{:S(2)}) collective-permute-start(f32[16,96,128]{2,1,0:T(8,128)} %get-tuple-element.24), channel_id=1, source_target_pairs={{0,31},{1,0},{2,1},{3,2},{4,3},{5,4},{6,5},{7,6},{8,7},{9,8},{10,9... | collective-permute-start | bytes 2359304 | tf_op jit(solution)/shard_map/ppermute | solution.py:475
  7.7 0.2 collective-permute-start
  7.9 3.9 %collective-permute-start.1 = (f32[3,16,8,128]{3,2,1,0:T(8,128)}, f32[3,16,8,128]{3,2,1,0:T(8,128)}, u32[]{:S(2)}, u32[]{:S(2)}) collective-permute-start(f32[3,16,8,128]{3,2,1,0:T(8,128)} %get-tuple-element.22), channel_id=1, source_target_pairs={{0,224},{32,0},{64,32},{96,64},{128,96},{160,128},{192,160},{224,1... | collective-permute-start | bytes 589832 | tf_op jit(solution)/shard_map/ppermute | solution.py:473
  11.8 0.6 stack.87.tile_ref
  12.5 3.3 %collective-permute-done.low_ref = f32[3,16,8,128]{3,2,1,0:T(8,128)} collective-permute-done((f32[3,16,8,128]{3,2,1,0:T(8,128)}, f32[3,16,8,128]{3,2,1,0:T(8,128)}, u32[]{:S(2)}, u32[]{:S(2)}) %collective-permute-start) | collective-permute-done | bytes 196640 | tf_op jit(solution)/shard_map/ppermute | solution.py:472
  15.8 0.0 collective-permute-done.1.high_ref
  15.8 1.7 %pack_corners.1 = (f32[16,8,128]{2,1,0:T(8,128)}, f32[16,8,128]{2,1,0:T(8,128)}) custom-call(f32[3,16,8,128]{3,2,1,0:T(8,128)} %collective-permute-done.low_ref, f32[3,16,8,128]{3,2,1,0:T(8,128)} %collective-permute-done.1.high_ref), custom_call_target="tpu_custom_call" | custom-call | flops 400000000 | bytes 80000000 | tf_op jit(solution)/shard_map/pack_corners/pallas_call | solution.py:476
  17.5 0.1 collective-permute-start.4
  17.6 5.1 %collective-permute-start.5 = (f32[16,8,128]{2,1,0:T(8,128)}, f32[16,8,128]{2,1,0:T(8,128)}, u32[]{:S(2)}, u32[]{:S(2)}) collective-permute-start(f32[16,8,128]{2,1,0:T(8,128)} %get-tuple-element.26), channel_id=1, source_target_pairs={{0,31},{1,0},{2,1},{3,2},{4,3},{5,4},{6,5},{7,6},{8,7},{9,8},{10,9... | collective-permute-start | bytes 196616 | tf_op jit(solution)/shard_map/ppermute | solution.py:489
  22.7 0.7 add_convert_fusion.edge_ref
  23.3 1.6 %collective-permute-done.4.top_corner_ref = f32[16,8,128]{2,1,0:T(8,128)} collective-permute-done((f32[16,8,128]{2,1,0:T(8,128)}, f32[16,8,128]{2,1,0:T(8,128)}, u32[]{:S(2)}, u32[]{:S(2)}) %collective-permute-start.4) | collective-permute-done | bytes 65568 | tf_op jit(solution)/shard_map/ppermute | solution.py:488
  24.9 0.0 collective-permute-done.5.bottom_corner_ref
  24.9 0.0 collective-permute-done.2.top_ref
  24.9 0.0 collective-permute-done.3.bottom_ref
  24.9 18.3 %render.1 = (f32[13,2,8,128]{3,2,1,0:T(8,128)}, f32[13,2,8,128]{3,2,1,0:T(8,128)}, f32[13,2,8,128]{3,2,1,0:T(8,128)}, f32[10,34,16,128]{3,2,1,0:T(8,128)}, f32[10,33,8,128]{3,2,1,0:T(8,128)}) custom-call(f32[4]{0:T(128)} %add_convert_fusion.edge_ref, s32[16]{0:T(128)} %stack.87.tile_ref, f32[3,4]{1,0:T(4,128)} %colour_ref.3, f32[4]{0:T(128)} %opacity_ref.3, ...), custom_call_target="tpu_custom_call" | custom-call | tf_op jit(solution)/shard_map/render/pallas_call | solution.py:497
  43.3 5.2 %collective-permute-start.6 = (f32[13,2,8,128]{3,2,1,0:T(8,128)}, f32[13,2,8,128]{3,2,1,0:T(8,128)}, u32[]{:S(2)}, u32[]{:S(2)}) collective-permute-start(f32[13,2,8,128]{3,2,1,0:T(8,128)} %get-tuple-element.27), channel_id=1, source_target_pairs={{0,96},{32,128},{64,160},{96,192},{128,224},{160,0},{192,32},{224,... | collective-permute-start | bytes 319496 | tf_op jit(solution)/shard_map/ppermute | solution.py:554
  48.5 0.0 collective-permute-start.7
  48.5 4.5 %collective-permute-start.8 = (f32[13,2,8,128]{3,2,1,0:T(8,128)}, f32[13,2,8,128]{3,2,1,0:T(8,128)}, u32[]{:S(2)}, u32[]{:S(2)}) collective-permute-start(f32[13,2,8,128]{3,2,1,0:T(8,128)} %get-tuple-element.29), channel_id=1, source_target_pairs={{0,128},{32,160},{64,192},{96,224},{128,0},{160,32},{192,64},{224,... | collective-permute-start | bytes 319496 | tf_op jit(solution)/shard_map/ppermute | solution.py:554
  52.9 7.7 %render_rest.1 = (f32[13,2,8,128]{3,2,1,0:T(8,128)}, f32[13,2,8,128]{3,2,1,0:T(8,128)}, f32[13,2,8,128]{3,2,1,0:T(8,128)}, f32[13,2,8,128]{3,2,1,0:T(8,128)}, f32[13,2,8,128]{3,2,1,0:T(8,128)}) custom-call(f32[3,4]{1,0:T(4,128)} %colour_ref.3, f32[4]{0:T(128)} %opacity_ref.3, f32[4,3]{1,0:T(4,128)} %dir_ref.3, f32[4,3]{1,0:T(4,128)} %light_ref.3, ...), custom_call_target="tpu_custom_call" | custom-call | flops 50000000 | bytes 20000000 | tf_op jit(solution)/shard_map/render_rest/pallas_call | solution.py:535
  60.7 1.4 %collective-permute-start.9 = (f32[13,2,8,128]{3,2,1,0:T(8,128)}, f32[13,2,8,128]{3,2,1,0:T(8,128)}, u32[]{:S(2)}, u32[]{:S(2)}) collective-permute-start(f32[13,2,8,128]{3,2,1,0:T(8,128)} %get-tuple-element.32), channel_id=1, source_target_pairs={{0,64},{32,96},{64,128},{96,160},{128,192},{160,224},{192,0},{224,... | collective-permute-start | bytes 319496 | tf_op jit(solution)/shard_map/ppermute | solution.py:554
  62.0 2.9 %collective-permute-start.10 = (f32[13,2,8,128]{3,2,1,0:T(8,128)}, f32[13,2,8,128]{3,2,1,0:T(8,128)}, u32[]{:S(2)}, u32[]{:S(2)}) collective-permute-start(f32[13,2,8,128]{3,2,1,0:T(8,128)} %get-tuple-element.33), channel_id=1, source_target_pairs={{0,192},{32,224},{64,0},{96,32},{128,64},{160,96},{192,128},{224,1... | collective-permute-start | bytes 319496 | tf_op jit(solution)/shard_map/ppermute | solution.py:554
  64.9 0.0 collective-permute-done.6.refs_0_
  64.9 0.8 collective-permute-start.11
  65.7 2.4 %collective-permute-start.12 = (f32[13,2,8,128]{3,2,1,0:T(8,128)}, f32[13,2,8,128]{3,2,1,0:T(8,128)}, u32[]{:S(2)}, u32[]{:S(2)}) collective-permute-start(f32[13,2,8,128]{3,2,1,0:T(8,128)} %get-tuple-element.35), channel_id=1, source_target_pairs={{0,224},{32,0},{64,32},{96,64},{128,96},{160,128},{192,160},{224,1... | collective-permute-start | bytes 319496 | tf_op jit(solution)/shard_map/ppermute | solution.py:554
  68.1 0.0 collective-permute-done.8.refs_2_
  68.1 0.2 collective-permute-done.9.refs_3_
  68.4 0.3 collective-permute-done.10.refs_4_
  68.6 2.5 %collective-permute-done.11.refs_5_ = f32[13,2,8,128]{3,2,1,0:T(8,128)} collective-permute-done((f32[13,2,8,128]{3,2,1,0:T(8,128)}, f32[13,2,8,128]{3,2,1,0:T(8,128)}, u32[]{:S(2)}, u32[]{:S(2)}) %collective-permute-start.11) | collective-permute-done | bytes 106528 | tf_op jit(solution)/shard_map/ppermute | solution.py:554
  71.1 0.5 collective-permute-done.12.refs_6_
  71.6 2.0 %fold.1.refs_0_ = f32[13,2,8,128]{3,2,1,0:T(8,128)} custom-call(s32[1]{0:T(128)} %bitcast.place_ref, f32[13,2,8,128]{3,2,1,0:T(8,128)} %collective-permute-done.6.refs_0_, f32[13,2,8,128]{3,2,1,0:T(8,128)} %collective-permute-done.7.refs_1_, f32[13,2,8,128]{3,2,1,0:T(8,128)} %collective-permute-done.8.refs_2_, ...), custom_call_target="tpu_custom_call" | custom-call | tf_op jit(solution)/shard_map/fold/pallas_call | solution.py:557
  73.6 2.7 %collective-permute-start.16 = (f32[13,2,8,128]{3,2,1,0:T(8,128)}, f32[13,2,8,128]{3,2,1,0:T(8,128)S(1)}, u32[]{:S(2)}, u32[]{:S(2)}) collective-permute-start(f32[13,2,8,128]{3,2,1,0:T(8,128)} %fold.1.refs_0_), channel_id=1, source_target_pairs={{0,192},{32,224},{64,0},{96,32},{128,64},{160,96},{192,128},{224,1... | collective-permute-start | bytes 319496 | tf_op jit(solution)/shard_map/ppermute | solution.py:567
  76.2 0.2 collective-permute-start.15
  76.5 6.0 %collective-permute-start.14 = (f32[13,2,8,128]{3,2,1,0:T(8,128)}, f32[13,2,8,128]{3,2,1,0:T(8,128)S(1)}, u32[]{:S(2)}, u32[]{:S(2)}) collective-permute-start(f32[13,2,8,128]{3,2,1,0:T(8,128)} %fold.1.refs_0_), channel_id=1, source_target_pairs={{0,224},{32,0},{64,32},{96,64},{128,96},{160,128},{192,160},{224,1... | collective-permute-start | bytes 319496 | tf_op jit(solution)/shard_map/ppermute | solution.py:567
  82.5 0.0 collective-permute-start.13
  82.5 0.6 copy-done
  83.1 3.2 %collective-permute-start.18 = (f32[13,2,8,128]{3,2,1,0:T(8,128)S(1)}, f32[13,2,8,128]{3,2,1,0:T(8,128)S(1)}, u32[]{:S(2)}, u32[]{:S(2)}) collective-permute-start(f32[13,2,8,128]{3,2,1,0:T(8,128)S(1)} %collective-permute-done.16.refs_4_), channel_id=1, source_target_pairs={{0,224},{32,0},{64,32},{96,64},{128,96},{160,128},{192,160},{224,1... | collective-permute-start | bytes 319496 | tf_op jit(solution)/shard_map/ppermute | solution.py:569
  86.4 0.1 collective-permute-done.15.refs_3_
  86.5 0.0 collective-permute-start.19
  86.5 1.6 %collective-permute-start.17 = (f32[13,2,8,128]{3,2,1,0:T(8,128)S(1)}, f32[13,2,8,128]{3,2,1,0:T(8,128)}, u32[]{:S(2)}, u32[]{:S(2)}) collective-permute-start(f32[13,2,8,128]{3,2,1,0:T(8,128)S(1)} %collective-permute-done.15.refs_3_), channel_id=1, source_target_pairs={{0,32},{32,64},{64,96},{96,128},{128,160},{160,192},{192,224},{224... | collective-permute-start | bytes 319496 | tf_op jit(solution)/shard_map/ppermute | solution.py:569
  88.1 0.0 collective-permute-done.14.refs_2_
  88.1 0.5 collective-permute-done.13.refs_1_
  88.6 0.1 collective-permute-done.18.refs_6_
  88.7 4.9 %collective-permute-done.19.refs_7_ = f32[13,2,8,128]{3,2,1,0:T(8,128)S(1)} collective-permute-done((f32[13,2,8,128]{3,2,1,0:T(8,128)S(1)}, f32[13,2,8,128]{3,2,1,0:T(8,128)S(1)}, u32[]{:S(2)}, u32[]{:S(2)}) %collective-permute-start.19) | collective-permute-done | bytes 106528 | tf_op jit(solution)/shard_map/ppermute | solution.py:569
  93.6 0.6 copy-done.5
  94.2 1.6 %collective-permute-done.17.refs_5_ = f32[13,2,8,128]{3,2,1,0:T(8,128)} collective-permute-done((f32[13,2,8,128]{3,2,1,0:T(8,128)S(1)}, f32[13,2,8,128]{3,2,1,0:T(8,128)}, u32[]{:S(2)}, u32[]{:S(2)}) %collective-permute-start.17) | collective-permute-done | bytes 106528 | tf_op jit(solution)/shard_map/ppermute | solution.py:569
  95.9 2.2 %spread.1 = f32[13,16,8,128]{3,2,1,0:T(8,128)} custom-call(s32[1]{0:T(128)} %bitcast.place_ref, f32[13,2,8,128]{3,2,1,0:T(8,128)} %fold.1.refs_0_, f32[13,2,8,128]{3,2,1,0:T(8,128)} %copy-done.3, f32[13,2,8,128]{3,2,1,0:T(8,128)} %copy-done.2, f32[13,2,8,128]{3,2,1,0:T(8,128)} %copy-done.1, f32[13,2,8,128]{3,2,1,0:T(8,128)} %copy-done, ...), custom_call_target="tpu_custom_call" | custom-call | tf_op jit(solution)/shard_map/spread/pallas_call | solution.py:570
  (12 shorter events, 0.0 us)
Async XLA Ops:
  2.6 22.4 %collective-permute-start.2 = (f32[16,96,128]{2,1,0:T(8,128)}, f32[16,96,128]{2,1,0:T(8,128)}, u32[]{:S(2)}, u32[]{:S(2)}) collective-permute-start(f32[16,96,128]{2,1,0:T(8,128)} %get-tuple-element.23), channel_id=1, source_target_pairs={{0,1},{1,2},{2,3},{3,4},{4,5},{5,6},{6,7},{7,8},{8,9},{9,10},{10,1... | collective-permute-start | bytes 2359304 | tf_op jit(solution)/shard_map/ppermute | solution.py:474
  2.7 22.3 %collective-permute-start.3 = (f32[16,96,128]{2,1,0:T(8,128)}, f32[16,96,128]{2,1,0:T(8,128)}, u32[]{:S(2)}, u32[]{:S(2)}) collective-permute-start(f32[16,96,128]{2,1,0:T(8,128)} %get-tuple-element.24), channel_id=1, source_target_pairs={{0,31},{1,0},{2,1},{3,2},{4,3},{5,4},{6,5},{7,6},{8,7},{9,8},{10,9... | collective-permute-start | bytes 2359304 | tf_op jit(solution)/shard_map/ppermute | solution.py:475
  7.7 8.1 %collective-permute-start = (f32[3,16,8,128]{3,2,1,0:T(8,128)}, f32[3,16,8,128]{3,2,1,0:T(8,128)}, u32[]{:S(2)}, u32[]{:S(2)}) collective-permute-start(f32[3,16,8,128]{3,2,1,0:T(8,128)} %get-tuple-element.21), channel_id=1, source_target_pairs={{0,32},{32,64},{64,96},{96,128},{128,160},{160,192},{192,224},{224... | collective-permute-start | bytes 589832 | tf_op jit(solution)/shard_map/ppermute | solution.py:472
  7.9 7.9 %collective-permute-start.1 = (f32[3,16,8,128]{3,2,1,0:T(8,128)}, f32[3,16,8,128]{3,2,1,0:T(8,128)}, u32[]{:S(2)}, u32[]{:S(2)}) collective-permute-start(f32[3,16,8,128]{3,2,1,0:T(8,128)} %get-tuple-element.22), channel_id=1, source_target_pairs={{0,224},{32,0},{64,32},{96,64},{128,96},{160,128},{192,160},{224,1... | collective-permute-start | bytes 589832 | tf_op jit(solution)/shard_map/ppermute | solution.py:473
  17.5 7.4 %collective-permute-start.4 = (f32[16,8,128]{2,1,0:T(8,128)}, f32[16,8,128]{2,1,0:T(8,128)}, u32[]{:S(2)}, u32[]{:S(2)}) collective-permute-start(f32[16,8,128]{2,1,0:T(8,128)} %get-tuple-element.25), channel_id=1, source_target_pairs={{0,1},{1,2},{2,3},{3,4},{4,5},{5,6},{6,7},{7,8},{8,9},{9,10},{10,1... | collective-permute-start | bytes 196616 | tf_op jit(solution)/shard_map/ppermute | solution.py:488
  17.6 7.3 %collective-permute-start.5 = (f32[16,8,128]{2,1,0:T(8,128)}, f32[16,8,128]{2,1,0:T(8,128)}, u32[]{:S(2)}, u32[]{:S(2)}) collective-permute-start(f32[16,8,128]{2,1,0:T(8,128)} %get-tuple-element.26), channel_id=1, source_target_pairs={{0,31},{1,0},{2,1},{3,2},{4,3},{5,4},{6,5},{7,6},{8,7},{9,8},{10,9... | collective-permute-start | bytes 196616 | tf_op jit(solution)/shard_map/ppermute | solution.py:489
  43.3 21.6 %collective-permute-start.6 = (f32[13,2,8,128]{3,2,1,0:T(8,128)}, f32[13,2,8,128]{3,2,1,0:T(8,128)}, u32[]{:S(2)}, u32[]{:S(2)}) collective-permute-start(f32[13,2,8,128]{3,2,1,0:T(8,128)} %get-tuple-element.27), channel_id=1, source_target_pairs={{0,96},{32,128},{64,160},{96,192},{128,224},{160,0},{192,32},{224,... | collective-permute-start | bytes 319496 | tf_op jit(solution)/shard_map/ppermute | solution.py:554
  48.5 17.2 %collective-permute-start.7 = (f32[13,2,8,128]{3,2,1,0:T(8,128)}, f32[13,2,8,128]{3,2,1,0:T(8,128)}, u32[]{:S(2)}, u32[]{:S(2)}) collective-permute-start(f32[13,2,8,128]{3,2,1,0:T(8,128)} %get-tuple-element.28), channel_id=1, source_target_pairs={{0,160},{32,192},{64,224},{96,0},{128,32},{160,64},{192,96},{224,1... | collective-permute-start | bytes 319496 | tf_op jit(solution)/shard_map/ppermute | solution.py:554
  48.5 19.7 %collective-permute-start.8 = (f32[13,2,8,128]{3,2,1,0:T(8,128)}, f32[13,2,8,128]{3,2,1,0:T(8,128)}, u32[]{:S(2)}, u32[]{:S(2)}) collective-permute-start(f32[13,2,8,128]{3,2,1,0:T(8,128)} %get-tuple-element.29), channel_id=1, source_target_pairs={{0,128},{32,160},{64,192},{96,224},{128,0},{160,32},{192,64},{224,... | collective-permute-start | bytes 319496 | tf_op jit(solution)/shard_map/ppermute | solution.py:554
  60.7 7.7 %collective-permute-start.9 = (f32[13,2,8,128]{3,2,1,0:T(8,128)}, f32[13,2,8,128]{3,2,1,0:T(8,128)}, u32[]{:S(2)}, u32[]{:S(2)}) collective-permute-start(f32[13,2,8,128]{3,2,1,0:T(8,128)} %get-tuple-element.32), channel_id=1, source_target_pairs={{0,64},{32,96},{64,128},{96,160},{128,192},{160,224},{192,0},{224,... | collective-permute-start | bytes 319496 | tf_op jit(solution)/shard_map/ppermute | solution.py:554
  62.0 6.6 %collective-permute-start.10 = (f32[13,2,8,128]{3,2,1,0:T(8,128)}, f32[13,2,8,128]{3,2,1,0:T(8,128)}, u32[]{:S(2)}, u32[]{:S(2)}) collective-permute-start(f32[13,2,8,128]{3,2,1,0:T(8,128)} %get-tuple-element.33), channel_id=1, source_target_pairs={{0,192},{32,224},{64,0},{96,32},{128,64},{160,96},{192,128},{224,1... | collective-permute-start | bytes 319496 | tf_op jit(solution)/shard_map/ppermute | solution.py:554
  64.9 6.2 %collective-permute-start.11 = (f32[13,2,8,128]{3,2,1,0:T(8,128)}, f32[13,2,8,128]{3,2,1,0:T(8,128)}, u32[]{:S(2)}, u32[]{:S(2)}) collective-permute-start(f32[13,2,8,128]{3,2,1,0:T(8,128)} %get-tuple-element.34), channel_id=1, source_target_pairs={{0,32},{32,64},{64,96},{96,128},{128,160},{160,192},{192,224},{224... | collective-permute-start | bytes 319496 | tf_op jit(solution)/shard_map/ppermute | solution.py:554
  65.7 5.9 %collective-permute-start.12 = (f32[13,2,8,128]{3,2,1,0:T(8,128)}, f32[13,2,8,128]{3,2,1,0:T(8,128)}, u32[]{:S(2)}, u32[]{:S(2)}) collective-permute-start(f32[13,2,8,128]{3,2,1,0:T(8,128)} %get-tuple-element.35), channel_id=1, source_target_pairs={{0,224},{32,0},{64,32},{96,64},{128,96},{160,128},{192,160},{224,1... | collective-permute-start | bytes 319496 | tf_op jit(solution)/shard_map/ppermute | solution.py:554
  73.6 8.9 %collective-permute-start.16 = (f32[13,2,8,128]{3,2,1,0:T(8,128)}, f32[13,2,8,128]{3,2,1,0:T(8,128)S(1)}, u32[]{:S(2)}, u32[]{:S(2)}) collective-permute-start(f32[13,2,8,128]{3,2,1,0:T(8,128)} %fold.1.refs_0_), channel_id=1, source_target_pairs={{0,192},{32,224},{64,0},{96,32},{128,64},{160,96},{192,128},{224,1... | collective-permute-start | bytes 319496 | tf_op jit(solution)/shard_map/ppermute | solution.py:567
  76.2 10.3 %collective-permute-start.15 = (f32[13,2,8,128]{3,2,1,0:T(8,128)}, f32[13,2,8,128]{3,2,1,0:T(8,128)S(1)}, u32[]{:S(2)}, u32[]{:S(2)}) collective-permute-start(f32[13,2,8,128]{3,2,1,0:T(8,128)} %fold.1.refs_0_), channel_id=1, source_target_pairs={{0,64},{32,96},{64,128},{96,160},{128,192},{160,224},{192,0},{224,... | collective-permute-start | bytes 319496 | tf_op jit(solution)/shard_map/ppermute | solution.py:567
  76.5 11.7 %collective-permute-start.14 = (f32[13,2,8,128]{3,2,1,0:T(8,128)}, f32[13,2,8,128]{3,2,1,0:T(8,128)S(1)}, u32[]{:S(2)}, u32[]{:S(2)}) collective-permute-start(f32[13,2,8,128]{3,2,1,0:T(8,128)} %fold.1.refs_0_), channel_id=1, source_target_pairs={{0,224},{32,0},{64,32},{96,64},{128,96},{160,128},{192,160},{224,1... | collective-permute-start | bytes 319496 | tf_op jit(solution)/shard_map/ppermute | solution.py:567
  82.5 6.1 %collective-permute-start.13 = (f32[13,2,8,128]{3,2,1,0:T(8,128)}, f32[13,2,8,128]{3,2,1,0:T(8,128)S(1)}, u32[]{:S(2)}, u32[]{:S(2)}) collective-permute-start(f32[13,2,8,128]{3,2,1,0:T(8,128)} %fold.1.refs_0_), channel_id=1, source_target_pairs={{0,32},{32,64},{64,96},{96,128},{128,160},{160,192},{192,224},{224... | collective-permute-start | bytes 319496 | tf_op jit(solution)/shard_map/ppermute | solution.py:567
  82.5 0.7 copy-start
  83.1 5.5 %collective-permute-start.18 = (f32[13,2,8,128]{3,2,1,0:T(8,128)S(1)}, f32[13,2,8,128]{3,2,1,0:T(8,128)S(1)}, u32[]{:S(2)}, u32[]{:S(2)}) collective-permute-start(f32[13,2,8,128]{3,2,1,0:T(8,128)S(1)} %collective-permute-done.16.refs_4_), channel_id=1, source_target_pairs={{0,224},{32,0},{64,32},{96,64},{128,96},{160,128},{192,160},{224,1... | collective-permute-start | bytes 319496 | tf_op jit(solution)/shard_map/ppermute | solution.py:569
  86.5 2.1 %copy-start.1 = (f32[13,2,8,128]{3,2,1,0:T(8,128)}, f32[13,2,8,128]{3,2,1,0:T(8,128)S(1)}, u32[]{:S(2)}) copy-start(f32[13,2,8,128]{3,2,1,0:T(8,128)S(1)} %collective-permute-done.15.refs_3_) | copy-start | bytes 319492
  86.5 7.1 %collective-permute-start.19 = (f32[13,2,8,128]{3,2,1,0:T(8,128)S(1)}, f32[13,2,8,128]{3,2,1,0:T(8,128)S(1)}, u32[]{:S(2)}, u32[]{:S(2)}) collective-permute-start(f32[13,2,8,128]{3,2,1,0:T(8,128)S(1)} %collective-permute-done.15.refs_3_), channel_id=1, source_target_pairs={{0,64},{32,96},{64,128},{96,160},{128,192},{160,224},{192,0},{224,... | collective-permute-start | bytes 319496 | tf_op jit(solution)/shard_map/ppermute | solution.py:569
  86.5 9.3 %collective-permute-start.17 = (f32[13,2,8,128]{3,2,1,0:T(8,128)S(1)}, f32[13,2,8,128]{3,2,1,0:T(8,128)}, u32[]{:S(2)}, u32[]{:S(2)}) collective-permute-start(f32[13,2,8,128]{3,2,1,0:T(8,128)S(1)} %collective-permute-done.15.refs_3_), channel_id=1, source_target_pairs={{0,32},{32,64},{64,96},{96,128},{128,160},{160,192},{192,224},{224... | collective-permute-start | bytes 319496 | tf_op jit(solution)/shard_map/ppermute | solution.py:569
  88.1 5.5 %copy-start.2 = (f32[13,2,8,128]{3,2,1,0:T(8,128)}, f32[13,2,8,128]{3,2,1,0:T(8,128)S(1)}, u32[]{:S(2)}) copy-start(f32[13,2,8,128]{3,2,1,0:T(8,128)S(1)} %collective-permute-done.14.refs_2_) | copy-start | bytes 319492
  88.6 5.0 %copy-start.3 = (f32[13,2,8,128]{3,2,1,0:T(8,128)}, f32[13,2,8,128]{3,2,1,0:T(8,128)S(1)}, u32[]{:S(2)}) copy-start(f32[13,2,8,128]{3,2,1,0:T(8,128)S(1)} %collective-permute-done.13.refs_1_) | copy-start | bytes 319492
  88.7 4.9 %copy-start.4 = (f32[13,2,8,128]{3,2,1,0:T(8,128)}, f32[13,2,8,128]{3,2,1,0:T(8,128)S(1)}, u32[]{:S(2)}) copy-start(f32[13,2,8,128]{3,2,1,0:T(8,128)S(1)} %collective-permute-done.18.refs_6_) | copy-start | bytes 319492
  93.6 0.6 copy-start.5

commit v12 on v10

--- a/solution.py
+++ b/solution.py
@@ -44,11 +44,14 @@
             edges[0].start()
         if g == groups - 1:
             edges[1].start()
-        for k in range(8):
-            z = 8 * g + k
-            for tile in range(tiles):
+
+        def rows_of(tile, carry):
+            for z in range(8 * g, 8 * g + 8):
                 up[tile, 3 * z : 3 * z + 3, :] = held[z, tile, 0:3, :]
                 down[tile, 3 * z : 3 * z + 3, :] = held[z, tile, 5:8, :]
+            return carry
+
+        lax.fori_loop(0, tiles, rows_of, 0)
         part = pl.ds(24 * g, 24)
         for i, (ref, out_ref) in enumerate(((down, down_ref), (up, up_ref))):
             copy = pltpu.make_async_copy(

time: 99.2 us -> 99.1 us (level)
  starting transfers between devices: 45.2 us -> 44.2 us
where the time goes in v12:
time: 99.1 us; the launch traced here: 98.2 us
  starting transfers between devices  44.2 us (45%)
  Pallas kernels  34.6 us (35%)
  waiting for transfers between devices  16.6 us (17%)
  local copies, waits for them, and re-layouts  1.93 us (2%)
    pallas_call x1, Pallas kernels, per_device(): pl.pallas_call(functools.partial(render, alpha_top=alpha_top), out_shape=...  18.3 us
    ppermute x7, starting transfers between devices, per_device(): lax.ppermute(value, 'depth', ring('depth', by))  17.1 us
    ppermute x4, starting transfers between devices, per_device(): known[by] = lax.ppermute(own, 'depth', ring('depth', by))  7.97 us
    pallas_call x1, Pallas kernels, per_device(): pl.pallas_call(functools.partial(render_rest, alpha_top=alpha_top), out_s...  7.72 us
    ppermute x3, waiting for transfers between devices, per_device(): known[held + by] = lax.ppermute(known[held], 'depth', ring('depth', by))  6.38 us
    ppermute x1, starting transfers between devices, per_device(): bottom_corner = lax.ppermute(corner_up, 'height', ring('height', -1))  5.05 us
    ppermute x1, starting transfers between devices, per_device(): bottom = lax.ppermute(up, 'height', ring('height', -1))  5.05 us
    ppermute x3, starting transfers between devices, per_device(): known[held + by] = lax.ppermute(known[held], 'depth', ring('depth', by))  4.68 us
  transfers between devices with their start and end apart: 20, of which 11 were waited for; matrix products, arithmetic and copies ran while one was open for 1% of the time, Pallas kernels for 10%

profile of v12, /device:TPU:0, one launch (start us, length us, event | category | flops | bytes accessed | tf_op | source)
XLA Modules:
  0.0 98.2 jit_solution(11782382952083661918)
XLA Ops:
  0.0 2.7 %pack.1 = (f32[16,96,128]{2,1,0:T(8,128)}, f32[16,96,128]{2,1,0:T(8,128)}, f32[3,16,8,128]{3,2,1,0:T(8,128)}, f32[3,16,8,128]{3,2,1,0:T(8,128)}) custom-call(f32[32,16,8,128]{3,2,1,0:T(8,128)} %bitcast.27), custom_call_target="tpu_custom_call" | custom-call | tf_op jit(solution)/shard_map/pack/pallas_call | solution.py:459
  2.7 0.1 collective-permute-start.2
  2.8 5.1 %collective-permute-start.3 = (f32[16,96,128]{2,1,0:T(8,128)}, f32[16,96,128]{2,1,0:T(8,128)}, u32[]{:S(2)}, u32[]{:S(2)}) collective-permute-start(f32[16,96,128]{2,1,0:T(8,128)} %get-tuple-element.24), channel_id=1, source_target_pairs={{0,31},{1,0},{2,1},{3,2},{4,3},{5,4},{6,5},{7,6},{8,7},{9,8},{10,9... | collective-permute-start | bytes 2359304 | tf_op jit(solution)/shard_map/ppermute | solution.py:478
  7.8 0.2 collective-permute-start
  8.0 3.9 %collective-permute-start.1 = (f32[3,16,8,128]{3,2,1,0:T(8,128)}, f32[3,16,8,128]{3,2,1,0:T(8,128)}, u32[]{:S(2)}, u32[]{:S(2)}) collective-permute-start(f32[3,16,8,128]{3,2,1,0:T(8,128)} %get-tuple-element.22), channel_id=1, source_target_pairs={{0,224},{32,0},{64,32},{96,64},{128,96},{160,128},{192,160},{224,1... | collective-permute-start | bytes 589832 | tf_op jit(solution)/shard_map/ppermute | solution.py:476
  11.9 0.6 stack.87.tile_ref
  12.6 3.3 %collective-permute-done.low_ref = f32[3,16,8,128]{3,2,1,0:T(8,128)} collective-permute-done((f32[3,16,8,128]{3,2,1,0:T(8,128)}, f32[3,16,8,128]{3,2,1,0:T(8,128)}, u32[]{:S(2)}, u32[]{:S(2)}) %collective-permute-start) | collective-permute-done | bytes 196640 | tf_op jit(solution)/shard_map/ppermute | solution.py:475
  15.9 0.0 collective-permute-done.1.high_ref
  15.9 1.7 %pack_corners.1 = (f32[16,8,128]{2,1,0:T(8,128)}, f32[16,8,128]{2,1,0:T(8,128)}) custom-call(f32[3,16,8,128]{3,2,1,0:T(8,128)} %collective-permute-done.low_ref, f32[3,16,8,128]{3,2,1,0:T(8,128)} %collective-permute-done.1.high_ref), custom_call_target="tpu_custom_call" | custom-call | flops 400000000 | bytes 80000000 | tf_op jit(solution)/shard_map/pack_corners/pallas_call | solution.py:479
  17.6 0.1 collective-permute-start.4
  17.7 5.1 %collective-permute-start.5 = (f32[16,8,128]{2,1,0:T(8,128)}, f32[16,8,128]{2,1,0:T(8,128)}, u32[]{:S(2)}, u32[]{:S(2)}) collective-permute-start(f32[16,8,128]{2,1,0:T(8,128)} %get-tuple-element.26), channel_id=1, source_target_pairs={{0,31},{1,0},{2,1},{3,2},{4,3},{5,4},{6,5},{7,6},{8,7},{9,8},{10,9... | collective-permute-start | bytes 196616 | tf_op jit(solution)/shard_map/ppermute | solution.py:492
  22.8 0.7 add_convert_fusion.edge_ref
  23.4 1.6 %collective-permute-done.4.top_corner_ref = f32[16,8,128]{2,1,0:T(8,128)} collective-permute-done((f32[16,8,128]{2,1,0:T(8,128)}, f32[16,8,128]{2,1,0:T(8,128)}, u32[]{:S(2)}, u32[]{:S(2)}) %collective-permute-start.4) | collective-permute-done | bytes 65568 | tf_op jit(solution)/shard_map/ppermute | solution.py:491
  25.0 0.0 collective-permute-done.5.bottom_corner_ref
  25.0 0.0 collective-permute-done.2.top_ref
  25.0 18.3 %render.1 = (f32[13,2,8,128]{3,2,1,0:T(8,128)}, f32[13,2,8,128]{3,2,1,0:T(8,128)}, f32[13,2,8,128]{3,2,1,0:T(8,128)}, f32[10,34,16,128]{3,2,1,0:T(8,128)}, f32[10,33,8,128]{3,2,1,0:T(8,128)}) custom-call(f32[4]{0:T(128)} %add_convert_fusion.edge_ref, s32[16]{0:T(128)} %stack.87.tile_ref, f32[3,4]{1,0:T(4,128)} %colour_ref.3, f32[4]{0:T(128)} %opacity_ref.3, ...), custom_call_target="tpu_custom_call" | custom-call | tf_op jit(solution)/shard_map/render/pallas_call | solution.py:500
  43.4 4.7 %collective-permute-start.6 = (f32[13,2,8,128]{3,2,1,0:T(8,128)}, f32[13,2,8,128]{3,2,1,0:T(8,128)}, u32[]{:S(2)}, u32[]{:S(2)}) collective-permute-start(f32[13,2,8,128]{3,2,1,0:T(8,128)} %get-tuple-element.27), channel_id=1, source_target_pairs={{0,128},{32,160},{64,192},{96,224},{128,0},{160,32},{192,64},{224,... | collective-permute-start | bytes 319496 | tf_op jit(solution)/shard_map/ppermute | solution.py:557
  48.0 1.9 %collective-permute-start.7 = (f32[13,2,8,128]{3,2,1,0:T(8,128)}, f32[13,2,8,128]{3,2,1,0:T(8,128)}, u32[]{:S(2)}, u32[]{:S(2)}) collective-permute-start(f32[13,2,8,128]{3,2,1,0:T(8,128)} %get-tuple-element.28), channel_id=1, source_target_pairs={{0,96},{32,128},{64,160},{96,192},{128,224},{160,0},{192,32},{224,... | collective-permute-start | bytes 319496 | tf_op jit(solution)/shard_map/ppermute | solution.py:557
  49.9 3.1 %collective-permute-start.8 = (f32[13,2,8,128]{3,2,1,0:T(8,128)}, f32[13,2,8,128]{3,2,1,0:T(8,128)}, u32[]{:S(2)}, u32[]{:S(2)}) collective-permute-start(f32[13,2,8,128]{3,2,1,0:T(8,128)} %get-tuple-element.29), channel_id=1, source_target_pairs={{0,160},{32,192},{64,224},{96,0},{128,32},{160,64},{192,96},{224,1... | collective-permute-start | bytes 319496 | tf_op jit(solution)/shard_map/ppermute | solution.py:557
  53.0 7.7 %render_rest.1 = (f32[13,2,8,128]{3,2,1,0:T(8,128)}, f32[13,2,8,128]{3,2,1,0:T(8,128)}, f32[13,2,8,128]{3,2,1,0:T(8,128)}, f32[13,2,8,128]{3,2,1,0:T(8,128)}, f32[13,2,8,128]{3,2,1,0:T(8,128)}) custom-call(f32[3,4]{1,0:T(4,128)} %colour_ref.3, f32[4]{0:T(128)} %opacity_ref.3, f32[4,3]{1,0:T(4,128)} %dir_ref.3, f32[4,3]{1,0:T(4,128)} %light_ref.3, ...), custom_call_target="tpu_custom_call" | custom-call | flops 50000000 | bytes 20000000 | tf_op jit(solution)/shard_map/render_rest/pallas_call | solution.py:538
  60.8 1.4 %collective-permute-start.9 = (f32[13,2,8,128]{3,2,1,0:T(8,128)}, f32[13,2,8,128]{3,2,1,0:T(8,128)}, u32[]{:S(2)}, u32[]{:S(2)}) collective-permute-start(f32[13,2,8,128]{3,2,1,0:T(8,128)} %get-tuple-element.32), channel_id=1, source_target_pairs={{0,64},{32,96},{64,128},{96,160},{128,192},{160,224},{192,0},{224,... | collective-permute-start | bytes 319496 | tf_op jit(solution)/shard_map/ppermute | solution.py:557
  62.1 2.9 %collective-permute-start.10 = (f32[13,2,8,128]{3,2,1,0:T(8,128)}, f32[13,2,8,128]{3,2,1,0:T(8,128)}, u32[]{:S(2)}, u32[]{:S(2)}) collective-permute-start(f32[13,2,8,128]{3,2,1,0:T(8,128)} %get-tuple-element.33), channel_id=1, source_target_pairs={{0,192},{32,224},{64,0},{96,32},{128,64},{160,96},{192,128},{224,1... | collective-permute-start | bytes 319496 | tf_op jit(solution)/shard_map/ppermute | solution.py:557
  65.0 0.0 collective-permute-done.6.refs_0_
  65.0 0.8 collective-permute-start.11
  65.8 0.0 collective-permute-done.7.refs_1_
  65.8 2.4 %collective-permute-start.12 = (f32[13,2,8,128]{3,2,1,0:T(8,128)}, f32[13,2,8,128]{3,2,1,0:T(8,128)}, u32[]{:S(2)}, u32[]{:S(2)}) collective-permute-start(f32[13,2,8,128]{3,2,1,0:T(8,128)} %get-tuple-element.35), channel_id=1, source_target_pairs={{0,224},{32,0},{64,32},{96,64},{128,96},{160,128},{192,160},{224,1... | collective-permute-start | bytes 319496 | tf_op jit(solution)/shard_map/ppermute | solution.py:557
  68.2 0.0 collective-permute-done.8.refs_2_
  68.2 0.2 collective-permute-done.9.refs_3_
  68.5 0.3 collective-permute-done.10.refs_4_
  68.7 2.5 %collective-permute-done.11.refs_5_ = f32[13,2,8,128]{3,2,1,0:T(8,128)} collective-permute-done((f32[13,2,8,128]{3,2,1,0:T(8,128)}, f32[13,2,8,128]{3,2,1,0:T(8,128)}, u32[]{:S(2)}, u32[]{:S(2)}) %collective-permute-start.11) | collective-permute-done | bytes 106528 | tf_op jit(solution)/shard_map/ppermute | solution.py:557
  71.2 1.5 %collective-permute-done.12.refs_6_ = f32[13,2,8,128]{3,2,1,0:T(8,128)} collective-permute-done((f32[13,2,8,128]{3,2,1,0:T(8,128)}, f32[13,2,8,128]{3,2,1,0:T(8,128)}, u32[]{:S(2)}, u32[]{:S(2)}) %collective-permute-start.12) | collective-permute-done | bytes 106528 | tf_op jit(solution)/shard_map/ppermute | solution.py:557
  72.7 2.0 %fold.1.refs_0_ = f32[13,2,8,128]{3,2,1,0:T(8,128)} custom-call(s32[1]{0:T(128)} %bitcast.place_ref, f32[13,2,8,128]{3,2,1,0:T(8,128)} %collective-permute-done.6.refs_0_, f32[13,2,8,128]{3,2,1,0:T(8,128)} %collective-permute-done.7.refs_1_, f32[13,2,8,128]{3,2,1,0:T(8,128)} %collective-permute-done.8.refs_2_, ...), custom_call_target="tpu_custom_call" | custom-call | tf_op jit(solution)/shard_map/fold/pallas_call | solution.py:560
  74.7 1.7 %collective-permute-start.16 = (f32[13,2,8,128]{3,2,1,0:T(8,128)}, f32[13,2,8,128]{3,2,1,0:T(8,128)S(1)}, u32[]{:S(2)}, u32[]{:S(2)}) collective-permute-start(f32[13,2,8,128]{3,2,1,0:T(8,128)} %fold.1.refs_0_), channel_id=1, source_target_pairs={{0,192},{32,224},{64,0},{96,32},{128,64},{160,96},{192,128},{224,1... | collective-permute-start | bytes 319496 | tf_op jit(solution)/shard_map/ppermute | solution.py:570
  76.4 1.3 %collective-permute-start.15 = (f32[13,2,8,128]{3,2,1,0:T(8,128)}, f32[13,2,8,128]{3,2,1,0:T(8,128)S(1)}, u32[]{:S(2)}, u32[]{:S(2)}) collective-permute-start(f32[13,2,8,128]{3,2,1,0:T(8,128)} %fold.1.refs_0_), channel_id=1, source_target_pairs={{0,64},{32,96},{64,128},{96,160},{128,192},{160,224},{192,0},{224,... | collective-permute-start | bytes 319496 | tf_op jit(solution)/shard_map/ppermute | solution.py:570
  77.6 5.0 %collective-permute-start.14 = (f32[13,2,8,128]{3,2,1,0:T(8,128)}, f32[13,2,8,128]{3,2,1,0:T(8,128)S(1)}, u32[]{:S(2)}, u32[]{:S(2)}) collective-permute-start(f32[13,2,8,128]{3,2,1,0:T(8,128)} %fold.1.refs_0_), channel_id=1, source_target_pairs={{0,224},{32,0},{64,32},{96,64},{128,96},{160,128},{192,160},{224,1... | collective-permute-start | bytes 319496 | tf_op jit(solution)/shard_map/ppermute | solution.py:570
  82.7 0.0 collective-permute-start.13
  82.7 0.0 collective-permute-done.16.refs_4_
  82.7 0.6 copy-done
  83.3 3.2 %collective-permute-start.18 = (f32[13,2,8,128]{3,2,1,0:T(8,128)S(1)}, f32[13,2,8,128]{3,2,1,0:T(8,128)S(1)}, u32[]{:S(2)}, u32[]{:S(2)}) collective-permute-start(f32[13,2,8,128]{3,2,1,0:T(8,128)S(1)} %collective-permute-done.16.refs_4_), channel_id=1, source_target_pairs={{0,224},{32,0},{64,32},{96,64},{128,96},{160,128},{192,160},{224,1... | collective-permute-start | bytes 319496 | tf_op jit(solution)/shard_map/ppermute | solution.py:572
  86.5 0.1 collective-permute-done.15.refs_3_
  86.6 1.4 %collective-permute-start.17 = (f32[13,2,8,128]{3,2,1,0:T(8,128)S(1)}, f32[13,2,8,128]{3,2,1,0:T(8,128)}, u32[]{:S(2)}, u32[]{:S(2)}) collective-permute-start(f32[13,2,8,128]{3,2,1,0:T(8,128)S(1)} %collective-permute-done.15.refs_3_), channel_id=1, source_target_pairs={{0,32},{32,64},{64,96},{96,128},{128,160},{160,192},{192,224},{224... | collective-permute-start | bytes 319496 | tf_op jit(solution)/shard_map/ppermute | solution.py:572
  88.1 0.0 collective-permute-done.14.refs_2_
  88.1 0.7 collective-permute-done.13.refs_1_
  88.8 0.1 collective-permute-done.18.refs_6_
  88.8 4.9 %collective-permute-done.19.refs_7_ = f32[13,2,8,128]{3,2,1,0:T(8,128)S(1)} collective-permute-done((f32[13,2,8,128]{3,2,1,0:T(8,128)S(1)}, f32[13,2,8,128]{3,2,1,0:T(8,128)S(1)}, u32[]{:S(2)}, u32[]{:S(2)}) %collective-permute-start.19) | collective-permute-done | bytes 106528 | tf_op jit(solution)/shard_map/ppermute | solution.py:572
  93.7 0.6 copy-done.5
  94.3 1.5 %collective-permute-done.17.refs_5_ = f32[13,2,8,128]{3,2,1,0:T(8,128)} collective-permute-done((f32[13,2,8,128]{3,2,1,0:T(8,128)S(1)}, f32[13,2,8,128]{3,2,1,0:T(8,128)}, u32[]{:S(2)}, u32[]{:S(2)}) %collective-permute-start.17) | collective-permute-done | bytes 106528 | tf_op jit(solution)/shard_map/ppermute | solution.py:572
  95.8 2.2 %spread.1 = f32[13,16,8,128]{3,2,1,0:T(8,128)} custom-call(s32[1]{0:T(128)} %bitcast.place_ref, f32[13,2,8,128]{3,2,1,0:T(8,128)} %fold.1.refs_0_, f32[13,2,8,128]{3,2,1,0:T(8,128)} %copy-done.3, f32[13,2,8,128]{3,2,1,0:T(8,128)} %copy-done.2, f32[13,2,8,128]{3,2,1,0:T(8,128)} %copy-done.1, f32[13,2,8,128]{3,2,1,0:T(8,128)} %copy-done, ...), custom_call_target="tpu_custom_call" | custom-call | tf_op jit(solution)/shard_map/spread/pallas_call | solution.py:573
  (12 shorter events, 0.0 us)
Async XLA Ops:
  2.7 22.4 %collective-permute-start.2 = (f32[16,96,128]{2,1,0:T(8,128)}, f32[16,96,128]{2,1,0:T(8,128)}, u32[]{:S(2)}, u32[]{:S(2)}) collective-permute-start(f32[16,96,128]{2,1,0:T(8,128)} %get-tuple-element.23), channel_id=1, source_target_pairs={{0,1},{1,2},{2,3},{3,4},{4,5},{5,6},{6,7},{7,8},{8,9},{9,10},{10,1... | collective-permute-start | bytes 2359304 | tf_op jit(solution)/shard_map/ppermute | solution.py:477
  2.8 22.3 %collective-permute-start.3 = (f32[16,96,128]{2,1,0:T(8,128)}, f32[16,96,128]{2,1,0:T(8,128)}, u32[]{:S(2)}, u32[]{:S(2)}) collective-permute-start(f32[16,96,128]{2,1,0:T(8,128)} %get-tuple-element.24), channel_id=1, source_target_pairs={{0,31},{1,0},{2,1},{3,2},{4,3},{5,4},{6,5},{7,6},{8,7},{9,8},{10,9... | collective-permute-start | bytes 2359304 | tf_op jit(solution)/shard_map/ppermute | solution.py:478
  7.8 8.1 %collective-permute-start = (f32[3,16,8,128]{3,2,1,0:T(8,128)}, f32[3,16,8,128]{3,2,1,0:T(8,128)}, u32[]{:S(2)}, u32[]{:S(2)}) collective-permute-start(f32[3,16,8,128]{3,2,1,0:T(8,128)} %get-tuple-element.21), channel_id=1, source_target_pairs={{0,32},{32,64},{64,96},{96,128},{128,160},{160,192},{192,224},{224... | collective-permute-start | bytes 589832 | tf_op jit(solution)/shard_map/ppermute | solution.py:475
  8.0 7.9 %collective-permute-start.1 = (f32[3,16,8,128]{3,2,1,0:T(8,128)}, f32[3,16,8,128]{3,2,1,0:T(8,128)}, u32[]{:S(2)}, u32[]{:S(2)}) collective-permute-start(f32[3,16,8,128]{3,2,1,0:T(8,128)} %get-tuple-element.22), channel_id=1, source_target_pairs={{0,224},{32,0},{64,32},{96,64},{128,96},{160,128},{192,160},{224,1... | collective-permute-start | bytes 589832 | tf_op jit(solution)/shard_map/ppermute | solution.py:476
  17.6 7.4 %collective-permute-start.4 = (f32[16,8,128]{2,1,0:T(8,128)}, f32[16,8,128]{2,1,0:T(8,128)}, u32[]{:S(2)}, u32[]{:S(2)}) collective-permute-start(f32[16,8,128]{2,1,0:T(8,128)} %get-tuple-element.25), channel_id=1, source_target_pairs={{0,1},{1,2},{2,3},{3,4},{4,5},{5,6},{6,7},{7,8},{8,9},{9,10},{10,1... | collective-permute-start | bytes 196616 | tf_op jit(solution)/shard_map/ppermute | solution.py:491
  17.7 7.3 %collective-permute-start.5 = (f32[16,8,128]{2,1,0:T(8,128)}, f32[16,8,128]{2,1,0:T(8,128)}, u32[]{:S(2)}, u32[]{:S(2)}) collective-permute-start(f32[16,8,128]{2,1,0:T(8,128)} %get-tuple-element.26), channel_id=1, source_target_pairs={{0,31},{1,0},{2,1},{3,2},{4,3},{5,4},{6,5},{7,6},{8,7},{9,8},{10,9... | collective-permute-start | bytes 196616 | tf_op jit(solution)/shard_map/ppermute | solution.py:492
  43.4 21.6 %collective-permute-start.6 = (f32[13,2,8,128]{3,2,1,0:T(8,128)}, f32[13,2,8,128]{3,2,1,0:T(8,128)}, u32[]{:S(2)}, u32[]{:S(2)}) collective-permute-start(f32[13,2,8,128]{3,2,1,0:T(8,128)} %get-tuple-element.27), channel_id=1, source_target_pairs={{0,128},{32,160},{64,192},{96,224},{128,0},{160,32},{192,64},{224,... | collective-permute-start | bytes 319496 | tf_op jit(solution)/shard_map/ppermute | solution.py:557
  48.0 17.8 %collective-permute-start.7 = (f32[13,2,8,128]{3,2,1,0:T(8,128)}, f32[13,2,8,128]{3,2,1,0:T(8,128)}, u32[]{:S(2)}, u32[]{:S(2)}) collective-permute-start(f32[13,2,8,128]{3,2,1,0:T(8,128)} %get-tuple-element.28), channel_id=1, source_target_pairs={{0,96},{32,128},{64,160},{96,192},{128,224},{160,0},{192,32},{224,... | collective-permute-start | bytes 319496 | tf_op jit(solution)/shard_map/ppermute | solution.py:557
  49.9 18.3 %collective-permute-start.8 = (f32[13,2,8,128]{3,2,1,0:T(8,128)}, f32[13,2,8,128]{3,2,1,0:T(8,128)}, u32[]{:S(2)}, u32[]{:S(2)}) collective-permute-start(f32[13,2,8,128]{3,2,1,0:T(8,128)} %get-tuple-element.29), channel_id=1, source_target_pairs={{0,160},{32,192},{64,224},{96,0},{128,32},{160,64},{192,96},{224,1... | collective-permute-start | bytes 319496 | tf_op jit(solution)/shard_map/ppermute | solution.py:557
  60.8 7.7 %collective-permute-start.9 = (f32[13,2,8,128]{3,2,1,0:T(8,128)}, f32[13,2,8,128]{3,2,1,0:T(8,128)}, u32[]{:S(2)}, u32[]{:S(2)}) collective-permute-start(f32[13,2,8,128]{3,2,1,0:T(8,128)} %get-tuple-element.32), channel_id=1, source_target_pairs={{0,64},{32,96},{64,128},{96,160},{128,192},{160,224},{192,0},{224,... | collective-permute-start | bytes 319496 | tf_op jit(solution)/shard_map/ppermute | solution.py:557
  62.1 6.6 %collective-permute-start.10 = (f32[13,2,8,128]{3,2,1,0:T(8,128)}, f32[13,2,8,128]{3,2,1,0:T(8,128)}, u32[]{:S(2)}, u32[]{:S(2)}) collective-permute-start(f32[13,2,8,128]{3,2,1,0:T(8,128)} %get-tuple-element.33), channel_id=1, source_target_pairs={{0,192},{32,224},{64,0},{96,32},{128,64},{160,96},{192,128},{224,1... | collective-permute-start | bytes 319496 | tf_op jit(solution)/shard_map/ppermute | solution.py:557
  65.0 6.2 %collective-permute-start.11 = (f32[13,2,8,128]{3,2,1,0:T(8,128)}, f32[13,2,8,128]{3,2,1,0:T(8,128)}, u32[]{:S(2)}, u32[]{:S(2)}) collective-permute-start(f32[13,2,8,128]{3,2,1,0:T(8,128)} %get-tuple-element.34), channel_id=1, source_target_pairs={{0,32},{32,64},{64,96},{96,128},{128,160},{160,192},{192,224},{224... | collective-permute-start | bytes 319496 | tf_op jit(solution)/shard_map/ppermute | solution.py:557
  65.8 6.9 %collective-permute-start.12 = (f32[13,2,8,128]{3,2,1,0:T(8,128)}, f32[13,2,8,128]{3,2,1,0:T(8,128)}, u32[]{:S(2)}, u32[]{:S(2)}) collective-permute-start(f32[13,2,8,128]{3,2,1,0:T(8,128)} %get-tuple-element.35), channel_id=1, source_target_pairs={{0,224},{32,0},{64,32},{96,64},{128,96},{160,128},{192,160},{224,1... | collective-permute-start | bytes 319496 | tf_op jit(solution)/shard_map/ppermute | solution.py:557
  74.7 8.0 %collective-permute-start.16 = (f32[13,2,8,128]{3,2,1,0:T(8,128)}, f32[13,2,8,128]{3,2,1,0:T(8,128)S(1)}, u32[]{:S(2)}, u32[]{:S(2)}) collective-permute-start(f32[13,2,8,128]{3,2,1,0:T(8,128)} %fold.1.refs_0_), channel_id=1, source_target_pairs={{0,192},{32,224},{64,0},{96,32},{128,64},{160,96},{192,128},{224,1... | collective-permute-start | bytes 319496 | tf_op jit(solution)/shard_map/ppermute | solution.py:570
  76.4 10.3 %collective-permute-start.15 = (f32[13,2,8,128]{3,2,1,0:T(8,128)}, f32[13,2,8,128]{3,2,1,0:T(8,128)S(1)}, u32[]{:S(2)}, u32[]{:S(2)}) collective-permute-start(f32[13,2,8,128]{3,2,1,0:T(8,128)} %fold.1.refs_0_), channel_id=1, source_target_pairs={{0,64},{32,96},{64,128},{96,160},{128,192},{160,224},{192,0},{224,... | collective-permute-start | bytes 319496 | tf_op jit(solution)/shard_map/ppermute | solution.py:570
  77.6 10.5 %collective-permute-start.14 = (f32[13,2,8,128]{3,2,1,0:T(8,128)}, f32[13,2,8,128]{3,2,1,0:T(8,128)S(1)}, u32[]{:S(2)}, u32[]{:S(2)}) collective-permute-start(f32[13,2,8,128]{3,2,1,0:T(8,128)} %fold.1.refs_0_), channel_id=1, source_target_pairs={{0,224},{32,0},{64,32},{96,64},{128,96},{160,128},{192,160},{224,1... | collective-permute-start | bytes 319496 | tf_op jit(solution)/shard_map/ppermute | solution.py:570
  82.7 6.1 %collective-permute-start.13 = (f32[13,2,8,128]{3,2,1,0:T(8,128)}, f32[13,2,8,128]{3,2,1,0:T(8,128)S(1)}, u32[]{:S(2)}, u32[]{:S(2)}) collective-permute-start(f32[13,2,8,128]{3,2,1,0:T(8,128)} %fold.1.refs_0_), channel_id=1, source_target_pairs={{0,32},{32,64},{64,96},{96,128},{128,160},{160,192},{192,224},{224... | collective-permute-start | bytes 319496 | tf_op jit(solution)/shard_map/ppermute | solution.py:570
  82.7 0.7 copy-start
  83.3 5.5 %collective-permute-start.18 = (f32[13,2,8,128]{3,2,1,0:T(8,128)S(1)}, f32[13,2,8,128]{3,2,1,0:T(8,128)S(1)}, u32[]{:S(2)}, u32[]{:S(2)}) collective-permute-start(f32[13,2,8,128]{3,2,1,0:T(8,128)S(1)} %collective-permute-done.16.refs_4_), channel_id=1, source_target_pairs={{0,224},{32,0},{64,32},{96,64},{128,96},{160,128},{192,160},{224,1... | collective-permute-start | bytes 319496 | tf_op jit(solution)/shard_map/ppermute | solution.py:572
  86.6 2.2 %copy-start.1 = (f32[13,2,8,128]{3,2,1,0:T(8,128)}, f32[13,2,8,128]{3,2,1,0:T(8,128)S(1)}, u32[]{:S(2)}) copy-start(f32[13,2,8,128]{3,2,1,0:T(8,128)S(1)} %collective-permute-done.15.refs_3_) | copy-start | bytes 319492
  86.6 7.1 %collective-permute-start.19 = (f32[13,2,8,128]{3,2,1,0:T(8,128)S(1)}, f32[13,2,8,128]{3,2,1,0:T(8,128)S(1)}, u32[]{:S(2)}, u32[]{:S(2)}) collective-permute-start(f32[13,2,8,128]{3,2,1,0:T(8,128)S(1)} %collective-permute-done.15.refs_3_), channel_id=1, source_target_pairs={{0,64},{32,96},{64,128},{96,160},{128,192},{160,224},{192,0},{224,... | collective-permute-start | bytes 319496 | tf_op jit(solution)/shard_map/ppermute | solution.py:572
  86.6 9.2 %collective-permute-start.17 = (f32[13,2,8,128]{3,2,1,0:T(8,128)S(1)}, f32[13,2,8,128]{3,2,1,0:T(8,128)}, u32[]{:S(2)}, u32[]{:S(2)}) collective-permute-start(f32[13,2,8,128]{3,2,1,0:T(8,128)S(1)} %collective-permute-done.15.refs_3_), channel_id=1, source_target_pairs={{0,32},{32,64},{64,96},{96,128},{128,160},{160,192},{192,224},{224... | collective-permute-start | bytes 319496 | tf_op jit(solution)/shard_map/ppermute | solution.py:572
  88.1 5.6 %copy-start.2 = (f32[13,2,8,128]{3,2,1,0:T(8,128)}, f32[13,2,8,128]{3,2,1,0:T(8,128)S(1)}, u32[]{:S(2)}) copy-start(f32[13,2,8,128]{3,2,1,0:T(8,128)S(1)} %collective-permute-done.14.refs_2_) | copy-start | bytes 319492
  88.8 4.9 %copy-start.3 = (f32[13,2,8,128]{3,2,1,0:T(8,128)}, f32[13,2,8,128]{3,2,1,0:T(8,128)S(1)}, u32[]{:S(2)}) copy-start(f32[13,2,8,128]{3,2,1,0:T(8,128)S(1)} %collective-permute-done.13.refs_1_) | copy-start | bytes 319492
  88.8 4.9 %copy-start.4 = (f32[13,2,8,128]{3,2,1,0:T(8,128)}, f32[13,2,8,128]{3,2,1,0:T(8,128)S(1)}, u32[]{:S(2)}) copy-start(f32[13,2,8,128]{3,2,1,0:T(8,128)S(1)} %collective-permute-done.18.refs_6_) | copy-start | bytes 319492
  93.7 0.6 copy-start.5

commit v13 on v10

--- a/solution.py
+++ b/solution.py
@@ -174,7 +174,7 @@
 
 
 SHIFTS = (4, 3, 5, 2, 6, 1, 7, 0)
-FAR = 3
+FAR = 4
 
 
 def render(

time: 99.2 us -> 98.7 us (level)
  starting transfers between devices: 45.2 us -> 43.8 us
  waiting for transfers between devices: 15.7 us -> 16.7 us
    pallas_call x1, Pallas kernels: 7.72 us -> 6.6 us  [per_device(): pl.pallas_call(functools.partial(render_rest, alpha_top=alpha_top), out_s...]
    ppermute x7, waiting for transfers between devices: 3.58 us -> 4.68 us  [per_device(): lax.ppermute(value, 'depth', ring('depth', by))]
    pallas_call x1, Pallas kernels: 18.3 us -> 19.3 us  [per_device(): pl.pallas_call(functools.partial(render, alpha_top=alpha_top), out_shape=...]
  transfers between devices with their start and end apart: 20 -> 20, of which waited for: 11 -> 9; matrix products, arithmetic and copies ran while one was open for 1% -> 1% of each run, Pallas kernels for 10% -> 9%
where the time goes in v13:
time: 98.7 us; the launch traced here: 97.7 us
  starting transfers between devices  43.8 us (44%)
  Pallas kernels  34.4 us (35%)
  waiting for transfers between devices  16.7 us (17%)
  local copies, waits for them, and re-layouts  1.93 us (2%)
    pallas_call x1, Pallas kernels, per_device(): pl.pallas_call(functools.partial(render, alpha_top=alpha_top), out_shape=...  19.3 us
    ppermute x7, starting transfers between devices, per_device(): lax.ppermute(value, 'depth', ring('depth', by))  17.1 us
    ppermute x4, starting transfers between devices, per_device(): known[by] = lax.ppermute(own, 'depth', ring('depth', by))  7.97 us
    pallas_call x1, Pallas kernels, per_device(): pl.pallas_call(functools.partial(render_rest, alpha_top=alpha_top), out_s...  6.6 us
    ppermute x3, waiting for transfers between devices, per_device(): known[held + by] = lax.ppermute(known[held], 'depth', ring('depth', by))  5.91 us
    ppermute x1, starting transfers between devices, per_device(): bottom_corner = lax.ppermute(corner_up, 'height', ring('height', -1))  5.05 us
    ppermute x1, starting transfers between devices, per_device(): bottom = lax.ppermute(up, 'height', ring('height', -1))  5.05 us
    ppermute x7, waiting for transfers between devices, per_device(): lax.ppermute(value, 'depth', ring('depth', by))  4.68 us
  transfers between devices with their start and end apart: 20, of which 9 were waited for; matrix products, arithmetic and copies ran while one was open for 1% of the time, Pallas kernels for 9%

profile of v13, /device:TPU:0, one launch (start us, length us, event | category | flops | bytes accessed | tf_op | source)
XLA Modules:
  0.0 97.7 jit_solution(2487906532771901007)
XLA Ops:
  0.0 2.6 %pack.1 = (f32[16,96,128]{2,1,0:T(8,128)}, f32[16,96,128]{2,1,0:T(8,128)}, f32[3,16,8,128]{3,2,1,0:T(8,128)}, f32[3,16,8,128]{3,2,1,0:T(8,128)}) custom-call(f32[32,16,8,128]{3,2,1,0:T(8,128)} %bitcast.27), custom_call_target="tpu_custom_call" | custom-call | tf_op jit(solution)/shard_map/pack/pallas_call | solution.py:456
  2.6 0.1 collective-permute-start.2
  2.7 5.1 %collective-permute-start.3 = (f32[16,96,128]{2,1,0:T(8,128)}, f32[16,96,128]{2,1,0:T(8,128)}, u32[]{:S(2)}, u32[]{:S(2)}) collective-permute-start(f32[16,96,128]{2,1,0:T(8,128)} %get-tuple-element.24), channel_id=1, source_target_pairs={{0,31},{1,0},{2,1},{3,2},{4,3},{5,4},{6,5},{7,6},{8,7},{9,8},{10,9... | collective-permute-start | bytes 2359304 | tf_op jit(solution)/shard_map/ppermute | solution.py:475
  7.7 0.2 collective-permute-start
  7.9 3.9 %collective-permute-start.1 = (f32[3,16,8,128]{3,2,1,0:T(8,128)}, f32[3,16,8,128]{3,2,1,0:T(8,128)}, u32[]{:S(2)}, u32[]{:S(2)}) collective-permute-start(f32[3,16,8,128]{3,2,1,0:T(8,128)} %get-tuple-element.22), channel_id=1, source_target_pairs={{0,224},{32,0},{64,32},{96,64},{128,96},{160,128},{192,160},{224,1... | collective-permute-start | bytes 589832 | tf_op jit(solution)/shard_map/ppermute | solution.py:473
  11.8 0.6 stack.87.tile_ref
  12.5 3.3 %collective-permute-done.low_ref = f32[3,16,8,128]{3,2,1,0:T(8,128)} collective-permute-done((f32[3,16,8,128]{3,2,1,0:T(8,128)}, f32[3,16,8,128]{3,2,1,0:T(8,128)}, u32[]{:S(2)}, u32[]{:S(2)}) %collective-permute-start) | collective-permute-done | bytes 196640 | tf_op jit(solution)/shard_map/ppermute | solution.py:472
  15.8 0.0 collective-permute-done.1.high_ref
  15.8 1.7 %pack_corners.1 = (f32[16,8,128]{2,1,0:T(8,128)}, f32[16,8,128]{2,1,0:T(8,128)}) custom-call(f32[3,16,8,128]{3,2,1,0:T(8,128)} %collective-permute-done.low_ref, f32[3,16,8,128]{3,2,1,0:T(8,128)} %collective-permute-done.1.high_ref), custom_call_target="tpu_custom_call" | custom-call | flops 400000000 | bytes 80000000 | tf_op jit(solution)/shard_map/pack_corners/pallas_call | solution.py:476
  17.5 0.1 collective-permute-start.4
  17.6 5.1 %collective-permute-start.5 = (f32[16,8,128]{2,1,0:T(8,128)}, f32[16,8,128]{2,1,0:T(8,128)}, u32[]{:S(2)}, u32[]{:S(2)}) collective-permute-start(f32[16,8,128]{2,1,0:T(8,128)} %get-tuple-element.26), channel_id=1, source_target_pairs={{0,31},{1,0},{2,1},{3,2},{4,3},{5,4},{6,5},{7,6},{8,7},{9,8},{10,9... | collective-permute-start | bytes 196616 | tf_op jit(solution)/shard_map/ppermute | solution.py:489
  22.7 0.7 add_convert_fusion.edge_ref
  23.3 1.6 %collective-permute-done.4.top_corner_ref = f32[16,8,128]{2,1,0:T(8,128)} collective-permute-done((f32[16,8,128]{2,1,0:T(8,128)}, f32[16,8,128]{2,1,0:T(8,128)}, u32[]{:S(2)}, u32[]{:S(2)}) %collective-permute-start.4) | collective-permute-done | bytes 65568 | tf_op jit(solution)/shard_map/ppermute | solution.py:488
  24.9 0.0 collective-permute-done.5.bottom_corner_ref
  24.9 0.0 collective-permute-done.2.top_ref
  24.9 0.0 collective-permute-done.3.bottom_ref
  24.9 19.3 %render.1 = (f32[13,2,8,128]{3,2,1,0:T(8,128)}, f32[13,2,8,128]{3,2,1,0:T(8,128)}, f32[13,2,8,128]{3,2,1,0:T(8,128)}, f32[13,2,8,128]{3,2,1,0:T(8,128)}, f32[8,3...) custom-call(f32[4]{0:T(128)} %add_convert_fusion.edge_ref, s32[16]{0:T(128)} %stack.87.tile_ref, f32[3,4]{1,0:T(4,128)} %colour_ref.3, ...), custom_call_target="tpu_custom_call" | custom-call | tf_op jit(solution)/shard_map/render/pallas_call | solution.py:497
  44.3 4.7 %collective-permute-start.6 = (f32[13,2,8,128]{3,2,1,0:T(8,128)}, f32[13,2,8,128]{3,2,1,0:T(8,128)}, u32[]{:S(2)}, u32[]{:S(2)}) collective-permute-start(f32[13,2,8,128]{3,2,1,0:T(8,128)} %get-tuple-element.27), channel_id=1, source_target_pairs={{0,128},{32,160},{64,192},{96,224},{128,0},{160,32},{192,64},{224,... | collective-permute-start | bytes 319496 | tf_op jit(solution)/shard_map/ppermute | solution.py:554
  48.9 1.9 %collective-permute-start.7 = (f32[13,2,8,128]{3,2,1,0:T(8,128)}, f32[13,2,8,128]{3,2,1,0:T(8,128)}, u32[]{:S(2)}, u32[]{:S(2)}) collective-permute-start(f32[13,2,8,128]{3,2,1,0:T(8,128)} %get-tuple-element.28), channel_id=1, source_target_pairs={{0,96},{32,128},{64,160},{96,192},{128,224},{160,0},{192,32},{224,... | collective-permute-start | bytes 319496 | tf_op jit(solution)/shard_map/ppermute | solution.py:554
  50.9 3.1 %collective-permute-start.8 = (f32[13,2,8,128]{3,2,1,0:T(8,128)}, f32[13,2,8,128]{3,2,1,0:T(8,128)}, u32[]{:S(2)}, u32[]{:S(2)}) collective-permute-start(f32[13,2,8,128]{3,2,1,0:T(8,128)} %get-tuple-element.29), channel_id=1, source_target_pairs={{0,160},{32,192},{64,224},{96,0},{128,32},{160,64},{192,96},{224,1... | collective-permute-start | bytes 319496 | tf_op jit(solution)/shard_map/ppermute | solution.py:554
  54.0 1.3 %collective-permute-start.9 = (f32[13,2,8,128]{3,2,1,0:T(8,128)}, f32[13,2,8,128]{3,2,1,0:T(8,128)}, u32[]{:S(2)}, u32[]{:S(2)}) collective-permute-start(f32[13,2,8,128]{3,2,1,0:T(8,128)} %get-tuple-element.30), channel_id=1, source_target_pairs={{0,64},{32,96},{64,128},{96,160},{128,192},{160,224},{192,0},{224,... | collective-permute-start | bytes 319496 | tf_op jit(solution)/shard_map/ppermute | solution.py:554
  55.3 6.6 %render_rest.1 = (f32[13,2,8,128]{3,2,1,0:T(8,128)}, f32[13,2,8,128]{3,2,1,0:T(8,128)}, f32[13,2,8,128]{3,2,1,0:T(8,128)}, f32[13,2,8,128]{3,2,1,0:T(8,128)}) custom-call(f32[3,4]{1,0:T(4,128)} %colour_ref.3, f32[4]{0:T(128)} %opacity_ref.3, f32[4,3]{1,0:T(4,128)} %dir_ref.3, f32[4,3]{1,0:T(4,128)} %light_ref.3, ...), custom_call_target="tpu_custom_call" | custom-call | flops 50000000 | bytes 20000000 | tf_op jit(solution)/shard_map/render_rest/pallas_call | solution.py:535
  61.9 2.9 %collective-permute-start.10 = (f32[13,2,8,128]{3,2,1,0:T(8,128)}, f32[13,2,8,128]{3,2,1,0:T(8,128)}, u32[]{:S(2)}, u32[]{:S(2)}) collective-permute-start(f32[13,2,8,128]{3,2,1,0:T(8,128)} %get-tuple-element.33), channel_id=1, source_target_pairs={{0,192},{32,224},{64,0},{96,32},{128,64},{160,96},{192,128},{224,1... | collective-permute-start | bytes 319496 | tf_op jit(solution)/shard_map/ppermute | solution.py:554
  64.8 0.0 collective-permute-done.6.refs_0_
  64.8 0.8 collective-permute-start.11
  65.6 0.0 collective-permute-done.7.refs_1_
  65.6 2.4 %collective-permute-start.12 = (f32[13,2,8,128]{3,2,1,0:T(8,128)}, f32[13,2,8,128]{3,2,1,0:T(8,128)}, u32[]{:S(2)}, u32[]{:S(2)}) collective-permute-start(f32[13,2,8,128]{3,2,1,0:T(8,128)} %get-tuple-element.35), channel_id=1, source_target_pairs={{0,224},{32,0},{64,32},{96,64},{128,96},{160,128},{192,160},{224,1... | collective-permute-start | bytes 319496 | tf_op jit(solution)/shard_map/ppermute | solution.py:554
  68.0 0.0 collective-permute-done.8.refs_2_
  68.0 0.0 collective-permute-done.9.refs_3_
  68.1 0.5 collective-permute-done.10.refs_4_
  68.5 2.5 %collective-permute-done.11.refs_5_ = f32[13,2,8,128]{3,2,1,0:T(8,128)} collective-permute-done((f32[13,2,8,128]{3,2,1,0:T(8,128)}, f32[13,2,8,128]{3,2,1,0:T(8,128)}, u32[]{:S(2)}, u32[]{:S(2)}) %collective-permute-start.11) | collective-permute-done | bytes 106528 | tf_op jit(solution)/shard_map/ppermute | solution.py:554
  71.0 1.7 %collective-permute-done.12.refs_6_ = f32[13,2,8,128]{3,2,1,0:T(8,128)} collective-permute-done((f32[13,2,8,128]{3,2,1,0:T(8,128)}, f32[13,2,8,128]{3,2,1,0:T(8,128)}, u32[]{:S(2)}, u32[]{:S(2)}) %collective-permute-start.12) | collective-permute-done | bytes 106528 | tf_op jit(solution)/shard_map/ppermute | solution.py:554
  72.7 2.0 %fold.1.refs_0_ = f32[13,2,8,128]{3,2,1,0:T(8,128)} custom-call(s32[1]{0:T(128)} %bitcast.place_ref, f32[13,2,8,128]{3,2,1,0:T(8,128)} %collective-permute-done.6.refs_0_, f32[13,2,8,128]{3,2,1,0:T(8,128)} %collective-permute-done.7.refs_1_, f32[13,2,8,128]{3,2,1,0:T(8,128)} %collective-permute-done.8.refs_2_, ...), custom_call_target="tpu_custom_call" | custom-call | tf_op jit(solution)/shard_map/fold/pallas_call | solution.py:557
  74.7 1.6 %collective-permute-start.16 = (f32[13,2,8,128]{3,2,1,0:T(8,128)}, f32[13,2,8,128]{3,2,1,0:T(8,128)S(1)}, u32[]{:S(2)}, u32[]{:S(2)}) collective-permute-start(f32[13,2,8,128]{3,2,1,0:T(8,128)} %fold.1.refs_0_), channel_id=1, source_target_pairs={{0,192},{32,224},{64,0},{96,32},{128,64},{160,96},{192,128},{224,1... | collective-permute-start | bytes 319496 | tf_op jit(solution)/shard_map/ppermute | solution.py:567
  76.3 1.3 %collective-permute-start.15 = (f32[13,2,8,128]{3,2,1,0:T(8,128)}, f32[13,2,8,128]{3,2,1,0:T(8,128)S(1)}, u32[]{:S(2)}, u32[]{:S(2)}) collective-permute-start(f32[13,2,8,128]{3,2,1,0:T(8,128)} %fold.1.refs_0_), channel_id=1, source_target_pairs={{0,64},{32,96},{64,128},{96,160},{128,192},{160,224},{192,0},{224,... | collective-permute-start | bytes 319496 | tf_op jit(solution)/shard_map/ppermute | solution.py:567
  77.6 5.0 %collective-permute-start.14 = (f32[13,2,8,128]{3,2,1,0:T(8,128)}, f32[13,2,8,128]{3,2,1,0:T(8,128)S(1)}, u32[]{:S(2)}, u32[]{:S(2)}) collective-permute-start(f32[13,2,8,128]{3,2,1,0:T(8,128)} %fold.1.refs_0_), channel_id=1, source_target_pairs={{0,224},{32,0},{64,32},{96,64},{128,96},{160,128},{192,160},{224,1... | collective-permute-start | bytes 319496 | tf_op jit(solution)/shard_map/ppermute | solution.py:567
  82.7 0.0 collective-permute-start.13
  82.7 0.0 collective-permute-done.16.refs_4_
  82.7 0.6 copy-done
  83.3 3.2 %collective-permute-start.18 = (f32[13,2,8,128]{3,2,1,0:T(8,128)S(1)}, f32[13,2,8,128]{3,2,1,0:T(8,128)S(1)}, u32[]{:S(2)}, u32[]{:S(2)}) collective-permute-start(f32[13,2,8,128]{3,2,1,0:T(8,128)S(1)} %collective-permute-done.16.refs_4_), channel_id=1, source_target_pairs={{0,224},{32,0},{64,32},{96,64},{128,96},{160,128},{192,160},{224,1... | collective-permute-start | bytes 319496 | tf_op jit(solution)/shard_map/ppermute | solution.py:569
  86.6 1.0 %collective-permute-start.17 = (f32[13,2,8,128]{3,2,1,0:T(8,128)S(1)}, f32[13,2,8,128]{3,2,1,0:T(8,128)}, u32[]{:S(2)}, u32[]{:S(2)}) collective-permute-start(f32[13,2,8,128]{3,2,1,0:T(8,128)S(1)} %collective-permute-done.15.refs_3_), channel_id=1, source_target_pairs={{0,32},{32,64},{64,96},{96,128},{128,160},{160,192},{192,224},{224... | collective-permute-start | bytes 319496 | tf_op jit(solution)/shard_map/ppermute | solution.py:569
  87.6 0.0 collective-permute-done.14.refs_2_
  87.6 1.2 %collective-permute-done.13.refs_1_ = f32[13,2,8,128]{3,2,1,0:T(8,128)S(1)} collective-permute-done((f32[13,2,8,128]{3,2,1,0:T(8,128)}, f32[13,2,8,128]{3,2,1,0:T(8,128)S(1)}, u32[]{:S(2)}, u32[]{:S(2)}) %collective-permute-start.13) | collective-permute-done | bytes 106528 | tf_op jit(solution)/shard_map/ppermute | solution.py:567
  88.8 0.1 collective-permute-done.18.refs_6_
  88.9 4.7 %collective-permute-done.19.refs_7_ = f32[13,2,8,128]{3,2,1,0:T(8,128)S(1)} collective-permute-done((f32[13,2,8,128]{3,2,1,0:T(8,128)S(1)}, f32[13,2,8,128]{3,2,1,0:T(8,128)S(1)}, u32[]{:S(2)}, u32[]{:S(2)}) %collective-permute-start.19) | collective-permute-done | bytes 106528 | tf_op jit(solution)/shard_map/ppermute | solution.py:569
  93.6 0.6 copy-done.5
  94.3 1.1 %collective-permute-done.17.refs_5_ = f32[13,2,8,128]{3,2,1,0:T(8,128)} collective-permute-done((f32[13,2,8,128]{3,2,1,0:T(8,128)S(1)}, f32[13,2,8,128]{3,2,1,0:T(8,128)}, u32[]{:S(2)}, u32[]{:S(2)}) %collective-permute-start.17) | collective-permute-done | bytes 106528 | tf_op jit(solution)/shard_map/ppermute | solution.py:569
  95.4 2.2 %spread.1 = f32[13,16,8,128]{3,2,1,0:T(8,128)} custom-call(s32[1]{0:T(128)} %bitcast.place_ref, f32[13,2,8,128]{3,2,1,0:T(8,128)} %fold.1.refs_0_, f32[13,2,8,128]{3,2,1,0:T(8,128)} %copy-done.3, f32[13,2,8,128]{3,2,1,0:T(8,128)} %copy-done.2, f32[13,2,8,128]{3,2,1,0:T(8,128)} %copy-done.1, f32[13,2,8,128]{3,2,1,0:T(8,128)} %copy-done, ...), custom_call_target="tpu_custom_call" | custom-call | tf_op jit(solution)/shard_map/spread/pallas_call | solution.py:570
  (12 shorter events, 0.0 us)
Async XLA Ops:
  2.6 22.4 %collective-permute-start.2 = (f32[16,96,128]{2,1,0:T(8,128)}, f32[16,96,128]{2,1,0:T(8,128)}, u32[]{:S(2)}, u32[]{:S(2)}) collective-permute-start(f32[16,96,128]{2,1,0:T(8,128)} %get-tuple-element.23), channel_id=1, source_target_pairs={{0,1},{1,2},{2,3},{3,4},{4,5},{5,6},{6,7},{7,8},{8,9},{9,10},{10,1... | collective-permute-start | bytes 2359304 | tf_op jit(solution)/shard_map/ppermute | solution.py:474
  2.7 22.3 %collective-permute-start.3 = (f32[16,96,128]{2,1,0:T(8,128)}, f32[16,96,128]{2,1,0:T(8,128)}, u32[]{:S(2)}, u32[]{:S(2)}) collective-permute-start(f32[16,96,128]{2,1,0:T(8,128)} %get-tuple-element.24), channel_id=1, source_target_pairs={{0,31},{1,0},{2,1},{3,2},{4,3},{5,4},{6,5},{7,6},{8,7},{9,8},{10,9... | collective-permute-start | bytes 2359304 | tf_op jit(solution)/shard_map/ppermute | solution.py:475
  7.7 8.1 %collective-permute-start = (f32[3,16,8,128]{3,2,1,0:T(8,128)}, f32[3,16,8,128]{3,2,1,0:T(8,128)}, u32[]{:S(2)}, u32[]{:S(2)}) collective-permute-start(f32[3,16,8,128]{3,2,1,0:T(8,128)} %get-tuple-element.21), channel_id=1, source_target_pairs={{0,32},{32,64},{64,96},{96,128},{128,160},{160,192},{192,224},{224... | collective-permute-start | bytes 589832 | tf_op jit(solution)/shard_map/ppermute | solution.py:472
  7.9 7.9 %collective-permute-start.1 = (f32[3,16,8,128]{3,2,1,0:T(8,128)}, f32[3,16,8,128]{3,2,1,0:T(8,128)}, u32[]{:S(2)}, u32[]{:S(2)}) collective-permute-start(f32[3,16,8,128]{3,2,1,0:T(8,128)} %get-tuple-element.22), channel_id=1, source_target_pairs={{0,224},{32,0},{64,32},{96,64},{128,96},{160,128},{192,160},{224,1... | collective-permute-start | bytes 589832 | tf_op jit(solution)/shard_map/ppermute | solution.py:473
  17.5 7.4 %collective-permute-start.4 = (f32[16,8,128]{2,1,0:T(8,128)}, f32[16,8,128]{2,1,0:T(8,128)}, u32[]{:S(2)}, u32[]{:S(2)}) collective-permute-start(f32[16,8,128]{2,1,0:T(8,128)} %get-tuple-element.25), channel_id=1, source_target_pairs={{0,1},{1,2},{2,3},{3,4},{4,5},{5,6},{6,7},{7,8},{8,9},{9,10},{10,1... | collective-permute-start | bytes 196616 | tf_op jit(solution)/shard_map/ppermute | solution.py:488
  17.6 7.3 %collective-permute-start.5 = (f32[16,8,128]{2,1,0:T(8,128)}, f32[16,8,128]{2,1,0:T(8,128)}, u32[]{:S(2)}, u32[]{:S(2)}) collective-permute-start(f32[16,8,128]{2,1,0:T(8,128)} %get-tuple-element.26), channel_id=1, source_target_pairs={{0,31},{1,0},{2,1},{3,2},{4,3},{5,4},{6,5},{7,6},{8,7},{9,8},{10,9... | collective-permute-start | bytes 196616 | tf_op jit(solution)/shard_map/ppermute | solution.py:489
  44.3 20.5 %collective-permute-start.6 = (f32[13,2,8,128]{3,2,1,0:T(8,128)}, f32[13,2,8,128]{3,2,1,0:T(8,128)}, u32[]{:S(2)}, u32[]{:S(2)}) collective-permute-start(f32[13,2,8,128]{3,2,1,0:T(8,128)} %get-tuple-element.27), channel_id=1, source_target_pairs={{0,128},{32,160},{64,192},{96,224},{128,0},{160,32},{192,64},{224,... | collective-permute-start | bytes 319496 | tf_op jit(solution)/shard_map/ppermute | solution.py:554
  48.9 16.7 %collective-permute-start.7 = (f32[13,2,8,128]{3,2,1,0:T(8,128)}, f32[13,2,8,128]{3,2,1,0:T(8,128)}, u32[]{:S(2)}, u32[]{:S(2)}) collective-permute-start(f32[13,2,8,128]{3,2,1,0:T(8,128)} %get-tuple-element.28), channel_id=1, source_target_pairs={{0,96},{32,128},{64,160},{96,192},{128,224},{160,0},{192,32},{224,... | collective-permute-start | bytes 319496 | tf_op jit(solution)/shard_map/ppermute | solution.py:554
  50.9 17.2 %collective-permute-start.8 = (f32[13,2,8,128]{3,2,1,0:T(8,128)}, f32[13,2,8,128]{3,2,1,0:T(8,128)}, u32[]{:S(2)}, u32[]{:S(2)}) collective-permute-start(f32[13,2,8,128]{3,2,1,0:T(8,128)} %get-tuple-element.29), channel_id=1, source_target_pairs={{0,160},{32,192},{64,224},{96,0},{128,32},{160,64},{192,96},{224,1... | collective-permute-start | bytes 319496 | tf_op jit(solution)/shard_map/ppermute | solution.py:554
  54.0 14.1 %collective-permute-start.9 = (f32[13,2,8,128]{3,2,1,0:T(8,128)}, f32[13,2,8,128]{3,2,1,0:T(8,128)}, u32[]{:S(2)}, u32[]{:S(2)}) collective-permute-start(f32[13,2,8,128]{3,2,1,0:T(8,128)} %get-tuple-element.30), channel_id=1, source_target_pairs={{0,64},{32,96},{64,128},{96,160},{128,192},{160,224},{192,0},{224,... | collective-permute-start | bytes 319496 | tf_op jit(solution)/shard_map/ppermute | solution.py:554
  61.9 6.7 %collective-permute-start.10 = (f32[13,2,8,128]{3,2,1,0:T(8,128)}, f32[13,2,8,128]{3,2,1,0:T(8,128)}, u32[]{:S(2)}, u32[]{:S(2)}) collective-permute-start(f32[13,2,8,128]{3,2,1,0:T(8,128)} %get-tuple-element.33), channel_id=1, source_target_pairs={{0,192},{32,224},{64,0},{96,32},{128,64},{160,96},{192,128},{224,1... | collective-permute-start | bytes 319496 | tf_op jit(solution)/shard_map/ppermute | solution.py:554
  64.8 6.2 %collective-permute-start.11 = (f32[13,2,8,128]{3,2,1,0:T(8,128)}, f32[13,2,8,128]{3,2,1,0:T(8,128)}, u32[]{:S(2)}, u32[]{:S(2)}) collective-permute-start(f32[13,2,8,128]{3,2,1,0:T(8,128)} %get-tuple-element.34), channel_id=1, source_target_pairs={{0,32},{32,64},{64,96},{96,128},{128,160},{160,192},{192,224},{224... | collective-permute-start | bytes 319496 | tf_op jit(solution)/shard_map/ppermute | solution.py:554
  65.6 7.1 %collective-permute-start.12 = (f32[13,2,8,128]{3,2,1,0:T(8,128)}, f32[13,2,8,128]{3,2,1,0:T(8,128)}, u32[]{:S(2)}, u32[]{:S(2)}) collective-permute-start(f32[13,2,8,128]{3,2,1,0:T(8,128)} %get-tuple-element.35), channel_id=1, source_target_pairs={{0,224},{32,0},{64,32},{96,64},{128,96},{160,128},{192,160},{224,1... | collective-permute-start | bytes 319496 | tf_op jit(solution)/shard_map/ppermute | solution.py:554
  74.7 8.0 %collective-permute-start.16 = (f32[13,2,8,128]{3,2,1,0:T(8,128)}, f32[13,2,8,128]{3,2,1,0:T(8,128)S(1)}, u32[]{:S(2)}, u32[]{:S(2)}) collective-permute-start(f32[13,2,8,128]{3,2,1,0:T(8,128)} %fold.1.refs_0_), channel_id=1, source_target_pairs={{0,192},{32,224},{64,0},{96,32},{128,64},{160,96},{192,128},{224,1... | collective-permute-start | bytes 319496 | tf_op jit(solution)/shard_map/ppermute | solution.py:567
  76.3 10.3 %collective-permute-start.15 = (f32[13,2,8,128]{3,2,1,0:T(8,128)}, f32[13,2,8,128]{3,2,1,0:T(8,128)S(1)}, u32[]{:S(2)}, u32[]{:S(2)}) collective-permute-start(f32[13,2,8,128]{3,2,1,0:T(8,128)} %fold.1.refs_0_), channel_id=1, source_target_pairs={{0,64},{32,96},{64,128},{96,160},{128,192},{160,224},{192,0},{224,... | collective-permute-start | bytes 319496 | tf_op jit(solution)/shard_map/ppermute | solution.py:567
  77.6 10.0 %collective-permute-start.14 = (f32[13,2,8,128]{3,2,1,0:T(8,128)}, f32[13,2,8,128]{3,2,1,0:T(8,128)S(1)}, u32[]{:S(2)}, u32[]{:S(2)}) collective-permute-start(f32[13,2,8,128]{3,2,1,0:T(8,128)} %fold.1.refs_0_), channel_id=1, source_target_pairs={{0,224},{32,0},{64,32},{96,64},{128,96},{160,128},{192,160},{224,1... | collective-permute-start | bytes 319496 | tf_op jit(solution)/shard_map/ppermute | solution.py:567
  82.7 6.1 %collective-permute-start.13 = (f32[13,2,8,128]{3,2,1,0:T(8,128)}, f32[13,2,8,128]{3,2,1,0:T(8,128)S(1)}, u32[]{:S(2)}, u32[]{:S(2)}) collective-permute-start(f32[13,2,8,128]{3,2,1,0:T(8,128)} %fold.1.refs_0_), channel_id=1, source_target_pairs={{0,32},{32,64},{64,96},{96,128},{128,160},{160,192},{192,224},{224... | collective-permute-start | bytes 319496 | tf_op jit(solution)/shard_map/ppermute | solution.py:567
  82.7 0.7 copy-start
  83.3 5.5 %collective-permute-start.18 = (f32[13,2,8,128]{3,2,1,0:T(8,128)S(1)}, f32[13,2,8,128]{3,2,1,0:T(8,128)S(1)}, u32[]{:S(2)}, u32[]{:S(2)}) collective-permute-start(f32[13,2,8,128]{3,2,1,0:T(8,128)S(1)} %collective-permute-done.16.refs_4_), channel_id=1, source_target_pairs={{0,224},{32,0},{64,32},{96,64},{128,96},{160,128},{192,160},{224,1... | collective-permute-start | bytes 319496 | tf_op jit(solution)/shard_map/ppermute | solution.py:569
  86.6 2.3 %copy-start.1 = (f32[13,2,8,128]{3,2,1,0:T(8,128)}, f32[13,2,8,128]{3,2,1,0:T(8,128)S(1)}, u32[]{:S(2)}) copy-start(f32[13,2,8,128]{3,2,1,0:T(8,128)S(1)} %collective-permute-done.15.refs_3_) | copy-start | bytes 319492
  86.6 7.0 %collective-permute-start.19 = (f32[13,2,8,128]{3,2,1,0:T(8,128)S(1)}, f32[13,2,8,128]{3,2,1,0:T(8,128)S(1)}, u32[]{:S(2)}, u32[]{:S(2)}) collective-permute-start(f32[13,2,8,128]{3,2,1,0:T(8,128)S(1)} %collective-permute-done.15.refs_3_), channel_id=1, source_target_pairs={{0,64},{32,96},{64,128},{96,160},{128,192},{160,224},{192,0},{224,... | collective-permute-start | bytes 319496 | tf_op jit(solution)/shard_map/ppermute | solution.py:569
  86.6 8.8 %collective-permute-start.17 = (f32[13,2,8,128]{3,2,1,0:T(8,128)S(1)}, f32[13,2,8,128]{3,2,1,0:T(8,128)}, u32[]{:S(2)}, u32[]{:S(2)}) collective-permute-start(f32[13,2,8,128]{3,2,1,0:T(8,128)S(1)} %collective-permute-done.15.refs_3_), channel_id=1, source_target_pairs={{0,32},{32,64},{64,96},{96,128},{128,160},{160,192},{192,224},{224... | collective-permute-start | bytes 319496 | tf_op jit(solution)/shard_map/ppermute | solution.py:569
  87.6 6.0 %copy-start.2 = (f32[13,2,8,128]{3,2,1,0:T(8,128)}, f32[13,2,8,128]{3,2,1,0:T(8,128)S(1)}, u32[]{:S(2)}) copy-start(f32[13,2,8,128]{3,2,1,0:T(8,128)S(1)} %collective-permute-done.14.refs_2_) | copy-start | bytes 319492
  88.8 4.8 %copy-start.3 = (f32[13,2,8,128]{3,2,1,0:T(8,128)}, f32[13,2,8,128]{3,2,1,0:T(8,128)S(1)}, u32[]{:S(2)}) copy-start(f32[13,2,8,128]{3,2,1,0:T(8,128)S(1)} %collective-permute-done.13.refs_1_) | copy-start | bytes 319492
  88.9 4.7 %copy-start.4 = (f32[13,2,8,128]{3,2,1,0:T(8,128)}, f32[13,2,8,128]{3,2,1,0:T(8,128)S(1)}, u32[]{:S(2)}) copy-start(f32[13,2,8,128]{3,2,1,0:T(8,128)S(1)} %collective-permute-done.18.refs_6_) | copy-start | bytes 319492
  93.6 0.6 copy-start.5

commit v14 on v13

--- a/solution.py
+++ b/solution.py
@@ -174,7 +174,7 @@
 
 
 SHIFTS = (4, 3, 5, 2, 6, 1, 7, 0)
-FAR = 4
+FAR = 5
 
 
 def render(

time: 98.7 us -> 96.5 us (0.978)
  waiting for transfers between devices: 16.7 us -> 13.9 us
    ppermute x7, waiting for transfers between devices: 4.68 us -> 2.99 us  [per_device(): lax.ppermute(value, 'depth', ring('depth', by))]
    ppermute x3, starting transfers between devices: 4.28 us -> 5.61 us  [per_device(): known[held + by] = lax.ppermute(known[held], 'depth', ring('depth', by))]
    ppermute x3, waiting for transfers between devices: 5.91 us -> 4.83 us  [per_device(): known[held + by] = lax.ppermute(known[held], 'depth', ring('depth', by))]
    pallas_call x1, Pallas kernels: 6.6 us -> 5.53 us  [per_device(): pl.pallas_call(functools.partial(render_rest, alpha_top=alpha_top), out_s...]
  transfers between devices with their start and end apart: 20 -> 20, of which waited for: 9 -> 6; matrix products, arithmetic and copies ran while one was open for 1% -> 1% of each run, Pallas kernels for 9% -> 8%
where the time goes in v14:
time: 96.5 us; the launch traced here: 95.6 us
  starting transfers between devices  44.5 us (46%)
  Pallas kernels  34.3 us (36%)
  waiting for transfers between devices  13.9 us (14%)
  local copies, waits for them, and re-layouts  1.97 us (2%)
    pallas_call x1, Pallas kernels, per_device(): pl.pallas_call(functools.partial(render, alpha_top=alpha_top), out_shape=...  20.3 us
    ppermute x7, starting transfers between devices, per_device(): lax.ppermute(value, 'depth', ring('depth', by))  17.1 us
    ppermute x4, starting transfers between devices, per_device(): known[by] = lax.ppermute(own, 'depth', ring('depth', by))  7.37 us
    ppermute x3, starting transfers between devices, per_device(): known[held + by] = lax.ppermute(known[held], 'depth', ring('depth', by))  5.61 us
    pallas_call x1, Pallas kernels, per_device(): pl.pallas_call(functools.partial(render_rest, alpha_top=alpha_top), out_s...  5.53 us
    ppermute x1, starting transfers between devices, per_device(): bottom_corner = lax.ppermute(corner_up, 'height', ring('height', -1))  5.05 us
    ppermute x1, starting transfers between devices, per_device(): bottom = lax.ppermute(up, 'height', ring('height', -1))  5.05 us
    ppermute x3, waiting for transfers between devices, per_device(): known[held + by] = lax.ppermute(known[held], 'depth', ring('depth', by))  4.83 us
  transfers between devices with their start and end apart: 20, of which 6 were waited for; matrix products, arithmetic and copies ran while one was open for 1% of the time, Pallas kernels for 8%

profile of v14, /device:TPU:0, one launch (start us, length us, event | category | flops | bytes accessed | tf_op | source)
XLA Modules:
  0.0 95.6 jit_solution(18435086638518487966)
XLA Ops:
  0.0 2.6 %pack.1 = (f32[16,96,128]{2,1,0:T(8,128)}, f32[16,96,128]{2,1,0:T(8,128)}, f32[3,16,8,128]{3,2,1,0:T(8,128)}, f32[3,16,8,128]{3,2,1,0:T(8,128)}) custom-call(f32[32,16,8,128]{3,2,1,0:T(8,128)} %bitcast.27), custom_call_target="tpu_custom_call" | custom-call | tf_op jit(solution)/shard_map/pack/pallas_call | solution.py:456
  2.6 0.1 collective-permute-start.2
  2.7 5.1 %collective-permute-start.3 = (f32[16,96,128]{2,1,0:T(8,128)}, f32[16,96,128]{2,1,0:T(8,128)}, u32[]{:S(2)}, u32[]{:S(2)}) collective-permute-start(f32[16,96,128]{2,1,0:T(8,128)} %get-tuple-element.24), channel_id=1, source_target_pairs={{0,31},{1,0},{2,1},{3,2},{4,3},{5,4},{6,5},{7,6},{8,7},{9,8},{10,9... | collective-permute-start | bytes 2359304 | tf_op jit(solution)/shard_map/ppermute | solution.py:475
  7.7 0.2 collective-permute-start
  7.9 3.9 %collective-permute-start.1 = (f32[3,16,8,128]{3,2,1,0:T(8,128)}, f32[3,16,8,128]{3,2,1,0:T(8,128)}, u32[]{:S(2)}, u32[]{:S(2)}) collective-permute-start(f32[3,16,8,128]{3,2,1,0:T(8,128)} %get-tuple-element.22), channel_id=1, source_target_pairs={{0,224},{32,0},{64,32},{96,64},{128,96},{160,128},{192,160},{224,1... | collective-permute-start | bytes 589832 | tf_op jit(solution)/shard_map/ppermute | solution.py:473
  11.8 0.7 stack.87.tile_ref
  12.5 3.3 %collective-permute-done.low_ref = f32[3,16,8,128]{3,2,1,0:T(8,128)} collective-permute-done((f32[3,16,8,128]{3,2,1,0:T(8,128)}, f32[3,16,8,128]{3,2,1,0:T(8,128)}, u32[]{:S(2)}, u32[]{:S(2)}) %collective-permute-start) | collective-permute-done | bytes 196640 | tf_op jit(solution)/shard_map/ppermute | solution.py:472
  15.8 0.0 collective-permute-done.1.high_ref
  15.8 1.7 %pack_corners.1 = (f32[16,8,128]{2,1,0:T(8,128)}, f32[16,8,128]{2,1,0:T(8,128)}) custom-call(f32[3,16,8,128]{3,2,1,0:T(8,128)} %collective-permute-done.low_ref, f32[3,16,8,128]{3,2,1,0:T(8,128)} %collective-permute-done.1.high_ref), custom_call_target="tpu_custom_call" | custom-call | flops 400000000 | bytes 80000000 | tf_op jit(solution)/shard_map/pack_corners/pallas_call | solution.py:476
  17.5 0.1 collective-permute-start.4
  17.6 5.1 %collective-permute-start.5 = (f32[16,8,128]{2,1,0:T(8,128)}, f32[16,8,128]{2,1,0:T(8,128)}, u32[]{:S(2)}, u32[]{:S(2)}) collective-permute-start(f32[16,8,128]{2,1,0:T(8,128)} %get-tuple-element.26), channel_id=1, source_target_pairs={{0,31},{1,0},{2,1},{3,2},{4,3},{5,4},{6,5},{7,6},{8,7},{9,8},{10,9... | collective-permute-start | bytes 196616 | tf_op jit(solution)/shard_map/ppermute | solution.py:489
  22.7 0.7 add_convert_fusion.edge_ref
  23.3 1.6 %collective-permute-done.4.top_corner_ref = f32[16,8,128]{2,1,0:T(8,128)} collective-permute-done((f32[16,8,128]{2,1,0:T(8,128)}, f32[16,8,128]{2,1,0:T(8,128)}, u32[]{:S(2)}, u32[]{:S(2)}) %collective-permute-start.4) | collective-permute-done | bytes 65568 | tf_op jit(solution)/shard_map/ppermute | solution.py:488
  24.9 0.0 collective-permute-done.5.bottom_corner_ref
  24.9 0.0 collective-permute-done.2.top_ref
  24.9 0.0 collective-permute-done.3.bottom_ref
  24.9 20.3 %render.1 = (f32[13,2,8,128]{3,2,1,0:T(8,128)}, f32[13,2,8,128]{3,2,1,0:T(8,128)}, f32[13,2,8,128]{3,2,1,0:T(8,128)}, f32[13,2,8,128]{3,2,1,0:T(8,128)}, f32[13,...) custom-call(f32[4]{0:T(128)} %add_convert_fusion.edge_ref, s32[16]{0:T(128)} %stack.87.tile_ref, ...), custom_call_target="tpu_custom_call" | custom-call | tf_op jit(solution)/shard_map/render/pallas_call | solution.py:497
  45.2 4.7 %collective-permute-start.6 = (f32[13,2,8,128]{3,2,1,0:T(8,128)}, f32[13,2,8,128]{3,2,1,0:T(8,128)}, u32[]{:S(2)}, u32[]{:S(2)}) collective-permute-start(f32[13,2,8,128]{3,2,1,0:T(8,128)} %get-tuple-element.27), channel_id=1, source_target_pairs={{0,128},{32,160},{64,192},{96,224},{128,0},{160,32},{192,64},{224,... | collective-permute-start | bytes 319496 | tf_op jit(solution)/shard_map/ppermute | solution.py:554
  49.9 1.9 %collective-permute-start.7 = (f32[13,2,8,128]{3,2,1,0:T(8,128)}, f32[13,2,8,128]{3,2,1,0:T(8,128)}, u32[]{:S(2)}, u32[]{:S(2)}) collective-permute-start(f32[13,2,8,128]{3,2,1,0:T(8,128)} %get-tuple-element.28), channel_id=1, source_target_pairs={{0,96},{32,128},{64,160},{96,192},{128,224},{160,0},{192,32},{224,... | collective-permute-start | bytes 319496 | tf_op jit(solution)/shard_map/ppermute | solution.py:554
  51.8 3.1 %collective-permute-start.8 = (f32[13,2,8,128]{3,2,1,0:T(8,128)}, f32[13,2,8,128]{3,2,1,0:T(8,128)}, u32[]{:S(2)}, u32[]{:S(2)}) collective-permute-start(f32[13,2,8,128]{3,2,1,0:T(8,128)} %get-tuple-element.29), channel_id=1, source_target_pairs={{0,160},{32,192},{64,224},{96,0},{128,32},{160,64},{192,96},{224,1... | collective-permute-start | bytes 319496 | tf_op jit(solution)/shard_map/ppermute | solution.py:554
  54.9 1.3 %collective-permute-start.9 = (f32[13,2,8,128]{3,2,1,0:T(8,128)}, f32[13,2,8,128]{3,2,1,0:T(8,128)}, u32[]{:S(2)}, u32[]{:S(2)}) collective-permute-start(f32[13,2,8,128]{3,2,1,0:T(8,128)} %get-tuple-element.30), channel_id=1, source_target_pairs={{0,64},{32,96},{64,128},{96,160},{128,192},{160,224},{192,0},{224,... | collective-permute-start | bytes 319496 | tf_op jit(solution)/shard_map/ppermute | solution.py:554
  56.2 2.9 %collective-permute-start.10 = (f32[13,2,8,128]{3,2,1,0:T(8,128)}, f32[13,2,8,128]{3,2,1,0:T(8,128)}, u32[]{:S(2)}, u32[]{:S(2)}) collective-permute-start(f32[13,2,8,128]{3,2,1,0:T(8,128)} %get-tuple-element.31), channel_id=1, source_target_pairs={{0,192},{32,224},{64,0},{96,32},{128,64},{160,96},{192,128},{224,1... | collective-permute-start | bytes 319496 | tf_op jit(solution)/shard_map/ppermute | solution.py:554
  59.0 5.5 %render_rest.1 = (f32[13,2,8,128]{3,2,1,0:T(8,128)}, f32[13,2,8,128]{3,2,1,0:T(8,128)}, f32[13,2,8,128]{3,2,1,0:T(8,128)}) custom-call(f32[3,4]{1,0:T(4,128)} %colour_ref.3, f32[4]{0:T(128)} %opacity_ref.3, f32[4,3]{1,0:T(4,128)} %dir_ref.3, f32[4,3]{1,0:T(4,128)} %light_ref.3, f32[6,34,16,128]{3,2,1,0:T(8,128)} %get-tuple-element.32.twice_ref, ...), custom_call_target="tpu_custom_call" | custom-call | flops 50000000 | bytes 20000000 | tf_op jit(solution)/shard_map/render_rest/pallas_call | solution.py:535
  64.6 0.0 collective-permute-done.6.refs_0_
  64.6 0.9 collective-permute-start.11
  65.5 0.0 collective-permute-done.7.refs_1_
  65.5 2.4 %collective-permute-start.12 = (f32[13,2,8,128]{3,2,1,0:T(8,128)}, f32[13,2,8,128]{3,2,1,0:T(8,128)}, u32[]{:S(2)}, u32[]{:S(2)}) collective-permute-start(f32[13,2,8,128]{3,2,1,0:T(8,128)} %get-tuple-element.35), channel_id=1, source_target_pairs={{0,224},{32,0},{64,32},{96,64},{128,96},{160,128},{192,160},{224,1... | collective-permute-start | bytes 319496 | tf_op jit(solution)/shard_map/ppermute | solution.py:554
  67.9 0.0 collective-permute-done.8.refs_2_
  67.9 0.0 collective-permute-done.9.refs_3_
  67.9 0.0 collective-permute-done.10.refs_4_
  67.9 3.0 %collective-permute-done.11.refs_5_ = f32[13,2,8,128]{3,2,1,0:T(8,128)} collective-permute-done((f32[13,2,8,128]{3,2,1,0:T(8,128)}, f32[13,2,8,128]{3,2,1,0:T(8,128)}, u32[]{:S(2)}, u32[]{:S(2)}) %collective-permute-start.11) | collective-permute-done | bytes 106528 | tf_op jit(solution)/shard_map/ppermute | solution.py:554
  70.9 0.0 collective-permute-done.12.refs_6_
  70.9 2.0 %fold.1.refs_0_ = f32[13,2,8,128]{3,2,1,0:T(8,128)} custom-call(s32[1]{0:T(128)} %bitcast.place_ref, f32[13,2,8,128]{3,2,1,0:T(8,128)} %collective-permute-done.6.refs_0_, f32[13,2,8,128]{3,2,1,0:T(8,128)} %collective-permute-done.7.refs_1_, f32[13,2,8,128]{3,2,1,0:T(8,128)} %collective-permute-done.8.refs_2_, ...), custom_call_target="tpu_custom_call" | custom-call | tf_op jit(solution)/shard_map/fold/pallas_call | solution.py:557
  72.9 1.5 %collective-permute-start.16 = (f32[13,2,8,128]{3,2,1,0:T(8,128)}, f32[13,2,8,128]{3,2,1,0:T(8,128)S(1)}, u32[]{:S(2)}, u32[]{:S(2)}) collective-permute-start(f32[13,2,8,128]{3,2,1,0:T(8,128)} %fold.1.refs_0_), channel_id=1, source_target_pairs={{0,192},{32,224},{64,0},{96,32},{128,64},{160,96},{192,128},{224,1... | collective-permute-start | bytes 319496 | tf_op jit(solution)/shard_map/ppermute | solution.py:567
  74.4 1.5 %collective-permute-start.15 = (f32[13,2,8,128]{3,2,1,0:T(8,128)}, f32[13,2,8,128]{3,2,1,0:T(8,128)S(1)}, u32[]{:S(2)}, u32[]{:S(2)}) collective-permute-start(f32[13,2,8,128]{3,2,1,0:T(8,128)} %fold.1.refs_0_), channel_id=1, source_target_pairs={{0,64},{32,96},{64,128},{96,160},{128,192},{160,224},{192,0},{224,... | collective-permute-start | bytes 319496 | tf_op jit(solution)/shard_map/ppermute | solution.py:567
  75.8 4.4 %collective-permute-start.14 = (f32[13,2,8,128]{3,2,1,0:T(8,128)}, f32[13,2,8,128]{3,2,1,0:T(8,128)S(1)}, u32[]{:S(2)}, u32[]{:S(2)}) collective-permute-start(f32[13,2,8,128]{3,2,1,0:T(8,128)} %fold.1.refs_0_), channel_id=1, source_target_pairs={{0,224},{32,0},{64,32},{96,64},{128,96},{160,128},{192,160},{224,1... | collective-permute-start | bytes 319496 | tf_op jit(solution)/shard_map/ppermute | solution.py:567
  80.3 0.0 collective-permute-start.13
  80.3 0.6 copy-done
  80.9 3.5 %collective-permute-start.18 = (f32[13,2,8,128]{3,2,1,0:T(8,128)S(1)}, f32[13,2,8,128]{3,2,1,0:T(8,128)S(1)}, u32[]{:S(2)}, u32[]{:S(2)}) collective-permute-start(f32[13,2,8,128]{3,2,1,0:T(8,128)S(1)} %collective-permute-done.16.refs_4_), channel_id=1, source_target_pairs={{0,224},{32,0},{64,32},{96,64},{128,96},{160,128},{192,160},{224,1... | collective-permute-start | bytes 319496 | tf_op jit(solution)/shard_map/ppermute | solution.py:569
  84.4 0.0 collective-permute-done.15.refs_3_
  84.4 2.1 %collective-permute-start.17 = (f32[13,2,8,128]{3,2,1,0:T(8,128)S(1)}, f32[13,2,8,128]{3,2,1,0:T(8,128)}, u32[]{:S(2)}, u32[]{:S(2)}) collective-permute-start(f32[13,2,8,128]{3,2,1,0:T(8,128)S(1)} %collective-permute-done.15.refs_3_), channel_id=1, source_target_pairs={{0,32},{32,64},{64,96},{96,128},{128,160},{160,192},{192,224},{224... | collective-permute-start | bytes 319496 | tf_op jit(solution)/shard_map/ppermute | solution.py:569
  86.6 0.0 collective-permute-done.14.refs_2_
  86.6 1.2 %collective-permute-done.13.refs_1_ = f32[13,2,8,128]{3,2,1,0:T(8,128)S(1)} collective-permute-done((f32[13,2,8,128]{3,2,1,0:T(8,128)}, f32[13,2,8,128]{3,2,1,0:T(8,128)S(1)}, u32[]{:S(2)}, u32[]{:S(2)}) %collective-permute-start.13) | collective-permute-done | bytes 106528 | tf_op jit(solution)/shard_map/ppermute | solution.py:567
  87.7 0.0 collective-permute-done.18.refs_6_
  87.7 3.6 %collective-permute-done.19.refs_7_ = f32[13,2,8,128]{3,2,1,0:T(8,128)S(1)} collective-permute-done((f32[13,2,8,128]{3,2,1,0:T(8,128)S(1)}, f32[13,2,8,128]{3,2,1,0:T(8,128)S(1)}, u32[]{:S(2)}, u32[]{:S(2)}) %collective-permute-start.19) | collective-permute-done | bytes 106528 | tf_op jit(solution)/shard_map/ppermute | solution.py:569
  91.4 0.6 copy-done.5
  92.0 1.2 %collective-permute-done.17.refs_5_ = f32[13,2,8,128]{3,2,1,0:T(8,128)} collective-permute-done((f32[13,2,8,128]{3,2,1,0:T(8,128)S(1)}, f32[13,2,8,128]{3,2,1,0:T(8,128)}, u32[]{:S(2)}, u32[]{:S(2)}) %collective-permute-start.17) | collective-permute-done | bytes 106528 | tf_op jit(solution)/shard_map/ppermute | solution.py:569
  93.2 2.2 %spread.1 = f32[13,16,8,128]{3,2,1,0:T(8,128)} custom-call(s32[1]{0:T(128)} %bitcast.place_ref, f32[13,2,8,128]{3,2,1,0:T(8,128)} %fold.1.refs_0_, f32[13,2,8,128]{3,2,1,0:T(8,128)} %copy-done.3, f32[13,2,8,128]{3,2,1,0:T(8,128)} %copy-done.2, f32[13,2,8,128]{3,2,1,0:T(8,128)} %copy-done.1, f32[13,2,8,128]{3,2,1,0:T(8,128)} %copy-done, ...), custom_call_target="tpu_custom_call" | custom-call | tf_op jit(solution)/shard_map/spread/pallas_call | solution.py:570
  (12 shorter events, 0.0 us)
Async XLA Ops:
  2.6 22.4 %collective-permute-start.2 = (f32[16,96,128]{2,1,0:T(8,128)}, f32[16,96,128]{2,1,0:T(8,128)}, u32[]{:S(2)}, u32[]{:S(2)}) collective-permute-start(f32[16,96,128]{2,1,0:T(8,128)} %get-tuple-element.23), channel_id=1, source_target_pairs={{0,1},{1,2},{2,3},{3,4},{4,5},{5,6},{6,7},{7,8},{8,9},{9,10},{10,1... | collective-permute-start | bytes 2359304 | tf_op jit(solution)/shard_map/ppermute | solution.py:474
  2.7 22.3 %collective-permute-start.3 = (f32[16,96,128]{2,1,0:T(8,128)}, f32[16,96,128]{2,1,0:T(8,128)}, u32[]{:S(2)}, u32[]{:S(2)}) collective-permute-start(f32[16,96,128]{2,1,0:T(8,128)} %get-tuple-element.24), channel_id=1, source_target_pairs={{0,31},{1,0},{2,1},{3,2},{4,3},{5,4},{6,5},{7,6},{8,7},{9,8},{10,9... | collective-permute-start | bytes 2359304 | tf_op jit(solution)/shard_map/ppermute | solution.py:475
  7.7 8.1 %collective-permute-start = (f32[3,16,8,128]{3,2,1,0:T(8,128)}, f32[3,16,8,128]{3,2,1,0:T(8,128)}, u32[]{:S(2)}, u32[]{:S(2)}) collective-permute-start(f32[3,16,8,128]{3,2,1,0:T(8,128)} %get-tuple-element.21), channel_id=1, source_target_pairs={{0,32},{32,64},{64,96},{96,128},{128,160},{160,192},{192,224},{224... | collective-permute-start | bytes 589832 | tf_op jit(solution)/shard_map/ppermute | solution.py:472
  7.9 7.9 %collective-permute-start.1 = (f32[3,16,8,128]{3,2,1,0:T(8,128)}, f32[3,16,8,128]{3,2,1,0:T(8,128)}, u32[]{:S(2)}, u32[]{:S(2)}) collective-permute-start(f32[3,16,8,128]{3,2,1,0:T(8,128)} %get-tuple-element.22), channel_id=1, source_target_pairs={{0,224},{32,0},{64,32},{96,64},{128,96},{160,128},{192,160},{224,1... | collective-permute-start | bytes 589832 | tf_op jit(solution)/shard_map/ppermute | solution.py:473
  17.5 7.4 %collective-permute-start.4 = (f32[16,8,128]{2,1,0:T(8,128)}, f32[16,8,128]{2,1,0:T(8,128)}, u32[]{:S(2)}, u32[]{:S(2)}) collective-permute-start(f32[16,8,128]{2,1,0:T(8,128)} %get-tuple-element.25), channel_id=1, source_target_pairs={{0,1},{1,2},{2,3},{3,4},{4,5},{5,6},{6,7},{7,8},{8,9},{9,10},{10,1... | collective-permute-start | bytes 196616 | tf_op jit(solution)/shard_map/ppermute | solution.py:488
  17.6 7.3 %collective-permute-start.5 = (f32[16,8,128]{2,1,0:T(8,128)}, f32[16,8,128]{2,1,0:T(8,128)}, u32[]{:S(2)}, u32[]{:S(2)}) collective-permute-start(f32[16,8,128]{2,1,0:T(8,128)} %get-tuple-element.26), channel_id=1, source_target_pairs={{0,31},{1,0},{2,1},{3,2},{4,3},{5,4},{6,5},{7,6},{8,7},{9,8},{10,9... | collective-permute-start | bytes 196616 | tf_op jit(solution)/shard_map/ppermute | solution.py:489
  45.2 19.4 %collective-permute-start.6 = (f32[13,2,8,128]{3,2,1,0:T(8,128)}, f32[13,2,8,128]{3,2,1,0:T(8,128)}, u32[]{:S(2)}, u32[]{:S(2)}) collective-permute-start(f32[13,2,8,128]{3,2,1,0:T(8,128)} %get-tuple-element.27), channel_id=1, source_target_pairs={{0,128},{32,160},{64,192},{96,224},{128,0},{160,32},{192,64},{224,... | collective-permute-start | bytes 319496 | tf_op jit(solution)/shard_map/ppermute | solution.py:554
  49.9 15.6 %collective-permute-start.7 = (f32[13,2,8,128]{3,2,1,0:T(8,128)}, f32[13,2,8,128]{3,2,1,0:T(8,128)}, u32[]{:S(2)}, u32[]{:S(2)}) collective-permute-start(f32[13,2,8,128]{3,2,1,0:T(8,128)} %get-tuple-element.28), channel_id=1, source_target_pairs={{0,96},{32,128},{64,160},{96,192},{128,224},{160,0},{192,32},{224,... | collective-permute-start | bytes 319496 | tf_op jit(solution)/shard_map/ppermute | solution.py:554
  51.8 16.1 %collective-permute-start.8 = (f32[13,2,8,128]{3,2,1,0:T(8,128)}, f32[13,2,8,128]{3,2,1,0:T(8,128)}, u32[]{:S(2)}, u32[]{:S(2)}) collective-permute-start(f32[13,2,8,128]{3,2,1,0:T(8,128)} %get-tuple-element.29), channel_id=1, source_target_pairs={{0,160},{32,192},{64,224},{96,0},{128,32},{160,64},{192,96},{224,1... | collective-permute-start | bytes 319496 | tf_op jit(solution)/shard_map/ppermute | solution.py:554
  54.9 13.0 %collective-permute-start.9 = (f32[13,2,8,128]{3,2,1,0:T(8,128)}, f32[13,2,8,128]{3,2,1,0:T(8,128)}, u32[]{:S(2)}, u32[]{:S(2)}) collective-permute-start(f32[13,2,8,128]{3,2,1,0:T(8,128)} %get-tuple-element.30), channel_id=1, source_target_pairs={{0,64},{32,96},{64,128},{96,160},{128,192},{160,224},{192,0},{224,... | collective-permute-start | bytes 319496 | tf_op jit(solution)/shard_map/ppermute | solution.py:554
  56.2 11.7 %collective-permute-start.10 = (f32[13,2,8,128]{3,2,1,0:T(8,128)}, f32[13,2,8,128]{3,2,1,0:T(8,128)}, u32[]{:S(2)}, u32[]{:S(2)}) collective-permute-start(f32[13,2,8,128]{3,2,1,0:T(8,128)} %get-tuple-element.31), channel_id=1, source_target_pairs={{0,192},{32,224},{64,0},{96,32},{128,64},{160,96},{192,128},{224,1... | collective-permute-start | bytes 319496 | tf_op jit(solution)/shard_map/ppermute | solution.py:554
  64.6 6.3 %collective-permute-start.11 = (f32[13,2,8,128]{3,2,1,0:T(8,128)}, f32[13,2,8,128]{3,2,1,0:T(8,128)}, u32[]{:S(2)}, u32[]{:S(2)}) collective-permute-start(f32[13,2,8,128]{3,2,1,0:T(8,128)} %get-tuple-element.34), channel_id=1, source_target_pairs={{0,32},{32,64},{64,96},{96,128},{128,160},{160,192},{192,224},{224... | collective-permute-start | bytes 319496 | tf_op jit(solution)/shard_map/ppermute | solution.py:554
  65.5 5.4 %collective-permute-start.12 = (f32[13,2,8,128]{3,2,1,0:T(8,128)}, f32[13,2,8,128]{3,2,1,0:T(8,128)}, u32[]{:S(2)}, u32[]{:S(2)}) collective-permute-start(f32[13,2,8,128]{3,2,1,0:T(8,128)} %get-tuple-element.35), channel_id=1, source_target_pairs={{0,224},{32,0},{64,32},{96,64},{128,96},{160,128},{192,160},{224,1... | collective-permute-start | bytes 319496 | tf_op jit(solution)/shard_map/ppermute | solution.py:554
  72.9 7.4 %collective-permute-start.16 = (f32[13,2,8,128]{3,2,1,0:T(8,128)}, f32[13,2,8,128]{3,2,1,0:T(8,128)S(1)}, u32[]{:S(2)}, u32[]{:S(2)}) collective-permute-start(f32[13,2,8,128]{3,2,1,0:T(8,128)} %fold.1.refs_0_), channel_id=1, source_target_pairs={{0,192},{32,224},{64,0},{96,32},{128,64},{160,96},{192,128},{224,1... | collective-permute-start | bytes 319496 | tf_op jit(solution)/shard_map/ppermute | solution.py:567
  74.4 10.1 %collective-permute-start.15 = (f32[13,2,8,128]{3,2,1,0:T(8,128)}, f32[13,2,8,128]{3,2,1,0:T(8,128)S(1)}, u32[]{:S(2)}, u32[]{:S(2)}) collective-permute-start(f32[13,2,8,128]{3,2,1,0:T(8,128)} %fold.1.refs_0_), channel_id=1, source_target_pairs={{0,64},{32,96},{64,128},{96,160},{128,192},{160,224},{192,0},{224,... | collective-permute-start | bytes 319496 | tf_op jit(solution)/shard_map/ppermute | solution.py:567
  75.8 10.7 %collective-permute-start.14 = (f32[13,2,8,128]{3,2,1,0:T(8,128)}, f32[13,2,8,128]{3,2,1,0:T(8,128)S(1)}, u32[]{:S(2)}, u32[]{:S(2)}) collective-permute-start(f32[13,2,8,128]{3,2,1,0:T(8,128)} %fold.1.refs_0_), channel_id=1, source_target_pairs={{0,224},{32,0},{64,32},{96,64},{128,96},{160,128},{192,160},{224,1... | collective-permute-start | bytes 319496 | tf_op jit(solution)/shard_map/ppermute | solution.py:567
  80.3 7.5 %collective-permute-start.13 = (f32[13,2,8,128]{3,2,1,0:T(8,128)}, f32[13,2,8,128]{3,2,1,0:T(8,128)S(1)}, u32[]{:S(2)}, u32[]{:S(2)}) collective-permute-start(f32[13,2,8,128]{3,2,1,0:T(8,128)} %fold.1.refs_0_), channel_id=1, source_target_pairs={{0,32},{32,64},{64,96},{96,128},{128,160},{160,192},{192,224},{224... | collective-permute-start | bytes 319496 | tf_op jit(solution)/shard_map/ppermute | solution.py:567
  80.3 0.7 copy-start
  80.9 6.8 %collective-permute-start.18 = (f32[13,2,8,128]{3,2,1,0:T(8,128)S(1)}, f32[13,2,8,128]{3,2,1,0:T(8,128)S(1)}, u32[]{:S(2)}, u32[]{:S(2)}) collective-permute-start(f32[13,2,8,128]{3,2,1,0:T(8,128)S(1)} %collective-permute-done.16.refs_4_), channel_id=1, source_target_pairs={{0,224},{32,0},{64,32},{96,64},{128,96},{160,128},{192,160},{224,1... | collective-permute-start | bytes 319496 | tf_op jit(solution)/shard_map/ppermute | solution.py:569
  84.4 3.3 %copy-start.1 = (f32[13,2,8,128]{3,2,1,0:T(8,128)}, f32[13,2,8,128]{3,2,1,0:T(8,128)S(1)}, u32[]{:S(2)}) copy-start(f32[13,2,8,128]{3,2,1,0:T(8,128)S(1)} %collective-permute-done.15.refs_3_) | copy-start | bytes 319492
  84.4 6.9 %collective-permute-start.19 = (f32[13,2,8,128]{3,2,1,0:T(8,128)S(1)}, f32[13,2,8,128]{3,2,1,0:T(8,128)S(1)}, u32[]{:S(2)}, u32[]{:S(2)}) collective-permute-start(f32[13,2,8,128]{3,2,1,0:T(8,128)S(1)} %collective-permute-done.15.refs_3_), channel_id=1, source_target_pairs={{0,64},{32,96},{64,128},{96,160},{128,192},{160,224},{192,0},{224,... | collective-permute-start | bytes 319496 | tf_op jit(solution)/shard_map/ppermute | solution.py:569
  84.4 8.8 %collective-permute-start.17 = (f32[13,2,8,128]{3,2,1,0:T(8,128)S(1)}, f32[13,2,8,128]{3,2,1,0:T(8,128)}, u32[]{:S(2)}, u32[]{:S(2)}) collective-permute-start(f32[13,2,8,128]{3,2,1,0:T(8,128)S(1)} %collective-permute-done.15.refs_3_), channel_id=1, source_target_pairs={{0,32},{32,64},{64,96},{96,128},{128,160},{160,192},{192,224},{224... | collective-permute-start | bytes 319496 | tf_op jit(solution)/shard_map/ppermute | solution.py:569
  86.6 4.8 %copy-start.2 = (f32[13,2,8,128]{3,2,1,0:T(8,128)}, f32[13,2,8,128]{3,2,1,0:T(8,128)S(1)}, u32[]{:S(2)}) copy-start(f32[13,2,8,128]{3,2,1,0:T(8,128)S(1)} %collective-permute-done.14.refs_2_) | copy-start | bytes 319492
  87.7 3.6 %copy-start.3 = (f32[13,2,8,128]{3,2,1,0:T(8,128)}, f32[13,2,8,128]{3,2,1,0:T(8,128)S(1)}, u32[]{:S(2)}) copy-start(f32[13,2,8,128]{3,2,1,0:T(8,128)S(1)} %collective-permute-done.13.refs_1_) | copy-start | bytes 319492
  87.7 3.6 %copy-start.4 = (f32[13,2,8,128]{3,2,1,0:T(8,128)}, f32[13,2,8,128]{3,2,1,0:T(8,128)S(1)}, u32[]{:S(2)}) copy-start(f32[13,2,8,128]{3,2,1,0:T(8,128)S(1)} %collective-permute-done.18.refs_6_) | copy-start | bytes 319492
  91.4 0.6 copy-start.5
